TPU v7x, 32 devices: a whole 2x2x4 slice. The times are simulated.
32 devices in a mesh: basin: 2 (over x), blk: 16 (over z, y, core).
Axes of the slice: x: 2, y: 2, z: 4, core: 2. Of those that a mesh axis runs over, the one named last changes fastest.
Arguments:
- tracers: bfloat16 [4096, 50, 128], P(('basin', 'blk')), may hold values from -6 to 6
- nbr_cols: int32 [4, 4096], P(None, ('basin', 'blk')), may hold values from 0 to 127
- nbr_wts: float32 [4, 50, 4096], P(None, None, ('basin', 'blk')), may hold values from 0.05 to 0.3
- self_wts: float32 [50, 4096], P(None, ('basin', 'blk')), may hold values from 0.2 to 0.9
- send_cols: int32 [3, 512], P(None, ('basin', 'blk')), may hold values from 0 to 127
- recv_cols: int32 [3, 512], P(None, ('basin', 'blk')), may hold values from 0 to 127
- edge_wts: float32 [3, 50, 512], P(None, None, ('basin', 'blk')), may hold values from 0.1 to 0.4
- wet_levels: int32 [4096], P(('basin', 'blk')), may hold values from 1 to 50
- vert_inv: bfloat16 [50, 50, 4096], P(None, None, ('basin', 'blk')), may hold values from -1 to 2
Outputs:
- advanced: bfloat16 [4096, 50, 128], P(('basin', 'blk'))
Inputs may be any that keep to these rules, and one draw needn't show every extreme that they name: `nbr_cols`: local column indices within a block. `send_cols`: local column indices within the sending block. `recv_cols`: local column indices within the receiving block.
All inputs are finite; a program needn't handle non-finite values.
Results may differ from a plain program's by a relative error of at most 0.013.
Values may be sent and summed in bfloat16 or wider, within the bound.
No kernel may reach another device: no remote copies, remote signals or barrier semaphores. Data moves between devices by JAX's collectives and lax.ppermute only.
A program may use at most 64 MiB of HBM per device.

v0:
```python
import jax
import jax.numpy as jnp
from jax import lax
from jax.sharding import PartitionSpec as P

NSTEP = 2


def passed_along(value, axis, steps):
    count = lax.axis_size(axis)
    initial, last = (max(0, -steps), min(count, count - steps))
    return lax.ppermute(value, axis, [(source, source + steps) for source in range(initial, last)])


def shifted(block, axis, distance):
    devices = range(lax.axis_size(axis))
    route = [((i - distance) % len(devices), i) for i in devices]
    return lax.ppermute(block, axis, route)


def target_table(targets, columns):
    positions = jnp.arange(columns, dtype=jnp.int32)
    return (positions[:, None] == targets[None, :]).astype(jnp.float32)


def add_pushed(total, received):
    contrib, targets = received
    table = target_table(targets, total.shape[0])
    return total + jnp.einsum("je,elt->jlt", table, contrib, precision=lax.Precision.HIGHEST)


def local(
    tracers, nbr_cols, nbr_wts, self_wts, send_cols, recv_cols, edge_wts, wet_levels, vert_inv
):
    columns = tracers.shape[0]
    levels = jnp.arange(tracers.shape[1], dtype=jnp.int32)
    mask = (levels[None, :] < wet_levels[:, None]).astype(jnp.float32)
    positions = jnp.arange(columns, dtype=jnp.int32)
    onehot = (positions[None, :, None] == nbr_cols[:, None, :]).astype(jnp.float32)
    operator = jnp.einsum("nji,nli->lji", onehot, nbr_wts, precision=lax.Precision.HIGHEST).astype(
        jnp.bfloat16
    )
    state = tracers
    for step in range(NSTEP):
        own = state.astype(jnp.float32)
        total = self_wts.T[:, :, None] * own
        total = total + jnp.einsum(
            "lji,ilt->jlt", operator, state, preferred_element_type=jnp.float32
        )
        outgoing = []
        for d in range(3):
            contrib = edge_wts[d].T[:, :, None] * own[send_cols[d]]
            outgoing.append((contrib, recv_cols[d]))
        total = add_pushed(
            total,
            (
                passed_along(outgoing[0][0].astype(jnp.bfloat16), "blk", 1).astype(jnp.float32),
                passed_along(outgoing[0][1], "blk", 1),
            ),
        )
        total = add_pushed(
            total,
            (
                passed_along(outgoing[1][0].astype(jnp.bfloat16), "blk", -1).astype(jnp.float32),
                passed_along(outgoing[1][1], "blk", -1),
            ),
        )
        total = add_pushed(
            total,
            (
                shifted(outgoing[2][0].astype(jnp.bfloat16), "basin", 1).astype(jnp.float32),
                shifted(outgoing[2][1], "basin", 1),
            ),
        )
        explicit = (mask[:, :, None] * total).astype(jnp.bfloat16)
        mixed = jnp.einsum("mlc,cmt->clt", vert_inv, explicit, preferred_element_type=jnp.float32)
        state = (mask[:, :, None] * mixed).astype(jnp.bfloat16)
    return state


def solution(mesh):
    in_specs = (
        P(("basin", "blk"), None, None),
        P(None, ("basin", "blk")),
        P(None, None, ("basin", "blk")),
        P(None, ("basin", "blk")),
        P(None, ("basin", "blk")),
        P(None, ("basin", "blk")),
        P(None, None, ("basin", "blk")),
        P(("basin", "blk")),
        P(None, None, ("basin", "blk")),
    )
    out_specs = P(("basin", "blk"), None, None)
    return jax.shard_map(local, mesh=mesh, in_specs=in_specs, out_specs=out_specs, check_vma=False)
```

profile of v0, /device:TPU:5, one launch (start us, length us, event | category | flops | bytes accessed | tf_op | source)
XLA Modules:
  0.0 117.6 jit_solution(15166409324090860195)
XLA Ops:
  1.3 3.7 %collective-permute-start = (s32[16]{0:T(128)}, s32[16]{0:T(128)}, u32[]{:S(2)}, u32[]{:S(2)}) collective-permute-start(s32[16]{0:T(128)} %get-tuple-element.8), channel_id=1, source_target_pairs={{0,1},{1,2},{2,3},{3,4},{4,5},{5,6},{6,7},{7,8},{8,9},{9,10},{10,1... | collective-permute-start | bytes 200 | tf_op jit(solution)/shard_map/ppermute | solution.py:12
  6.3 1.9 %collective-permute-start.2 = (s32[16]{0:T(128)}, s32[16]{0:T(128)}, u32[]{:S(2)}, u32[]{:S(2)}) collective-permute-start(s32[16]{0:T(128)} %get-tuple-element.10), channel_id=1, source_target_pairs={{1,0},{2,1},{3,2},{4,3},{5,4},{6,5},{7,6},{8,7},{9,8},{10,9},{11,1... | collective-permute-start | bytes 200 | tf_op jit(solution)/shard_map/ppermute | solution.py:12
  9.8 4.2 %copy_convert_fusion = f32[128,50,128]{2,1,0:T(8,128)} fusion(bf16[128,50,128]{2,0,1:T(8,128)(2,1)} %param.9), kind=kLoop, calls=%fused_computation.20 | loop fusion | flops 819200 | bytes 4915200 | tf_op jit(solution)/shard_map/convert_element_type | solution.py:45
  14.1 2.7 %gather_fusion.1 = f32[16,50,128]{2,1,0:T(8,128)S(1)} fusion(f32[128,50,128]{2,1,0:T(8,128)} %copy_convert_fusion, s32[1024]{0:T(1024)S(1)} %get-tuple-element.17), kind=kCustom, calls=%fused_computation.1 | custom fusion | bytes 819264 | tf_op jit(solution)/shard_map/gather | solution.py:52
  17.7 2.5 %collective-permute-start.3 = (bf16[16,50,128]{2,1,0:T(8,128)(2,1)}, bf16[16,50,128]{2,1,0:T(8,128)(2,1)}, u32[]{:S(2)}, u32[]{:S(2)}) collective-permute-start(bf16[16,50,128]{2,1,0:T(8,128)(2,1)} %multiply_convert_fusion.6), channel_id=1, source_target_pairs={{1,0},{2,1},{3,2},{4,3},{5,4},{6,5},{7,6},{8,7},{9,8},{10,9},{11,1... | collective-permute-start | bytes 614408 | tf_op jit(solution)/shard_map/ppermute | solution.py:12
  20.2 2.6 %gather_fusion.2 = f32[16,50,128]{2,1,0:T(8,128)S(1)} fusion(f32[128,50,128]{2,1,0:T(8,128)} %copy_convert_fusion, s32[1024]{0:T(1024)S(1)} %get-tuple-element.16), kind=kCustom, calls=%fused_computation.2 | custom fusion | bytes 819264 | tf_op jit(solution)/shard_map/gather | solution.py:52
  24.4 3.3 %convert_bitcast_fusion = bf16[50,128,128]{1,0,2:T(8,128)(2,1)S(1)} fusion(f32[4,50,128]{1,0,2:T(4,128)S(1)} %copy.13, s32[4,128]{0,1:T(8,128)S(1)} %copy.12), kind=kOutput, calls=%fused_computation.21 | convolution fusion | flops 40206336 | bytes 1742848 | tf_op jit(solution)/shard_map/nji,nli->lji/dot_general | solution.py:40
  29.0 2.4 %fusion.24 = f32[50,128,128]{2,1,0:T(8,128)} fusion(bf16[128,50,128]{2,0,1:T(8,128)(2,1)S(1)} %copy-done, bf16[50,128,128]{1,0,2:T(8,128)(2,1)S(1)} %convert_bitcast_fusion), kind=kOutput, calls=%fused_computation.30 | convolution fusion | flops 209715200 | bytes 6553600 | tf_op jit(solution)/shard_map/lji,ilt->jlt/dot_general | solution.py:47
  31.5 2.6 %gather_fusion = f32[16,50,128]{2,1,0:T(8,128)S(1)} fusion(f32[128,50,128]{2,1,0:T(8,128)} %copy_convert_fusion, s32[1024]{0:T(1024)S(1)} %pad_clamp_fusion.2), kind=kCustom, calls=%fused_computation | custom fusion | bytes 819264 | tf_op jit(solution)/shard_map/gather | solution.py:52
  35.7 4.5 %copy.14 = bf16[50,50,128]{0,1,2:T(8,128)(2,1)S(1)} copy(bf16[50,50,128]{2,1,0:T(8,128)(2,1)} %param.17) | data formatting | bytes 1280000 | tf_op args[8]
  40.2 4.4 %collective-permute-start.1 = (bf16[16,50,128]{2,1,0:T(8,128)(2,1)}, bf16[16,50,128]{2,1,0:T(8,128)(2,1)S(1)}, u32[]{:S(2)}, u32[]{:S(2)}) collective-permute-start(bf16[16,50,128]{2,1,0:T(8,128)(2,1)} %multiply_convert_fusion.7), channel_id=1, source_target_pairs={{0,1},{1,2},{2,3},{3,4},{4,5},{5,6},{6,7},{7,8},{8,9},{9,10},{10,1... | collective-permute-start | bytes 614408 | tf_op jit(solution)/shard_map/ppermute | solution.py:12
  44.6 1.5 %fusion.34 = f32[128,50,128]{2,0,1:T(8,128)S(1)} fusion(bf16[16,50,128]{2,1,0:T(8,128)(2,1)} %collective-permute-done.5, s32[16]{0:T(128)} %collective-permute-done.4), kind=kOutput, calls=%fused_computation.47 | convolution fusion | flops 26216448 | bytes 3481664 | tf_op jit(solution)/shard_map/je,elt->jlt/dot_general | solution.py:29
  46.1 1.5 %collective-permute-done.1 = bf16[16,50,128]{2,1,0:T(8,128)(2,1)S(1)} collective-permute-done((bf16[16,50,128]{2,1,0:T(8,128)(2,1)}, bf16[16,50,128]{2,1,0:T(8,128)(2,1)S(1)}, u32[]{:S(2)}, u32[]{:S(2)}) %collective-permute-start.1) | collective-permute-done | bytes 204832 | tf_op jit(solution)/shard_map/ppermute | solution.py:12
  48.9 1.5 %fusion.36 = f32[128,50,128]{2,0,1:T(8,128)S(1)} fusion(bf16[16,50,128]{2,1,0:T(8,128)(2,1)} %collective-permute-done.3, s32[16]{0:T(128)} %collective-permute-done.2), kind=kOutput, calls=%fused_computation.49 | convolution fusion | flops 26216448 | bytes 3481664 | tf_op jit(solution)/shard_map/je,elt->jlt/dot_general | solution.py:29
  50.4 21.5 %fusion.60 = (f32[128,50,128]{2,1,0:T(8,128)}, bf16[128,50,128]{2,1,0:T(8,128)(2,1)}) fusion(bf16[50,50,128]{0,1,2:T(8,128)(2,1)S(1)} %copy.14, f32[128,50,128]{2,0,1:T(8,128)S(1)} %fusion.34, f32[128,50,128]{2,0,1:T(8,128)S(1)} %fusion.36, f32[128,50,128]{2,0,1:T(8,128)S(1)} %fusion.38, f32[50,128,128]{2,1,0:T(8,128)S(1)} %copy-done.2, ...), kind=kOutput, calls=%fused_computation.83 | convolution fusion | flops 90931200 | bytes 20352000 | tf_op jit(solution)/shard_map/mlc,cmt->clt/dot_general | solution.py:76
  71.9 2.7 %gather_fusion.4 = f32[16,50,128]{2,1,0:T(8,128)S(1)} fusion(f32[128,50,128]{2,1,0:T(8,128)} %get-tuple-element.14, s32[1024]{0:T(1024)} %copy-done.11), kind=kCustom, calls=%fused_computation.4 | custom fusion | bytes 819264 | tf_op jit(solution)/shard_map/gather | solution.py:52
  74.6 2.7 %gather_fusion.3 = f32[16,50,128]{2,1,0:T(8,128)S(1)} fusion(f32[128,50,128]{2,1,0:T(8,128)} %get-tuple-element.14, s32[1024]{0:T(1024)} %copy-done.12), kind=kCustom, calls=%fused_computation.3 | custom fusion | bytes 819264 | tf_op jit(solution)/shard_map/gather | solution.py:52
  77.4 2.7 %gather_fusion.5 = f32[16,50,128]{2,1,0:T(8,128)S(1)} fusion(f32[128,50,128]{2,1,0:T(8,128)} %get-tuple-element.14, s32[1024]{0:T(1024)} %copy-done.10), kind=kCustom, calls=%fused_computation.5 | custom fusion | bytes 819264 | tf_op jit(solution)/shard_map/gather | solution.py:52
  81.0 2.3 %collective-permute-start.7 = (bf16[16,50,128]{2,1,0:T(8,128)(2,1)S(1)}, bf16[16,50,128]{2,1,0:T(8,128)(2,1)S(1)}, u32[]{:S(2)}, u32[]{:S(2)}) collective-permute-start(bf16[16,50,128]{2,1,0:T(8,128)(2,1)S(1)} %multiply_convert_fusion.3), channel_id=1, source_target_pairs={{1,0},{2,1},{3,2},{4,3},{5,4},{6,5},{7,6},{8,7},{9,8},{10,9},{11,1... | collective-permute-start | bytes 614408 | tf_op jit(solution)/shard_map/ppermute | solution.py:12
  83.6 4.8 %collective-permute-start.6 = (bf16[16,50,128]{2,1,0:T(8,128)(2,1)S(1)}, bf16[16,50,128]{2,1,0:T(8,128)(2,1)S(1)}, u32[]{:S(2)}, u32[]{:S(2)}) collective-permute-start(bf16[16,50,128]{2,1,0:T(8,128)(2,1)S(1)} %multiply_convert_fusion.4), channel_id=1, source_target_pairs={{0,1},{1,2},{2,3},{3,4},{4,5},{5,6},{6,7},{7,8},{8,9},{9,10},{10,1... | collective-permute-start | bytes 614408 | tf_op jit(solution)/shard_map/ppermute | solution.py:12
  89.8 4.5 %fusion.16 = f32[50,128,128]{2,1,0:T(8,128)} fusion(bf16[128,50,128]{2,1,0:T(8,128)(2,1)} %get-tuple-element.15, bf16[50,128,128]{1,0,2:T(8,128)(2,1)} %copy-done.4), kind=kOutput, calls=%fused_computation.26 | convolution fusion | flops 209715200 | bytes 6553600 | tf_op jit(solution)/shard_map/lji,ilt->jlt/dot_general | solution.py:47
  94.3 4.4 %copy.27 = f32[50,128,128]{1,0,2:T(8,128)} copy(f32[50,128,128]{2,1,0:T(8,128)} %fusion.16) | data formatting | bytes 6553600 | tf_op jit(solution)/shard_map/lji,ilt->jlt/dot_general | solution.py:47
  102.8 13.2 %fusion.21 = bf16[128,50,128]{2,1,0:T(8,128)(2,1)S(1)} fusion(bf16[50,50,128]{0,1,2:T(8,128)(2,1)S(1)} %copy.14, f32[50,128,128]{1,0,2:T(8,128)S(1)} %copy-done.3, f32[128,50,128]{2,0,1:T(8,128)S(1)} %fusion.28, f32[128,50,128]{2,0,1:T(8,128)S(1)} %fusion.30, f32[128,50,128]{2,0,1:T(8,128)S(1)} %fusion.32, f32[128,50]{1,0:T(8,128)S(1)} %copy.10, ...), kind=kOutput, calls=%fused_computation.29 | convolution fusion | flops 90112000 | bytes 17075200 | tf_op jit(solution)/shard_map/mlc,cmt->clt/dot_general | solution.py:76
  116.0 1.6 %copy.16 = bf16[128,50,128]{2,0,1:T(8,128)(2,1)} copy(bf16[128,50,128]{2,1,0:T(8,128)(2,1)S(1)} %fusion.21) | data formatting | bytes 3276800 | tf_op jit(solution)/shard_map/convert_element_type | solution.py:77
  (60 shorter events, 17.3 us)
Async XLA Ops:
  1.3 44.8 %collective-permute-start = (s32[16]{0:T(128)}, s32[16]{0:T(128)}, u32[]{:S(2)}, u32[]{:S(2)}) collective-permute-start(s32[16]{0:T(128)} %get-tuple-element.8), channel_id=1, source_target_pairs={{0,1},{1,2},{2,3},{3,4},{4,5},{5,6},{6,7},{7,8},{8,9},{9,10},{10,1... | collective-permute-start | bytes 200 | tf_op jit(solution)/shard_map/ppermute | solution.py:12
  5.1 35.1 %collective-permute-start.4 = (s32[16]{0:T(128)}, s32[16]{0:T(128)}, u32[]{:S(2)}, u32[]{:S(2)}) collective-permute-start(s32[16]{0:T(128)} %get-tuple-element.9), channel_id=1, source_target_pairs={{16,0},{0,16},{17,1},{1,17},{18,2},{2,18},{19,3},{3,19},{20,4},{4,... | collective-permute-start | bytes 200 | tf_op jit(solution)/shard_map/ppermute | solution.py:18
  6.3 42.5 %collective-permute-start.2 = (s32[16]{0:T(128)}, s32[16]{0:T(128)}, u32[]{:S(2)}, u32[]{:S(2)}) collective-permute-start(s32[16]{0:T(128)} %get-tuple-element.10), channel_id=1, source_target_pairs={{1,0},{2,1},{3,2},{4,3},{5,4},{6,5},{7,6},{8,7},{9,8},{10,9},{11,1... | collective-permute-start | bytes 200 | tf_op jit(solution)/shard_map/ppermute | solution.py:12
  9.8 7.9 %copy-start.8 = (f32[16,50]{1,0:T(8,128)}, f32[16,50]{1,0:T(8,128)S(1)}, u32[]{:S(2)}) copy-start(f32[16,50]{1,0:T(8,128)S(1)} %get-tuple-element.7) | copy-start | bytes 9604
  9.8 14.2 %copy-start.9 = (f32[50,128]{1,0:T(8,128)S(1)}, f32[50,128]{1,0:T(8,128)}, u32[]{:S(2)}) copy-start(f32[50,128]{1,0:T(8,128)} %param.12) | copy-start | bytes 76804
  9.8 14.3 %copy-start.13 = (s32[4,128]{1,0:T(4,128)S(1)}, s32[4,128]{1,0:T(4,128)}, u32[]{:S(2)}) copy-start(s32[4,128]{1,0:T(4,128)} %param.10) | copy-start | bytes 6148
  9.8 14.4 %copy-start.7 = (f32[4,50,128]{2,0,1:T(4,128)S(1)}, f32[4,50,128]{2,0,1:T(4,128)}, u32[]{:S(2)}) copy-start(f32[4,50,128]{2,0,1:T(4,128)} %param.11) | copy-start | bytes 307204
  14.0 15.0 %copy-start = (bf16[128,50,128]{2,0,1:T(8,128)(2,1)S(1)}, bf16[128,50,128]{2,0,1:T(8,128)(2,1)}, u32[]{:S(2)}) copy-start(bf16[128,50,128]{2,0,1:T(8,128)(2,1)} %param.9) | copy-start | bytes 4915204
  14.0 17.4 %copy-start.10 = (s32[1024]{0:T(1024)}, s32[1024]{0:T(1024)S(1)}, u32[]{:S(2)}) copy-start(s32[1024]{0:T(1024)S(1)} %get-tuple-element.16) | copy-start | bytes 12292
  14.0 17.4 %copy-start.11 = (s32[1024]{0:T(1024)}, s32[1024]{0:T(1024)S(1)}, u32[]{:S(2)}) copy-start(s32[1024]{0:T(1024)S(1)} %get-tuple-element.17) | copy-start | bytes 12292
  17.7 31.2 %collective-permute-start.3 = (bf16[16,50,128]{2,1,0:T(8,128)(2,1)}, bf16[16,50,128]{2,1,0:T(8,128)(2,1)}, u32[]{:S(2)}, u32[]{:S(2)}) collective-permute-start(bf16[16,50,128]{2,1,0:T(8,128)(2,1)} %multiply_convert_fusion.6), channel_id=1, source_target_pairs={{1,0},{2,1},{3,2},{4,3},{5,4},{6,5},{7,6},{8,7},{9,8},{10,9},{11,1... | collective-permute-start | bytes 614408 | tf_op jit(solution)/shard_map/ppermute | solution.py:12
  23.7 20.9 %collective-permute-start.5 = (bf16[16,50,128]{2,1,0:T(8,128)(2,1)}, bf16[16,50,128]{2,1,0:T(8,128)(2,1)}, u32[]{:S(2)}, u32[]{:S(2)}) collective-permute-start(bf16[16,50,128]{2,1,0:T(8,128)(2,1)} %multiply_convert_fusion.5), channel_id=1, source_target_pairs={{16,0},{0,16},{17,1},{1,17},{18,2},{2,18},{19,3},{3,19},{20,4},{4,... | collective-permute-start | bytes 614408 | tf_op jit(solution)/shard_map/ppermute | solution.py:18
  24.0 7.5 %copy-start.12 = (s32[1024]{0:T(1024)}, s32[1024]{0:T(1024)S(1)}, u32[]{:S(2)}) copy-start(s32[1024]{0:T(1024)S(1)} %pad_clamp_fusion.2) | copy-start | bytes 12292
  27.7 1.3 %copy-start.4 = (bf16[50,128,128]{1,0,2:T(8,128)(2,1)}, bf16[50,128,128]{1,0,2:T(8,128)(2,1)S(1)}, u32[]{:S(2)}) copy-start(bf16[50,128,128]{1,0,2:T(8,128)(2,1)S(1)} %convert_bitcast_fusion) | copy-start | bytes 4915204
  29.0 6.0 %copy-start.14 = (s32[128]{0:T(128)S(1)}, s32[128]{0:T(128)}, u32[]{:S(2)}) copy-start(s32[128]{0:T(128)} %param.16) | copy-start | bytes 1540
  40.2 7.5 %collective-permute-start.1 = (bf16[16,50,128]{2,1,0:T(8,128)(2,1)}, bf16[16,50,128]{2,1,0:T(8,128)(2,1)S(1)}, u32[]{:S(2)}, u32[]{:S(2)}) collective-permute-start(bf16[16,50,128]{2,1,0:T(8,128)(2,1)} %multiply_convert_fusion.7), channel_id=1, source_target_pairs={{0,1},{1,2},{2,3},{3,4},{4,5},{5,6},{6,7},{7,8},{8,9},{9,10},{10,1... | collective-permute-start | bytes 614408 | tf_op jit(solution)/shard_map/ppermute | solution.py:12
  46.1 4.3 %copy-start.2 = (f32[50,128,128]{2,1,0:T(8,128)S(1)}, f32[50,128,128]{2,1,0:T(8,128)}, u32[]{:S(2)}) copy-start(f32[50,128,128]{2,1,0:T(8,128)} %fusion.24) | copy-start | bytes 9830404
  46.1 4.3 %copy-start.5 = (f32[128,50]{1,0:T(8,128)S(1)}, f32[128,50]{1,0:T(8,128)}, u32[]{:S(2)}) copy-start(f32[128,50]{1,0:T(8,128)} %fusion.41) | copy-start | bytes 76804
  81.0 20.3 %collective-permute-start.7 = (bf16[16,50,128]{2,1,0:T(8,128)(2,1)S(1)}, bf16[16,50,128]{2,1,0:T(8,128)(2,1)S(1)}, u32[]{:S(2)}, u32[]{:S(2)}) collective-permute-start(bf16[16,50,128]{2,1,0:T(8,128)(2,1)S(1)} %multiply_convert_fusion.3), channel_id=1, source_target_pairs={{1,0},{2,1},{3,2},{4,3},{5,4},{6,5},{7,6},{8,7},{9,8},{10,9},{11,1... | collective-permute-start | bytes 614408 | tf_op jit(solution)/shard_map/ppermute | solution.py:12
  83.6 16.3 %collective-permute-start.6 = (bf16[16,50,128]{2,1,0:T(8,128)(2,1)S(1)}, bf16[16,50,128]{2,1,0:T(8,128)(2,1)S(1)}, u32[]{:S(2)}, u32[]{:S(2)}) collective-permute-start(bf16[16,50,128]{2,1,0:T(8,128)(2,1)S(1)} %multiply_convert_fusion.4), channel_id=1, source_target_pairs={{0,1},{1,2},{2,3},{3,4},{4,5},{5,6},{6,7},{7,8},{8,9},{9,10},{10,1... | collective-permute-start | bytes 614408 | tf_op jit(solution)/shard_map/ppermute | solution.py:12
  88.5 10.1 %collective-permute-start.8 = (bf16[16,50,128]{2,1,0:T(8,128)(2,1)S(1)}, bf16[16,50,128]{2,1,0:T(8,128)(2,1)S(1)}, u32[]{:S(2)}, u32[]{:S(2)}) collective-permute-start(bf16[16,50,128]{2,1,0:T(8,128)(2,1)S(1)} %multiply_convert_fusion.2), channel_id=1, source_target_pairs={{16,0},{0,16},{17,1},{1,17},{18,2},{2,18},{19,3},{3,19},{20,4},{4,... | collective-permute-start | bytes 614408 | tf_op jit(solution)/shard_map/ppermute | solution.py:18
  99.9 2.9 %copy-start.1 = (bf16[128,50,128]{2,1,0:T(8,128)(2,1)S(1)}, bf16[128,50,128]{2,1,0:T(8,128)(2,1)}, u32[]{:S(2)}) copy-start(bf16[128,50,128]{2,1,0:T(8,128)(2,1)} %get-tuple-element.15) | copy-start | bytes 4915204
  99.9 2.9 %copy-start.3 = (f32[50,128,128]{1,0,2:T(8,128)S(1)}, f32[50,128,128]{1,0,2:T(8,128)}, u32[]{:S(2)}) copy-start(f32[50,128,128]{1,0,2:T(8,128)} %copy.27) | copy-start | bytes 9830404
  99.9 2.9 %copy-start.6 = (f32[128,50]{1,0:T(8,128)S(1)}, f32[128,50]{1,0:T(8,128)}, u32[]{:S(2)}) copy-start(f32[128,50]{1,0:T(8,128)} %fusion.41) | copy-start | bytes 76804
where the time goes:
time: 118 us
  matrix products  53.2 us (45%)
  local copies, waits for them, and re-layouts  30.4 us (26%)
  starting transfers between devices  22.4 us (19%)
  other arithmetic  9.65 us (8%)
  waiting for transfers between devices  1.54 us (1%)
    dot_general x2, matrix products, local(): jnp.einsum('mlc,cmt->clt', vert_inv, explicit, preferred_element_type=jnp...  34.7 us
    ppermute x6, starting transfers between devices, passed_along(): lax.ppermute(value, axis, [(source, source + steps) for source in range(i...  19.6 us
    gather x6, local copies, waits for them, and re-layouts, local(): contrib = edge_wts[d].T[:, :, None] * own[send_cols[d]]  16.2 us
    dot_general x6, matrix products, add_pushed(): jnp.einsum('je,elt->jlt', table, contrib, precision=lax.Precision.HIGHEST)  8.22 us
    dot_general x2, matrix products, local(): jnp.einsum('lji,ilt->jlt', operator, state, preferred_element_type=jnp.fl...  6.92 us
    unnamed x33, local copies, waits for them, and re-layouts  6.12 us
    dot_general x1, local copies, waits for them, and re-layouts, local(): jnp.einsum('lji,ilt->jlt', operator, state, preferred_element_type=jnp.fl...  4.37 us
    convert_element_type x1, other arithmetic, local(): own = state.astype(jnp.float32)  4.22 us
  transfers between devices with their start and end apart: 9, of which 1 were waited for; matrix products, arithmetic and copies ran while one was open for 36% of the time, Pallas kernels for 0%

commit v1 on v0

v1 whole, which is shorter than its diff:
```python
import functools

import jax
import jax.numpy as jnp
from jax import lax
from jax.experimental import pallas as pl
from jax.experimental.pallas import tpu as pltpu
from jax.sharding import PartitionSpec as P

NSTEP = 2
F32 = jnp.float32
BF16 = jnp.bfloat16


def padded(levels):
    return -(-(levels + 1) // 8) * 8


def direction(slot, parity):
    return 2 if slot == 2 else lax.bitwise_xor(parity, jnp.int32(slot))


def edge_tables(parity, edge_ref, recv_ref, wts, tbl):
    nedge, levels = edge_ref.shape[1:]
    wts[...] = jnp.zeros_like(wts)
    tbl[...] = jnp.zeros_like(tbl)
    for slot in range(3):
        d = direction(slot, parity)
        wts[slot * nedge : (slot + 1) * nedge, 0:levels] = edge_ref[d]
        tbl[slot : slot + 1, 0:nedge] = recv_ref[pl.ds(d, 1), :].astype(F32)
    return wts[...].T


def pack_edges(parity, levels, send_ref, weights, tbl, column, outs):
    rows = padded(levels)
    nedge, _, width = outs[0].shape
    is_level = lax.broadcasted_iota(jnp.int32, (rows, width), 0) < levels
    for slot, out in enumerate(outs):
        d = direction(slot, parity)
        table = jnp.broadcast_to(tbl[slot : slot + 1, :], (rows, width))
        for e in range(nedge):
            k = slot * nedge + e
            w = weights[0:rows, k : k + 1]
            out[e] = jnp.where(is_level, column(send_ref[d, e]) * w, table).astype(BF16)


def add_edges(edges, total, tbl_v, tbl_s, sem):
    levels_at = edges[0].shape[1] - 8
    for slot, ref in enumerate(edges):
        tbl_v[slot] = ref[0, levels_at:, :].astype(F32).astype(jnp.int32)
    copy = pltpu.make_async_copy(tbl_v, tbl_s, sem)
    copy.start()
    copy.wait()
    for slot, ref in enumerate(edges):
        for e in range(ref.shape[0]):
            j = tbl_s[slot, 7, e]
            total[j] = total[j] + ref[e].astype(F32)


def vertical(vt_ref, total, out):
    def column(j, _):
        rows = total[j]
        pad = jnp.zeros((64 - rows.shape[0], rows.shape[1]), F32)
        ex = jnp.concatenate([rows, pad], axis=0).astype(BF16)
        out[j] = jnp.dot(vt_ref[j][:, 0:64], ex, preferred_element_type=F32)
        return _
    lax.fori_loop(0, total.shape[0], column, 0, unroll=8)


def gather_kernel(blk, c_ref, send_ref, recv_ref, edge_ref, s0, s1, s2, cf, wts, tbl):
    levels, cols, width = c_ref.shape
    parity = lax.bitwise_and(lax.axis_index(blk), jnp.int32(1))
    weights = edge_tables(parity, edge_ref, recv_ref, wts, tbl)
    for l in range(levels):
        cf[l * cols : (l + 1) * cols, :] = c_ref[l].astype(F32)
    column = lambda s: cf[pl.ds(s, padded(levels), stride=cols), :]
    pack_edges(parity, levels, send_ref, weights, tbl, column, (s0, s1, s2))


def operator_kernel(c_ref, nbr_ref, nw_ref, sw_ref, wet_ref, v_ref, a_ref, ex_ref, vt_ref, exs, merged, vf, vts):
    levels, cols, width = c_ref.shape
    rows = padded(levels)
    nbr = nbr_ref.shape[0]
    lane = lax.broadcasted_iota(jnp.int32, (8, cols), 1)
    sub = lax.broadcasted_iota(jnp.int32, (8, cols), 0)
    target = jnp.where(sub == nbr, lane, -1)
    for n in range(nbr):
        target = jnp.where(sub == n, nbr_ref[n : n + 1, :], target)
    same = [(target == nbr_ref[n : n + 1, :]).astype(F32) for n in range(nbr)]
    same.append((target == lane).astype(F32))
    for l in range(levels):
        total = same[nbr] * sw_ref[l : l + 1, :]
        for n in range(nbr):
            total = total + same[n] * nw_ref[l, n : n + 1, :]
        merged[l] = total
    half = 16
    for jt in range(cols // half):
        j = lax.broadcasted_iota(jnp.int32, (half, cols), 0) + jt * half
        hits = [j == nbr_ref[n : n + 1, :] for n in range(nbr)]
        hits.append(j == lax.broadcasted_iota(jnp.int32, (half, cols), 1))
        def fill(l, _):
            value = jnp.zeros((half, cols), F32)
            for n in range(nbr, -1, -1):
                value = jnp.where(hits[n], merged[l, n : n + 1, :], value)
            a_ref[l, jt * half : (jt + 1) * half, :] = value.astype(BF16)
            return _
        lax.fori_loop(0, levels, fill, 0, unroll=5)
    for l in range(levels):
        exs[pl.ds(l, cols, stride=rows), :] = jnp.dot(a_ref[l], c_ref[l], preferred_element_type=F32)
    for l in range(levels, rows):
        exs[pl.ds(l, cols, stride=rows), :] = jnp.zeros((cols, width), F32)
    ex_ref[...] = exs[...].reshape(cols, rows, width)
    level = lax.broadcasted_iota(jnp.int32, (levels, cols), 0)
    wet = wet_ref[...]
    vf[...] = jnp.zeros_like(vf)
    for m in range(levels):
        keep = jnp.maximum(level, m) < wet
        vf[m * rows : m * rows + levels, :] = jnp.where(keep, v_ref[m].astype(F32), 0.0)
    for l in range(rows):
        block = vf[pl.ds(l, rows, stride=rows), :]
        block = jnp.concatenate([block, jnp.zeros((128 - rows, cols), F32)], axis=0)
        vts[pl.ds(l, cols, stride=rows), :] = block.T
    vt_ref[...] = vts[...].reshape(cols, rows, 128).astype(BF16)


def first_kernel(blk, r0, r1, r2, ex_ref, vt_ref, send_ref, recv_ref, edge_ref, c_ref, s0, s1, s2, exs, wts, tbl, tbl_v, tbl_s, sem):
    levels = edge_ref.shape[2]
    parity = lax.bitwise_and(lax.axis_index(blk), jnp.int32(1))
    weights = edge_tables(parity, edge_ref, recv_ref, wts, tbl)
    exs[...] = ex_ref[...]
    add_edges((r0, r1, r2), exs, tbl_v, tbl_s, sem)
    vertical(vt_ref, exs, c_ref)
    pack_edges(parity, levels, send_ref, weights, tbl, lambda s: c_ref[s], (s0, s1, s2))


def middle_kernel(c_ref, a_ref, ex_ref, cs, exs):
    levels = a_ref.shape[0]
    cols, rows, width = c_ref.shape
    cs[...] = c_ref[...].reshape(cols * rows, width)
    for l in range(levels):
        state = cs[pl.ds(l, cols, stride=rows), :].astype(BF16)
        exs[pl.ds(l, cols, stride=rows), :] = jnp.dot(a_ref[l], state, preferred_element_type=F32)
    for l in range(levels, rows):
        exs[pl.ds(l, cols, stride=rows), :] = jnp.zeros((cols, width), F32)
    ex_ref[...] = exs[...].reshape(cols, rows, width)


def last_kernel(r0, r1, r2, ex_ref, vt_ref, out_ref, exs, cs, tbl_v, tbl_s, sem):
    levels = out_ref.shape[0]
    cols, rows, width = ex_ref.shape
    exs[...] = ex_ref[...]
    add_edges((r0, r1, r2), exs, tbl_v, tbl_s, sem)
    def column(j, _):
        pad = jnp.zeros((64 - rows, width), F32)
        ex = jnp.concatenate([exs[j], pad], axis=0).astype(BF16)
        cs[pl.ds(pl.multiple_of(j * rows, 8), rows), :] = jnp.dot(vt_ref[j][:, 0:64], ex, preferred_element_type=F32)
        return _
    lax.fori_loop(0, cols, column, 0, unroll=8)
    for l in range(levels):
        out_ref[l] = cs[pl.ds(l, cols, stride=rows), :].astype(BF16)


VM = pl.BlockSpec(memory_space=pltpu.VMEM)
SM = pl.BlockSpec(memory_space=pltpu.SMEM)


def call(kernel, ins, specs, outs, scratch, limit, flops=0):
    size = sum(x.size * x.dtype.itemsize for x in (*ins, *outs))
    return pl.pallas_call(
        kernel,
        out_shape=outs,
        in_specs=specs,
        out_specs=[VM] * len(outs),
        scratch_shapes=scratch,
        compiler_params=pltpu.CompilerParams(vmem_limit_bytes=limit * 2**20),
        cost_estimate=pl.CostEstimate(flops=flops, bytes_accessed=size, transcendentals=0),
    )(*ins)


def swapped(values, blk, basin):
    n, b = lax.axis_size(blk), lax.axis_size(basin)
    out = []
    for slot in range(2):
        pairs = []
        for i in range(slot, n - 1, 2):
            pairs += [(i, i + 1), (i + 1, i)]
        out.append(lax.ppermute(values[slot], blk, pairs))
    out.append(lax.ppermute(values[2], basin, [(i, (i + 1) % b) for i in range(b)]))
    return out


def local(tracers, nbr_cols, nbr_wts, self_wts, send_cols, recv_cols, edge_wts, wet_levels, vert_inv):
    cols, levels, width = tracers.shape
    rows = padded(levels)
    nedge = send_cols.shape[1]
    shape = jax.ShapeDtypeStruct
    by_level = jnp.transpose(tracers, (1, 0, 2))
    nbr_by_level = jnp.transpose(nbr_wts, (1, 0, 2))
    edge_by_entry = jnp.transpose(edge_wts, (0, 2, 1))
    wet = wet_levels.reshape(1, cols)
    packed = [shape((nedge, rows, width), BF16)] * 3
    table_scratch = [pltpu.VMEM((128, 128), F32), pltpu.VMEM((8, 128), F32)]
    scatter_scratch = [pltpu.VMEM((3, 8, 128), jnp.int32), pltpu.SMEM((3, 8, 128), jnp.int32), pltpu.SemaphoreType.DMA]
    flat = pltpu.VMEM((cols * rows, width), F32)
    stack = pltpu.VMEM((cols, rows, width), F32)

    sends = call(
        functools.partial(gather_kernel, "blk"),
        (by_level, send_cols, recv_cols, edge_by_entry),
        [VM, SM, VM, VM], packed,
        [pltpu.VMEM((rows * cols, width), F32)] + table_scratch, 16,
    )
    received = swapped(sends, "blk", "basin")
    operator, explicit, vt = call(
        operator_kernel,
        (by_level, nbr_cols, nbr_by_level, self_wts, wet, vert_inv),
        [VM] * 6,
        [shape((levels, cols, cols), BF16), shape((cols, rows, width), F32), shape((cols, rows, 128), BF16)],
        [flat, pltpu.VMEM((levels, 8, cols), F32), pltpu.VMEM((rows * rows, cols), F32), pltpu.VMEM((cols * rows, 128), F32)], 32,
        flops=2 * levels * cols * cols * width,
    )
    state, *sends = call(
        functools.partial(first_kernel, "blk"),
        (*received, explicit, vt, send_cols, recv_cols, edge_by_entry),
        [VM] * 5 + [SM, VM, VM],
        [shape((cols, rows, width), F32)] + packed,
        [stack] + table_scratch + scatter_scratch, 32,
        flops=2 * cols * rows * rows * width,
    )
    received = swapped(sends, "blk", "basin")
    (explicit,) = call(
        middle_kernel, (state, operator), [VM] * 2, [shape((cols, rows, width), F32)], [flat, flat], 32,
        flops=2 * levels * cols * cols * width,
    )
    (out,) = call(
        last_kernel, (*received, explicit, vt), [VM] * 5, [shape((levels, cols, width), BF16)],
        [stack, flat] + scatter_scratch, 32,
        flops=2 * cols * rows * rows * width,
    )
    return jnp.transpose(out, (1, 0, 2))


def solution(mesh):
    in_specs = (
        P(("basin", "blk"), None, None),
        P(None, ("basin", "blk")),
        P(None, None, ("basin", "blk")),
        P(None, ("basin", "blk")),
        P(None, ("basin", "blk")),
        P(None, ("basin", "blk")),
        P(None, None, ("basin", "blk")),
        P(("basin", "blk")),
        P(None, None, ("basin", "blk")),
    )
    out_specs = P(("basin", "blk"), None, None)
    return jax.shard_map(local, mesh=mesh, in_specs=in_specs, out_specs=out_specs, check_vma=False)
```

time: 118 us -> 40.1 us (0.34)
  the two profiles are of different devices: /device:TPU:5 before, /device:TPU:13 now
where the time goes in v1:
time: 40.1 us; the launch traced here: 39.6 us
  Pallas kernels  17.1 us (43%)
  starting transfers between devices  9.14 us (23%)
  local copies, waits for them, and re-layouts  7.63 us (19%)
  waiting for transfers between devices  5.63 us (14%)
    pallas_call x5, Pallas kernels, call(): pl.pallas_call(kernel, out_shape=outs, in_specs=specs, out_specs=[VM] * l...  17.1 us
    unnamed x26, local copies, waits for them, and re-layouts  7.63 us
    ppermute x4, starting transfers between devices, swapped(): out.append(lax.ppermute(values[slot], blk, pairs))  7.54 us
    ppermute x2, waiting for transfers between devices, swapped(): lax.ppermute(values[2], basin, [(i, (i + 1) % b) for i in range(b)])  2.9 us
    ppermute x4, waiting for transfers between devices, swapped(): out.append(lax.ppermute(values[slot], blk, pairs))  2.73 us
    ppermute x2, starting transfers between devices, swapped(): lax.ppermute(values[2], basin, [(i, (i + 1) % b) for i in range(b)])  1.59 us
  transfers between devices with their start and end apart: 6, of which 2 were waited for; matrix products, arithmetic and copies ran while one was open for 0% of the time, Pallas kernels for 12%

profile of v1, /device:TPU:13, one launch (start us, length us, event | category | flops | bytes accessed | tf_op | source)
XLA Modules:
  0.0 39.6 jit_solution(18011338310702713358)
XLA Ops:
  0.0 1.4 %copy-done = bf16[128,50,128]{2,0,1:T(8,128)(2,1)S(1)} copy-done((bf16[128,50,128]{2,0,1:T(8,128)(2,1)S(1)}, bf16[128,50,128]{2,0,1:T(8,128)(2,1)}, u32[]{:S(2)}) %copy-start) | copy-done | bytes 1638424
  1.4 0.7 %copy-done.4 = f32[3,50,16]{1,2,0:T(8,128)S(1)} copy-done((f32[3,50,16]{1,2,0:T(8,128)S(1)}, f32[3,50,16]{1,2,0:T(8,128)}, u32[]{:S(2)}) %copy-start.4) | copy-done | bytes 9624
  2.2 0.7 %copy-done.7 = s32[3,16]{1,0:T(4,128)S(1)} copy-done((s32[3,16]{1,0:T(4,128)S(1)}, s32[3,16]{1,0:T(4,128)}, u32[]{:S(2)}) %copy-start.7) | copy-done | bytes 216
  2.9 0.7 %copy-done.9 = s32[3,16]{1,0:T(4,128)S(1)} copy-done((s32[3,16]{1,0:T(4,128)S(1)}, s32[3,16]{1,0:T(4,128)}, u32[]{:S(2)}) %copy-start.9) | copy-done | bytes 216
  3.5 2.2 %shard_map.91 = (bf16[16,56,128]{2,1,0:T(8,128)(2,1)S(1)}, bf16[16,56,128]{2,1,0:T(8,128)(2,1)S(1)}, bf16[16,56,128]{2,1,0:T(8,128)(2,1)S(1)}) custom-call(bf16[50,128,128]{2,1,0:T(8,128)(2,1)S(1)} %bitcast.5, s32[3,16]{1,0:T(4,128)S(1)} %copy-done.7, s32[3,16]{1,0:T(4,128)S(1)} %copy-done.9, f32[3,16,50]{2,1,0:T(8,128)S(1)} %bitcast.8), custom_call_target="tpu_custom_call" | custom-call | bytes 2336512 | tf_op jit(solution)/shard_map/pallas_call | solution.py:169
  5.8 0.7 %collective-permute-start = (bf16[16,56,128]{2,1,0:T(8,128)(2,1)S(1)}, bf16[16,56,128]{2,1,0:T(8,128)(2,1)S(1)}, u32[]{:S(2)}, u32[]{:S(2)}) collective-permute-start(bf16[16,56,128]{2,1,0:T(8,128)(2,1)S(1)} %get-tuple-element.15), channel_id=1, source_target_pairs={{0,1},{1,0},{2,3},{3,2},{4,5},{5,4},{6,7},{7,6},{8,9},{9,8},{10,11... | collective-permute-start | bytes 688136 | tf_op jit(solution)/shard_map/ppermute | solution.py:187
  6.5 3.0 %collective-permute-start.1 = (bf16[16,56,128]{2,1,0:T(8,128)(2,1)S(1)}, bf16[16,56,128]{2,1,0:T(8,128)(2,1)S(1)}, u32[]{:S(2)}, u32[]{:S(2)}) collective-permute-start(bf16[16,56,128]{2,1,0:T(8,128)(2,1)S(1)} %get-tuple-element.16), channel_id=1, source_target_pairs={{1,2},{2,1},{3,4},{4,3},{5,6},{6,5},{7,8},{8,7},{9,10},{10,9},{11,... | collective-permute-start | bytes 688136 | tf_op jit(solution)/shard_map/ppermute | solution.py:187
  9.6 1.3 %collective-permute-start.2 = (bf16[16,56,128]{2,1,0:T(8,128)(2,1)S(1)}, bf16[16,56,128]{2,1,0:T(8,128)(2,1)S(1)}, u32[]{:S(2)}, u32[]{:S(2)}) collective-permute-start(bf16[16,56,128]{2,1,0:T(8,128)(2,1)S(1)} %get-tuple-element.17), channel_id=1, source_target_pairs={{0,16},{16,0},{1,17},{17,1},{2,18},{18,2},{3,19},{19,3},{4,20},{20... | collective-permute-start | bytes 688136 | tf_op jit(solution)/shard_map/ppermute | solution.py:188
  10.9 1.1 %copy-done.2 = bf16[50,50,128]{2,1,0:T(8,128)(2,1)S(1)} copy-done((bf16[50,50,128]{2,1,0:T(8,128)(2,1)S(1)}, bf16[50,50,128]{2,1,0:T(8,128)(2,1)}, u32[]{:S(2)}) %copy-start.2) | copy-done | bytes 640024
  12.0 0.9 %copy-done.3 = f32[4,50,128]{2,0,1:T(4,128)S(1)} copy-done((f32[4,50,128]{2,0,1:T(4,128)S(1)}, f32[4,50,128]{2,0,1:T(4,128)}, u32[]{:S(2)}) %copy-start.3) | copy-done | bytes 102424
  12.9 0.7 %copy-done.6 = f32[50,128]{1,0:T(8,128)S(1)} copy-done((f32[50,128]{1,0:T(8,128)S(1)}, f32[50,128]{1,0:T(8,128)}, u32[]{:S(2)}) %copy-start.6) | copy-done | bytes 25624
  13.6 0.7 %copy-done.11 = s32[4,128]{1,0:T(4,128)S(1)} copy-done((s32[4,128]{1,0:T(4,128)S(1)}, s32[4,128]{1,0:T(4,128)}, u32[]{:S(2)}) %copy-start.11) | copy-done | bytes 2072
  14.3 0.7 %copy-done.12 = s32[128]{0:T(128)S(1)} copy-done((s32[128]{0:T(128)S(1)}, s32[128]{0:T(128)}, u32[]{:S(2)}) %copy-start.12) | copy-done | bytes 536
  14.9 3.0 %shard_map.92 = (bf16[50,128,128]{2,1,0:T(8,128)(2,1)S(1)}, f32[128,56,128]{2,1,0:T(8,128)S(1)}, bf16[128,56,128]{2,1,0:T(8,128)(2,1)S(1)}) custom-call(bf16[50,128,128]{2,1,0:T(8,128)(2,1)S(1)} %bitcast.6, s32[4,128]{1,0:T(4,128)S(1)} %copy-done.11, f32[50,4,128]{2,1,0:T(4,128)S(1)} %bitcast.7, f32[50,128]{1,0:T(8,128)S(1)} %copy-done.6, ...), custom_call_target="tpu_custom_call" | custom-call | flops 209715200 | bytes 9552384 | tf_op jit(solution)/shard_map/pallas_call | solution.py:169
  17.9 0.0 collective-permute-done.r0
  17.9 0.0 collective-permute-done.1.r1
  18.0 5.0 %shard_map.93 = (f32[128,56,128]{2,1,0:T(8,128)S(1)}, bf16[16,56,128]{2,1,0:T(8,128)(2,1)S(1)}, bf16[16,56,128]{2,1,0:T(8,128)(2,1)S(1)}, bf16[16,56,128]{2,1,0:T(8,128)(2,1)S(1)}) custom-call(bf16[16,56,128]{2,1,0:T(8,128)(2,1)S(1)} %collective-permute-done.r0, bf16[16,56,128]{2,1,0:T(8,128)(2,1)S(1)} %collective-permute-done.1.r1, ...), custom_call_target="tpu_custom_call" | custom-call | flops 102760448 | bytes 10561280 | tf_op jit(solution)/shard_map/pallas_call | solution.py:169
  23.0 0.1 collective-permute-start.3
  23.0 3.7 %collective-permute-start.4 = (bf16[16,56,128]{2,1,0:T(8,128)(2,1)S(1)}, bf16[16,56,128]{2,1,0:T(8,128)(2,1)S(1)}, u32[]{:S(2)}, u32[]{:S(2)}) collective-permute-start(bf16[16,56,128]{2,1,0:T(8,128)(2,1)S(1)} %get-tuple-element.21), channel_id=1, source_target_pairs={{1,2},{2,1},{3,4},{4,3},{5,6},{6,5},{7,8},{8,7},{9,10},{10,9},{11,... | collective-permute-start | bytes 688136 | tf_op jit(solution)/shard_map/ppermute | solution.py:187
  26.7 0.3 collective-permute-start.5
  27.1 1.6 %shard_map.94.ex_ref = f32[128,56,128]{2,1,0:T(8,128)S(1)} custom-call(f32[128,56,128]{2,1,0:T(8,128)S(1)} %get-tuple-element.23.c_ref, bf16[50,128,128]{2,1,0:T(8,128)(2,1)S(1)} %get-tuple-element.24.a_ref), custom_call_target="tpu_custom_call" | custom-call | flops 209715200 | bytes 8978432 | tf_op jit(solution)/shard_map/pallas_call | solution.py:169
  28.7 2.7 %collective-permute-done.4.r1 = bf16[16,56,128]{2,1,0:T(8,128)(2,1)S(1)} collective-permute-done((bf16[16,56,128]{2,1,0:T(8,128)(2,1)S(1)}, bf16[16,56,128]{2,1,0:T(8,128)(2,1)S(1)}, u32[]{:S(2)}, u32[]{:S(2)}) %collective-permute-start.4) | collective-permute-done | bytes 229408 | tf_op jit(solution)/shard_map/ppermute | solution.py:187
  31.4 2.9 %collective-permute-done.5.r2 = bf16[16,56,128]{2,1,0:T(8,128)(2,1)S(1)} collective-permute-done((bf16[16,56,128]{2,1,0:T(8,128)(2,1)S(1)}, bf16[16,56,128]{2,1,0:T(8,128)(2,1)S(1)}, u32[]{:S(2)}, u32[]{:S(2)}) %collective-permute-start.5) | collective-permute-done | bytes 229408 | tf_op jit(solution)/shard_map/ppermute | solution.py:188
  34.3 5.3 %shard_map.95 = bf16[50,128,128]{2,1,0:T(8,128)(2,1)} custom-call(bf16[16,56,128]{2,1,0:T(8,128)(2,1)S(1)} %collective-permute-done.3.r0, bf16[16,56,128]{2,1,0:T(8,128)(2,1)S(1)} %collective-permute-done.4.r1, bf16[16,56,128]{2,1,0:T(8,128)(2,1)S(1)} %collective-permute-done.5.r2, f32[128,56,128]{2,1,0:T(8,128)S(1)} %shard_map.94.ex_ref, ...), custom_call_target="tpu_custom_call" | custom-call | flops 102760448 | bytes 7831552 | tf_op jit(solution)/shard_map/pallas_call | solution.py:169
  (19 shorter events, 0.0 us)
Async XLA Ops:
  0.0 1.4 %copy-start = (bf16[128,50,128]{2,0,1:T(8,128)(2,1)S(1)}, bf16[128,50,128]{2,0,1:T(8,128)(2,1)}, u32[]{:S(2)}) copy-start(bf16[128,50,128]{2,0,1:T(8,128)(2,1)} %param.9) | copy-start | bytes 4915204
  1.4 0.7 %copy-start.4 = (f32[3,50,16]{1,2,0:T(8,128)S(1)}, f32[3,50,16]{1,2,0:T(8,128)}, u32[]{:S(2)}) copy-start(f32[3,50,16]{1,2,0:T(8,128)} %param.15) | copy-start | bytes 28804
  2.2 0.7 %copy-start.7 = (s32[3,16]{1,0:T(4,128)S(1)}, s32[3,16]{1,0:T(4,128)}, u32[]{:S(2)}) copy-start(s32[3,16]{1,0:T(4,128)} %send_ref.3) | copy-start | bytes 580
  2.9 0.7 %copy-start.9 = (s32[3,16]{1,0:T(4,128)S(1)}, s32[3,16]{1,0:T(4,128)}, u32[]{:S(2)}) copy-start(s32[3,16]{1,0:T(4,128)} %recv_ref.3) | copy-start | bytes 580
  3.5 7.3 %copy-start.1 = (bf16[128,50,128]{2,0,1:T(8,128)(2,1)S(1)}, bf16[128,50,128]{2,0,1:T(8,128)(2,1)}, u32[]{:S(2)}) copy-start(bf16[128,50,128]{2,0,1:T(8,128)(2,1)} %param.9) | copy-start | bytes 4915204
  3.5 14.4 %copy-start.5 = (f32[3,50,16]{1,2,0:T(8,128)S(1)}, f32[3,50,16]{1,2,0:T(8,128)}, u32[]{:S(2)}) copy-start(f32[3,50,16]{1,2,0:T(8,128)} %param.15) | copy-start | bytes 28804
  3.5 14.4 %copy-start.8 = (s32[3,16]{1,0:T(4,128)S(1)}, s32[3,16]{1,0:T(4,128)}, u32[]{:S(2)}) copy-start(s32[3,16]{1,0:T(4,128)} %send_ref.3) | copy-start | bytes 580
  3.5 14.4 %copy-start.10 = (s32[3,16]{1,0:T(4,128)S(1)}, s32[3,16]{1,0:T(4,128)}, u32[]{:S(2)}) copy-start(s32[3,16]{1,0:T(4,128)} %recv_ref.3) | copy-start | bytes 580
  5.8 12.2 %collective-permute-start = (bf16[16,56,128]{2,1,0:T(8,128)(2,1)S(1)}, bf16[16,56,128]{2,1,0:T(8,128)(2,1)S(1)}, u32[]{:S(2)}, u32[]{:S(2)}) collective-permute-start(bf16[16,56,128]{2,1,0:T(8,128)(2,1)S(1)} %get-tuple-element.15), channel_id=1, source_target_pairs={{0,1},{1,0},{2,3},{3,2},{4,5},{5,4},{6,7},{7,6},{8,9},{9,8},{10,11... | collective-permute-start | bytes 688136 | tf_op jit(solution)/shard_map/ppermute | solution.py:187
  6.5 11.4 %collective-permute-start.1 = (bf16[16,56,128]{2,1,0:T(8,128)(2,1)S(1)}, bf16[16,56,128]{2,1,0:T(8,128)(2,1)S(1)}, u32[]{:S(2)}, u32[]{:S(2)}) collective-permute-start(bf16[16,56,128]{2,1,0:T(8,128)(2,1)S(1)} %get-tuple-element.16), channel_id=1, source_target_pairs={{1,2},{2,1},{3,4},{4,3},{5,6},{6,5},{7,8},{8,7},{9,10},{10,9},{11,... | collective-permute-start | bytes 688136 | tf_op jit(solution)/shard_map/ppermute | solution.py:187
  9.6 8.4 %collective-permute-start.2 = (bf16[16,56,128]{2,1,0:T(8,128)(2,1)S(1)}, bf16[16,56,128]{2,1,0:T(8,128)(2,1)S(1)}, u32[]{:S(2)}, u32[]{:S(2)}) collective-permute-start(bf16[16,56,128]{2,1,0:T(8,128)(2,1)S(1)} %get-tuple-element.17), channel_id=1, source_target_pairs={{0,16},{16,0},{1,17},{17,1},{2,18},{18,2},{3,19},{19,3},{4,20},{20... | collective-permute-start | bytes 688136 | tf_op jit(solution)/shard_map/ppermute | solution.py:188
  10.9 1.1 %copy-start.2 = (bf16[50,50,128]{2,1,0:T(8,128)(2,1)S(1)}, bf16[50,50,128]{2,1,0:T(8,128)(2,1)}, u32[]{:S(2)}) copy-start(bf16[50,50,128]{2,1,0:T(8,128)(2,1)} %v_ref.1) | copy-start | bytes 1920004
  12.0 0.9 %copy-start.3 = (f32[4,50,128]{2,0,1:T(4,128)S(1)}, f32[4,50,128]{2,0,1:T(4,128)}, u32[]{:S(2)}) copy-start(f32[4,50,128]{2,0,1:T(4,128)} %param.11) | copy-start | bytes 307204
  12.9 0.7 %copy-start.6 = (f32[50,128]{1,0:T(8,128)S(1)}, f32[50,128]{1,0:T(8,128)}, u32[]{:S(2)}) copy-start(f32[50,128]{1,0:T(8,128)} %sw_ref.1) | copy-start | bytes 76804
  13.6 0.7 %copy-start.11 = (s32[4,128]{1,0:T(4,128)S(1)}, s32[4,128]{1,0:T(4,128)}, u32[]{:S(2)}) copy-start(s32[4,128]{1,0:T(4,128)} %nbr_ref.1) | copy-start | bytes 6148
  14.3 0.7 %copy-start.12 = (s32[128]{0:T(128)S(1)}, s32[128]{0:T(128)}, u32[]{:S(2)}) copy-start(s32[128]{0:T(128)} %param.16) | copy-start | bytes 1540
  23.0 5.7 %collective-permute-start.3 = (bf16[16,56,128]{2,1,0:T(8,128)(2,1)S(1)}, bf16[16,56,128]{2,1,0:T(8,128)(2,1)S(1)}, u32[]{:S(2)}, u32[]{:S(2)}) collective-permute-start(bf16[16,56,128]{2,1,0:T(8,128)(2,1)S(1)} %get-tuple-element.20), channel_id=1, source_target_pairs={{0,1},{1,0},{2,3},{3,2},{4,5},{5,4},{6,7},{7,6},{8,9},{9,8},{10,11... | collective-permute-start | bytes 688136 | tf_op jit(solution)/shard_map/ppermute | solution.py:187
  23.0 8.3 %collective-permute-start.4 = (bf16[16,56,128]{2,1,0:T(8,128)(2,1)S(1)}, bf16[16,56,128]{2,1,0:T(8,128)(2,1)S(1)}, u32[]{:S(2)}, u32[]{:S(2)}) collective-permute-start(bf16[16,56,128]{2,1,0:T(8,128)(2,1)S(1)} %get-tuple-element.21), channel_id=1, source_target_pairs={{1,2},{2,1},{3,4},{4,3},{5,6},{6,5},{7,8},{8,7},{9,10},{10,9},{11,... | collective-permute-start | bytes 688136 | tf_op jit(solution)/shard_map/ppermute | solution.py:187
  26.7 7.6 %collective-permute-start.5 = (bf16[16,56,128]{2,1,0:T(8,128)(2,1)S(1)}, bf16[16,56,128]{2,1,0:T(8,128)(2,1)S(1)}, u32[]{:S(2)}, u32[]{:S(2)}) collective-permute-start(bf16[16,56,128]{2,1,0:T(8,128)(2,1)S(1)} %get-tuple-element.22), channel_id=1, source_target_pairs={{0,16},{16,0},{1,17},{17,1},{2,18},{18,2},{3,19},{19,3},{4,20},{20... | collective-permute-start | bytes 688136 | tf_op jit(solution)/shard_map/ppermute | solution.py:188

commit v2 on v1

v2 whole, which is shorter than its diff:
```python
import functools

import jax
import jax.numpy as jnp
from jax import lax
from jax.experimental import pallas as pl
from jax.experimental.pallas import tpu as pltpu
from jax.sharding import PartitionSpec as P

NSTEP = 2
F32 = jnp.float32
BF16 = jnp.bfloat16


def padded(levels):
    return -(-(levels + 1) // 8) * 8


def direction(slot, parity):
    return 2 if slot == 2 else lax.bitwise_xor(parity, jnp.int32(slot))


def pack_edges(parity, levels, send, weights, tbl, column, outs):
    rows = padded(levels)
    nedge, _, width = outs[0].shape
    is_level = lax.broadcasted_iota(jnp.int32, (rows, width), 0) < levels
    for slot, out in enumerate(outs):
        d = direction(slot, parity)
        table = jnp.broadcast_to(tbl[slot : slot + 1, :], (rows, width))
        for e in range(nedge):
            k = slot * nedge + e
            w = weights[0:rows, k : k + 1]
            out[e] = jnp.where(is_level, column(send[d, e]) * w, table).astype(BF16)


def product(operator, x):
    pad = jnp.zeros((64 - x.shape[0], x.shape[1]), F32)
    x = jnp.concatenate([x.astype(F32), pad], axis=0).astype(BF16)
    return jnp.dot(operator[:, 0:64], x, preferred_element_type=F32)


def vertical(vt_ref, exs, out):
    cols, rows, _ = vt_ref.shape

    def column(j, _):
        out[j] = product(vt_ref[j], exs[pl.ds(pl.multiple_of(j * rows, 8), rows), :])
        return _

    lax.fori_loop(0, cols, column, 0, unroll=16)


def add_edges(edges, vt_ref, total, tbl_v, tbl_s, sem):
    levels_at = edges[0].shape[1] - 8
    for slot, ref in enumerate(edges):
        tbl_v[slot] = ref[0, levels_at:, :].astype(F32).astype(jnp.int32)
    copy = pltpu.make_async_copy(tbl_v, tbl_s, sem)
    copy.start()
    copy.wait()
    group = 4
    for slot, ref in enumerate(edges):
        for first in range(0, ref.shape[0], group):
            at = [tbl_s[slot, 7, e] for e in range(first, first + group)]
            parts = [product(vt_ref[j], ref[first + i]) for i, j in enumerate(at)]
            for j, part in zip(at, parts):
                total[j] = total[j] + part


def gather_kernel(
    blk, c_h, send_h, recv_h, edge_h, nbr_h, nw_h, sw_h, wet_h, v_h,
    s0, s1, s2, c_v, nbr_v, nw_v, sw_v, wet_v, v_v, wts_o, tbl_o,
    cf, wts, recv_v, edge_v, send_s, sems,
):
    levels, cols, width = c_h.shape
    nedge = edge_h.shape[1]
    pitch = cols + 8
    count = 5
    edges = [levels * i // count for i in range(count + 1)]
    pairs = [(send_h, send_s), (recv_h, recv_v), (edge_h, edge_v)]
    pairs += [(c_h.at[pl.ds(lo, hi - lo)], c_v.at[pl.ds(lo, hi - lo)]) for lo, hi in zip(edges, edges[1:])]
    pairs += [(nbr_h, nbr_v), (nw_h, nw_v), (sw_h, sw_v), (wet_h, wet_v), (v_h, v_v)]
    copies = [pltpu.make_async_copy(a, b, sems.at[i]) for i, (a, b) in enumerate(pairs)]
    for copy in copies:
        copy.start()
    parity = lax.bitwise_and(lax.axis_index(blk), jnp.int32(1))
    wts[...] = jnp.zeros_like(wts)
    tbl_o[...] = jnp.zeros_like(tbl_o)
    for copy in copies[:3]:
        copy.wait()
    for slot in range(3):
        d = direction(slot, parity)
        wts[slot * nedge : (slot + 1) * nedge, 0:levels] = edge_v[d]
        tbl_o[slot : slot + 1, 0:nedge] = recv_v[pl.ds(d, 1), :].astype(F32)
    weights = wts[...].T
    wts_o[...] = weights
    for i, (lo, hi) in enumerate(zip(edges, edges[1:])):
        copies[3 + i].wait()
        for l in range(lo, hi):
            cf[l * pitch : l * pitch + cols, :] = c_v[l].astype(F32)
    column = lambda s: cf[pl.ds(s, padded(levels), stride=pitch), :]
    pack_edges(parity, levels, send_s, weights, tbl_o, column, (s0, s1, s2))
    for copy in copies[3 + count :]:
        copy.wait()


def operator_kernel(c_ref, nbr_ref, nw_ref, sw_ref, wet_ref, v_ref, a_ref, state_ref, vt_ref, exs, merged, vf, vts):
    levels, cols, width = c_ref.shape
    rows = padded(levels)
    nbr = nbr_ref.shape[0]
    lane = lax.broadcasted_iota(jnp.int32, (8, cols), 1)
    sub = lax.broadcasted_iota(jnp.int32, (8, cols), 0)
    target = jnp.where(sub == nbr, lane, -1)
    for n in range(nbr):
        target = jnp.where(sub == n, nbr_ref[n : n + 1, :], target)
    same = [(target == nbr_ref[n : n + 1, :]).astype(F32) for n in range(nbr)]
    same.append((target == lane).astype(F32))
    for l in range(levels):
        total = same[nbr] * sw_ref[l : l + 1, :]
        for n in range(nbr):
            total = total + same[n] * nw_ref[l, n : n + 1, :]
        merged[l] = total
    half = 16
    for jt in range(cols // half):
        j = lax.broadcasted_iota(jnp.int32, (half, cols), 0) + jt * half
        hits = [j == nbr_ref[n : n + 1, :] for n in range(nbr)]
        hits.append(j == lax.broadcasted_iota(jnp.int32, (half, cols), 1))

        def fill(l, _):
            value = jnp.zeros((half, cols), F32)
            for n in range(nbr, -1, -1):
                value = jnp.where(hits[n], merged[l, n : n + 1, :], value)
            a_ref[l, jt * half : (jt + 1) * half, :] = value.astype(BF16)
            return _

        lax.fori_loop(0, levels, fill, 0, unroll=5)
    for l in range(levels):
        exs[pl.ds(l, cols, stride=rows), :] = jnp.dot(a_ref[l], c_ref[l], preferred_element_type=F32)
    for l in range(levels, rows):
        exs[pl.ds(l, cols, stride=rows), :] = jnp.zeros((cols, width), F32)
    level = lax.broadcasted_iota(jnp.int32, (levels, cols), 0)
    wet = wet_ref[...]
    vf[...] = jnp.zeros_like(vf)
    for m in range(levels):
        keep = jnp.maximum(level, m) < wet
        vf[m * rows : m * rows + levels, :] = jnp.where(keep, v_ref[m].astype(F32), 0.0)
    for l in range(rows):
        block = vf[pl.ds(l, rows, stride=rows), :]
        block = jnp.concatenate([block, jnp.zeros((128 - rows, cols), F32)], axis=0)
        vts[pl.ds(l, cols, stride=rows), :] = block.T
    vt_ref[...] = vts[...].reshape(cols, rows, 128).astype(BF16)
    vertical(vt_ref, exs, state_ref)


def first_kernel(blk, levels, r0, r1, r2, local_ref, vt_ref, wts_ref, tbl_ref, send_h, state_ref, s0, s1, s2, tbl_v, tbl_s, send_s, sems):
    copy = pltpu.make_async_copy(send_h, send_s, sems.at[1])
    copy.start()
    parity = lax.bitwise_and(lax.axis_index(blk), jnp.int32(1))
    add_edges((r0, r1, r2), vt_ref, state_ref, tbl_v, tbl_s, sems.at[0])
    copy.wait()
    pack_edges(parity, levels, send_s, wts_ref, tbl_ref, lambda s: state_ref[s], (s0, s1, s2))


def middle_kernel(c_ref, a_ref, vt_ref, out_ref, cs, exs):
    levels = a_ref.shape[0]
    cols, rows, width = c_ref.shape
    cs[...] = c_ref[...].reshape(cols * rows, width)
    for l in range(levels):
        state = cs[pl.ds(l, cols, stride=rows), :].astype(BF16)
        exs[pl.ds(l, cols, stride=rows), :] = jnp.dot(a_ref[l], state, preferred_element_type=F32)
    for l in range(levels, rows):
        exs[pl.ds(l, cols, stride=rows), :] = jnp.zeros((cols, width), F32)
    vertical(vt_ref, exs, out_ref)


def last_kernel(r0, r1, r2, local_ref, vt_ref, out_h, total, cs, out_v, tbl_v, tbl_s, sems):
    levels = out_h.shape[0]
    cols, rows, width = total.shape
    add_edges((r0, r1, r2), vt_ref, total, tbl_v, tbl_s, sems.at[0])
    cs[...] = total[...].reshape(cols * rows, width)
    count = 5
    edges = [levels * i // count for i in range(count + 1)]
    copies = []
    for i, (lo, hi) in enumerate(zip(edges, edges[1:])):
        for l in range(lo, hi):
            out_v[l] = cs[pl.ds(l, cols, stride=rows), :].astype(BF16)
        copies.append(pltpu.make_async_copy(out_v.at[pl.ds(lo, hi - lo)], out_h.at[pl.ds(lo, hi - lo)], sems.at[1 + i]))
        copies[-1].start()
    for copy in copies:
        copy.wait()


VM = pl.BlockSpec(memory_space=pltpu.VMEM)
HB = pl.BlockSpec(memory_space=pltpu.HBM)
DMA = pltpu.SemaphoreType.DMA


def call(kernel, ins, specs, outs, out_specs, scratch, limit, flops=0, aliases=None):
    size = sum(x.size * x.dtype.itemsize for x in (*ins, *outs))
    return pl.pallas_call(
        kernel,
        out_shape=outs,
        in_specs=specs,
        out_specs=out_specs,
        scratch_shapes=scratch,
        input_output_aliases=aliases or {},
        compiler_params=pltpu.CompilerParams(vmem_limit_bytes=limit * 2**20),
        cost_estimate=pl.CostEstimate(flops=flops, bytes_accessed=size, transcendentals=0),
    )(*ins)


def swapped(values, blk, basin):
    n, b = lax.axis_size(blk), lax.axis_size(basin)
    third = lax.ppermute(values[2], basin, [(i, (i + 1) % b) for i in range(b)])
    out = []
    for slot in (1, 0):
        pairs = []
        for i in range(slot, n - 1, 2):
            pairs += [(i, i + 1), (i + 1, i)]
        out.append(lax.ppermute(values[slot], blk, pairs))
    return out[1], out[0], third


def local(tracers, nbr_cols, nbr_wts, self_wts, send_cols, recv_cols, edge_wts, wet_levels, vert_inv):
    cols, levels, width = tracers.shape
    rows = padded(levels)
    nedge = send_cols.shape[1]
    shape = jax.ShapeDtypeStruct
    by_level = jnp.transpose(tracers, (1, 0, 2))
    nbr_by_level = jnp.transpose(nbr_wts, (1, 0, 2))
    edge_by_entry = jnp.transpose(edge_wts, (0, 2, 1))
    wet = wet_levels.reshape(1, cols)
    in_hbm = lambda x: pltpu.with_memory_space_constraint(x, pltpu.HBM)
    send_h = in_hbm(send_cols)
    loads = [by_level, nbr_cols, nbr_by_level, self_wts, wet, vert_inv]
    same = lambda x: shape(x.shape, x.dtype)
    packed = [shape((nedge, rows, width), BF16)] * 3
    flat = pltpu.VMEM((cols * rows, width), F32)
    columns = shape((cols, rows, width), F32)
    tables = [pltpu.VMEM((3, 8, 128), jnp.int32), pltpu.SMEM((3, 8, 128), jnp.int32)]

    first = call(
        functools.partial(gather_kernel, "blk"),
        (in_hbm(by_level), send_h, *map(in_hbm, (recv_cols, edge_by_entry, *loads[1:]))),
        [HB] * 9,
        packed + [same(x) for x in loads] + [shape((128, 128), F32), shape((8, 128), F32)],
        [VM] * 11,
        [
            pltpu.VMEM((rows * (cols + 8), width), F32), pltpu.VMEM((128, 128), F32),
            pltpu.VMEM(recv_cols.shape, jnp.int32), pltpu.VMEM(edge_by_entry.shape, F32),
            pltpu.SMEM(send_cols.shape, jnp.int32), DMA((13,)),
        ],
        16,
    )
    sends, loads, (wts, tbl) = first[:3], first[3:9], first[9:]
    received = swapped(sends, "blk", "basin")
    operator, partial, vt = call(
        operator_kernel, loads, [VM] * 6,
        [shape((levels, cols, cols), BF16), columns, shape((cols, rows, 128), BF16)], [VM] * 3,
        [flat, pltpu.VMEM((levels, 8, cols), F32), pltpu.VMEM((rows * rows, cols), F32), pltpu.VMEM((cols * rows, 128), F32)],
        32, flops=2 * levels * cols * cols * width,
    )
    state, *sends = call(
        functools.partial(first_kernel, "blk", levels),
        (*received, partial, vt, wts, tbl, send_h), [VM] * 7 + [HB],
        [columns] + packed, [VM] * 4,
        tables + [pltpu.SMEM(send_cols.shape, jnp.int32), DMA((2,))], 16,
        flops=2 * cols * rows * rows * width, aliases={3: 0},
    )
    received = swapped(sends, "blk", "basin")
    (partial,) = call(
        middle_kernel, (state, operator, vt), [VM] * 3, [columns], [VM], [flat, flat], 32,
        flops=2 * levels * cols * cols * width,
    )
    out, _ = call(
        last_kernel, (*received, partial, vt), [VM] * 5,
        [shape((levels, cols, width), BF16), columns], [HB, VM],
        [flat, pltpu.VMEM((levels, cols, width), BF16)] + tables + [DMA((6,))], 16,
        flops=2 * cols * rows * rows * width, aliases={3: 1},
    )
    return jnp.transpose(out, (1, 0, 2))


def solution(mesh):
    in_specs = (
        P(("basin", "blk"), None, None),
        P(None, ("basin", "blk")),
        P(None, None, ("basin", "blk")),
        P(None, ("basin", "blk")),
        P(None, ("basin", "blk")),
        P(None, ("basin", "blk")),
        P(None, None, ("basin", "blk")),
        P(("basin", "blk")),
        P(None, None, ("basin", "blk")),
    )
    out_specs = P(("basin", "blk"), None, None)
    return jax.shard_map(local, mesh=mesh, in_specs=in_specs, out_specs=out_specs, check_vma=False)
```

time: 40.1 us -> 29.2 us (0.73)
  local copies, waits for them, and re-layouts: 7.63 us -> 0 us
  Pallas kernels: 17.1 us -> 14.1 us
  starting transfers between devices: 9.14 us -> 9.98 us
  waiting for transfers between devices: 5.63 us -> 4.84 us
    unnamed x26 -> x0, local copies, waits for them, and re-layouts: 7.63 us -> none
    pallas_call x5, Pallas kernels: 17.1 us -> 14.1 us  [call(): pl.pallas_call(kernel, out_shape=outs, in_specs=specs, out_specs=out_spec...]
    ppermute x4, waiting for transfers between devices: 2.73 us -> 0.7 us  [swapped(): out.append(lax.ppermute(values[slot], blk, pairs))]
    ppermute x2, waiting for transfers between devices: 2.9 us -> 4.14 us  [swapped(): third = lax.ppermute(values[2], basin, [(i, (i + 1) % b) for i in range(b)])]
    ppermute x2, starting transfers between devices: 1.59 us -> 2.55 us  [swapped(): third = lax.ppermute(values[2], basin, [(i, (i + 1) % b) for i in range(b)])]
  transfers between devices with their start and end apart: 6 -> 6, of which waited for: 2 -> 3; matrix products, arithmetic and copies ran while one was open for 0% -> 0% of each run, Pallas kernels for 12% -> 26%
where the time goes in v2:
time: 29.2 us; the launch traced here: 29 us
  Pallas kernels  14.1 us (48%)
  starting transfers between devices  9.98 us (34%)
  waiting for transfers between devices  4.84 us (17%)
    pallas_call x5, Pallas kernels, call(): pl.pallas_call(kernel, out_shape=outs, in_specs=specs, out_specs=out_spec...  14.1 us
    ppermute x4, starting transfers between devices, swapped(): out.append(lax.ppermute(values[slot], blk, pairs))  7.42 us
    ppermute x2, waiting for transfers between devices, swapped(): third = lax.ppermute(values[2], basin, [(i, (i + 1) % b) for i in range(b)])  4.14 us
    ppermute x2, starting transfers between devices, swapped(): third = lax.ppermute(values[2], basin, [(i, (i + 1) % b) for i in range(b)])  2.55 us
    ppermute x4, waiting for transfers between devices, swapped(): out.append(lax.ppermute(values[slot], blk, pairs))  0.7 us
  transfers between devices with their start and end apart: 6, of which 3 were waited for; matrix products, arithmetic and copies ran while one was open for 0% of the time, Pallas kernels for 26%

profile of v2, /device:TPU:13, one launch (start us, length us, event | category | flops | bytes accessed | tf_op | source)
XLA Modules:
  0.0 29.0 jit_solution(5538228602023007103)
XLA Ops:
  0.0 2.0 %shard_map.91 = (bf16[16,56,128]{2,1,0:T(8,128)(2,1)S(1)}, bf16[16,56,128]{2,1,0:T(8,128)(2,1)S(1)}, bf16[16,56,128]{2,1,0:T(8,128)(2,1)S(1)}, bf16[50,128,128]{...) custom-call(bf16[50,128,128]{2,1,0:T(8,128)(2,1)} %bitcast.5, ...), custom_call_target="tpu_custom_call" | custom-call | bytes 5585664 | tf_op jit(solution)/shard_map/pallas_call | solution.py:198
  2.0 0.7 %collective-permute-start = (bf16[16,56,128]{2,1,0:T(8,128)(2,1)S(1)}, bf16[16,56,128]{2,1,0:T(8,128)(2,1)S(1)}, u32[]{:S(2)}, u32[]{:S(2)}) collective-permute-start(bf16[16,56,128]{2,1,0:T(8,128)(2,1)S(1)} %get-tuple-element.24), channel_id=1, source_target_pairs={{0,1},{1,0},{2,3},{3,2},{4,5},{5,4},{6,7},{7,6},{8,9},{9,8},{10,11... | collective-permute-start | bytes 688136 | tf_op jit(solution)/shard_map/ppermute | solution.py:218
  2.8 3.0 %collective-permute-start.1 = (bf16[16,56,128]{2,1,0:T(8,128)(2,1)S(1)}, bf16[16,56,128]{2,1,0:T(8,128)(2,1)S(1)}, u32[]{:S(2)}, u32[]{:S(2)}) collective-permute-start(bf16[16,56,128]{2,1,0:T(8,128)(2,1)S(1)} %get-tuple-element.25), channel_id=1, source_target_pairs={{1,2},{2,1},{3,4},{4,3},{5,6},{6,5},{7,8},{8,7},{9,10},{10,9},{11,... | collective-permute-start | bytes 688136 | tf_op jit(solution)/shard_map/ppermute | solution.py:218
  5.8 1.3 %collective-permute-start.2 = (bf16[16,56,128]{2,1,0:T(8,128)(2,1)S(1)}, bf16[16,56,128]{2,1,0:T(8,128)(2,1)S(1)}, u32[]{:S(2)}, u32[]{:S(2)}) collective-permute-start(bf16[16,56,128]{2,1,0:T(8,128)(2,1)S(1)} %get-tuple-element.26), channel_id=1, source_target_pairs={{0,16},{16,0},{1,17},{17,1},{2,18},{18,2},{3,19},{19,3},{4,20},{20... | collective-permute-start | bytes 688136 | tf_op jit(solution)/shard_map/ppermute | solution.py:212
  7.1 4.5 %shard_map.92 = (bf16[50,128,128]{2,1,0:T(8,128)(2,1)S(1)}, f32[128,56,128]{2,1,0:T(8,128)S(1)}, bf16[128,56,128]{2,1,0:T(8,128)(2,1)S(1)}) custom-call(bf16[50,128,128]{2,1,0:T(8,128)(2,1)S(1)} %get-tuple-element.27.c_ref, s32[4,128]{1,0:T(4,128)S(1)} %get-tuple-element.28.nbr_ref, f32[50,4,128]{2,1,0:T(4,128)S(1)} %get-tuple-element.29.nw_ref, ...), custom_call_target="tpu_custom_call" | custom-call | flops 209715200 | bytes 9552384 | tf_op jit(solution)/shard_map/pallas_call | solution.py:198
  11.6 0.0 collective-permute-done.r0
  11.6 0.0 collective-permute-done.1.r1
  11.7 1.7 %collective-permute-done.2.r2 = bf16[16,56,128]{2,1,0:T(8,128)(2,1)S(1)} collective-permute-done((bf16[16,56,128]{2,1,0:T(8,128)(2,1)S(1)}, bf16[16,56,128]{2,1,0:T(8,128)(2,1)S(1)}, u32[]{:S(2)}, u32[]{:S(2)}) %collective-permute-start.2) | collective-permute-done | bytes 229408 | tf_op jit(solution)/shard_map/ppermute | solution.py:212
  13.4 1.7 %shard_map.93 = (f32[128,56,128]{2,1,0:T(8,128)S(1)}, bf16[16,56,128]{2,1,0:T(8,128)(2,1)S(1)}, bf16[16,56,128]{2,1,0:T(8,128)(2,1)S(1)}, bf16[16,56,128]{2,1,0:T(8,128)(2,1)S(1)}) custom-call(bf16[16,56,128]{2,1,0:T(8,128)(2,1)S(1)} %collective-permute-done.r0, bf16[16,56,128]{2,1,0:T(8,128)(2,1)S(1)} %collective-permute-done.1.r1, ...), custom_call_target="tpu_custom_call", output_to_operand_aliasing={{0}: (3, {})} | custom-call | flops 102760448 | bytes 10621120 | tf_op jit(solution)/shard_map/pallas_call | solution.py:198
  15.1 0.5 %collective-permute-start.3 = (bf16[16,56,128]{2,1,0:T(8,128)(2,1)S(1)}, bf16[16,56,128]{2,1,0:T(8,128)(2,1)S(1)}, u32[]{:S(2)}, u32[]{:S(2)}) collective-permute-start(bf16[16,56,128]{2,1,0:T(8,128)(2,1)S(1)} %get-tuple-element.37), channel_id=1, source_target_pairs={{0,1},{1,0},{2,3},{3,2},{4,5},{5,4},{6,7},{7,6},{8,9},{9,8},{10,11... | collective-permute-start | bytes 688136 | tf_op jit(solution)/shard_map/ppermute | solution.py:218
  15.6 3.2 %collective-permute-start.4 = (bf16[16,56,128]{2,1,0:T(8,128)(2,1)S(1)}, bf16[16,56,128]{2,1,0:T(8,128)(2,1)S(1)}, u32[]{:S(2)}, u32[]{:S(2)}) collective-permute-start(bf16[16,56,128]{2,1,0:T(8,128)(2,1)S(1)} %get-tuple-element.38), channel_id=1, source_target_pairs={{1,2},{2,1},{3,4},{4,3},{5,6},{6,5},{7,8},{8,7},{9,10},{10,9},{11,... | collective-permute-start | bytes 688136 | tf_op jit(solution)/shard_map/ppermute | solution.py:218
  18.8 1.3 %collective-permute-start.5 = (bf16[16,56,128]{2,1,0:T(8,128)(2,1)S(1)}, bf16[16,56,128]{2,1,0:T(8,128)(2,1)S(1)}, u32[]{:S(2)}, u32[]{:S(2)}) collective-permute-start(bf16[16,56,128]{2,1,0:T(8,128)(2,1)S(1)} %get-tuple-element.39), channel_id=1, source_target_pairs={{0,16},{16,0},{1,17},{17,1},{2,18},{18,2},{3,19},{19,3},{4,20},{20... | collective-permute-start | bytes 688136 | tf_op jit(solution)/shard_map/ppermute | solution.py:212
  20.0 3.2 %shard_map.94.local_ref = f32[128,56,128]{2,1,0:T(8,128)S(1)} custom-call(f32[128,56,128]{2,1,0:T(8,128)S(1)} %get-tuple-element.40.c_ref, bf16[50,128,128]{2,1,0:T(8,128)(2,1)S(1)} %get-tuple-element.41.a_ref, bf16[128,56,128]{2,1,0:T(8,128)(2,1)S(1)} %get-tuple-element.34.vt_ref), custom_call_target="tpu_custom_call" | custom-call | flops 209715200 | bytes 10813440 | tf_op jit(solution)/shard_map/pallas_call | solution.py:198
  23.2 0.0 collective-permute-done.3.r0
  23.2 0.7 %collective-permute-done.4.r1 = bf16[16,56,128]{2,1,0:T(8,128)(2,1)S(1)} collective-permute-done((bf16[16,56,128]{2,1,0:T(8,128)(2,1)S(1)}, bf16[16,56,128]{2,1,0:T(8,128)(2,1)S(1)}, u32[]{:S(2)}, u32[]{:S(2)}) %collective-permute-start.4) | collective-permute-done | bytes 229408 | tf_op jit(solution)/shard_map/ppermute | solution.py:218
  23.9 2.4 %collective-permute-done.5.r2 = bf16[16,56,128]{2,1,0:T(8,128)(2,1)S(1)} collective-permute-done((bf16[16,56,128]{2,1,0:T(8,128)(2,1)S(1)}, bf16[16,56,128]{2,1,0:T(8,128)(2,1)S(1)}, u32[]{:S(2)}, u32[]{:S(2)}) %collective-permute-start.5) | collective-permute-done | bytes 229408 | tf_op jit(solution)/shard_map/ppermute | solution.py:212
  26.3 2.7 %shard_map.95 = (bf16[50,128,128]{2,1,0:T(8,128)(2,1)}, f32[128,56,128]{2,1,0:T(8,128)S(1)}) custom-call(bf16[16,56,128]{2,1,0:T(8,128)(2,1)S(1)} %collective-permute-done.3.r0, bf16[16,56,128]{2,1,0:T(8,128)(2,1)S(1)} %collective-permute-done.4.r1, bf16[16,56,128]{2,1,0:T(8,128)(2,1)S(1)} %collective-permute-done.5.r2, ...), custom_call_target="tpu_custom_call", output_to_operand_aliasing={{1}: (3, {})} | custom-call | flops 102760448 | bytes 11501568 | tf_op jit(solution)/shard_map/pallas_call | solution.py:198
Async XLA Ops:
  2.0 9.6 %collective-permute-start = (bf16[16,56,128]{2,1,0:T(8,128)(2,1)S(1)}, bf16[16,56,128]{2,1,0:T(8,128)(2,1)S(1)}, u32[]{:S(2)}, u32[]{:S(2)}) collective-permute-start(bf16[16,56,128]{2,1,0:T(8,128)(2,1)S(1)} %get-tuple-element.24), channel_id=1, source_target_pairs={{0,1},{1,0},{2,3},{3,2},{4,5},{5,4},{6,7},{7,6},{8,9},{9,8},{10,11... | collective-permute-start | bytes 688136 | tf_op jit(solution)/shard_map/ppermute | solution.py:218
  2.8 8.9 %collective-permute-start.1 = (bf16[16,56,128]{2,1,0:T(8,128)(2,1)S(1)}, bf16[16,56,128]{2,1,0:T(8,128)(2,1)S(1)}, u32[]{:S(2)}, u32[]{:S(2)}) collective-permute-start(bf16[16,56,128]{2,1,0:T(8,128)(2,1)S(1)} %get-tuple-element.25), channel_id=1, source_target_pairs={{1,2},{2,1},{3,4},{4,3},{5,6},{6,5},{7,8},{8,7},{9,10},{10,9},{11,... | collective-permute-start | bytes 688136 | tf_op jit(solution)/shard_map/ppermute | solution.py:218
  5.8 7.5 %collective-permute-start.2 = (bf16[16,56,128]{2,1,0:T(8,128)(2,1)S(1)}, bf16[16,56,128]{2,1,0:T(8,128)(2,1)S(1)}, u32[]{:S(2)}, u32[]{:S(2)}) collective-permute-start(bf16[16,56,128]{2,1,0:T(8,128)(2,1)S(1)} %get-tuple-element.26), channel_id=1, source_target_pairs={{0,16},{16,0},{1,17},{17,1},{2,18},{18,2},{3,19},{19,3},{4,20},{20... | collective-permute-start | bytes 688136 | tf_op jit(solution)/shard_map/ppermute | solution.py:212
  15.1 8.1 %collective-permute-start.3 = (bf16[16,56,128]{2,1,0:T(8,128)(2,1)S(1)}, bf16[16,56,128]{2,1,0:T(8,128)(2,1)S(1)}, u32[]{:S(2)}, u32[]{:S(2)}) collective-permute-start(bf16[16,56,128]{2,1,0:T(8,128)(2,1)S(1)} %get-tuple-element.37), channel_id=1, source_target_pairs={{0,1},{1,0},{2,3},{3,2},{4,5},{5,4},{6,7},{7,6},{8,9},{9,8},{10,11... | collective-permute-start | bytes 688136 | tf_op jit(solution)/shard_map/ppermute | solution.py:218
  15.6 8.3 %collective-permute-start.4 = (bf16[16,56,128]{2,1,0:T(8,128)(2,1)S(1)}, bf16[16,56,128]{2,1,0:T(8,128)(2,1)S(1)}, u32[]{:S(2)}, u32[]{:S(2)}) collective-permute-start(bf16[16,56,128]{2,1,0:T(8,128)(2,1)S(1)} %get-tuple-element.38), channel_id=1, source_target_pairs={{1,2},{2,1},{3,4},{4,3},{5,6},{6,5},{7,8},{8,7},{9,10},{10,9},{11,... | collective-permute-start | bytes 688136 | tf_op jit(solution)/shard_map/ppermute | solution.py:218
  18.8 7.5 %collective-permute-start.5 = (bf16[16,56,128]{2,1,0:T(8,128)(2,1)S(1)}, bf16[16,56,128]{2,1,0:T(8,128)(2,1)S(1)}, u32[]{:S(2)}, u32[]{:S(2)}) collective-permute-start(bf16[16,56,128]{2,1,0:T(8,128)(2,1)S(1)} %get-tuple-element.39), channel_id=1, source_target_pairs={{0,16},{16,0},{1,17},{17,1},{2,18},{18,2},{3,19},{19,3},{4,20},{20... | collective-permute-start | bytes 688136 | tf_op jit(solution)/shard_map/ppermute | solution.py:212

commit v3 on v2

--- a/solution.py
+++ b/solution.py
@@ -17,7 +17,7 @@
 
 
 def direction(slot, parity):
-    return 2 if slot == 2 else lax.bitwise_xor(parity, jnp.int32(slot))
+    return 2 if slot == 1 else lax.bitwise_xor(parity, jnp.int32(1 - slot // 2))
 
 
 def pack_edges(parity, levels, send, weights, tbl, column, outs):
@@ -209,14 +209,12 @@
 
 def swapped(values, blk, basin):
     n, b = lax.axis_size(blk), lax.axis_size(basin)
-    third = lax.ppermute(values[2], basin, [(i, (i + 1) % b) for i in range(b)])
-    out = []
-    for slot in (1, 0):
-        pairs = []
-        for i in range(slot, n - 1, 2):
-            pairs += [(i, i + 1), (i + 1, i)]
-        out.append(lax.ppermute(values[slot], blk, pairs))
-    return out[1], out[0], third
+    pairs = lambda first: [pair for i in range(first, n - 1, 2) for pair in ((i, i + 1), (i + 1, i))]
+    return (
+        lax.ppermute(values[0], blk, pairs(1)),
+        lax.ppermute(values[1], basin, [(i, (i + 1) % b) for i in range(b)]),
+        lax.ppermute(values[2], blk, pairs(0)),
+    )
 
 
 def local(tracers, nbr_cols, nbr_wts, self_wts, send_cols, recv_cols, edge_wts, wet_levels, vert_inv):

time: 29.2 us -> 28.3 us (0.969)
  the two profiles are of different devices: /device:TPU:13 before, /device:TPU:15 now
where the time goes in v3:
time: 28.3 us; the launch traced here: 28.1 us
  Pallas kernels  14.1 us (50%)
  starting transfers between devices  8.73 us (31%)
  waiting for transfers between devices  5.18 us (18%)
    pallas_call x5, Pallas kernels, call(): pl.pallas_call(kernel, out_shape=outs, in_specs=specs, out_specs=out_spec...  14.1 us
    ppermute x2, starting transfers between devices, swapped(): lax.ppermute(values[0], blk, pairs(1))  8.08 us
    ppermute x2, waiting for transfers between devices, swapped(): lax.ppermute(values[1], basin, [(i, (i + 1) % b) for i in range(b)])  4.7 us
    ppermute x2, starting transfers between devices, swapped(): lax.ppermute(values[1], basin, [(i, (i + 1) % b) for i in range(b)])  0.64 us
  transfers between devices with their start and end apart: 6, of which 3 were waited for; matrix products, arithmetic and copies ran while one was open for 0% of the time, Pallas kernels for 27%

profile of v3, /device:TPU:15, one launch (start us, length us, event | category | flops | bytes accessed | tf_op | source)
XLA Modules:
  0.0 28.1 jit_solution(11282415987747221049)
XLA Ops:
  0.0 2.0 %shard_map.91 = (bf16[16,56,128]{2,1,0:T(8,128)(2,1)S(1)}, bf16[16,56,128]{2,1,0:T(8,128)(2,1)S(1)}, bf16[16,56,128]{2,1,0:T(8,128)(2,1)S(1)}, bf16[50,128,128]{...) custom-call(bf16[50,128,128]{2,1,0:T(8,128)(2,1)} %bitcast.5, ...), custom_call_target="tpu_custom_call" | custom-call | bytes 5585664 | tf_op jit(solution)/shard_map/pallas_call | solution.py:198
  2.0 3.7 %collective-permute-start = (bf16[16,56,128]{2,1,0:T(8,128)(2,1)S(1)}, bf16[16,56,128]{2,1,0:T(8,128)(2,1)S(1)}, u32[]{:S(2)}, u32[]{:S(2)}) collective-permute-start(bf16[16,56,128]{2,1,0:T(8,128)(2,1)S(1)} %get-tuple-element.24), channel_id=1, source_target_pairs={{1,2},{2,1},{3,4},{4,3},{5,6},{6,5},{7,8},{8,7},{9,10},{10,9},{11,... | collective-permute-start | bytes 688136 | tf_op jit(solution)/shard_map/ppermute | solution.py:214
  5.8 0.3 %collective-permute-start.1 = (bf16[16,56,128]{2,1,0:T(8,128)(2,1)S(1)}, bf16[16,56,128]{2,1,0:T(8,128)(2,1)S(1)}, u32[]{:S(2)}, u32[]{:S(2)}) collective-permute-start(bf16[16,56,128]{2,1,0:T(8,128)(2,1)S(1)} %get-tuple-element.25), channel_id=1, source_target_pairs={{0,16},{16,0},{1,17},{17,1},{2,18},{18,2},{3,19},{19,3},{4,20},{20... | collective-permute-start | bytes 688136 | tf_op jit(solution)/shard_map/ppermute | solution.py:215
  6.1 0.0 collective-permute-start.2
  6.1 4.5 %shard_map.92 = (bf16[50,128,128]{2,1,0:T(8,128)(2,1)S(1)}, f32[128,56,128]{2,1,0:T(8,128)S(1)}, bf16[128,56,128]{2,1,0:T(8,128)(2,1)S(1)}) custom-call(bf16[50,128,128]{2,1,0:T(8,128)(2,1)S(1)} %get-tuple-element.27.c_ref, s32[4,128]{1,0:T(4,128)S(1)} %get-tuple-element.28.nbr_ref, f32[50,4,128]{2,1,0:T(4,128)S(1)} %get-tuple-element.29.nw_ref, ...), custom_call_target="tpu_custom_call" | custom-call | flops 209715200 | bytes 9552384 | tf_op jit(solution)/shard_map/pallas_call | solution.py:198
  10.6 0.0 collective-permute-done.r0
  10.6 1.9 %collective-permute-done.1.r1 = bf16[16,56,128]{2,1,0:T(8,128)(2,1)S(1)} collective-permute-done((bf16[16,56,128]{2,1,0:T(8,128)(2,1)S(1)}, bf16[16,56,128]{2,1,0:T(8,128)(2,1)S(1)}, u32[]{:S(2)}, u32[]{:S(2)}) %collective-permute-start.1) | collective-permute-done | bytes 229408 | tf_op jit(solution)/shard_map/ppermute | solution.py:215
  12.5 0.0 collective-permute-done.2.r2
  12.5 1.7 %shard_map.93 = (f32[128,56,128]{2,1,0:T(8,128)S(1)}, bf16[16,56,128]{2,1,0:T(8,128)(2,1)S(1)}, bf16[16,56,128]{2,1,0:T(8,128)(2,1)S(1)}, bf16[16,56,128]{2,1,0:T(8,128)(2,1)S(1)}) custom-call(bf16[16,56,128]{2,1,0:T(8,128)(2,1)S(1)} %collective-permute-done.r0, bf16[16,56,128]{2,1,0:T(8,128)(2,1)S(1)} %collective-permute-done.1.r1, ...), custom_call_target="tpu_custom_call", output_to_operand_aliasing={{0}: (3, {})} | custom-call | flops 102760448 | bytes 10621120 | tf_op jit(solution)/shard_map/pallas_call | solution.py:198
  14.2 4.4 %collective-permute-start.3 = (bf16[16,56,128]{2,1,0:T(8,128)(2,1)S(1)}, bf16[16,56,128]{2,1,0:T(8,128)(2,1)S(1)}, u32[]{:S(2)}, u32[]{:S(2)}) collective-permute-start(bf16[16,56,128]{2,1,0:T(8,128)(2,1)S(1)} %get-tuple-element.37), channel_id=1, source_target_pairs={{1,2},{2,1},{3,4},{4,3},{5,6},{6,5},{7,8},{8,7},{9,10},{10,9},{11,... | collective-permute-start | bytes 688136 | tf_op jit(solution)/shard_map/ppermute | solution.py:214
  18.6 0.3 %collective-permute-start.4 = (bf16[16,56,128]{2,1,0:T(8,128)(2,1)S(1)}, bf16[16,56,128]{2,1,0:T(8,128)(2,1)S(1)}, u32[]{:S(2)}, u32[]{:S(2)}) collective-permute-start(bf16[16,56,128]{2,1,0:T(8,128)(2,1)S(1)} %get-tuple-element.38), channel_id=1, source_target_pairs={{0,16},{16,0},{1,17},{17,1},{2,18},{18,2},{3,19},{19,3},{4,20},{20... | collective-permute-start | bytes 688136 | tf_op jit(solution)/shard_map/ppermute | solution.py:215
  18.9 0.0 collective-permute-start.5
  18.9 3.2 %shard_map.94.local_ref = f32[128,56,128]{2,1,0:T(8,128)S(1)} custom-call(f32[128,56,128]{2,1,0:T(8,128)S(1)} %get-tuple-element.40.c_ref, bf16[50,128,128]{2,1,0:T(8,128)(2,1)S(1)} %get-tuple-element.41.a_ref, bf16[128,56,128]{2,1,0:T(8,128)(2,1)S(1)} %get-tuple-element.34.vt_ref), custom_call_target="tpu_custom_call" | custom-call | flops 209715200 | bytes 10813440 | tf_op jit(solution)/shard_map/pallas_call | solution.py:198
  22.1 0.5 %collective-permute-done.3.r0 = bf16[16,56,128]{2,1,0:T(8,128)(2,1)S(1)} collective-permute-done((bf16[16,56,128]{2,1,0:T(8,128)(2,1)S(1)}, bf16[16,56,128]{2,1,0:T(8,128)(2,1)S(1)}, u32[]{:S(2)}, u32[]{:S(2)}) %collective-permute-start.3) | collective-permute-done | bytes 229408 | tf_op jit(solution)/shard_map/ppermute | solution.py:214
  22.6 2.8 %collective-permute-done.4.r1 = bf16[16,56,128]{2,1,0:T(8,128)(2,1)S(1)} collective-permute-done((bf16[16,56,128]{2,1,0:T(8,128)(2,1)S(1)}, bf16[16,56,128]{2,1,0:T(8,128)(2,1)S(1)}, u32[]{:S(2)}, u32[]{:S(2)}) %collective-permute-start.4) | collective-permute-done | bytes 229408 | tf_op jit(solution)/shard_map/ppermute | solution.py:215
  25.4 0.0 collective-permute-done.5.r2
  25.4 2.7 %shard_map.95 = (bf16[50,128,128]{2,1,0:T(8,128)(2,1)}, f32[128,56,128]{2,1,0:T(8,128)S(1)}) custom-call(bf16[16,56,128]{2,1,0:T(8,128)(2,1)S(1)} %collective-permute-done.3.r0, bf16[16,56,128]{2,1,0:T(8,128)(2,1)S(1)} %collective-permute-done.4.r1, bf16[16,56,128]{2,1,0:T(8,128)(2,1)S(1)} %collective-permute-done.5.r2, ...), custom_call_target="tpu_custom_call", output_to_operand_aliasing={{1}: (3, {})} | custom-call | flops 102760448 | bytes 11501568 | tf_op jit(solution)/shard_map/pallas_call | solution.py:198
Async XLA Ops:
  2.0 8.6 %collective-permute-start = (bf16[16,56,128]{2,1,0:T(8,128)(2,1)S(1)}, bf16[16,56,128]{2,1,0:T(8,128)(2,1)S(1)}, u32[]{:S(2)}, u32[]{:S(2)}) collective-permute-start(bf16[16,56,128]{2,1,0:T(8,128)(2,1)S(1)} %get-tuple-element.24), channel_id=1, source_target_pairs={{1,2},{2,1},{3,4},{4,3},{5,6},{6,5},{7,8},{8,7},{9,10},{10,9},{11,... | collective-permute-start | bytes 688136 | tf_op jit(solution)/shard_map/ppermute | solution.py:214
  5.8 6.7 %collective-permute-start.1 = (bf16[16,56,128]{2,1,0:T(8,128)(2,1)S(1)}, bf16[16,56,128]{2,1,0:T(8,128)(2,1)S(1)}, u32[]{:S(2)}, u32[]{:S(2)}) collective-permute-start(bf16[16,56,128]{2,1,0:T(8,128)(2,1)S(1)} %get-tuple-element.25), channel_id=1, source_target_pairs={{0,16},{16,0},{1,17},{17,1},{2,18},{18,2},{3,19},{19,3},{4,20},{20... | collective-permute-start | bytes 688136 | tf_op jit(solution)/shard_map/ppermute | solution.py:215
  6.1 6.4 %collective-permute-start.2 = (bf16[16,56,128]{2,1,0:T(8,128)(2,1)S(1)}, bf16[16,56,128]{2,1,0:T(8,128)(2,1)S(1)}, u32[]{:S(2)}, u32[]{:S(2)}) collective-permute-start(bf16[16,56,128]{2,1,0:T(8,128)(2,1)S(1)} %get-tuple-element.26), channel_id=1, source_target_pairs={{0,1},{1,0},{2,3},{3,2},{4,5},{5,4},{6,7},{7,6},{8,9},{9,8},{10,11... | collective-permute-start | bytes 688136 | tf_op jit(solution)/shard_map/ppermute | solution.py:216
  14.2 8.3 %collective-permute-start.3 = (bf16[16,56,128]{2,1,0:T(8,128)(2,1)S(1)}, bf16[16,56,128]{2,1,0:T(8,128)(2,1)S(1)}, u32[]{:S(2)}, u32[]{:S(2)}) collective-permute-start(bf16[16,56,128]{2,1,0:T(8,128)(2,1)S(1)} %get-tuple-element.37), channel_id=1, source_target_pairs={{1,2},{2,1},{3,4},{4,3},{5,6},{6,5},{7,8},{8,7},{9,10},{10,9},{11,... | collective-permute-start | bytes 688136 | tf_op jit(solution)/shard_map/ppermute | solution.py:214
  18.6 6.8 %collective-permute-start.4 = (bf16[16,56,128]{2,1,0:T(8,128)(2,1)S(1)}, bf16[16,56,128]{2,1,0:T(8,128)(2,1)S(1)}, u32[]{:S(2)}, u32[]{:S(2)}) collective-permute-start(bf16[16,56,128]{2,1,0:T(8,128)(2,1)S(1)} %get-tuple-element.38), channel_id=1, source_target_pairs={{0,16},{16,0},{1,17},{17,1},{2,18},{18,2},{3,19},{19,3},{4,20},{20... | collective-permute-start | bytes 688136 | tf_op jit(solution)/shard_map/ppermute | solution.py:215
  18.9 6.5 %collective-permute-start.5 = (bf16[16,56,128]{2,1,0:T(8,128)(2,1)S(1)}, bf16[16,56,128]{2,1,0:T(8,128)(2,1)S(1)}, u32[]{:S(2)}, u32[]{:S(2)}) collective-permute-start(bf16[16,56,128]{2,1,0:T(8,128)(2,1)S(1)} %get-tuple-element.39), channel_id=1, source_target_pairs={{0,1},{1,0},{2,3},{3,2},{4,5},{5,4},{6,7},{7,6},{8,9},{9,8},{10,11... | collective-permute-start | bytes 688136 | tf_op jit(solution)/shard_map/ppermute | solution.py:216

commit v4 on v3

--- a/solution.py
+++ b/solution.py
@@ -18,6 +18,11 @@
 
 def direction(slot, parity):
     return 2 if slot == 1 else lax.bitwise_xor(parity, jnp.int32(1 - slot // 2))
+
+
+def has_partner(slot, at, count):
+    first = lax.bitwise_and(at + slot // 2, jnp.int32(1)) == 1
+    return jnp.where(first, at + 1 < count, at > 0)
 
 
 def pack_edges(parity, levels, send, weights, tbl, column, outs):
@@ -88,7 +93,10 @@
         copy.wait()
     for slot in range(3):
         d = direction(slot, parity)
-        wts[slot * nedge : (slot + 1) * nedge, 0:levels] = edge_v[d]
+        weight = edge_v[d]
+        if slot != 1:
+            weight = jnp.where(has_partner(slot, lax.axis_index(blk), lax.axis_size(blk)), weight, 0.0)
+        wts[slot * nedge : (slot + 1) * nedge, 0:levels] = weight
         tbl_o[slot : slot + 1, 0:nedge] = recv_v[pl.ds(d, 1), :].astype(F32)
     weights = wts[...].T
     wts_o[...] = weights
@@ -209,7 +217,12 @@
 
 def swapped(values, blk, basin):
     n, b = lax.axis_size(blk), lax.axis_size(basin)
-    pairs = lambda first: [pair for i in range(first, n - 1, 2) for pair in ((i, i + 1), (i + 1, i))]
+
+    def pairs(first):
+        partner = {i: i + 1 for i in range(first, n - 1, 2)}
+        partner |= {j: i for i, j in partner.items()}
+        return [(i, partner.get(i, i)) for i in range(n)]
+
     return (
         lax.ppermute(values[0], blk, pairs(1)),
         lax.ppermute(values[1], basin, [(i, (i + 1) % b) for i in range(b)]),

time: 28.3 us -> 28.3 us (level)
  the two profiles are of different devices: /device:TPU:15 before, /device:TPU:23 now
where the time goes in v4:
time: 28.3 us; the launch traced here: 28.1 us
  Pallas kernels  14.1 us (50%)
  starting transfers between devices  8.72 us (31%)
  waiting for transfers between devices  5.18 us (18%)
    pallas_call x5, Pallas kernels, call(): pl.pallas_call(kernel, out_shape=outs, in_specs=specs, out_specs=out_spec...  14.1 us
    ppermute x2, starting transfers between devices, swapped(): lax.ppermute(values[0], blk, pairs(1))  8.08 us
    ppermute x2, waiting for transfers between devices, swapped(): lax.ppermute(values[1], basin, [(i, (i + 1) % b) for i in range(b)])  4.7 us
    ppermute x2, starting transfers between devices, swapped(): lax.ppermute(values[1], basin, [(i, (i + 1) % b) for i in range(b)])  0.64 us
  transfers between devices with their start and end apart: 6, of which 3 were waited for; matrix products, arithmetic and copies ran while one was open for 0% of the time, Pallas kernels for 27%

profile of v4, /device:TPU:23, one launch (start us, length us, event | category | flops | bytes accessed | tf_op | source)
XLA Modules:
  0.0 28.1 jit_solution(12848169995498848676)
XLA Ops:
  0.0 2.0 %shard_map.91 = (bf16[16,56,128]{2,1,0:T(8,128)(2,1)S(1)}, bf16[16,56,128]{2,1,0:T(8,128)(2,1)S(1)}, bf16[16,56,128]{2,1,0:T(8,128)(2,1)S(1)}, bf16[50,128,128]{...) custom-call(bf16[50,128,128]{2,1,0:T(8,128)(2,1)} %bitcast.5, ...), custom_call_target="tpu_custom_call" | custom-call | bytes 5585664 | tf_op jit(solution)/shard_map/pallas_call | solution.py:206
  2.0 3.7 %collective-permute-start = (bf16[16,56,128]{2,1,0:T(8,128)(2,1)S(1)}, bf16[16,56,128]{2,1,0:T(8,128)(2,1)S(1)}, u32[]{:S(2)}, u32[]{:S(2)}) collective-permute-start(bf16[16,56,128]{2,1,0:T(8,128)(2,1)S(1)} %get-tuple-element.24), channel_id=1, source_target_pairs={{0,0},{1,2},{2,1},{3,4},{4,3},{5,6},{6,5},{7,8},{8,7},{9,10},{10,9... | collective-permute-start | bytes 688136 | tf_op jit(solution)/shard_map/ppermute | solution.py:227
  5.8 0.3 %collective-permute-start.1 = (bf16[16,56,128]{2,1,0:T(8,128)(2,1)S(1)}, bf16[16,56,128]{2,1,0:T(8,128)(2,1)S(1)}, u32[]{:S(2)}, u32[]{:S(2)}) collective-permute-start(bf16[16,56,128]{2,1,0:T(8,128)(2,1)S(1)} %get-tuple-element.25), channel_id=1, source_target_pairs={{0,16},{16,0},{1,17},{17,1},{2,18},{18,2},{3,19},{19,3},{4,20},{20... | collective-permute-start | bytes 688136 | tf_op jit(solution)/shard_map/ppermute | solution.py:228
  6.1 0.0 collective-permute-start.2
  6.1 4.5 %shard_map.92 = (bf16[50,128,128]{2,1,0:T(8,128)(2,1)S(1)}, f32[128,56,128]{2,1,0:T(8,128)S(1)}, bf16[128,56,128]{2,1,0:T(8,128)(2,1)S(1)}) custom-call(bf16[50,128,128]{2,1,0:T(8,128)(2,1)S(1)} %get-tuple-element.27.c_ref, s32[4,128]{1,0:T(4,128)S(1)} %get-tuple-element.28.nbr_ref, f32[50,4,128]{2,1,0:T(4,128)S(1)} %get-tuple-element.29.nw_ref, ...), custom_call_target="tpu_custom_call" | custom-call | flops 209715200 | bytes 9552384 | tf_op jit(solution)/shard_map/pallas_call | solution.py:206
  10.6 0.0 collective-permute-done.r0
  10.6 1.9 %collective-permute-done.1.r1 = bf16[16,56,128]{2,1,0:T(8,128)(2,1)S(1)} collective-permute-done((bf16[16,56,128]{2,1,0:T(8,128)(2,1)S(1)}, bf16[16,56,128]{2,1,0:T(8,128)(2,1)S(1)}, u32[]{:S(2)}, u32[]{:S(2)}) %collective-permute-start.1) | collective-permute-done | bytes 229408 | tf_op jit(solution)/shard_map/ppermute | solution.py:228
  12.5 0.0 collective-permute-done.2.r2
  12.5 1.7 %shard_map.93 = (f32[128,56,128]{2,1,0:T(8,128)S(1)}, bf16[16,56,128]{2,1,0:T(8,128)(2,1)S(1)}, bf16[16,56,128]{2,1,0:T(8,128)(2,1)S(1)}, bf16[16,56,128]{2,1,0:T(8,128)(2,1)S(1)}) custom-call(bf16[16,56,128]{2,1,0:T(8,128)(2,1)S(1)} %collective-permute-done.r0, bf16[16,56,128]{2,1,0:T(8,128)(2,1)S(1)} %collective-permute-done.1.r1, ...), custom_call_target="tpu_custom_call", output_to_operand_aliasing={{0}: (3, {})} | custom-call | flops 102760448 | bytes 10621120 | tf_op jit(solution)/shard_map/pallas_call | solution.py:206
  14.2 4.4 %collective-permute-start.3 = (bf16[16,56,128]{2,1,0:T(8,128)(2,1)S(1)}, bf16[16,56,128]{2,1,0:T(8,128)(2,1)S(1)}, u32[]{:S(2)}, u32[]{:S(2)}) collective-permute-start(bf16[16,56,128]{2,1,0:T(8,128)(2,1)S(1)} %get-tuple-element.37), channel_id=1, source_target_pairs={{0,0},{1,2},{2,1},{3,4},{4,3},{5,6},{6,5},{7,8},{8,7},{9,10},{10,9... | collective-permute-start | bytes 688136 | tf_op jit(solution)/shard_map/ppermute | solution.py:227
  18.6 0.3 %collective-permute-start.4 = (bf16[16,56,128]{2,1,0:T(8,128)(2,1)S(1)}, bf16[16,56,128]{2,1,0:T(8,128)(2,1)S(1)}, u32[]{:S(2)}, u32[]{:S(2)}) collective-permute-start(bf16[16,56,128]{2,1,0:T(8,128)(2,1)S(1)} %get-tuple-element.38), channel_id=1, source_target_pairs={{0,16},{16,0},{1,17},{17,1},{2,18},{18,2},{3,19},{19,3},{4,20},{20... | collective-permute-start | bytes 688136 | tf_op jit(solution)/shard_map/ppermute | solution.py:228
  18.9 0.0 collective-permute-start.5
  18.9 3.2 %shard_map.94.local_ref = f32[128,56,128]{2,1,0:T(8,128)S(1)} custom-call(f32[128,56,128]{2,1,0:T(8,128)S(1)} %get-tuple-element.40.c_ref, bf16[50,128,128]{2,1,0:T(8,128)(2,1)S(1)} %get-tuple-element.41.a_ref, bf16[128,56,128]{2,1,0:T(8,128)(2,1)S(1)} %get-tuple-element.34.vt_ref), custom_call_target="tpu_custom_call" | custom-call | flops 209715200 | bytes 10813440 | tf_op jit(solution)/shard_map/pallas_call | solution.py:206
  22.1 0.5 %collective-permute-done.3.r0 = bf16[16,56,128]{2,1,0:T(8,128)(2,1)S(1)} collective-permute-done((bf16[16,56,128]{2,1,0:T(8,128)(2,1)S(1)}, bf16[16,56,128]{2,1,0:T(8,128)(2,1)S(1)}, u32[]{:S(2)}, u32[]{:S(2)}) %collective-permute-start.3) | collective-permute-done | bytes 229408 | tf_op jit(solution)/shard_map/ppermute | solution.py:227
  22.6 2.8 %collective-permute-done.4.r1 = bf16[16,56,128]{2,1,0:T(8,128)(2,1)S(1)} collective-permute-done((bf16[16,56,128]{2,1,0:T(8,128)(2,1)S(1)}, bf16[16,56,128]{2,1,0:T(8,128)(2,1)S(1)}, u32[]{:S(2)}, u32[]{:S(2)}) %collective-permute-start.4) | collective-permute-done | bytes 229408 | tf_op jit(solution)/shard_map/ppermute | solution.py:228
  25.4 0.0 collective-permute-done.5.r2
  25.4 2.7 %shard_map.95 = (bf16[50,128,128]{2,1,0:T(8,128)(2,1)}, f32[128,56,128]{2,1,0:T(8,128)S(1)}) custom-call(bf16[16,56,128]{2,1,0:T(8,128)(2,1)S(1)} %collective-permute-done.3.r0, bf16[16,56,128]{2,1,0:T(8,128)(2,1)S(1)} %collective-permute-done.4.r1, bf16[16,56,128]{2,1,0:T(8,128)(2,1)S(1)} %collective-permute-done.5.r2, ...), custom_call_target="tpu_custom_call", output_to_operand_aliasing={{1}: (3, {})} | custom-call | flops 102760448 | bytes 11501568 | tf_op jit(solution)/shard_map/pallas_call | solution.py:206
Async XLA Ops:
  2.0 8.6 %collective-permute-start = (bf16[16,56,128]{2,1,0:T(8,128)(2,1)S(1)}, bf16[16,56,128]{2,1,0:T(8,128)(2,1)S(1)}, u32[]{:S(2)}, u32[]{:S(2)}) collective-permute-start(bf16[16,56,128]{2,1,0:T(8,128)(2,1)S(1)} %get-tuple-element.24), channel_id=1, source_target_pairs={{0,0},{1,2},{2,1},{3,4},{4,3},{5,6},{6,5},{7,8},{8,7},{9,10},{10,9... | collective-permute-start | bytes 688136 | tf_op jit(solution)/shard_map/ppermute | solution.py:227
  5.8 6.7 %collective-permute-start.1 = (bf16[16,56,128]{2,1,0:T(8,128)(2,1)S(1)}, bf16[16,56,128]{2,1,0:T(8,128)(2,1)S(1)}, u32[]{:S(2)}, u32[]{:S(2)}) collective-permute-start(bf16[16,56,128]{2,1,0:T(8,128)(2,1)S(1)} %get-tuple-element.25), channel_id=1, source_target_pairs={{0,16},{16,0},{1,17},{17,1},{2,18},{18,2},{3,19},{19,3},{4,20},{20... | collective-permute-start | bytes 688136 | tf_op jit(solution)/shard_map/ppermute | solution.py:228
  6.1 6.4 %collective-permute-start.2 = (bf16[16,56,128]{2,1,0:T(8,128)(2,1)S(1)}, bf16[16,56,128]{2,1,0:T(8,128)(2,1)S(1)}, u32[]{:S(2)}, u32[]{:S(2)}) collective-permute-start(bf16[16,56,128]{2,1,0:T(8,128)(2,1)S(1)} %get-tuple-element.26), channel_id=1, source_target_pairs={{0,1},{1,0},{2,3},{3,2},{4,5},{5,4},{6,7},{7,6},{8,9},{9,8},{10,11... | collective-permute-start | bytes 688136 | tf_op jit(solution)/shard_map/ppermute | solution.py:229
  14.2 8.3 %collective-permute-start.3 = (bf16[16,56,128]{2,1,0:T(8,128)(2,1)S(1)}, bf16[16,56,128]{2,1,0:T(8,128)(2,1)S(1)}, u32[]{:S(2)}, u32[]{:S(2)}) collective-permute-start(bf16[16,56,128]{2,1,0:T(8,128)(2,1)S(1)} %get-tuple-element.37), channel_id=1, source_target_pairs={{0,0},{1,2},{2,1},{3,4},{4,3},{5,6},{6,5},{7,8},{8,7},{9,10},{10,9... | collective-permute-start | bytes 688136 | tf_op jit(solution)/shard_map/ppermute | solution.py:227
  18.6 6.8 %collective-permute-start.4 = (bf16[16,56,128]{2,1,0:T(8,128)(2,1)S(1)}, bf16[16,56,128]{2,1,0:T(8,128)(2,1)S(1)}, u32[]{:S(2)}, u32[]{:S(2)}) collective-permute-start(bf16[16,56,128]{2,1,0:T(8,128)(2,1)S(1)} %get-tuple-element.38), channel_id=1, source_target_pairs={{0,16},{16,0},{1,17},{17,1},{2,18},{18,2},{3,19},{19,3},{4,20},{20... | collective-permute-start | bytes 688136 | tf_op jit(solution)/shard_map/ppermute | solution.py:228
  18.9 6.5 %collective-permute-start.5 = (bf16[16,56,128]{2,1,0:T(8,128)(2,1)S(1)}, bf16[16,56,128]{2,1,0:T(8,128)(2,1)S(1)}, u32[]{:S(2)}, u32[]{:S(2)}) collective-permute-start(bf16[16,56,128]{2,1,0:T(8,128)(2,1)S(1)} %get-tuple-element.39), channel_id=1, source_target_pairs={{0,1},{1,0},{2,3},{3,2},{4,5},{5,4},{6,7},{7,6},{8,9},{9,8},{10,11... | collective-permute-start | bytes 688136 | tf_op jit(solution)/shard_map/ppermute | solution.py:229

commit v5 on v3

--- a/solution.py
+++ b/solution.py
@@ -210,11 +210,14 @@
 def swapped(values, blk, basin):
     n, b = lax.axis_size(blk), lax.axis_size(basin)
     pairs = lambda first: [pair for i in range(first, n - 1, 2) for pair in ((i, i + 1), (i + 1, i))]
-    return (
-        lax.ppermute(values[0], blk, pairs(1)),
-        lax.ppermute(values[1], basin, [(i, (i + 1) % b) for i in range(b)]),
-        lax.ppermute(values[2], blk, pairs(0)),
-    )
+    if n % 2:
+        odd = lax.ppermute(values[0], blk, pairs(1))
+    else:
+        held = lax.ppermute(values[0], blk, pairs(0))
+    along = lax.ppermute(values[1], basin, [(i, (i + 1) % b) for i in range(b)])
+    if not n % 2:
+        odd = lax.ppermute(held, blk, [pair for i in range(0, n - 2, 2) for pair in ((i, i + 2), (i + 3, i + 1))])
+    return odd, along, lax.ppermute(values[2], blk, pairs(0))
 
 
 def local(tracers, nbr_cols, nbr_wts, self_wts, send_cols, recv_cols, edge_wts, wet_levels, vert_inv):

time: 28.3 us -> 31.2 us (1.10)
  the two profiles are of different devices: /device:TPU:15 before, /device:TPU:0 now
where the time goes in v5:
time: 31.2 us; the launch traced here: 31 us
  Pallas kernels  14.1 us (45%)
  starting transfers between devices  12.6 us (40%)
  waiting for transfers between devices  4.23 us (14%)
    pallas_call x5, Pallas kernels, call(): pl.pallas_call(kernel, out_shape=outs, in_specs=specs, out_specs=out_spec...  14.1 us
    ppermute x2, starting transfers between devices, swapped(): lax.ppermute(held, blk, [pair for i in range(0, n - 2, 2) for pair in ((i...  7.81 us
    ppermute x2, waiting for transfers between devices, swapped(): lax.ppermute(held, blk, [pair for i in range(0, n - 2, 2) for pair in ((i...  4.2 us
    ppermute x2, starting transfers between devices, swapped(): along = lax.ppermute(values[1], basin, [(i, (i + 1) % b) for i in range(b)])  3.87 us
  transfers between devices with their start and end apart: 8, of which 2 were waited for; matrix products, arithmetic and copies ran while one was open for 0% of the time, Pallas kernels for 25%

profile of v5, /device:TPU:0, one launch (start us, length us, event | category | flops | bytes accessed | tf_op | source)
XLA Modules:
  0.0 31.0 jit_solution(3361208626801276546)
XLA Ops:
  0.0 2.0 %shard_map.91 = (bf16[16,56,128]{2,1,0:T(8,128)(2,1)S(1)}, bf16[16,56,128]{2,1,0:T(8,128)(2,1)S(1)}, bf16[16,56,128]{2,1,0:T(8,128)(2,1)S(1)}, bf16[50,128,128]{...) custom-call(bf16[50,128,128]{2,1,0:T(8,128)(2,1)} %bitcast.5, ...), custom_call_target="tpu_custom_call" | custom-call | bytes 5585664 | tf_op jit(solution)/shard_map/pallas_call | solution.py:198
  2.0 0.5 %collective-permute-start = (bf16[16,56,128]{2,1,0:T(8,128)(2,1)S(1)}, bf16[16,56,128]{2,1,0:T(8,128)(2,1)S(1)}, u32[]{:S(2)}, u32[]{:S(2)}) collective-permute-start(bf16[16,56,128]{2,1,0:T(8,128)(2,1)S(1)} %get-tuple-element.24), channel_id=1, source_target_pairs={{0,1},{1,0},{2,3},{3,2},{4,5},{5,4},{6,7},{7,6},{8,9},{9,8},{10,11... | collective-permute-start | bytes 688136 | tf_op jit(solution)/shard_map/ppermute | solution.py:216
  2.6 2.6 %collective-permute-start.2 = (bf16[16,56,128]{2,1,0:T(8,128)(2,1)S(1)}, bf16[16,56,128]{2,1,0:T(8,128)(2,1)S(1)}, u32[]{:S(2)}, u32[]{:S(2)}) collective-permute-start(bf16[16,56,128]{2,1,0:T(8,128)(2,1)S(1)} %get-tuple-element.25), channel_id=1, source_target_pairs={{0,16},{16,0},{1,17},{17,1},{2,18},{18,2},{3,19},{19,3},{4,20},{20... | collective-permute-start | bytes 688136 | tf_op jit(solution)/shard_map/ppermute | solution.py:217
  5.1 0.2 collective-permute-start.3
  5.3 0.0 collective-permute-done
  5.3 3.4 %collective-permute-start.1 = (bf16[16,56,128]{2,1,0:T(8,128)(2,1)S(1)}, bf16[16,56,128]{2,1,0:T(8,128)(2,1)S(1)}, u32[]{:S(2)}, u32[]{:S(2)}) collective-permute-start(bf16[16,56,128]{2,1,0:T(8,128)(2,1)S(1)} %collective-permute-done), channel_id=1, source_target_pairs={{0,2},{3,1},{2,4},{5,3},{4,6},{7,5},{6,8},{9,7},{8,10},{11,9},{10,... | collective-permute-start | bytes 688136 | tf_op jit(solution)/shard_map/ppermute | solution.py:219
  8.7 4.5 %shard_map.92 = (bf16[50,128,128]{2,1,0:T(8,128)(2,1)S(1)}, f32[128,56,128]{2,1,0:T(8,128)S(1)}, bf16[128,56,128]{2,1,0:T(8,128)(2,1)S(1)}) custom-call(bf16[50,128,128]{2,1,0:T(8,128)(2,1)S(1)} %get-tuple-element.27.c_ref, s32[4,128]{1,0:T(4,128)S(1)} %get-tuple-element.28.nbr_ref, f32[50,4,128]{2,1,0:T(4,128)S(1)} %get-tuple-element.29.nw_ref, ...), custom_call_target="tpu_custom_call" | custom-call | flops 209715200 | bytes 9552384 | tf_op jit(solution)/shard_map/pallas_call | solution.py:198
  13.2 0.0 collective-permute-done.2.r1
  13.3 0.0 collective-permute-done.3.r2
  13.3 1.4 %collective-permute-done.1.r0 = bf16[16,56,128]{2,1,0:T(8,128)(2,1)S(1)} collective-permute-done((bf16[16,56,128]{2,1,0:T(8,128)(2,1)S(1)}, bf16[16,56,128]{2,1,0:T(8,128)(2,1)S(1)}, u32[]{:S(2)}, u32[]{:S(2)}) %collective-permute-start.1) | collective-permute-done | bytes 229408 | tf_op jit(solution)/shard_map/ppermute | solution.py:219
  14.7 1.7 %shard_map.93 = (f32[128,56,128]{2,1,0:T(8,128)S(1)}, bf16[16,56,128]{2,1,0:T(8,128)(2,1)S(1)}, bf16[16,56,128]{2,1,0:T(8,128)(2,1)S(1)}, bf16[16,56,128]{2,1,0:T(8,128)(2,1)S(1)}) custom-call(bf16[16,56,128]{2,1,0:T(8,128)(2,1)S(1)} %collective-permute-done.1.r0, ...), custom_call_target="tpu_custom_call", output_to_operand_aliasing={{0}: (3, {})} | custom-call | flops 102760448 | bytes 10621120 | tf_op jit(solution)/shard_map/pallas_call | solution.py:198
  16.4 0.1 collective-permute-start.4
  16.5 1.3 %collective-permute-start.6 = (bf16[16,56,128]{2,1,0:T(8,128)(2,1)S(1)}, bf16[16,56,128]{2,1,0:T(8,128)(2,1)S(1)}, u32[]{:S(2)}, u32[]{:S(2)}) collective-permute-start(bf16[16,56,128]{2,1,0:T(8,128)(2,1)S(1)} %get-tuple-element.38), channel_id=1, source_target_pairs={{0,16},{16,0},{1,17},{17,1},{2,18},{18,2},{3,19},{19,3},{4,20},{20... | collective-permute-start | bytes 688136 | tf_op jit(solution)/shard_map/ppermute | solution.py:217
  17.8 0.2 collective-permute-start.7
  18.0 0.0 collective-permute-done.4
  18.0 4.4 %collective-permute-start.5 = (bf16[16,56,128]{2,1,0:T(8,128)(2,1)S(1)}, bf16[16,56,128]{2,1,0:T(8,128)(2,1)S(1)}, u32[]{:S(2)}, u32[]{:S(2)}) collective-permute-start(bf16[16,56,128]{2,1,0:T(8,128)(2,1)S(1)} %collective-permute-done.4), channel_id=1, source_target_pairs={{0,2},{3,1},{2,4},{5,3},{4,6},{7,5},{6,8},{9,7},{8,10},{11,9},{10,... | collective-permute-start | bytes 688136 | tf_op jit(solution)/shard_map/ppermute | solution.py:219
  22.4 3.2 %shard_map.94.local_ref = f32[128,56,128]{2,1,0:T(8,128)S(1)} custom-call(f32[128,56,128]{2,1,0:T(8,128)S(1)} %get-tuple-element.40.c_ref, bf16[50,128,128]{2,1,0:T(8,128)(2,1)S(1)} %get-tuple-element.41.a_ref, bf16[128,56,128]{2,1,0:T(8,128)(2,1)S(1)} %get-tuple-element.34.vt_ref), custom_call_target="tpu_custom_call" | custom-call | flops 209715200 | bytes 10813440 | tf_op jit(solution)/shard_map/pallas_call | solution.py:198
  25.5 0.0 collective-permute-done.6.r1
  25.5 0.0 collective-permute-done.7.r2
  25.5 2.8 %collective-permute-done.5.r0 = bf16[16,56,128]{2,1,0:T(8,128)(2,1)S(1)} collective-permute-done((bf16[16,56,128]{2,1,0:T(8,128)(2,1)S(1)}, bf16[16,56,128]{2,1,0:T(8,128)(2,1)S(1)}, u32[]{:S(2)}, u32[]{:S(2)}) %collective-permute-start.5) | collective-permute-done | bytes 229408 | tf_op jit(solution)/shard_map/ppermute | solution.py:219
  28.3 2.7 %shard_map.95 = (bf16[50,128,128]{2,1,0:T(8,128)(2,1)}, f32[128,56,128]{2,1,0:T(8,128)S(1)}) custom-call(bf16[16,56,128]{2,1,0:T(8,128)(2,1)S(1)} %collective-permute-done.5.r0, bf16[16,56,128]{2,1,0:T(8,128)(2,1)S(1)} %collective-permute-done.6.r1, bf16[16,56,128]{2,1,0:T(8,128)(2,1)S(1)} %collective-permute-done.7.r2, ...), custom_call_target="tpu_custom_call", output_to_operand_aliasing={{1}: (3, {})} | custom-call | flops 102760448 | bytes 11501568 | tf_op jit(solution)/shard_map/pallas_call | solution.py:198
Async XLA Ops:
  2.0 3.3 %collective-permute-start = (bf16[16,56,128]{2,1,0:T(8,128)(2,1)S(1)}, bf16[16,56,128]{2,1,0:T(8,128)(2,1)S(1)}, u32[]{:S(2)}, u32[]{:S(2)}) collective-permute-start(bf16[16,56,128]{2,1,0:T(8,128)(2,1)S(1)} %get-tuple-element.24), channel_id=1, source_target_pairs={{0,1},{1,0},{2,3},{3,2},{4,5},{5,4},{6,7},{7,6},{8,9},{9,8},{10,11... | collective-permute-start | bytes 688136 | tf_op jit(solution)/shard_map/ppermute | solution.py:216
  2.6 10.7 %collective-permute-start.2 = (bf16[16,56,128]{2,1,0:T(8,128)(2,1)S(1)}, bf16[16,56,128]{2,1,0:T(8,128)(2,1)S(1)}, u32[]{:S(2)}, u32[]{:S(2)}) collective-permute-start(bf16[16,56,128]{2,1,0:T(8,128)(2,1)S(1)} %get-tuple-element.25), channel_id=1, source_target_pairs={{0,16},{16,0},{1,17},{17,1},{2,18},{18,2},{3,19},{19,3},{4,20},{20... | collective-permute-start | bytes 688136 | tf_op jit(solution)/shard_map/ppermute | solution.py:217
  5.1 8.1 %collective-permute-start.3 = (bf16[16,56,128]{2,1,0:T(8,128)(2,1)S(1)}, bf16[16,56,128]{2,1,0:T(8,128)(2,1)S(1)}, u32[]{:S(2)}, u32[]{:S(2)}) collective-permute-start(bf16[16,56,128]{2,1,0:T(8,128)(2,1)S(1)} %get-tuple-element.26), channel_id=1, source_target_pairs={{0,1},{1,0},{2,3},{3,2},{4,5},{5,4},{6,7},{7,6},{8,9},{9,8},{10,11... | collective-permute-start | bytes 688136 | tf_op jit(solution)/shard_map/ppermute | solution.py:220
  5.3 9.4 %collective-permute-start.1 = (bf16[16,56,128]{2,1,0:T(8,128)(2,1)S(1)}, bf16[16,56,128]{2,1,0:T(8,128)(2,1)S(1)}, u32[]{:S(2)}, u32[]{:S(2)}) collective-permute-start(bf16[16,56,128]{2,1,0:T(8,128)(2,1)S(1)} %collective-permute-done), channel_id=1, source_target_pairs={{0,2},{3,1},{2,4},{5,3},{4,6},{7,5},{6,8},{9,7},{8,10},{11,9},{10,... | collective-permute-start | bytes 688136 | tf_op jit(solution)/shard_map/ppermute | solution.py:219
  16.4 1.6 %collective-permute-start.4 = (bf16[16,56,128]{2,1,0:T(8,128)(2,1)S(1)}, bf16[16,56,128]{2,1,0:T(8,128)(2,1)S(1)}, u32[]{:S(2)}, u32[]{:S(2)}) collective-permute-start(bf16[16,56,128]{2,1,0:T(8,128)(2,1)S(1)} %get-tuple-element.37), channel_id=1, source_target_pairs={{0,1},{1,0},{2,3},{3,2},{4,5},{5,4},{6,7},{7,6},{8,9},{9,8},{10,11... | collective-permute-start | bytes 688136 | tf_op jit(solution)/shard_map/ppermute | solution.py:216
  16.5 9.0 %collective-permute-start.6 = (bf16[16,56,128]{2,1,0:T(8,128)(2,1)S(1)}, bf16[16,56,128]{2,1,0:T(8,128)(2,1)S(1)}, u32[]{:S(2)}, u32[]{:S(2)}) collective-permute-start(bf16[16,56,128]{2,1,0:T(8,128)(2,1)S(1)} %get-tuple-element.38), channel_id=1, source_target_pairs={{0,16},{16,0},{1,17},{17,1},{2,18},{18,2},{3,19},{19,3},{4,20},{20... | collective-permute-start | bytes 688136 | tf_op jit(solution)/shard_map/ppermute | solution.py:217
  17.8 7.7 %collective-permute-start.7 = (bf16[16,56,128]{2,1,0:T(8,128)(2,1)S(1)}, bf16[16,56,128]{2,1,0:T(8,128)(2,1)S(1)}, u32[]{:S(2)}, u32[]{:S(2)}) collective-permute-start(bf16[16,56,128]{2,1,0:T(8,128)(2,1)S(1)} %get-tuple-element.39), channel_id=1, source_target_pairs={{0,1},{1,0},{2,3},{3,2},{4,5},{5,4},{6,7},{7,6},{8,9},{9,8},{10,11... | collective-permute-start | bytes 688136 | tf_op jit(solution)/shard_map/ppermute | solution.py:220
  18.0 10.4 %collective-permute-start.5 = (bf16[16,56,128]{2,1,0:T(8,128)(2,1)S(1)}, bf16[16,56,128]{2,1,0:T(8,128)(2,1)S(1)}, u32[]{:S(2)}, u32[]{:S(2)}) collective-permute-start(bf16[16,56,128]{2,1,0:T(8,128)(2,1)S(1)} %collective-permute-done.4), channel_id=1, source_target_pairs={{0,2},{3,1},{2,4},{5,3},{4,6},{7,5},{6,8},{9,7},{8,10},{11,9},{10,... | collective-permute-start | bytes 688136 | tf_op jit(solution)/shard_map/ppermute | solution.py:219

commit v6 on v4

--- a/solution.py
+++ b/solution.py
@@ -219,7 +219,8 @@
     n, b = lax.axis_size(blk), lax.axis_size(basin)
 
     def pairs(first):
-        partner = {i: i + 1 for i in range(first, n - 1, 2)}
+        order = [(i + first) % n for i in range(n)]
+        partner = {order[i]: order[i + 1] for i in range(0, n - 1, 2)}
         partner |= {j: i for i, j in partner.items()}
         return [(i, partner.get(i, i)) for i in range(n)]
 

time: 28.3 us -> 26.5 us (0.936)
  the two profiles are of different devices: /device:TPU:23 before, /device:TPU:0 now
where the time goes in v6:
time: 26.5 us; the launch traced here: 26.3 us
  Pallas kernels  14.1 us (53%)
  starting transfers between devices  10.7 us (40%)
  waiting for transfers between devices  1.5 us (6%)
    pallas_call x5, Pallas kernels, call(): pl.pallas_call(kernel, out_shape=outs, in_specs=specs, out_specs=out_spec...  14.1 us
    ppermute x2, starting transfers between devices, swapped(): lax.ppermute(values[0], blk, pairs(1))  7.68 us
    ppermute x2, starting transfers between devices, swapped(): lax.ppermute(values[1], basin, [(i, (i + 1) % b) for i in range(b)])  2.98 us
    ppermute x2, waiting for transfers between devices, swapped(): lax.ppermute(values[0], blk, pairs(1))  1.49 us
  transfers between devices with their start and end apart: 6, of which 1 were waited for; matrix products, arithmetic and copies ran while one was open for 0% of the time, Pallas kernels for 29%

profile of v6, /device:TPU:0, one launch (start us, length us, event | category | flops | bytes accessed | tf_op | source)
XLA Modules:
  0.0 26.3 jit_solution(16360642942764368917)
XLA Ops:
  0.0 2.0 %shard_map.91 = (bf16[16,56,128]{2,1,0:T(8,128)(2,1)S(1)}, bf16[16,56,128]{2,1,0:T(8,128)(2,1)S(1)}, bf16[16,56,128]{2,1,0:T(8,128)(2,1)S(1)}, bf16[50,128,128]{...) custom-call(bf16[50,128,128]{2,1,0:T(8,128)(2,1)} %bitcast.5, ...), custom_call_target="tpu_custom_call" | custom-call | bytes 5585664 | tf_op jit(solution)/shard_map/pallas_call | solution.py:206
  2.0 5.5 %collective-permute-start = (bf16[16,56,128]{2,1,0:T(8,128)(2,1)S(1)}, bf16[16,56,128]{2,1,0:T(8,128)(2,1)S(1)}, u32[]{:S(2)}, u32[]{:S(2)}) collective-permute-start(bf16[16,56,128]{2,1,0:T(8,128)(2,1)S(1)} %get-tuple-element.24), channel_id=1, source_target_pairs={{0,15},{1,2},{2,1},{3,4},{4,3},{5,6},{6,5},{7,8},{8,7},{9,10},{10,... | collective-permute-start | bytes 688136 | tf_op jit(solution)/shard_map/ppermute | solution.py:228
  7.5 1.5 %collective-permute-start.1 = (bf16[16,56,128]{2,1,0:T(8,128)(2,1)S(1)}, bf16[16,56,128]{2,1,0:T(8,128)(2,1)S(1)}, u32[]{:S(2)}, u32[]{:S(2)}) collective-permute-start(bf16[16,56,128]{2,1,0:T(8,128)(2,1)S(1)} %get-tuple-element.25), channel_id=1, source_target_pairs={{0,16},{16,0},{1,17},{17,1},{2,18},{18,2},{3,19},{19,3},{4,20},{20... | collective-permute-start | bytes 688136 | tf_op jit(solution)/shard_map/ppermute | solution.py:229
  9.0 0.0 collective-permute-start.2
  9.0 4.5 %shard_map.92 = (bf16[50,128,128]{2,1,0:T(8,128)(2,1)S(1)}, f32[128,56,128]{2,1,0:T(8,128)S(1)}, bf16[128,56,128]{2,1,0:T(8,128)(2,1)S(1)}) custom-call(bf16[50,128,128]{2,1,0:T(8,128)(2,1)S(1)} %get-tuple-element.27.c_ref, s32[4,128]{1,0:T(4,128)S(1)} %get-tuple-element.28.nbr_ref, f32[50,4,128]{2,1,0:T(4,128)S(1)} %get-tuple-element.29.nw_ref, ...), custom_call_target="tpu_custom_call" | custom-call | flops 209715200 | bytes 9552384 | tf_op jit(solution)/shard_map/pallas_call | solution.py:206
  13.6 0.0 collective-permute-done.r0
  13.6 0.0 collective-permute-done.1.r1
  13.6 0.0 collective-permute-done.2.r2
  13.6 1.7 %shard_map.93 = (f32[128,56,128]{2,1,0:T(8,128)S(1)}, bf16[16,56,128]{2,1,0:T(8,128)(2,1)S(1)}, bf16[16,56,128]{2,1,0:T(8,128)(2,1)S(1)}, bf16[16,56,128]{2,1,0:T(8,128)(2,1)S(1)}) custom-call(bf16[16,56,128]{2,1,0:T(8,128)(2,1)S(1)} %collective-permute-done.r0, bf16[16,56,128]{2,1,0:T(8,128)(2,1)S(1)} %collective-permute-done.1.r1, ...), custom_call_target="tpu_custom_call", output_to_operand_aliasing={{0}: (3, {})} | custom-call | flops 102760448 | bytes 10621120 | tf_op jit(solution)/shard_map/pallas_call | solution.py:206
  15.3 2.2 %collective-permute-start.3 = (bf16[16,56,128]{2,1,0:T(8,128)(2,1)S(1)}, bf16[16,56,128]{2,1,0:T(8,128)(2,1)S(1)}, u32[]{:S(2)}, u32[]{:S(2)}) collective-permute-start(bf16[16,56,128]{2,1,0:T(8,128)(2,1)S(1)} %get-tuple-element.37), channel_id=1, source_target_pairs={{0,15},{1,2},{2,1},{3,4},{4,3},{5,6},{6,5},{7,8},{8,7},{9,10},{10,... | collective-permute-start | bytes 688136 | tf_op jit(solution)/shard_map/ppermute | solution.py:228
  17.5 1.5 %collective-permute-start.4 = (bf16[16,56,128]{2,1,0:T(8,128)(2,1)S(1)}, bf16[16,56,128]{2,1,0:T(8,128)(2,1)S(1)}, u32[]{:S(2)}, u32[]{:S(2)}) collective-permute-start(bf16[16,56,128]{2,1,0:T(8,128)(2,1)S(1)} %get-tuple-element.38), channel_id=1, source_target_pairs={{0,16},{16,0},{1,17},{17,1},{2,18},{18,2},{3,19},{19,3},{4,20},{20... | collective-permute-start | bytes 688136 | tf_op jit(solution)/shard_map/ppermute | solution.py:229
  19.0 0.0 collective-permute-start.5
  19.0 3.2 %shard_map.94.local_ref = f32[128,56,128]{2,1,0:T(8,128)S(1)} custom-call(f32[128,56,128]{2,1,0:T(8,128)S(1)} %get-tuple-element.40.c_ref, bf16[50,128,128]{2,1,0:T(8,128)(2,1)S(1)} %get-tuple-element.41.a_ref, bf16[128,56,128]{2,1,0:T(8,128)(2,1)S(1)} %get-tuple-element.34.vt_ref), custom_call_target="tpu_custom_call" | custom-call | flops 209715200 | bytes 10813440 | tf_op jit(solution)/shard_map/pallas_call | solution.py:206
  22.1 1.5 %collective-permute-done.3.r0 = bf16[16,56,128]{2,1,0:T(8,128)(2,1)S(1)} collective-permute-done((bf16[16,56,128]{2,1,0:T(8,128)(2,1)S(1)}, bf16[16,56,128]{2,1,0:T(8,128)(2,1)S(1)}, u32[]{:S(2)}, u32[]{:S(2)}) %collective-permute-start.3) | collective-permute-done | bytes 229408 | tf_op jit(solution)/shard_map/ppermute | solution.py:228
  23.6 0.0 collective-permute-done.4.r1
  23.6 0.0 collective-permute-done.5.r2
  23.6 2.7 %shard_map.95 = (bf16[50,128,128]{2,1,0:T(8,128)(2,1)}, f32[128,56,128]{2,1,0:T(8,128)S(1)}) custom-call(bf16[16,56,128]{2,1,0:T(8,128)(2,1)S(1)} %collective-permute-done.3.r0, bf16[16,56,128]{2,1,0:T(8,128)(2,1)S(1)} %collective-permute-done.4.r1, bf16[16,56,128]{2,1,0:T(8,128)(2,1)S(1)} %collective-permute-done.5.r2, ...), custom_call_target="tpu_custom_call", output_to_operand_aliasing={{1}: (3, {})} | custom-call | flops 102760448 | bytes 11501568 | tf_op jit(solution)/shard_map/pallas_call | solution.py:206
Async XLA Ops:
  2.0 11.5 %collective-permute-start = (bf16[16,56,128]{2,1,0:T(8,128)(2,1)S(1)}, bf16[16,56,128]{2,1,0:T(8,128)(2,1)S(1)}, u32[]{:S(2)}, u32[]{:S(2)}) collective-permute-start(bf16[16,56,128]{2,1,0:T(8,128)(2,1)S(1)} %get-tuple-element.24), channel_id=1, source_target_pairs={{0,15},{1,2},{2,1},{3,4},{4,3},{5,6},{6,5},{7,8},{8,7},{9,10},{10,... | collective-permute-start | bytes 688136 | tf_op jit(solution)/shard_map/ppermute | solution.py:228
  7.5 6.0 %collective-permute-start.1 = (bf16[16,56,128]{2,1,0:T(8,128)(2,1)S(1)}, bf16[16,56,128]{2,1,0:T(8,128)(2,1)S(1)}, u32[]{:S(2)}, u32[]{:S(2)}) collective-permute-start(bf16[16,56,128]{2,1,0:T(8,128)(2,1)S(1)} %get-tuple-element.25), channel_id=1, source_target_pairs={{0,16},{16,0},{1,17},{17,1},{2,18},{18,2},{3,19},{19,3},{4,20},{20... | collective-permute-start | bytes 688136 | tf_op jit(solution)/shard_map/ppermute | solution.py:229
  9.0 4.5 %collective-permute-start.2 = (bf16[16,56,128]{2,1,0:T(8,128)(2,1)S(1)}, bf16[16,56,128]{2,1,0:T(8,128)(2,1)S(1)}, u32[]{:S(2)}, u32[]{:S(2)}) collective-permute-start(bf16[16,56,128]{2,1,0:T(8,128)(2,1)S(1)} %get-tuple-element.26), channel_id=1, source_target_pairs={{0,1},{1,0},{2,3},{3,2},{4,5},{5,4},{6,7},{7,6},{8,9},{9,8},{10,11... | collective-permute-start | bytes 688136 | tf_op jit(solution)/shard_map/ppermute | solution.py:230
  15.3 8.3 %collective-permute-start.3 = (bf16[16,56,128]{2,1,0:T(8,128)(2,1)S(1)}, bf16[16,56,128]{2,1,0:T(8,128)(2,1)S(1)}, u32[]{:S(2)}, u32[]{:S(2)}) collective-permute-start(bf16[16,56,128]{2,1,0:T(8,128)(2,1)S(1)} %get-tuple-element.37), channel_id=1, source_target_pairs={{0,15},{1,2},{2,1},{3,4},{4,3},{5,6},{6,5},{7,8},{8,7},{9,10},{10,... | collective-permute-start | bytes 688136 | tf_op jit(solution)/shard_map/ppermute | solution.py:228
  17.5 6.1 %collective-permute-start.4 = (bf16[16,56,128]{2,1,0:T(8,128)(2,1)S(1)}, bf16[16,56,128]{2,1,0:T(8,128)(2,1)S(1)}, u32[]{:S(2)}, u32[]{:S(2)}) collective-permute-start(bf16[16,56,128]{2,1,0:T(8,128)(2,1)S(1)} %get-tuple-element.38), channel_id=1, source_target_pairs={{0,16},{16,0},{1,17},{17,1},{2,18},{18,2},{3,19},{19,3},{4,20},{20... | collective-permute-start | bytes 688136 | tf_op jit(solution)/shard_map/ppermute | solution.py:229
  19.0 4.7 %collective-permute-start.5 = (bf16[16,56,128]{2,1,0:T(8,128)(2,1)S(1)}, bf16[16,56,128]{2,1,0:T(8,128)(2,1)S(1)}, u32[]{:S(2)}, u32[]{:S(2)}) collective-permute-start(bf16[16,56,128]{2,1,0:T(8,128)(2,1)S(1)} %get-tuple-element.39), channel_id=1, source_target_pairs={{0,1},{1,0},{2,3},{3,2},{4,5},{5,4},{6,7},{7,6},{8,9},{9,8},{10,11... | collective-permute-start | bytes 688136 | tf_op jit(solution)/shard_map/ppermute | solution.py:230

commit v7 on v6

--- a/solution.py
+++ b/solution.py
@@ -13,7 +13,15 @@
 
 
 def padded(levels):
-    return -(-(levels + 1) // 8) * 8
+    return -(-levels // 8) * 8
+
+
+def whole_rows(levels):
+    return levels // 16 * 16
+
+
+def message_rows(levels, nedge):
+    return levels * nedge + 16
 
 
 def direction(slot, parity):
@@ -25,49 +33,76 @@
     return jnp.where(first, at + 1 < count, at > 0)
 
 
-def pack_edges(parity, levels, send, weights, tbl, column, outs):
-    rows = padded(levels)
-    nedge, _, width = outs[0].shape
-    is_level = lax.broadcasted_iota(jnp.int32, (rows, width), 0) < levels
+def pack_chunk(parity, lo, levels, send, weights, tbl, rows_of, outs):
+    whole = whole_rows(levels)
+    nedge = send.shape[1]
+    rest = levels - whole
+    share = 8 // rest if rest else 0
     for slot, out in enumerate(outs):
         d = direction(slot, parity)
-        table = jnp.broadcast_to(tbl[slot : slot + 1, :], (rows, width))
-        for e in range(nedge):
-            k = slot * nedge + e
-            w = weights[0:rows, k : k + 1]
-            out[e] = jnp.where(is_level, column(send[d, e]) * w, table).astype(BF16)
-
-
-def product(operator, x):
-    pad = jnp.zeros((64 - x.shape[0], x.shape[1]), F32)
-    x = jnp.concatenate([x.astype(F32), pad], axis=0).astype(BF16)
-    return jnp.dot(operator[:, 0:64], x, preferred_element_type=F32)
+        if lo < whole:
+            for e in range(nedge):
+                k = slot * nedge + e
+                value = rows_of(send[d, e], lo, 16) * weights[lo : lo + 16, k : k + 1]
+                out[e * whole + lo : e * whole + lo + 16, :] = value.astype(BF16)
+            continue
+        sub = lax.broadcasted_iota(jnp.int32, (8, out.shape[1]), 0)
+        parts = []
+        for first in range(0, nedge, share or nedge):
+            part = None
+            for q in range(share):
+                k = slot * nedge + first + q
+                value = rows_of(send[d, first + q], lo, 8) * weights[lo : lo + 8, k : k + 1]
+                if q:
+                    value = pltpu.roll(value, q * rest, 0)
+                part = value if part is None else jnp.where(sub >= q * rest, value, part)
+            if share:
+                parts.append(part)
+        table = jnp.broadcast_to(tbl[slot : slot + 1, :], (16, out.shape[1]))
+        out[nedge * whole :, :] = jnp.concatenate(parts + [table], axis=0).astype(BF16)
 
 
 def vertical(vt_ref, exs, out):
     cols, rows, _ = vt_ref.shape
+    pad = jnp.zeros((64 - rows, out.shape[1]), F32)
 
     def column(j, _):
-        out[j] = product(vt_ref[j], exs[pl.ds(pl.multiple_of(j * rows, 8), rows), :])
+        at = pl.ds(pl.multiple_of(j * rows, 8), rows)
+        x = jnp.concatenate([exs[at, :], pad], axis=0).astype(BF16)
+        out[at, :] = jnp.dot(vt_ref[j][:, 0:64], x, preferred_element_type=F32)
         return _
 
     lax.fori_loop(0, cols, column, 0, unroll=16)
 
 
-def add_edges(edges, vt_ref, total, tbl_v, tbl_s, sem):
-    levels_at = edges[0].shape[1] - 8
-    for slot, ref in enumerate(edges):
-        tbl_v[slot] = ref[0, levels_at:, :].astype(F32).astype(jnp.int32)
+def add_edges(edges, levels, nedge, vt_ref, total, tbl_v, tbl_s, sem):
+    whole = whole_rows(levels)
+    rest = levels - whole
+    share = 8 // rest if rest else 0
+    rows = vt_ref.shape[1]
+    for i, ref in enumerate(edges):
+        tbl_v[i] = ref[levels * nedge :, :].astype(F32)[0:8].astype(jnp.int32)
     copy = pltpu.make_async_copy(tbl_v, tbl_s, sem)
     copy.start()
     copy.wait()
-    group = 4
-    for slot, ref in enumerate(edges):
-        for first in range(0, ref.shape[0], group):
-            at = [tbl_s[slot, 7, e] for e in range(first, first + group)]
-            parts = [product(vt_ref[j], ref[first + i]) for i, j in enumerate(at)]
-            for j, part in zip(at, parts):
-                total[j] = total[j] + part
+    group = max(share, 4)
+    pad = jnp.zeros((8, total.shape[1]), F32)
+    for i, ref in enumerate(edges):
+        tails = ref[whole * nedge : levels * nedge, :].astype(F32) if rest else None
+        for first in range(0, nedge, group):
+            targets = [tbl_s[i, 0, e] for e in range(first, first + group)]
+            products = []
+            for e, j in zip(range(first, first + group), targets):
+                x = ref[e * whole : (e + 1) * whole, :]
+                if rest:
+                    tail = tails[e // share * 8 : e // share * 8 + 8]
+                    if e % share:
+                        tail = pltpu.roll(tail, 8 - e % share * rest, 0)
+                    x = jnp.concatenate([x, jnp.concatenate([tail, pad], axis=0).astype(BF16)], axis=0)
+                products.append(jnp.dot(vt_ref[j][:, 0 : x.shape[0]], x, preferred_element_type=F32))
+            for j, part in zip(targets, products):
+                at = pl.ds(pl.multiple_of(j * rows, 8), rows)
+                total[at, :] = total[at, :] + part
 
 
 def gather_kernel(
@@ -78,10 +113,9 @@
     levels, cols, width = c_h.shape
     nedge = edge_h.shape[1]
     pitch = cols + 8
-    count = 5
-    edges = [levels * i // count for i in range(count + 1)]
+    bounds = [(lo, min(lo + 16, levels)) for lo in range(0, levels, 16)]
     pairs = [(send_h, send_s), (recv_h, recv_v), (edge_h, edge_v)]
-    pairs += [(c_h.at[pl.ds(lo, hi - lo)], c_v.at[pl.ds(lo, hi - lo)]) for lo, hi in zip(edges, edges[1:])]
+    pairs += [(c_h.at[pl.ds(lo, hi - lo)], c_v.at[pl.ds(lo, hi - lo)]) for lo, hi in bounds]
     pairs += [(nbr_h, nbr_v), (nw_h, nw_v), (sw_h, sw_v), (wet_h, wet_v), (v_h, v_v)]
     copies = [pltpu.make_async_copy(a, b, sems.at[i]) for i, (a, b) in enumerate(pairs)]
     for copy in copies:
@@ -100,13 +134,15 @@
         tbl_o[slot : slot + 1, 0:nedge] = recv_v[pl.ds(d, 1), :].astype(F32)
     weights = wts[...].T
     wts_o[...] = weights
-    for i, (lo, hi) in enumerate(zip(edges, edges[1:])):
+    rows_of = lambda s, lo, n: cf[pl.ds(lo * pitch + s, n, stride=pitch), :]
+    for i, (lo, hi) in enumerate(bounds):
         copies[3 + i].wait()
         for l in range(lo, hi):
             cf[l * pitch : l * pitch + cols, :] = c_v[l].astype(F32)
-    column = lambda s: cf[pl.ds(s, padded(levels), stride=pitch), :]
-    pack_edges(parity, levels, send_s, weights, tbl_o, column, (s0, s1, s2))
-    for copy in copies[3 + count :]:
+        pack_chunk(parity, lo, levels, send_s, weights, tbl_o, rows_of, (s0, s1, s2))
+    if levels % 16 == 0:
+        pack_chunk(parity, levels, levels, send_s, weights, tbl_o, rows_of, (s0, s1, s2))
+    for copy in copies[3 + len(bounds) :]:
         copy.wait()
 
 
@@ -158,38 +194,44 @@
     vertical(vt_ref, exs, state_ref)
 
 
-def first_kernel(blk, levels, r0, r1, r2, local_ref, vt_ref, wts_ref, tbl_ref, send_h, state_ref, s0, s1, s2, tbl_v, tbl_s, send_s, sems):
+def arrived_kernel(levels, nedge, *refs):
+    *edges, _, vt_ref, total, tbl_v, tbl_s, sem = refs
+    add_edges(edges, levels, nedge, vt_ref, total, tbl_v, tbl_s, sem)
+
+
+def send_kernel(blk, levels, r1, local_ref, vt_ref, wts_ref, tbl_ref, send_h, state, s0, s1, s2, tbl_v, tbl_s, send_s, sems):
     copy = pltpu.make_async_copy(send_h, send_s, sems.at[1])
     copy.start()
     parity = lax.bitwise_and(lax.axis_index(blk), jnp.int32(1))
-    add_edges((r0, r1, r2), vt_ref, state_ref, tbl_v, tbl_s, sems.at[0])
+    rows = vt_ref.shape[1]
+    add_edges((r1,), levels, send_h.shape[1], vt_ref, state, tbl_v, tbl_s, sems.at[0])
     copy.wait()
-    pack_edges(parity, levels, send_s, wts_ref, tbl_ref, lambda s: state_ref[s], (s0, s1, s2))
-
-
-def middle_kernel(c_ref, a_ref, vt_ref, out_ref, cs, exs):
-    levels = a_ref.shape[0]
-    cols, rows, width = c_ref.shape
-    cs[...] = c_ref[...].reshape(cols * rows, width)
+    rows_of = lambda s, lo, n: state[pl.ds(pl.multiple_of(s * rows + lo, 8), n), :]
+    for lo in range(0, levels + 1, 16):
+        pack_chunk(parity, lo, levels, send_s, wts_ref, tbl_ref, rows_of, (s0, s1, s2))
+
+
+def middle_kernel(cs, a_ref, vt_ref, out_ref, exs):
+    levels, cols, _ = a_ref.shape
+    rows = vt_ref.shape[1]
     for l in range(levels):
         state = cs[pl.ds(l, cols, stride=rows), :].astype(BF16)
         exs[pl.ds(l, cols, stride=rows), :] = jnp.dot(a_ref[l], state, preferred_element_type=F32)
     for l in range(levels, rows):
-        exs[pl.ds(l, cols, stride=rows), :] = jnp.zeros((cols, width), F32)
+        exs[pl.ds(l, cols, stride=rows), :] = jnp.zeros((cols, exs.shape[1]), F32)
     vertical(vt_ref, exs, out_ref)
 
 
-def last_kernel(r0, r1, r2, local_ref, vt_ref, out_h, total, cs, out_v, tbl_v, tbl_s, sems):
-    levels = out_h.shape[0]
-    cols, rows, width = total.shape
-    add_edges((r0, r1, r2), vt_ref, total, tbl_v, tbl_s, sems.at[0])
-    cs[...] = total[...].reshape(cols * rows, width)
+def last_kernel(nedge, r1, local_ref, vt_ref, out_h, total, out_v, tbl_v, tbl_s, sems):
+    levels, cols, width = out_h.shape
+    rows = vt_ref.shape[1]
+    add_edges((r1,), levels, nedge, vt_ref, total, tbl_v, tbl_s, sems.at[0])
     count = 5
     edges = [levels * i // count for i in range(count + 1)]
     copies = []
     for i, (lo, hi) in enumerate(zip(edges, edges[1:])):
         for l in range(lo, hi):
-            out_v[l] = cs[pl.ds(l, cols, stride=rows), :].astype(BF16)
+            out_v[l] = total[pl.ds(l, cols, stride=rows), :].astype(BF16)
         copies.append(pltpu.make_async_copy(out_v.at[pl.ds(lo, hi - lo)], out_h.at[pl.ds(lo, hi - lo)], sems.at[1 + i]))
         copies[-1].start()
     for copy in copies:
@@ -244,10 +286,9 @@
     send_h = in_hbm(send_cols)
     loads = [by_level, nbr_cols, nbr_by_level, self_wts, wet, vert_inv]
     same = lambda x: shape(x.shape, x.dtype)
-    packed = [shape((nedge, rows, width), BF16)] * 3
-    flat = pltpu.VMEM((cols * rows, width), F32)
-    columns = shape((cols, rows, width), F32)
-    tables = [pltpu.VMEM((3, 8, 128), jnp.int32), pltpu.SMEM((3, 8, 128), jnp.int32)]
+    packed = [shape((message_rows(levels, nedge), width), BF16)] * 3
+    columns = shape((cols * rows, width), F32)
+    flat = pltpu.VMEM(columns.shape, F32)
 
     first = call(
         functools.partial(gather_kernel, "blk"),
@@ -258,35 +299,45 @@
         [
             pltpu.VMEM((rows * (cols + 8), width), F32), pltpu.VMEM((128, 128), F32),
             pltpu.VMEM(recv_cols.shape, jnp.int32), pltpu.VMEM(edge_by_entry.shape, F32),
-            pltpu.SMEM(send_cols.shape, jnp.int32), DMA((13,)),
+            pltpu.SMEM(send_cols.shape, jnp.int32), DMA((8 + -(-levels // 16),)),
         ],
         16,
     )
     sends, loads, (wts, tbl) = first[:3], first[3:9], first[9:]
-    received = swapped(sends, "blk", "basin")
+    operator_flops = 2 * levels * cols * cols * width
+    vertical_flops = 2 * cols * rows * rows * width
+
+    def tables(count):
+        return [pltpu.VMEM((count, 8, 128), jnp.int32), pltpu.SMEM((count, 8, 128), jnp.int32)]
+
+    def arrived(partial, messages):
+        return call(
+            functools.partial(arrived_kernel, levels, nedge), (*messages, partial, vt), [VM] * (len(messages) + 2),
+            [columns], [VM], tables(len(messages)) + [DMA], 16,
+            flops=len(messages) * nedge * 2 * rows * rows * width, aliases={len(messages): 0},
+        )[0]
+
+    odd, along, even = swapped(sends, "blk", "basin")
     operator, partial, vt = call(
         operator_kernel, loads, [VM] * 6,
         [shape((levels, cols, cols), BF16), columns, shape((cols, rows, 128), BF16)], [VM] * 3,
         [flat, pltpu.VMEM((levels, 8, cols), F32), pltpu.VMEM((rows * rows, cols), F32), pltpu.VMEM((cols * rows, 128), F32)],
-        32, flops=2 * levels * cols * cols * width,
+        32, flops=operator_flops + vertical_flops,
     )
     state, *sends = call(
-        functools.partial(first_kernel, "blk", levels),
-        (*received, partial, vt, wts, tbl, send_h), [VM] * 7 + [HB],
+        functools.partial(send_kernel, "blk", levels),
+        (along, arrived(partial, (odd, even)), vt, wts, tbl, send_h), [VM] * 5 + [HB],
         [columns] + packed, [VM] * 4,
-        tables + [pltpu.SMEM(send_cols.shape, jnp.int32), DMA((2,))], 16,
-        flops=2 * cols * rows * rows * width, aliases={3: 0},
-    )
-    received = swapped(sends, "blk", "basin")
+        tables(1) + [pltpu.SMEM(send_cols.shape, jnp.int32), DMA((2,))], 16, aliases={1: 0},
+    )
+    odd, along, even = swapped(sends, "blk", "basin")
     (partial,) = call(
-        middle_kernel, (state, operator, vt), [VM] * 3, [columns], [VM], [flat, flat], 32,
-        flops=2 * levels * cols * cols * width,
+        middle_kernel, (state, operator, vt), [VM] * 3, [columns], [VM], [flat], 32, flops=operator_flops + vertical_flops,
     )
     out, _ = call(
-        last_kernel, (*received, partial, vt), [VM] * 5,
+        functools.partial(last_kernel, nedge), (along, arrived(partial, (odd, even)), vt), [VM] * 3,
         [shape((levels, cols, width), BF16), columns], [HB, VM],
-        [flat, pltpu.VMEM((levels, cols, width), BF16)] + tables + [DMA((6,))], 16,
-        flops=2 * cols * rows * rows * width, aliases={3: 1},
+        [pltpu.VMEM((levels, cols, width), BF16)] + tables(1) + [DMA((6,))], 16, aliases={1: 1},
     )
     return jnp.transpose(out, (1, 0, 2))
 

time: 26.5 us -> 28 us (1.057)
  waiting for transfers between devices: 1.5 us -> 2.6 us
  Pallas kernels: 14.1 us -> 15.2 us
  starting transfers between devices: 10.7 us -> 9.95 us
    pallas_call x5 -> x7, Pallas kernels: 14.1 us -> 15.2 us  [call(): pl.pallas_call(kernel, out_shape=outs, in_specs=specs, out_specs=out_spec...]
    ppermute x2, starting transfers between devices: 7.68 us -> 6.96 us  [swapped(): lax.ppermute(values[0], blk, pairs(1))]
    ppermute x2, waiting for transfers between devices: 1.49 us -> 2.06 us  [swapped(): lax.ppermute(values[0], blk, pairs(1))]
    ppermute x2, waiting for transfers between devices: 0.01 us -> 0.54 us  [swapped(): lax.ppermute(values[1], basin, [(i, (i + 1) % b) for i in range(b)])]
  transfers between devices with their start and end apart: 6 -> 6, of which waited for: 1 -> 2; matrix products, arithmetic and copies ran while one was open for 0% -> 0% of each run, Pallas kernels for 29% -> 34%
where the time goes in v7:
time: 28 us; the launch traced here: 27.8 us
  Pallas kernels  15.2 us (54%)
  starting transfers between devices  9.95 us (36%)
  waiting for transfers between devices  2.6 us (9%)
    pallas_call x7, Pallas kernels, call(): pl.pallas_call(kernel, out_shape=outs, in_specs=specs, out_specs=out_spec...  15.2 us
    ppermute x2, starting transfers between devices, swapped(): lax.ppermute(values[0], blk, pairs(1))  6.96 us
    ppermute x2, starting transfers between devices, swapped(): lax.ppermute(values[1], basin, [(i, (i + 1) % b) for i in range(b)])  2.99 us
    ppermute x2, waiting for transfers between devices, swapped(): lax.ppermute(values[0], blk, pairs(1))  2.06 us
  transfers between devices with their start and end apart: 6, of which 2 were waited for; matrix products, arithmetic and copies ran while one was open for 0% of the time, Pallas kernels for 34%

profile of v7, /device:TPU:0, one launch (start us, length us, event | category | flops | bytes accessed | tf_op | source)
XLA Modules:
  0.0 27.8 jit_solution(5815796115815082172)
XLA Ops:
  0.0 2.0 %shard_map.91 = (bf16[816,128]{1,0:T(8,128)(2,1)S(1)}, bf16[816,128]{1,0:T(8,128)(2,1)S(1)}, bf16[816,128]{1,0:T(8,128)(2,1)S(1)}, bf16[50,128,128]{2,1,0:T(8,12...) custom-call(bf16[50,128,128]{2,1,0:T(8,128)(2,1)} %bitcast.5, ...), custom_call_target="tpu_custom_call" | custom-call | bytes 5524224 | tf_op jit(solution)/shard_map/pallas_call | solution.py:248
  2.1 5.5 %collective-permute-start.1 = (bf16[816,128]{1,0:T(8,128)(2,1)S(1)}, bf16[816,128]{1,0:T(8,128)(2,1)S(1)}, u32[]{:S(2)}, u32[]{:S(2)}) collective-permute-start(bf16[816,128]{1,0:T(8,128)(2,1)S(1)} %get-tuple-element.25), channel_id=1, source_target_pairs={{0,15},{1,2},{2,1},{3,4},{4,3},{5,6},{6,5},{7,8},{8,7},{9,10},{10,... | collective-permute-start | bytes 626696 | tf_op jit(solution)/shard_map/ppermute | solution.py:270
  7.6 0.0 collective-permute-start.2
  7.6 1.5 %collective-permute-start = (bf16[816,128]{1,0:T(8,128)(2,1)S(1)}, bf16[816,128]{1,0:T(8,128)(2,1)S(1)}, u32[]{:S(2)}, u32[]{:S(2)}) collective-permute-start(bf16[816,128]{1,0:T(8,128)(2,1)S(1)} %get-tuple-element.24), channel_id=1, source_target_pairs={{0,16},{16,0},{1,17},{17,1},{2,18},{18,2},{3,19},{19,3},{4,20},{20... | collective-permute-start | bytes 626696 | tf_op jit(solution)/shard_map/ppermute | solution.py:271
  9.1 4.5 %shard_map.92 = (bf16[50,128,128]{2,1,0:T(8,128)(2,1)S(1)}, f32[7168,128]{1,0:T(8,128)S(1)}, bf16[128,56,128]{2,1,0:T(8,128)(2,1)S(1)}) custom-call(bf16[50,128,128]{2,1,0:T(8,128)(2,1)S(1)} %get-tuple-element.27.c_ref, s32[4,128]{1,0:T(4,128)S(1)} %get-tuple-element.28.nbr_ref, f32[50,4,128]{2,1,0:T(4,128)S(1)} %get-tuple-element.29.nw_ref, ...), custom_call_target="tpu_custom_call" | custom-call | flops 312475648 | bytes 9552384 | tf_op jit(solution)/shard_map/pallas_call | solution.py:248
  13.6 0.0 collective-permute-done.1.refs_0_
  13.6 0.0 collective-permute-done.2.refs_1_
  13.6 1.0 %shard_map.93.local_ref = f32[7168,128]{1,0:T(8,128)S(1)} custom-call(bf16[816,128]{1,0:T(8,128)(2,1)S(1)} %collective-permute-done.1.refs_0_, bf16[816,128]{1,0:T(8,128)(2,1)S(1)} %collective-permute-done.2.refs_1_, f32[7168,128]{1,0:T(8,128)S(1)} %get-tuple-element.33.refs_2_, ...), custom_call_target="tpu_custom_call", output_to_operand_aliasing={{}: (2, {})} | custom-call | flops 25690112 | bytes 9592832 | tf_op jit(solution)/shard_map/pallas_call | solution.py:248
  14.6 0.5 %collective-permute-done.r1 = bf16[816,128]{1,0:T(8,128)(2,1)S(1)} collective-permute-done((bf16[816,128]{1,0:T(8,128)(2,1)S(1)}, bf16[816,128]{1,0:T(8,128)(2,1)S(1)}, u32[]{:S(2)}, u32[]{:S(2)}) %collective-permute-start) | collective-permute-done | bytes 208928 | tf_op jit(solution)/shard_map/ppermute | solution.py:271
  15.1 1.5 %shard_map.94 = (f32[7168,128]{1,0:T(8,128)S(1)}, bf16[816,128]{1,0:T(8,128)(2,1)S(1)}, bf16[816,128]{1,0:T(8,128)(2,1)S(1)}, bf16[816,128]{1,0:T(8,128)(2,1)S(1)}) custom-call(bf16[816,128]{1,0:T(8,128)(2,1)S(1)} %collective-permute-done.r1, f32[7168,128]{1,0:T(8,128)S(1)} %shard_map.93.local_ref, ...), custom_call_target="tpu_custom_call", output_to_operand_aliasing={{0}: (1, {})} | custom-call | bytes 10080448 | tf_op jit(solution)/shard_map/pallas_call | solution.py:248
  16.7 1.4 %collective-permute-start.4 = (bf16[816,128]{1,0:T(8,128)(2,1)S(1)}, bf16[816,128]{1,0:T(8,128)(2,1)S(1)}, u32[]{:S(2)}, u32[]{:S(2)}) collective-permute-start(bf16[816,128]{1,0:T(8,128)(2,1)S(1)} %get-tuple-element.38), channel_id=1, source_target_pairs={{0,15},{1,2},{2,1},{3,4},{4,3},{5,6},{6,5},{7,8},{8,7},{9,10},{10,... | collective-permute-start | bytes 626696 | tf_op jit(solution)/shard_map/ppermute | solution.py:270
  18.1 0.0 collective-permute-start.5
  18.1 1.5 %collective-permute-start.3 = (bf16[816,128]{1,0:T(8,128)(2,1)S(1)}, bf16[816,128]{1,0:T(8,128)(2,1)S(1)}, u32[]{:S(2)}, u32[]{:S(2)}) collective-permute-start(bf16[816,128]{1,0:T(8,128)(2,1)S(1)} %get-tuple-element.37), channel_id=1, source_target_pairs={{0,16},{16,0},{1,17},{17,1},{2,18},{18,2},{3,19},{19,3},{4,20},{20... | collective-permute-start | bytes 626696 | tf_op jit(solution)/shard_map/ppermute | solution.py:271
  19.6 3.0 %shard_map.95.refs_2_ = f32[7168,128]{1,0:T(8,128)S(1)} custom-call(f32[7168,128]{1,0:T(8,128)S(1)} %get-tuple-element.40.cs, bf16[50,128,128]{2,1,0:T(8,128)(2,1)S(1)} %get-tuple-element.41.a_ref, bf16[128,56,128]{2,1,0:T(8,128)(2,1)S(1)} %get-tuple-element.34.refs_3_.vt_ref), custom_call_target="tpu_custom_call" | custom-call | flops 312475648 | bytes 10813440 | tf_op jit(solution)/shard_map/pallas_call | solution.py:248
  22.6 2.1 %collective-permute-done.4.refs_0_ = bf16[816,128]{1,0:T(8,128)(2,1)S(1)} collective-permute-done((bf16[816,128]{1,0:T(8,128)(2,1)S(1)}, bf16[816,128]{1,0:T(8,128)(2,1)S(1)}, u32[]{:S(2)}, u32[]{:S(2)}) %collective-permute-start.4) | collective-permute-done | bytes 208928 | tf_op jit(solution)/shard_map/ppermute | solution.py:270
  24.7 0.0 collective-permute-done.5.refs_1_
  24.7 1.0 %shard_map.96.local_ref = f32[7168,128]{1,0:T(8,128)S(1)} custom-call(bf16[816,128]{1,0:T(8,128)(2,1)S(1)} %collective-permute-done.4.refs_0_, bf16[816,128]{1,0:T(8,128)(2,1)S(1)} %collective-permute-done.5.refs_1_, f32[7168,128]{1,0:T(8,128)S(1)} %shard_map.95.refs_2_, ...), custom_call_target="tpu_custom_call", output_to_operand_aliasing={{}: (2, {})} | custom-call | flops 25690112 | bytes 9592832 | tf_op jit(solution)/shard_map/pallas_call | solution.py:248
  25.7 0.0 collective-permute-done.3.r1
  25.7 2.2 %shard_map.97 = (bf16[50,128,128]{2,1,0:T(8,128)(2,1)}, f32[7168,128]{1,0:T(8,128)S(1)}) custom-call(bf16[816,128]{1,0:T(8,128)(2,1)S(1)} %collective-permute-done.3.r1, f32[7168,128]{1,0:T(8,128)S(1)} %shard_map.96.local_ref, bf16[128,56,128]{2,1,0:T(8,128)(2,1)S(1)} %get-tuple-element.34.refs_3_.vt_ref), custom_call_target="tpu_custom_call", output_to_operand_aliasing={{1}: (1, {})} | custom-call | bytes 11022336 | tf_op jit(solution)/shard_map/pallas_call | solution.py:248
Async XLA Ops:
  2.1 11.5 %collective-permute-start.1 = (bf16[816,128]{1,0:T(8,128)(2,1)S(1)}, bf16[816,128]{1,0:T(8,128)(2,1)S(1)}, u32[]{:S(2)}, u32[]{:S(2)}) collective-permute-start(bf16[816,128]{1,0:T(8,128)(2,1)S(1)} %get-tuple-element.25), channel_id=1, source_target_pairs={{0,15},{1,2},{2,1},{3,4},{4,3},{5,6},{6,5},{7,8},{8,7},{9,10},{10,... | collective-permute-start | bytes 626696 | tf_op jit(solution)/shard_map/ppermute | solution.py:270
  7.6 6.0 %collective-permute-start.2 = (bf16[816,128]{1,0:T(8,128)(2,1)S(1)}, bf16[816,128]{1,0:T(8,128)(2,1)S(1)}, u32[]{:S(2)}, u32[]{:S(2)}) collective-permute-start(bf16[816,128]{1,0:T(8,128)(2,1)S(1)} %get-tuple-element.26), channel_id=1, source_target_pairs={{0,1},{1,0},{2,3},{3,2},{4,5},{5,4},{6,7},{7,6},{8,9},{9,8},{10,11... | collective-permute-start | bytes 626696 | tf_op jit(solution)/shard_map/ppermute | solution.py:272
  7.6 7.6 %collective-permute-start = (bf16[816,128]{1,0:T(8,128)(2,1)S(1)}, bf16[816,128]{1,0:T(8,128)(2,1)S(1)}, u32[]{:S(2)}, u32[]{:S(2)}) collective-permute-start(bf16[816,128]{1,0:T(8,128)(2,1)S(1)} %get-tuple-element.24), channel_id=1, source_target_pairs={{0,16},{16,0},{1,17},{17,1},{2,18},{18,2},{3,19},{19,3},{4,20},{20... | collective-permute-start | bytes 626696 | tf_op jit(solution)/shard_map/ppermute | solution.py:271
  16.7 8.0 %collective-permute-start.4 = (bf16[816,128]{1,0:T(8,128)(2,1)S(1)}, bf16[816,128]{1,0:T(8,128)(2,1)S(1)}, u32[]{:S(2)}, u32[]{:S(2)}) collective-permute-start(bf16[816,128]{1,0:T(8,128)(2,1)S(1)} %get-tuple-element.38), channel_id=1, source_target_pairs={{0,15},{1,2},{2,1},{3,4},{4,3},{5,6},{6,5},{7,8},{8,7},{9,10},{10,... | collective-permute-start | bytes 626696 | tf_op jit(solution)/shard_map/ppermute | solution.py:270
  18.1 6.5 %collective-permute-start.5 = (bf16[816,128]{1,0:T(8,128)(2,1)S(1)}, bf16[816,128]{1,0:T(8,128)(2,1)S(1)}, u32[]{:S(2)}, u32[]{:S(2)}) collective-permute-start(bf16[816,128]{1,0:T(8,128)(2,1)S(1)} %get-tuple-element.39), channel_id=1, source_target_pairs={{0,1},{1,0},{2,3},{3,2},{4,5},{5,4},{6,7},{7,6},{8,9},{9,8},{10,11... | collective-permute-start | bytes 626696 | tf_op jit(solution)/shard_map/ppermute | solution.py:272
  18.1 7.6 %collective-permute-start.3 = (bf16[816,128]{1,0:T(8,128)(2,1)S(1)}, bf16[816,128]{1,0:T(8,128)(2,1)S(1)}, u32[]{:S(2)}, u32[]{:S(2)}) collective-permute-start(bf16[816,128]{1,0:T(8,128)(2,1)S(1)} %get-tuple-element.37), channel_id=1, source_target_pairs={{0,16},{16,0},{1,17},{17,1},{2,18},{18,2},{3,19},{19,3},{4,20},{20... | collective-permute-start | bytes 626696 | tf_op jit(solution)/shard_map/ppermute | solution.py:271

commit v8 on v7

--- a/solution.py
+++ b/solution.py
@@ -106,8 +106,8 @@
 
 
 def gather_kernel(
-    blk, c_h, send_h, recv_h, edge_h, nbr_h, nw_h, sw_h, wet_h, v_h,
-    s0, s1, s2, c_v, nbr_v, nw_v, sw_v, wet_v, v_v, wts_o, tbl_o,
+    blk, c_h, send_h, recv_h, edge_h, nbr_h, nw_h, sw_h, wet_h,
+    s0, s1, s2, c_v, nbr_v, nw_v, sw_v, wet_v, wts_o, tbl_o,
     cf, wts, recv_v, edge_v, send_s, sems,
 ):
     levels, cols, width = c_h.shape
@@ -116,7 +116,7 @@
     bounds = [(lo, min(lo + 16, levels)) for lo in range(0, levels, 16)]
     pairs = [(send_h, send_s), (recv_h, recv_v), (edge_h, edge_v)]
     pairs += [(c_h.at[pl.ds(lo, hi - lo)], c_v.at[pl.ds(lo, hi - lo)]) for lo, hi in bounds]
-    pairs += [(nbr_h, nbr_v), (nw_h, nw_v), (sw_h, sw_v), (wet_h, wet_v), (v_h, v_v)]
+    pairs += [(nbr_h, nbr_v), (nw_h, nw_v), (sw_h, sw_v), (wet_h, wet_v)]
     copies = [pltpu.make_async_copy(a, b, sems.at[i]) for i, (a, b) in enumerate(pairs)]
     for copy in copies:
         copy.start()
@@ -146,8 +146,10 @@
         copy.wait()
 
 
-def operator_kernel(c_ref, nbr_ref, nw_ref, sw_ref, wet_ref, v_ref, a_ref, state_ref, vt_ref, exs, merged, vf, vts):
+def operator_kernel(c_ref, nbr_ref, nw_ref, sw_ref, wet_ref, v_h, a_ref, state_ref, vt_ref, exs, merged, vf, vts, v_ref, sem):
     levels, cols, width = c_ref.shape
+    load = pltpu.make_async_copy(v_h, v_ref, sem)
+    load.start()
     rows = padded(levels)
     nbr = nbr_ref.shape[0]
     lane = lax.broadcasted_iota(jnp.int32, (8, cols), 1)
@@ -182,6 +184,7 @@
         exs[pl.ds(l, cols, stride=rows), :] = jnp.zeros((cols, width), F32)
     level = lax.broadcasted_iota(jnp.int32, (levels, cols), 0)
     wet = wet_ref[...]
+    load.wait()
     vf[...] = jnp.zeros_like(vf)
     for m in range(levels):
         keep = jnp.maximum(level, m) < wet
@@ -261,15 +264,15 @@
     n, b = lax.axis_size(blk), lax.axis_size(basin)
 
     def pairs(first):
-        order = [(i + first) % n for i in range(n)]
-        partner = {order[i]: order[i + 1] for i in range(0, n - 1, 2)}
+        partner = {i: i + 1 for i in range(first, n - 1, 2)}
         partner |= {j: i for i, j in partner.items()}
-        return [(i, partner.get(i, i)) for i in range(n)]
+        across = lambda g: g ^ 1 if g ^ 1 < b else g
+        return [(g * n + i, g * n + partner[i] if i in partner else across(g) * n + i) for g in range(b) for i in range(n)]
 
     return (
-        lax.ppermute(values[0], blk, pairs(1)),
+        lax.ppermute(values[0], (basin, blk), pairs(1)),
         lax.ppermute(values[1], basin, [(i, (i + 1) % b) for i in range(b)]),
-        lax.ppermute(values[2], blk, pairs(0)),
+        lax.ppermute(values[2], (basin, blk), pairs(0)),
     )
 
 
@@ -284,7 +287,7 @@
     wet = wet_levels.reshape(1, cols)
     in_hbm = lambda x: pltpu.with_memory_space_constraint(x, pltpu.HBM)
     send_h = in_hbm(send_cols)
-    loads = [by_level, nbr_cols, nbr_by_level, self_wts, wet, vert_inv]
+    loads = [by_level, nbr_cols, nbr_by_level, self_wts, wet]
     same = lambda x: shape(x.shape, x.dtype)
     packed = [shape((message_rows(levels, nedge), width), BF16)] * 3
     columns = shape((cols * rows, width), F32)
@@ -293,17 +296,17 @@
     first = call(
         functools.partial(gather_kernel, "blk"),
         (in_hbm(by_level), send_h, *map(in_hbm, (recv_cols, edge_by_entry, *loads[1:]))),
-        [HB] * 9,
+        [HB] * 8,
         packed + [same(x) for x in loads] + [shape((128, 128), F32), shape((8, 128), F32)],
-        [VM] * 11,
+        [VM] * 10,
         [
             pltpu.VMEM((rows * (cols + 8), width), F32), pltpu.VMEM((128, 128), F32),
             pltpu.VMEM(recv_cols.shape, jnp.int32), pltpu.VMEM(edge_by_entry.shape, F32),
-            pltpu.SMEM(send_cols.shape, jnp.int32), DMA((8 + -(-levels // 16),)),
+            pltpu.SMEM(send_cols.shape, jnp.int32), DMA((7 + -(-levels // 16),)),
         ],
         16,
     )
-    sends, loads, (wts, tbl) = first[:3], first[3:9], first[9:]
+    sends, loads, (wts, tbl) = first[:3], first[3:8], first[8:]
     operator_flops = 2 * levels * cols * cols * width
     vertical_flops = 2 * cols * rows * rows * width
 
@@ -319,9 +322,10 @@
 
     odd, along, even = swapped(sends, "blk", "basin")
     operator, partial, vt = call(
-        operator_kernel, loads, [VM] * 6,
+        operator_kernel, (*loads, in_hbm(vert_inv)), [VM] * 5 + [HB],
         [shape((levels, cols, cols), BF16), columns, shape((cols, rows, 128), BF16)], [VM] * 3,
-        [flat, pltpu.VMEM((levels, 8, cols), F32), pltpu.VMEM((rows * rows, cols), F32), pltpu.VMEM((cols * rows, 128), F32)],
+        [flat, pltpu.VMEM((levels, 8, cols), F32), pltpu.VMEM((rows * rows, cols), F32), pltpu.VMEM((cols * rows, 128), F32),
+         pltpu.VMEM(vert_inv.shape, BF16), DMA],
         32, flops=operator_flops + vertical_flops,
     )
     state, *sends = call(

time: 28 us -> 27.5 us (0.982)
  starting transfers between devices: 9.95 us -> 6.88 us
  waiting for transfers between devices: 2.6 us -> 4.85 us
  Pallas kernels: 15.2 us -> 15.5 us
    ppermute x2, waiting for transfers between devices: 0.54 us -> 2.6 us  [swapped(): lax.ppermute(values[1], basin, [(i, (i + 1) % b) for i in range(b)])]
    ppermute x4, starting transfers between devices: 6.96 us -> 5.24 us  [the longest x2 5.09 us: swapped(): lax.ppermute(values[0], (basin, blk), pairs(1))]
    ppermute x2, starting transfers between devices: 2.99 us -> 1.64 us  [swapped(): lax.ppermute(values[1], basin, [(i, (i + 1) % b) for i in range(b)])]
    pallas_call x7, Pallas kernels: 15.2 us -> 15.5 us  [call(): pl.pallas_call(kernel, out_shape=outs, in_specs=specs, out_specs=out_spec...]
  transfers between devices with their start and end apart: 6 -> 6, of which waited for: 2 -> 3; matrix products, arithmetic and copies ran while one was open for 0% -> 0% of each run, Pallas kernels for 34% -> 36%
where the time goes in v8:
time: 27.5 us; the launch traced here: 27.3 us
  Pallas kernels  15.5 us (56%)
  starting transfers between devices  6.88 us (25%)
  waiting for transfers between devices  4.85 us (18%)
    pallas_call x7, Pallas kernels, call(): pl.pallas_call(kernel, out_shape=outs, in_specs=specs, out_specs=out_spec...  15.5 us
    ppermute x2, starting transfers between devices, swapped(): lax.ppermute(values[0], (basin, blk), pairs(1))  5.09 us
    ppermute x2, waiting for transfers between devices, swapped(): lax.ppermute(values[1], basin, [(i, (i + 1) % b) for i in range(b)])  2.6 us
    ppermute x2, waiting for transfers between devices, swapped(): lax.ppermute(values[0], (basin, blk), pairs(1))  2.24 us
    ppermute x2, starting transfers between devices, swapped(): lax.ppermute(values[1], basin, [(i, (i + 1) % b) for i in range(b)])  1.64 us
  transfers between devices with their start and end apart: 6, of which 3 were waited for; matrix products, arithmetic and copies ran while one was open for 0% of the time, Pallas kernels for 36%

profile of v8, /device:TPU:0, one launch (start us, length us, event | category | flops | bytes accessed | tf_op | source)
XLA Modules:
  0.0 27.3 jit_solution(16682031991204228340)
XLA Ops:
  0.0 2.0 %shard_map.91 = (bf16[816,128]{1,0:T(8,128)(2,1)S(1)}, bf16[816,128]{1,0:T(8,128)(2,1)S(1)}, bf16[816,128]{1,0:T(8,128)(2,1)S(1)}, bf16[50,128,128]{2,1,0:T(8,12...) custom-call(bf16[50,128,128]{2,1,0:T(8,128)(2,1)} %bitcast.5, ...), custom_call_target="tpu_custom_call" | custom-call | bytes 4244224 | tf_op jit(solution)/shard_map/pallas_call | solution.py:251
  2.0 3.0 %collective-permute-start.1 = (bf16[816,128]{1,0:T(8,128)(2,1)S(1)}, bf16[816,128]{1,0:T(8,128)(2,1)S(1)}, u32[]{:S(2)}, u32[]{:S(2)}) collective-permute-start(bf16[816,128]{1,0:T(8,128)(2,1)S(1)} %get-tuple-element.24), channel_id=1, source_target_pairs={{0,16},{1,2},{2,1},{3,4},{4,3},{5,6},{6,5},{7,8},{8,7},{9,10},{10,... | collective-permute-start | bytes 626696 | tf_op jit(solution)/shard_map/ppermute | solution.py:273
  5.0 0.1 collective-permute-start.2
  5.2 1.5 %collective-permute-start = (bf16[816,128]{1,0:T(8,128)(2,1)S(1)}, bf16[816,128]{1,0:T(8,128)(2,1)S(1)}, u32[]{:S(2)}, u32[]{:S(2)}) collective-permute-start(bf16[816,128]{1,0:T(8,128)(2,1)S(1)} %get-tuple-element.23), channel_id=1, source_target_pairs={{0,16},{16,0},{1,17},{17,1},{2,18},{18,2},{3,19},{19,3},{4,20},{20... | collective-permute-start | bytes 626696 | tf_op jit(solution)/shard_map/ppermute | solution.py:274
  6.7 4.8 %shard_map.92 = (bf16[50,128,128]{2,1,0:T(8,128)(2,1)S(1)}, f32[7168,128]{1,0:T(8,128)S(1)}, bf16[128,56,128]{2,1,0:T(8,128)(2,1)S(1)}) custom-call(bf16[50,128,128]{2,1,0:T(8,128)(2,1)S(1)} %get-tuple-element.26.c_ref, s32[4,128]{1,0:T(4,128)S(1)} %get-tuple-element.27.nbr_ref, f32[50,4,128]{2,1,0:T(4,128)S(1)} %get-tuple-element.28.nw_ref, ...), custom_call_target="tpu_custom_call" | custom-call | flops 312475648 | bytes 9552384 | tf_op jit(solution)/shard_map/pallas_call | solution.py:251
  11.5 0.0 collective-permute-done.1.refs_0_
  11.5 0.0 collective-permute-done.2.refs_1_
  11.5 1.0 %shard_map.93.local_ref = f32[7168,128]{1,0:T(8,128)S(1)} custom-call(bf16[816,128]{1,0:T(8,128)(2,1)S(1)} %collective-permute-done.1.refs_0_, bf16[816,128]{1,0:T(8,128)(2,1)S(1)} %collective-permute-done.2.refs_1_, f32[7168,128]{1,0:T(8,128)S(1)} %get-tuple-element.31.refs_2_, ...), custom_call_target="tpu_custom_call", output_to_operand_aliasing={{}: (2, {})} | custom-call | flops 25690112 | bytes 9592832 | tf_op jit(solution)/shard_map/pallas_call | solution.py:251
  12.6 0.8 %collective-permute-done.r1 = bf16[816,128]{1,0:T(8,128)(2,1)S(1)} collective-permute-done((bf16[816,128]{1,0:T(8,128)(2,1)S(1)}, bf16[816,128]{1,0:T(8,128)(2,1)S(1)}, u32[]{:S(2)}, u32[]{:S(2)}) %collective-permute-start) | collective-permute-done | bytes 208928 | tf_op jit(solution)/shard_map/ppermute | solution.py:274
  13.3 1.5 %shard_map.94 = (f32[7168,128]{1,0:T(8,128)S(1)}, bf16[816,128]{1,0:T(8,128)(2,1)S(1)}, bf16[816,128]{1,0:T(8,128)(2,1)S(1)}, bf16[816,128]{1,0:T(8,128)(2,1)S(1)}) custom-call(bf16[816,128]{1,0:T(8,128)(2,1)S(1)} %collective-permute-done.r1, f32[7168,128]{1,0:T(8,128)S(1)} %shard_map.93.local_ref, ...), custom_call_target="tpu_custom_call", output_to_operand_aliasing={{0}: (1, {})} | custom-call | bytes 10080448 | tf_op jit(solution)/shard_map/pallas_call | solution.py:251
  14.8 2.1 %collective-permute-start.4 = (bf16[816,128]{1,0:T(8,128)(2,1)S(1)}, bf16[816,128]{1,0:T(8,128)(2,1)S(1)}, u32[]{:S(2)}, u32[]{:S(2)}) collective-permute-start(bf16[816,128]{1,0:T(8,128)(2,1)S(1)} %get-tuple-element.36), channel_id=1, source_target_pairs={{0,16},{1,2},{2,1},{3,4},{4,3},{5,6},{6,5},{7,8},{8,7},{9,10},{10,... | collective-permute-start | bytes 626696 | tf_op jit(solution)/shard_map/ppermute | solution.py:273
  16.9 0.0 collective-permute-start.5
  16.9 0.2 collective-permute-start.3
  17.1 3.0 %shard_map.95.refs_2_ = f32[7168,128]{1,0:T(8,128)S(1)} custom-call(f32[7168,128]{1,0:T(8,128)S(1)} %get-tuple-element.38.cs, bf16[50,128,128]{2,1,0:T(8,128)(2,1)S(1)} %get-tuple-element.39.a_ref, bf16[128,56,128]{2,1,0:T(8,128)(2,1)S(1)} %get-tuple-element.32.refs_3_.vt_ref), custom_call_target="tpu_custom_call" | custom-call | flops 312475648 | bytes 10813440 | tf_op jit(solution)/shard_map/pallas_call | solution.py:251
  20.1 2.2 %collective-permute-done.4.refs_0_ = bf16[816,128]{1,0:T(8,128)(2,1)S(1)} collective-permute-done((bf16[816,128]{1,0:T(8,128)(2,1)S(1)}, bf16[816,128]{1,0:T(8,128)(2,1)S(1)}, u32[]{:S(2)}, u32[]{:S(2)}) %collective-permute-start.4) | collective-permute-done | bytes 208928 | tf_op jit(solution)/shard_map/ppermute | solution.py:273
  22.3 0.0 collective-permute-done.5.refs_1_
  22.3 1.0 %shard_map.96.local_ref = f32[7168,128]{1,0:T(8,128)S(1)} custom-call(bf16[816,128]{1,0:T(8,128)(2,1)S(1)} %collective-permute-done.4.refs_0_, bf16[816,128]{1,0:T(8,128)(2,1)S(1)} %collective-permute-done.5.refs_1_, f32[7168,128]{1,0:T(8,128)S(1)} %shard_map.95.refs_2_, ...), custom_call_target="tpu_custom_call", output_to_operand_aliasing={{}: (2, {})} | custom-call | flops 25690112 | bytes 9592832 | tf_op jit(solution)/shard_map/pallas_call | solution.py:251
  23.3 1.9 %collective-permute-done.3.r1 = bf16[816,128]{1,0:T(8,128)(2,1)S(1)} collective-permute-done((bf16[816,128]{1,0:T(8,128)(2,1)S(1)}, bf16[816,128]{1,0:T(8,128)(2,1)S(1)}, u32[]{:S(2)}, u32[]{:S(2)}) %collective-permute-start.3) | collective-permute-done | bytes 208928 | tf_op jit(solution)/shard_map/ppermute | solution.py:274
  25.2 2.1 %shard_map.97 = (bf16[50,128,128]{2,1,0:T(8,128)(2,1)}, f32[7168,128]{1,0:T(8,128)S(1)}) custom-call(bf16[816,128]{1,0:T(8,128)(2,1)S(1)} %collective-permute-done.3.r1, f32[7168,128]{1,0:T(8,128)S(1)} %shard_map.96.local_ref, bf16[128,56,128]{2,1,0:T(8,128)(2,1)S(1)} %get-tuple-element.32.refs_3_.vt_ref), custom_call_target="tpu_custom_call", output_to_operand_aliasing={{1}: (1, {})} | custom-call | bytes 11022336 | tf_op jit(solution)/shard_map/pallas_call | solution.py:251
Async XLA Ops:
  2.0 9.5 %collective-permute-start.1 = (bf16[816,128]{1,0:T(8,128)(2,1)S(1)}, bf16[816,128]{1,0:T(8,128)(2,1)S(1)}, u32[]{:S(2)}, u32[]{:S(2)}) collective-permute-start(bf16[816,128]{1,0:T(8,128)(2,1)S(1)} %get-tuple-element.24), channel_id=1, source_target_pairs={{0,16},{1,2},{2,1},{3,4},{4,3},{5,6},{6,5},{7,8},{8,7},{9,10},{10,... | collective-permute-start | bytes 626696 | tf_op jit(solution)/shard_map/ppermute | solution.py:273
  5.0 6.5 %collective-permute-start.2 = (bf16[816,128]{1,0:T(8,128)(2,1)S(1)}, bf16[816,128]{1,0:T(8,128)(2,1)S(1)}, u32[]{:S(2)}, u32[]{:S(2)}) collective-permute-start(bf16[816,128]{1,0:T(8,128)(2,1)S(1)} %get-tuple-element.25), channel_id=1, source_target_pairs={{0,1},{1,0},{2,3},{3,2},{4,5},{5,4},{6,7},{7,6},{8,9},{9,8},{10,11... | collective-permute-start | bytes 626696 | tf_op jit(solution)/shard_map/ppermute | solution.py:275
  5.2 8.1 %collective-permute-start = (bf16[816,128]{1,0:T(8,128)(2,1)S(1)}, bf16[816,128]{1,0:T(8,128)(2,1)S(1)}, u32[]{:S(2)}, u32[]{:S(2)}) collective-permute-start(bf16[816,128]{1,0:T(8,128)(2,1)S(1)} %get-tuple-element.23), channel_id=1, source_target_pairs={{0,16},{16,0},{1,17},{17,1},{2,18},{18,2},{3,19},{19,3},{4,20},{20... | collective-permute-start | bytes 626696 | tf_op jit(solution)/shard_map/ppermute | solution.py:274
  14.8 7.5 %collective-permute-start.4 = (bf16[816,128]{1,0:T(8,128)(2,1)S(1)}, bf16[816,128]{1,0:T(8,128)(2,1)S(1)}, u32[]{:S(2)}, u32[]{:S(2)}) collective-permute-start(bf16[816,128]{1,0:T(8,128)(2,1)S(1)} %get-tuple-element.36), channel_id=1, source_target_pairs={{0,16},{1,2},{2,1},{3,4},{4,3},{5,6},{6,5},{7,8},{8,7},{9,10},{10,... | collective-permute-start | bytes 626696 | tf_op jit(solution)/shard_map/ppermute | solution.py:273
  16.9 5.4 %collective-permute-start.5 = (bf16[816,128]{1,0:T(8,128)(2,1)S(1)}, bf16[816,128]{1,0:T(8,128)(2,1)S(1)}, u32[]{:S(2)}, u32[]{:S(2)}) collective-permute-start(bf16[816,128]{1,0:T(8,128)(2,1)S(1)} %get-tuple-element.37), channel_id=1, source_target_pairs={{0,1},{1,0},{2,3},{3,2},{4,5},{5,4},{6,7},{7,6},{8,9},{9,8},{10,11... | collective-permute-start | bytes 626696 | tf_op jit(solution)/shard_map/ppermute | solution.py:275
  16.9 8.3 %collective-permute-start.3 = (bf16[816,128]{1,0:T(8,128)(2,1)S(1)}, bf16[816,128]{1,0:T(8,128)(2,1)S(1)}, u32[]{:S(2)}, u32[]{:S(2)}) collective-permute-start(bf16[816,128]{1,0:T(8,128)(2,1)S(1)} %get-tuple-element.35), channel_id=1, source_target_pairs={{0,16},{16,0},{1,17},{17,1},{2,18},{18,2},{3,19},{19,3},{4,20},{20... | collective-permute-start | bytes 626696 | tf_op jit(solution)/shard_map/ppermute | solution.py:274

commit v9 on v8

--- a/solution.py
+++ b/solution.py
@@ -33,12 +33,12 @@
     return jnp.where(first, at + 1 < count, at > 0)
 
 
-def pack_chunk(parity, lo, levels, send, weights, tbl, rows_of, outs):
+def pack_chunk(parity, lo, levels, send, weights, tbl, rows_of, slots, outs):
     whole = whole_rows(levels)
     nedge = send.shape[1]
     rest = levels - whole
     share = 8 // rest if rest else 0
-    for slot, out in enumerate(outs):
+    for slot, out in zip(slots, outs):
         d = direction(slot, parity)
         if lo < whole:
             for e in range(nedge):
@@ -107,8 +107,8 @@
 
 def gather_kernel(
     blk, c_h, send_h, recv_h, edge_h, nbr_h, nw_h, sw_h, wet_h,
-    s0, s1, s2, c_v, nbr_v, nw_v, sw_v, wet_v, wts_o, tbl_o,
-    cf, wts, recv_v, edge_v, send_s, sems,
+    s0, s1, c_v, nbr_v, nw_v, sw_v, wet_v, wts_o, tbl_o, cf,
+    wts, recv_v, edge_v, send_s, sems,
 ):
     levels, cols, width = c_h.shape
     nedge = edge_h.shape[1]
@@ -139,18 +139,16 @@
         copies[3 + i].wait()
         for l in range(lo, hi):
             cf[l * pitch : l * pitch + cols, :] = c_v[l].astype(F32)
-        pack_chunk(parity, lo, levels, send_s, weights, tbl_o, rows_of, (s0, s1, s2))
+        pack_chunk(parity, lo, levels, send_s, weights, tbl_o, rows_of, (0, 1), (s0, s1))
     if levels % 16 == 0:
-        pack_chunk(parity, levels, levels, send_s, weights, tbl_o, rows_of, (s0, s1, s2))
+        pack_chunk(parity, levels, levels, send_s, weights, tbl_o, rows_of, (0, 1), (s0, s1))
     for copy in copies[3 + len(bounds) :]:
         copy.wait()
 
 
-def operator_kernel(c_ref, nbr_ref, nw_ref, sw_ref, wet_ref, v_h, a_ref, state_ref, vt_ref, exs, merged, vf, vts, v_ref, sem):
-    levels, cols, width = c_ref.shape
-    load = pltpu.make_async_copy(v_h, v_ref, sem)
-    load.start()
-    rows = padded(levels)
+def column_operator(nbr_ref, nw_ref, sw_ref, a_ref, merged):
+    levels = nw_ref.shape[0]
+    cols = nbr_ref.shape[1]
     nbr = nbr_ref.shape[0]
     lane = lax.broadcasted_iota(jnp.int32, (8, cols), 1)
     sub = lax.broadcasted_iota(jnp.int32, (8, cols), 0)
@@ -170,18 +168,49 @@
         hits = [j == nbr_ref[n : n + 1, :] for n in range(nbr)]
         hits.append(j == lax.broadcasted_iota(jnp.int32, (half, cols), 1))
 
-        def fill(l, _):
-            value = jnp.zeros((half, cols), F32)
-            for n in range(nbr, -1, -1):
-                value = jnp.where(hits[n], merged[l, n : n + 1, :], value)
-            a_ref[l, jt * half : (jt + 1) * half, :] = value.astype(BF16)
+        def fill(p, _):
+            for i in range(2):
+                value = jnp.zeros((half, cols), F32)
+                for n in range(nbr, -1, -1):
+                    value = jnp.where(hits[n], merged[p * 2 + i, n : n + 1, :], value)
+                a_ref[p, jt * half : (jt + 1) * half, i * cols : (i + 1) * cols] = value.astype(BF16)
             return _
 
-        lax.fori_loop(0, levels, fill, 0, unroll=5)
-    for l in range(levels):
-        exs[pl.ds(l, cols, stride=rows), :] = jnp.dot(a_ref[l], c_ref[l], preferred_element_type=F32)
-    for l in range(levels, rows):
+        lax.fori_loop(0, levels // 2, fill, 0, unroll=5)
+
+
+def level_products(a_ref, state_of, exs, rows):
+    pairs, cols, _ = a_ref.shape
+    width = exs.shape[1]
+    zero = jnp.zeros((cols, width), BF16)
+    for p in range(pairs):
+        left = jnp.concatenate([state_of(2 * p), zero], axis=1)
+        right = jnp.concatenate([zero, state_of(2 * p + 1)], axis=1)
+        both = jnp.dot(a_ref[p], jnp.concatenate([left, right], axis=0), preferred_element_type=F32)
+        exs[pl.ds(2 * p, cols, stride=rows), :] = both[:, 0:width]
+        exs[pl.ds(2 * p + 1, cols, stride=rows), :] = both[:, width:]
+    for l in range(2 * pairs, rows):
         exs[pl.ds(l, cols, stride=rows), :] = jnp.zeros((cols, width), F32)
+
+
+def operator_kernel(
+    blk, c_ref, nbr_ref, nw_ref, sw_ref, wet_ref, cf, wts_ref, tbl_ref, send_h, v_h,
+    a_ref, state_ref, vt_ref, s2, exs, merged, vf, vts, v_ref, send_s, sems,
+):
+    levels, cols, width = c_ref.shape
+    rows = padded(levels)
+    load = pltpu.make_async_copy(v_h, v_ref, sems.at[0])
+    load.start()
+    copy = pltpu.make_async_copy(send_h, send_s, sems.at[1])
+    copy.start()
+    column_operator(nbr_ref, nw_ref, sw_ref, a_ref, merged)
+    copy.wait()
+    parity = lax.bitwise_and(lax.axis_index(blk), jnp.int32(1))
+    pitch = cols + 8
+    rows_of = lambda s, lo, n: cf[pl.ds(lo * pitch + s, n, stride=pitch), :]
+    for lo in range(0, levels + 1, 16):
+        pack_chunk(parity, lo, levels, send_s, wts_ref, tbl_ref, rows_of, (2,), (s2,))
+    level_products(a_ref, lambda l: c_ref[l], exs, rows)
     level = lax.broadcasted_iota(jnp.int32, (levels, cols), 0)
     wet = wet_ref[...]
     load.wait()
@@ -202,33 +231,35 @@
     add_edges(edges, levels, nedge, vt_ref, total, tbl_v, tbl_s, sem)
 
 
-def send_kernel(blk, levels, r1, local_ref, vt_ref, wts_ref, tbl_ref, send_h, state, s0, s1, s2, tbl_v, tbl_s, send_s, sems):
+def send_kernel(blk, levels, r0, r2, local_ref, vt_ref, wts_ref, tbl_ref, send_h, state, s0, s1, tbl_v, tbl_s, send_s, sems):
     copy = pltpu.make_async_copy(send_h, send_s, sems.at[1])
     copy.start()
+    add_edges((r0, r2), levels, send_h.shape[1], vt_ref, state, tbl_v, tbl_s, sems.at[0])
+    copy.wait()
+    pack_state(blk, levels, send_s, wts_ref, tbl_ref, state, vt_ref.shape[1], (0, 1), (s0, s1))
+
+
+def pack_state(blk, levels, send, weights, tbl, state, rows, slots, outs):
     parity = lax.bitwise_and(lax.axis_index(blk), jnp.int32(1))
-    rows = vt_ref.shape[1]
-    add_edges((r1,), levels, send_h.shape[1], vt_ref, state, tbl_v, tbl_s, sems.at[0])
-    copy.wait()
     rows_of = lambda s, lo, n: state[pl.ds(pl.multiple_of(s * rows + lo, 8), n), :]
     for lo in range(0, levels + 1, 16):
-        pack_chunk(parity, lo, levels, send_s, wts_ref, tbl_ref, rows_of, (s0, s1, s2))
-
-
-def middle_kernel(cs, a_ref, vt_ref, out_ref, exs):
-    levels, cols, _ = a_ref.shape
-    rows = vt_ref.shape[1]
-    for l in range(levels):
-        state = cs[pl.ds(l, cols, stride=rows), :].astype(BF16)
-        exs[pl.ds(l, cols, stride=rows), :] = jnp.dot(a_ref[l], state, preferred_element_type=F32)
-    for l in range(levels, rows):
-        exs[pl.ds(l, cols, stride=rows), :] = jnp.zeros((cols, exs.shape[1]), F32)
+        pack_chunk(parity, lo, levels, send, weights, tbl, rows_of, slots, outs)
+
+
+def middle_kernel(blk, levels, cs, a_ref, vt_ref, wts_ref, tbl_ref, send_h, out_ref, s2, exs, send_s, sem):
+    copy = pltpu.make_async_copy(send_h, send_s, sem)
+    copy.start()
+    cols, rows, _ = vt_ref.shape
+    level_products(a_ref, lambda l: cs[pl.ds(l, cols, stride=rows), :].astype(BF16), exs, rows)
+    copy.wait()
+    pack_state(blk, levels, send_s, wts_ref, tbl_ref, cs, rows, (2,), (s2,))
     vertical(vt_ref, exs, out_ref)
 
 
-def last_kernel(nedge, r1, local_ref, vt_ref, out_h, total, out_v, tbl_v, tbl_s, sems):
+def last_kernel(nedge, r0, r2, local_ref, vt_ref, out_h, total, out_v, tbl_v, tbl_s, sems):
     levels, cols, width = out_h.shape
     rows = vt_ref.shape[1]
-    add_edges((r1,), levels, nedge, vt_ref, total, tbl_v, tbl_s, sems.at[0])
+    add_edges((r0, r2), levels, nedge, vt_ref, total, tbl_v, tbl_s, sems.at[0])
     count = 5
     edges = [levels * i // count for i in range(count + 1)]
     copies = []
@@ -260,20 +291,18 @@
     )(*ins)
 
 
-def swapped(values, blk, basin):
+def odd_or_even(value, first, blk, basin):
     n, b = lax.axis_size(blk), lax.axis_size(basin)
-
-    def pairs(first):
-        partner = {i: i + 1 for i in range(first, n - 1, 2)}
-        partner |= {j: i for i, j in partner.items()}
-        across = lambda g: g ^ 1 if g ^ 1 < b else g
-        return [(g * n + i, g * n + partner[i] if i in partner else across(g) * n + i) for g in range(b) for i in range(n)]
-
-    return (
-        lax.ppermute(values[0], (basin, blk), pairs(1)),
-        lax.ppermute(values[1], basin, [(i, (i + 1) % b) for i in range(b)]),
-        lax.ppermute(values[2], (basin, blk), pairs(0)),
-    )
+    partner = {i: i + 1 for i in range(first, n - 1, 2)}
+    partner |= {j: i for i, j in partner.items()}
+    across = lambda g: g ^ 1 if g ^ 1 < b else g
+    route = [(g * n + i, g * n + partner[i] if i in partner else across(g) * n + i) for g in range(b) for i in range(n)]
+    return lax.ppermute(value, (basin, blk), route)
+
+
+def along_basin(value, basin):
+    b = lax.axis_size(basin)
+    return lax.ppermute(value, basin, [(i, (i + 1) % b) for i in range(b)])
 
 
 def local(tracers, nbr_cols, nbr_wts, self_wts, send_cols, recv_cols, edge_wts, wet_levels, vert_inv):
@@ -289,59 +318,66 @@
     send_h = in_hbm(send_cols)
     loads = [by_level, nbr_cols, nbr_by_level, self_wts, wet]
     same = lambda x: shape(x.shape, x.dtype)
-    packed = [shape((message_rows(levels, nedge), width), BF16)] * 3
+    message = shape((message_rows(levels, nedge), width), BF16)
     columns = shape((cols * rows, width), F32)
     flat = pltpu.VMEM(columns.shape, F32)
+    send_table = pltpu.SMEM(send_cols.shape, jnp.int32)
 
     first = call(
         functools.partial(gather_kernel, "blk"),
         (in_hbm(by_level), send_h, *map(in_hbm, (recv_cols, edge_by_entry, *loads[1:]))),
         [HB] * 8,
-        packed + [same(x) for x in loads] + [shape((128, 128), F32), shape((8, 128), F32)],
+        [message] * 2 + [same(x) for x in loads]
+        + [shape((128, 128), F32), shape((8, 128), F32), shape((rows * (cols + 8), width), F32)],
         [VM] * 10,
         [
-            pltpu.VMEM((rows * (cols + 8), width), F32), pltpu.VMEM((128, 128), F32),
-            pltpu.VMEM(recv_cols.shape, jnp.int32), pltpu.VMEM(edge_by_entry.shape, F32),
-            pltpu.SMEM(send_cols.shape, jnp.int32), DMA((7 + -(-levels // 16),)),
+            pltpu.VMEM((128, 128), F32), pltpu.VMEM(recv_cols.shape, jnp.int32), pltpu.VMEM(edge_by_entry.shape, F32),
+            send_table, DMA((7 + -(-levels // 16),)),
         ],
         16,
     )
-    sends, loads, (wts, tbl) = first[:3], first[3:8], first[8:]
+    (to_odd, to_next), (state, nbr, nbr_w, self_w, wet), (wts, tbl, by_row) = first[:2], first[2:7], first[7:]
     operator_flops = 2 * levels * cols * cols * width
     vertical_flops = 2 * cols * rows * rows * width
 
     def tables(count):
         return [pltpu.VMEM((count, 8, 128), jnp.int32), pltpu.SMEM((count, 8, 128), jnp.int32)]
 
-    def arrived(partial, messages):
+    def arrived(partial, *messages):
         return call(
             functools.partial(arrived_kernel, levels, nedge), (*messages, partial, vt), [VM] * (len(messages) + 2),
             [columns], [VM], tables(len(messages)) + [DMA], 16,
             flops=len(messages) * nedge * 2 * rows * rows * width, aliases={len(messages): 0},
         )[0]
 
-    odd, along, even = swapped(sends, "blk", "basin")
-    operator, partial, vt = call(
-        operator_kernel, (*loads, in_hbm(vert_inv)), [VM] * 5 + [HB],
-        [shape((levels, cols, cols), BF16), columns, shape((cols, rows, 128), BF16)], [VM] * 3,
+    along = along_basin(to_next, "basin")
+    odd = odd_or_even(to_odd, 1, "blk", "basin")
+    operator, partial, vt, to_even = call(
+        functools.partial(operator_kernel, "blk"),
+        (state, nbr, nbr_w, self_w, wet, by_row, wts, tbl, send_h, in_hbm(vert_inv)), [VM] * 8 + [HB] * 2,
+        [shape((levels // 2, cols, 2 * cols), BF16), columns, shape((cols, rows, 128), BF16), message], [VM] * 4,
         [flat, pltpu.VMEM((levels, 8, cols), F32), pltpu.VMEM((rows * rows, cols), F32), pltpu.VMEM((cols * rows, 128), F32),
-         pltpu.VMEM(vert_inv.shape, BF16), DMA],
+         pltpu.VMEM(vert_inv.shape, BF16), send_table, DMA((2,))],
         32, flops=operator_flops + vertical_flops,
     )
-    state, *sends = call(
+    even = odd_or_even(to_even, 0, "blk", "basin")
+    state, to_odd, to_next = call(
         functools.partial(send_kernel, "blk", levels),
-        (along, arrived(partial, (odd, even)), vt, wts, tbl, send_h), [VM] * 5 + [HB],
-        [columns] + packed, [VM] * 4,
-        tables(1) + [pltpu.SMEM(send_cols.shape, jnp.int32), DMA((2,))], 16, aliases={1: 0},
-    )
-    odd, along, even = swapped(sends, "blk", "basin")
-    (partial,) = call(
-        middle_kernel, (state, operator, vt), [VM] * 3, [columns], [VM], [flat], 32, flops=operator_flops + vertical_flops,
-    )
+        (odd, even, arrived(partial, along), vt, wts, tbl, send_h), [VM] * 6 + [HB],
+        [columns] + [message] * 2, [VM] * 3,
+        tables(2) + [send_table, DMA((2,))], 16, aliases={2: 0},
+    )
+    along = along_basin(to_next, "basin")
+    odd = odd_or_even(to_odd, 1, "blk", "basin")
+    partial, to_even = call(
+        functools.partial(middle_kernel, "blk", levels), (state, operator, vt, wts, tbl, send_h), [VM] * 5 + [HB],
+        [columns, message], [VM] * 2, [flat, send_table, DMA], 32, flops=operator_flops + vertical_flops,
+    )
+    even = odd_or_even(to_even, 0, "blk", "basin")
     out, _ = call(
-        functools.partial(last_kernel, nedge), (along, arrived(partial, (odd, even)), vt), [VM] * 3,
+        functools.partial(last_kernel, nedge), (odd, even, arrived(partial, along), vt), [VM] * 4,
         [shape((levels, cols, width), BF16), columns], [HB, VM],
-        [pltpu.VMEM((levels, cols, width), BF16)] + tables(1) + [DMA((6,))], 16, aliases={1: 1},
+        [pltpu.VMEM((levels, cols, width), BF16)] + tables(2) + [DMA((6,))], 16, aliases={2: 1},
     )
     return jnp.transpose(out, (1, 0, 2))
 

time: 27.5 us -> 28 us (1.018)
  waiting for transfers between devices: 4.85 us -> 5.41 us
    ppermute x6, waiting for transfers between devices: 4.85 us -> 5.41 us  [the longest x2 5.4 us: along_basin(): return lax.ppermute(value, basin, [(i, (i + 1) % b) for i in range(b)])]
  transfers between devices with their start and end apart: 6 -> 6, of which waited for: 3 -> 2; matrix products, arithmetic and copies ran while one was open for 0% -> 0% of each run, Pallas kernels for 36% -> 36%
where the time goes in v9:
time: 28 us; the launch traced here: 27.8 us
  Pallas kernels  15.7 us (56%)
  starting transfers between devices  6.65 us (24%)
  waiting for transfers between devices  5.41 us (19%)
    pallas_call x7, Pallas kernels, call(): pl.pallas_call(kernel, out_shape=outs, in_specs=specs, out_specs=out_spec...  15.7 us
    ppermute x4, starting transfers between devices, odd_or_even(): return lax.ppermute(value, (basin, blk), route)  6.5 us
    ppermute x2, waiting for transfers between devices, along_basin(): return lax.ppermute(value, basin, [(i, (i + 1) % b) for i in range(b)])  5.4 us
  transfers between devices with their start and end apart: 6, of which 2 were waited for; matrix products, arithmetic and copies ran while one was open for 0% of the time, Pallas kernels for 36%

profile of v9, /device:TPU:0, one launch (start us, length us, event | category | flops | bytes accessed | tf_op | source)
XLA Modules:
  0.0 27.8 jit_solution(1881228239126132568)
XLA Ops:
  0.0 1.8 %shard_map.91 = (bf16[816,128]{1,0:T(8,128)(2,1)S(1)}, bf16[816,128]{1,0:T(8,128)(2,1)S(1)}, bf16[50,128,128]{2,1,0:T(8,128)(2,1)S(1)}, s32[4,128]{1,0:T(4,128)S...) custom-call(bf16[50,128,128]{2,1,0:T(8,128)(2,1)} %bitcast.5, ...), custom_call_target="tpu_custom_call" | custom-call | bytes 7934720 | tf_op jit(solution)/shard_map/pallas_call | solution.py:282
  1.9 3.0 %collective-permute-start = (bf16[816,128]{1,0:T(8,128)(2,1)S(1)}, bf16[816,128]{1,0:T(8,128)(2,1)S(1)}, u32[]{:S(2)}, u32[]{:S(2)}) collective-permute-start(bf16[816,128]{1,0:T(8,128)(2,1)S(1)} %get-tuple-element.25), channel_id=1, source_target_pairs={{0,16},{1,2},{2,1},{3,4},{4,3},{5,6},{6,5},{7,8},{8,7},{9,10},{10,... | collective-permute-start | bytes 626696 | tf_op jit(solution)/shard_map/ppermute | solution.py:300
  4.9 0.1 collective-permute-start.2
  4.9 4.7 %shard_map.92 = (bf16[25,128,256]{2,1,0:T(8,128)(2,1)S(1)}, f32[7168,128]{1,0:T(8,128)S(1)}, bf16[128,56,128]{2,1,0:T(8,128)(2,1)S(1)}, bf16[816,128]{1,0:T(8,128)(2,1)S(1)}) custom-call(bf16[50,128,128]{2,1,0:T(8,128)(2,1)S(1)} %get-tuple-element.26.c_ref, s32[4,128]{1,0:T(4,128)S(1)} %get-tuple-element.27.nbr_ref, ...), custom_call_target="tpu_custom_call" | custom-call | flops 312475648 | bytes 13730496 | tf_op jit(solution)/shard_map/pallas_call | solution.py:282
  9.7 1.3 %collective-permute-start.1 = (bf16[816,128]{1,0:T(8,128)(2,1)S(1)}, bf16[816,128]{1,0:T(8,128)(2,1)S(1)}, u32[]{:S(2)}, u32[]{:S(2)}) collective-permute-start(bf16[816,128]{1,0:T(8,128)(2,1)S(1)} %get-tuple-element.34), channel_id=1, source_target_pairs={{0,1},{1,0},{2,3},{3,2},{4,5},{5,4},{6,7},{7,6},{8,9},{9,8},{10,11... | collective-permute-start | bytes 626696 | tf_op jit(solution)/shard_map/ppermute | solution.py:300
  11.0 2.1 %collective-permute-done.2.refs_0_ = bf16[816,128]{1,0:T(8,128)(2,1)S(1)} collective-permute-done((bf16[816,128]{1,0:T(8,128)(2,1)S(1)}, bf16[816,128]{1,0:T(8,128)(2,1)S(1)}, u32[]{:S(2)}, u32[]{:S(2)}) %collective-permute-start.2) | collective-permute-done | bytes 208928 | tf_op jit(solution)/shard_map/ppermute | solution.py:305
  13.1 0.9 %shard_map.93.local_ref = f32[7168,128]{1,0:T(8,128)S(1)} custom-call(bf16[816,128]{1,0:T(8,128)(2,1)S(1)} %collective-permute-done.2.refs_0_, f32[7168,128]{1,0:T(8,128)S(1)} %get-tuple-element.36.refs_1_, bf16[128,56,128]{2,1,0:T(8,128)(2,1)S(1)} %get-tuple-element.37.refs_2_.vt_ref), custom_call_target="tpu_custom_call", output_to_operand_aliasing={{}: (1, {})} | custom-call | flops 12845056 | bytes 9383936 | tf_op jit(solution)/shard_map/pallas_call | solution.py:282
  14.0 0.0 collective-permute-done.r0
  14.0 0.0 collective-permute-done.1.r2
  14.0 1.5 %shard_map.94 = (f32[7168,128]{1,0:T(8,128)S(1)}, bf16[816,128]{1,0:T(8,128)(2,1)S(1)}, bf16[816,128]{1,0:T(8,128)(2,1)S(1)}) custom-call(bf16[816,128]{1,0:T(8,128)(2,1)S(1)} %collective-permute-done.r0, bf16[816,128]{1,0:T(8,128)(2,1)S(1)} %collective-permute-done.1.r2, f32[7168,128]{1,0:T(8,128)S(1)} %shard_map.93.local_ref, ...), custom_call_target="tpu_custom_call", output_to_operand_aliasing={{0}: (2, {})} | custom-call | bytes 10080448 | tf_op jit(solution)/shard_map/pallas_call | solution.py:282
  15.5 2.1 %collective-permute-start.3 = (bf16[816,128]{1,0:T(8,128)(2,1)S(1)}, bf16[816,128]{1,0:T(8,128)(2,1)S(1)}, u32[]{:S(2)}, u32[]{:S(2)}) collective-permute-start(bf16[816,128]{1,0:T(8,128)(2,1)S(1)} %get-tuple-element.38), channel_id=1, source_target_pairs={{0,16},{1,2},{2,1},{3,4},{4,3},{5,6},{6,5},{7,8},{8,7},{9,10},{10,... | collective-permute-start | bytes 626696 | tf_op jit(solution)/shard_map/ppermute | solution.py:300
  17.6 0.1 collective-permute-start.5
  17.7 3.6 %shard_map.95 = (f32[7168,128]{1,0:T(8,128)S(1)}, bf16[816,128]{1,0:T(8,128)(2,1)S(1)}) custom-call(f32[7168,128]{1,0:T(8,128)S(1)} %get-tuple-element.39.cs, bf16[25,128,256]{2,1,0:T(8,128)(2,1)S(1)} %get-tuple-element.40.a_ref, bf16[128,56,128]{2,1,0:T(8,128)(2,1)S(1)} %get-tuple-element.37.refs_2_.vt_ref, f32[128,128]{1,0:T(8,128)S(1)} %get-tuple-element.32.wts_ref, ...), custom_call_target="tpu_custom_call" | custom-call | flops 312475648 | bytes 11092160 | tf_op jit(solution)/shard_map/pallas_call | solution.py:282
  21.2 0.1 collective-permute-start.4
  21.3 3.3 %collective-permute-done.5.refs_0_ = bf16[816,128]{1,0:T(8,128)(2,1)S(1)} collective-permute-done((bf16[816,128]{1,0:T(8,128)(2,1)S(1)}, bf16[816,128]{1,0:T(8,128)(2,1)S(1)}, u32[]{:S(2)}, u32[]{:S(2)}) %collective-permute-start.5) | collective-permute-done | bytes 208928 | tf_op jit(solution)/shard_map/ppermute | solution.py:305
  24.6 0.9 %shard_map.96.local_ref = f32[7168,128]{1,0:T(8,128)S(1)} custom-call(bf16[816,128]{1,0:T(8,128)(2,1)S(1)} %collective-permute-done.5.refs_0_, f32[7168,128]{1,0:T(8,128)S(1)} %get-tuple-element.43.refs_1_, bf16[128,56,128]{2,1,0:T(8,128)(2,1)S(1)} %get-tuple-element.37.refs_2_.vt_ref), custom_call_target="tpu_custom_call", output_to_operand_aliasing={{}: (1, {})} | custom-call | flops 12845056 | bytes 9383936 | tf_op jit(solution)/shard_map/pallas_call | solution.py:282
  25.5 0.0 collective-permute-done.3.r0
  25.5 0.0 collective-permute-done.4.r2
  25.5 2.3 %shard_map.97 = (bf16[50,128,128]{2,1,0:T(8,128)(2,1)}, f32[7168,128]{1,0:T(8,128)S(1)}) custom-call(bf16[816,128]{1,0:T(8,128)(2,1)S(1)} %collective-permute-done.3.r0, bf16[816,128]{1,0:T(8,128)(2,1)S(1)} %collective-permute-done.4.r2, f32[7168,128]{1,0:T(8,128)S(1)} %shard_map.96.local_ref, ...), custom_call_target="tpu_custom_call", output_to_operand_aliasing={{1}: (2, {})} | custom-call | bytes 11231232 | tf_op jit(solution)/shard_map/pallas_call | solution.py:282
Async XLA Ops:
  1.9 12.1 %collective-permute-start = (bf16[816,128]{1,0:T(8,128)(2,1)S(1)}, bf16[816,128]{1,0:T(8,128)(2,1)S(1)}, u32[]{:S(2)}, u32[]{:S(2)}) collective-permute-start(bf16[816,128]{1,0:T(8,128)(2,1)S(1)} %get-tuple-element.25), channel_id=1, source_target_pairs={{0,16},{1,2},{2,1},{3,4},{4,3},{5,6},{6,5},{7,8},{8,7},{9,10},{10,... | collective-permute-start | bytes 626696 | tf_op jit(solution)/shard_map/ppermute | solution.py:300
  4.9 8.3 %collective-permute-start.2 = (bf16[816,128]{1,0:T(8,128)(2,1)S(1)}, bf16[816,128]{1,0:T(8,128)(2,1)S(1)}, u32[]{:S(2)}, u32[]{:S(2)}) collective-permute-start(bf16[816,128]{1,0:T(8,128)(2,1)S(1)} %get-tuple-element.35), channel_id=1, source_target_pairs={{0,16},{16,0},{1,17},{17,1},{2,18},{18,2},{3,19},{19,3},{4,20},{20... | collective-permute-start | bytes 626696 | tf_op jit(solution)/shard_map/ppermute | solution.py:305
  9.7 4.3 %collective-permute-start.1 = (bf16[816,128]{1,0:T(8,128)(2,1)S(1)}, bf16[816,128]{1,0:T(8,128)(2,1)S(1)}, u32[]{:S(2)}, u32[]{:S(2)}) collective-permute-start(bf16[816,128]{1,0:T(8,128)(2,1)S(1)} %get-tuple-element.34), channel_id=1, source_target_pairs={{0,1},{1,0},{2,3},{3,2},{4,5},{5,4},{6,7},{7,6},{8,9},{9,8},{10,11... | collective-permute-start | bytes 626696 | tf_op jit(solution)/shard_map/ppermute | solution.py:300
  15.5 10.0 %collective-permute-start.3 = (bf16[816,128]{1,0:T(8,128)(2,1)S(1)}, bf16[816,128]{1,0:T(8,128)(2,1)S(1)}, u32[]{:S(2)}, u32[]{:S(2)}) collective-permute-start(bf16[816,128]{1,0:T(8,128)(2,1)S(1)} %get-tuple-element.38), channel_id=1, source_target_pairs={{0,16},{1,2},{2,1},{3,4},{4,3},{5,6},{6,5},{7,8},{8,7},{9,10},{10,... | collective-permute-start | bytes 626696 | tf_op jit(solution)/shard_map/ppermute | solution.py:300
  17.6 7.0 %collective-permute-start.5 = (bf16[816,128]{1,0:T(8,128)(2,1)S(1)}, bf16[816,128]{1,0:T(8,128)(2,1)S(1)}, u32[]{:S(2)}, u32[]{:S(2)}) collective-permute-start(bf16[816,128]{1,0:T(8,128)(2,1)S(1)} %get-tuple-element.42), channel_id=1, source_target_pairs={{0,16},{16,0},{1,17},{17,1},{2,18},{18,2},{3,19},{19,3},{4,20},{20... | collective-permute-start | bytes 626696 | tf_op jit(solution)/shard_map/ppermute | solution.py:305
  21.2 4.3 %collective-permute-start.4 = (bf16[816,128]{1,0:T(8,128)(2,1)S(1)}, bf16[816,128]{1,0:T(8,128)(2,1)S(1)}, u32[]{:S(2)}, u32[]{:S(2)}) collective-permute-start(bf16[816,128]{1,0:T(8,128)(2,1)S(1)} %get-tuple-element.41), channel_id=1, source_target_pairs={{0,1},{1,0},{2,3},{3,2},{4,5},{5,4},{6,7},{7,6},{8,9},{9,8},{10,11... | collective-permute-start | bytes 626696 | tf_op jit(solution)/shard_map/ppermute | solution.py:300

commit v10 on v9

--- a/solution.py
+++ b/solution.py
@@ -25,7 +25,7 @@
 
 
 def direction(slot, parity):
-    return 2 if slot == 1 else lax.bitwise_xor(parity, jnp.int32(1 - slot // 2))
+    return lax.bitwise_xor(parity, jnp.int32(2 - slot)) if slot else 2
 
 
 def has_partner(slot, at, count):
@@ -128,7 +128,7 @@
     for slot in range(3):
         d = direction(slot, parity)
         weight = edge_v[d]
-        if slot != 1:
+        if slot:
             weight = jnp.where(has_partner(slot, lax.axis_index(blk), lax.axis_size(blk)), weight, 0.0)
         wts[slot * nedge : (slot + 1) * nedge, 0:levels] = weight
         tbl_o[slot : slot + 1, 0:nedge] = recv_v[pl.ds(d, 1), :].astype(F32)
@@ -226,15 +226,10 @@
     vertical(vt_ref, exs, state_ref)
 
 
-def arrived_kernel(levels, nedge, *refs):
-    *edges, _, vt_ref, total, tbl_v, tbl_s, sem = refs
-    add_edges(edges, levels, nedge, vt_ref, total, tbl_v, tbl_s, sem)
-
-
-def send_kernel(blk, levels, r0, r2, local_ref, vt_ref, wts_ref, tbl_ref, send_h, state, s0, s1, tbl_v, tbl_s, send_s, sems):
+def send_kernel(blk, levels, r0, r1, r2, local_ref, vt_ref, wts_ref, tbl_ref, send_h, state, s0, s1, tbl_v, tbl_s, send_s, sems):
     copy = pltpu.make_async_copy(send_h, send_s, sems.at[1])
     copy.start()
-    add_edges((r0, r2), levels, send_h.shape[1], vt_ref, state, tbl_v, tbl_s, sems.at[0])
+    add_edges((r0, r1, r2), levels, send_h.shape[1], vt_ref, state, tbl_v, tbl_s, sems.at[0])
     copy.wait()
     pack_state(blk, levels, send_s, wts_ref, tbl_ref, state, vt_ref.shape[1], (0, 1), (s0, s1))
 
@@ -256,10 +251,10 @@
     vertical(vt_ref, exs, out_ref)
 
 
-def last_kernel(nedge, r0, r2, local_ref, vt_ref, out_h, total, out_v, tbl_v, tbl_s, sems):
+def last_kernel(nedge, r0, r1, r2, local_ref, vt_ref, out_h, total, out_v, tbl_v, tbl_s, sems):
     levels, cols, width = out_h.shape
     rows = vt_ref.shape[1]
-    add_edges((r0, r2), levels, nedge, vt_ref, total, tbl_v, tbl_s, sems.at[0])
+    add_edges((r0, r1, r2), levels, nedge, vt_ref, total, tbl_v, tbl_s, sems.at[0])
     count = 5
     edges = [levels * i // count for i in range(count + 1)]
     copies = []
@@ -336,19 +331,12 @@
         ],
         16,
     )
-    (to_odd, to_next), (state, nbr, nbr_w, self_w, wet), (wts, tbl, by_row) = first[:2], first[2:7], first[7:]
+    (to_next, to_odd), (state, nbr, nbr_w, self_w, wet), (wts, tbl, by_row) = first[:2], first[2:7], first[7:]
     operator_flops = 2 * levels * cols * cols * width
     vertical_flops = 2 * cols * rows * rows * width
 
-    def tables(count):
-        return [pltpu.VMEM((count, 8, 128), jnp.int32), pltpu.SMEM((count, 8, 128), jnp.int32)]
-
-    def arrived(partial, *messages):
-        return call(
-            functools.partial(arrived_kernel, levels, nedge), (*messages, partial, vt), [VM] * (len(messages) + 2),
-            [columns], [VM], tables(len(messages)) + [DMA], 16,
-            flops=len(messages) * nedge * 2 * rows * rows * width, aliases={len(messages): 0},
-        )[0]
+    edge_flops = 3 * nedge * 2 * rows * rows * width
+    tables = [pltpu.VMEM((3, 8, 128), jnp.int32), pltpu.SMEM((3, 8, 128), jnp.int32)]
 
     along = along_basin(to_next, "basin")
     odd = odd_or_even(to_odd, 1, "blk", "basin")
@@ -361,11 +349,11 @@
         32, flops=operator_flops + vertical_flops,
     )
     even = odd_or_even(to_even, 0, "blk", "basin")
-    state, to_odd, to_next = call(
+    state, to_next, to_odd = call(
         functools.partial(send_kernel, "blk", levels),
-        (odd, even, arrived(partial, along), vt, wts, tbl, send_h), [VM] * 6 + [HB],
+        (along, odd, even, partial, vt, wts, tbl, send_h), [VM] * 7 + [HB],
         [columns] + [message] * 2, [VM] * 3,
-        tables(2) + [send_table, DMA((2,))], 16, aliases={2: 0},
+        tables + [send_table, DMA((2,))], 16, flops=edge_flops, aliases={3: 0},
     )
     along = along_basin(to_next, "basin")
     odd = odd_or_even(to_odd, 1, "blk", "basin")
@@ -375,9 +363,9 @@
     )
     even = odd_or_even(to_even, 0, "blk", "basin")
     out, _ = call(
-        functools.partial(last_kernel, nedge), (odd, even, arrived(partial, along), vt), [VM] * 4,
+        functools.partial(last_kernel, nedge), (along, odd, even, partial, vt), [VM] * 5,
         [shape((levels, cols, width), BF16), columns], [HB, VM],
-        [pltpu.VMEM((levels, cols, width), BF16)] + tables(2) + [DMA((6,))], 16, aliases={2: 1},
+        [pltpu.VMEM((levels, cols, width), BF16)] + tables + [DMA((6,))], 16, flops=edge_flops, aliases={3: 1},
     )
     return jnp.transpose(out, (1, 0, 2))
 

time: 28 us -> 26.4 us (0.943)
  Pallas kernels: 15.7 us -> 14.3 us
  waiting for transfers between devices: 5.41 us -> 4.94 us
  starting transfers between devices: 6.65 us -> 7.04 us
    ppermute x2, starting transfers between devices: 0.16 us -> 4.69 us  [along_basin(): return lax.ppermute(value, basin, [(i, (i + 1) % b) for i in range(b)])]
    ppermute x4, starting transfers between devices: 6.5 us -> 2.34 us  [odd_or_even(): return lax.ppermute(value, (basin, blk), route)]
    ppermute x2, waiting for transfers between devices: 5.4 us -> 1.62 us  [along_basin(): return lax.ppermute(value, basin, [(i, (i + 1) % b) for i in range(b)])]
    ppermute x4, waiting for transfers between devices: 0.01 us -> 3.32 us  [odd_or_even(): return lax.ppermute(value, (basin, blk), route)]
    pallas_call x7 -> x5, Pallas kernels: 15.7 us -> 14.3 us  [call(): pl.pallas_call(kernel, out_shape=outs, in_specs=specs, out_specs=out_spec...]
  transfers between devices with their start and end apart: 6 -> 6, of which waited for: 2 -> 4; matrix products, arithmetic and copies ran while one was open for 0% -> 0% of each run, Pallas kernels for 36% -> 32%
where the time goes in v10:
time: 26.4 us; the launch traced here: 26.3 us
  Pallas kernels  14.3 us (54%)
  starting transfers between devices  7.04 us (27%)
  waiting for transfers between devices  4.94 us (19%)
    pallas_call x5, Pallas kernels, call(): pl.pallas_call(kernel, out_shape=outs, in_specs=specs, out_specs=out_spec...  14.3 us
    ppermute x2, starting transfers between devices, along_basin(): return lax.ppermute(value, basin, [(i, (i + 1) % b) for i in range(b)])  4.69 us
    ppermute x4, waiting for transfers between devices, odd_or_even(): return lax.ppermute(value, (basin, blk), route)  3.32 us
    ppermute x4, starting transfers between devices, odd_or_even(): return lax.ppermute(value, (basin, blk), route)  2.34 us
    ppermute x2, waiting for transfers between devices, along_basin(): return lax.ppermute(value, basin, [(i, (i + 1) % b) for i in range(b)])  1.62 us
  transfers between devices with their start and end apart: 6, of which 4 were waited for; matrix products, arithmetic and copies ran while one was open for 0% of the time, Pallas kernels for 32%

profile of v10, /device:TPU:0, one launch (start us, length us, event | category | flops | bytes accessed | tf_op | source)
XLA Modules:
  0.0 26.3 jit_solution(666626870048899195)
XLA Ops:
  0.0 1.8 %shard_map.91 = (bf16[816,128]{1,0:T(8,128)(2,1)S(1)}, bf16[816,128]{1,0:T(8,128)(2,1)S(1)}, bf16[50,128,128]{2,1,0:T(8,128)(2,1)S(1)}, s32[4,128]{1,0:T(4,128)S...) custom-call(bf16[50,128,128]{2,1,0:T(8,128)(2,1)} %bitcast.5, ...), custom_call_target="tpu_custom_call" | custom-call | bytes 7934720 | tf_op jit(solution)/shard_map/pallas_call | solution.py:277
  1.9 3.0 %collective-permute-start = (bf16[816,128]{1,0:T(8,128)(2,1)S(1)}, bf16[816,128]{1,0:T(8,128)(2,1)S(1)}, u32[]{:S(2)}, u32[]{:S(2)}) collective-permute-start(bf16[816,128]{1,0:T(8,128)(2,1)S(1)} %get-tuple-element.25), channel_id=1, source_target_pairs={{0,16},{16,0},{1,17},{17,1},{2,18},{18,2},{3,19},{19,3},{4,20},{20... | collective-permute-start | bytes 626696 | tf_op jit(solution)/shard_map/ppermute | solution.py:300
  4.9 0.1 collective-permute-start.1
  4.9 4.7 %shard_map.92 = (bf16[25,128,256]{2,1,0:T(8,128)(2,1)S(1)}, f32[7168,128]{1,0:T(8,128)S(1)}, bf16[128,56,128]{2,1,0:T(8,128)(2,1)S(1)}, bf16[816,128]{1,0:T(8,128)(2,1)S(1)}) custom-call(bf16[50,128,128]{2,1,0:T(8,128)(2,1)S(1)} %get-tuple-element.27.c_ref, s32[4,128]{1,0:T(4,128)S(1)} %get-tuple-element.28.nbr_ref, ...), custom_call_target="tpu_custom_call" | custom-call | flops 312475648 | bytes 13730496 | tf_op jit(solution)/shard_map/pallas_call | solution.py:277
  9.7 1.6 %collective-permute-start.2 = (bf16[816,128]{1,0:T(8,128)(2,1)S(1)}, bf16[816,128]{1,0:T(8,128)(2,1)S(1)}, u32[]{:S(2)}, u32[]{:S(2)}) collective-permute-start(bf16[816,128]{1,0:T(8,128)(2,1)S(1)} %get-tuple-element.35), channel_id=1, source_target_pairs={{0,1},{1,0},{2,3},{3,2},{4,5},{5,4},{6,7},{7,6},{8,9},{9,8},{10,11... | collective-permute-start | bytes 626696 | tf_op jit(solution)/shard_map/ppermute | solution.py:295
  11.3 0.0 collective-permute-done.r0
  11.3 1.0 %collective-permute-done.1.r1 = bf16[816,128]{1,0:T(8,128)(2,1)S(1)} collective-permute-done((bf16[816,128]{1,0:T(8,128)(2,1)S(1)}, bf16[816,128]{1,0:T(8,128)(2,1)S(1)}, u32[]{:S(2)}, u32[]{:S(2)}) %collective-permute-start.1) | collective-permute-done | bytes 208928 | tf_op jit(solution)/shard_map/ppermute | solution.py:295
  12.3 0.1 collective-permute-done.2.r2
  12.4 1.6 %shard_map.93 = (f32[7168,128]{1,0:T(8,128)S(1)}, bf16[816,128]{1,0:T(8,128)(2,1)S(1)}, bf16[816,128]{1,0:T(8,128)(2,1)S(1)}) custom-call(bf16[816,128]{1,0:T(8,128)(2,1)S(1)} %collective-permute-done.r0, bf16[816,128]{1,0:T(8,128)(2,1)S(1)} %collective-permute-done.1.r1, ...), custom_call_target="tpu_custom_call", output_to_operand_aliasing={{0}: (3, {})} | custom-call | flops 38535168 | bytes 10289344 | tf_op jit(solution)/shard_map/pallas_call | solution.py:277
  14.0 1.7 %collective-permute-start.3 = (bf16[816,128]{1,0:T(8,128)(2,1)S(1)}, bf16[816,128]{1,0:T(8,128)(2,1)S(1)}, u32[]{:S(2)}, u32[]{:S(2)}) collective-permute-start(bf16[816,128]{1,0:T(8,128)(2,1)S(1)} %get-tuple-element.38), channel_id=1, source_target_pairs={{0,16},{16,0},{1,17},{17,1},{2,18},{18,2},{3,19},{19,3},{4,20},{20... | collective-permute-start | bytes 626696 | tf_op jit(solution)/shard_map/ppermute | solution.py:300
  15.7 0.4 %collective-permute-start.4 = (bf16[816,128]{1,0:T(8,128)(2,1)S(1)}, bf16[816,128]{1,0:T(8,128)(2,1)S(1)}, u32[]{:S(2)}, u32[]{:S(2)}) collective-permute-start(bf16[816,128]{1,0:T(8,128)(2,1)S(1)} %get-tuple-element.39), channel_id=1, source_target_pairs={{0,16},{1,2},{2,1},{3,4},{4,3},{5,6},{6,5},{7,8},{8,7},{9,10},{10,... | collective-permute-start | bytes 626696 | tf_op jit(solution)/shard_map/ppermute | solution.py:295
  16.2 3.6 %shard_map.94 = (f32[7168,128]{1,0:T(8,128)S(1)}, bf16[816,128]{1,0:T(8,128)(2,1)S(1)}) custom-call(f32[7168,128]{1,0:T(8,128)S(1)} %get-tuple-element.40.cs, bf16[25,128,256]{2,1,0:T(8,128)(2,1)S(1)} %get-tuple-element.41.a_ref, bf16[128,56,128]{2,1,0:T(8,128)(2,1)S(1)} %get-tuple-element.37.vt_ref, f32[128,128]{1,0:T(8,128)S(1)} %get-tuple-element.33.wts_ref, ...), custom_call_target="tpu_custom_call" | custom-call | flops 312475648 | bytes 11092160 | tf_op jit(solution)/shard_map/pallas_call | solution.py:277
  19.7 0.2 collective-permute-start.5
  19.9 1.6 %collective-permute-done.3.r0 = bf16[816,128]{1,0:T(8,128)(2,1)S(1)} collective-permute-done((bf16[816,128]{1,0:T(8,128)(2,1)S(1)}, bf16[816,128]{1,0:T(8,128)(2,1)S(1)}, u32[]{:S(2)}, u32[]{:S(2)}) %collective-permute-start.3) | collective-permute-done | bytes 208928 | tf_op jit(solution)/shard_map/ppermute | solution.py:300
  21.6 2.2 %collective-permute-done.4.r1 = bf16[816,128]{1,0:T(8,128)(2,1)S(1)} collective-permute-done((bf16[816,128]{1,0:T(8,128)(2,1)S(1)}, bf16[816,128]{1,0:T(8,128)(2,1)S(1)}, u32[]{:S(2)}, u32[]{:S(2)}) %collective-permute-start.4) | collective-permute-done | bytes 208928 | tf_op jit(solution)/shard_map/ppermute | solution.py:295
  23.8 0.0 collective-permute-done.5.r2
  23.8 2.5 %shard_map.95 = (bf16[50,128,128]{2,1,0:T(8,128)(2,1)}, f32[7168,128]{1,0:T(8,128)S(1)}) custom-call(bf16[816,128]{1,0:T(8,128)(2,1)S(1)} %collective-permute-done.3.r0, bf16[816,128]{1,0:T(8,128)(2,1)S(1)} %collective-permute-done.4.r1, bf16[816,128]{1,0:T(8,128)(2,1)S(1)} %collective-permute-done.5.r2, ...), custom_call_target="tpu_custom_call", output_to_operand_aliasing={{1}: (3, {})} | custom-call | flops 38535168 | bytes 11440128 | tf_op jit(solution)/shard_map/pallas_call | solution.py:277
Async XLA Ops:
  1.9 9.5 %collective-permute-start = (bf16[816,128]{1,0:T(8,128)(2,1)S(1)}, bf16[816,128]{1,0:T(8,128)(2,1)S(1)}, u32[]{:S(2)}, u32[]{:S(2)}) collective-permute-start(bf16[816,128]{1,0:T(8,128)(2,1)S(1)} %get-tuple-element.25), channel_id=1, source_target_pairs={{0,16},{16,0},{1,17},{17,1},{2,18},{18,2},{3,19},{19,3},{4,20},{20... | collective-permute-start | bytes 626696 | tf_op jit(solution)/shard_map/ppermute | solution.py:300
  4.9 7.4 %collective-permute-start.1 = (bf16[816,128]{1,0:T(8,128)(2,1)S(1)}, bf16[816,128]{1,0:T(8,128)(2,1)S(1)}, u32[]{:S(2)}, u32[]{:S(2)}) collective-permute-start(bf16[816,128]{1,0:T(8,128)(2,1)S(1)} %get-tuple-element.26), channel_id=1, source_target_pairs={{0,16},{1,2},{2,1},{3,4},{4,3},{5,6},{6,5},{7,8},{8,7},{9,10},{10,... | collective-permute-start | bytes 626696 | tf_op jit(solution)/shard_map/ppermute | solution.py:295
  9.7 2.7 %collective-permute-start.2 = (bf16[816,128]{1,0:T(8,128)(2,1)S(1)}, bf16[816,128]{1,0:T(8,128)(2,1)S(1)}, u32[]{:S(2)}, u32[]{:S(2)}) collective-permute-start(bf16[816,128]{1,0:T(8,128)(2,1)S(1)} %get-tuple-element.35), channel_id=1, source_target_pairs={{0,1},{1,0},{2,3},{3,2},{4,5},{5,4},{6,7},{7,6},{8,9},{9,8},{10,11... | collective-permute-start | bytes 626696 | tf_op jit(solution)/shard_map/ppermute | solution.py:295
  14.0 7.5 %collective-permute-start.3 = (bf16[816,128]{1,0:T(8,128)(2,1)S(1)}, bf16[816,128]{1,0:T(8,128)(2,1)S(1)}, u32[]{:S(2)}, u32[]{:S(2)}) collective-permute-start(bf16[816,128]{1,0:T(8,128)(2,1)S(1)} %get-tuple-element.38), channel_id=1, source_target_pairs={{0,16},{16,0},{1,17},{17,1},{2,18},{18,2},{3,19},{19,3},{4,20},{20... | collective-permute-start | bytes 626696 | tf_op jit(solution)/shard_map/ppermute | solution.py:300
  15.7 8.1 %collective-permute-start.4 = (bf16[816,128]{1,0:T(8,128)(2,1)S(1)}, bf16[816,128]{1,0:T(8,128)(2,1)S(1)}, u32[]{:S(2)}, u32[]{:S(2)}) collective-permute-start(bf16[816,128]{1,0:T(8,128)(2,1)S(1)} %get-tuple-element.39), channel_id=1, source_target_pairs={{0,16},{1,2},{2,1},{3,4},{4,3},{5,6},{6,5},{7,8},{8,7},{9,10},{10,... | collective-permute-start | bytes 626696 | tf_op jit(solution)/shard_map/ppermute | solution.py:295
  19.7 4.1 %collective-permute-start.5 = (bf16[816,128]{1,0:T(8,128)(2,1)S(1)}, bf16[816,128]{1,0:T(8,128)(2,1)S(1)}, u32[]{:S(2)}, u32[]{:S(2)}) collective-permute-start(bf16[816,128]{1,0:T(8,128)(2,1)S(1)} %get-tuple-element.42), channel_id=1, source_target_pairs={{0,1},{1,0},{2,3},{3,2},{4,5},{5,4},{6,7},{7,6},{8,9},{9,8},{10,11... | collective-permute-start | bytes 626696 | tf_op jit(solution)/shard_map/ppermute | solution.py:295

commit v11 on v10

--- a/solution.py
+++ b/solution.py
@@ -107,8 +107,8 @@
 
 def gather_kernel(
     blk, c_h, send_h, recv_h, edge_h, nbr_h, nw_h, sw_h, wet_h,
-    s0, s1, c_v, nbr_v, nw_v, sw_v, wet_v, wts_o, tbl_o, cf,
-    wts, recv_v, edge_v, send_s, sems,
+    s0, s1, s2, c_v, nbr_v, nw_v, sw_v, wet_v, wts_o, tbl_o,
+    cf, wts, recv_v, edge_v, send_s, sems,
 ):
     levels, cols, width = c_h.shape
     nedge = edge_h.shape[1]
@@ -139,9 +139,9 @@
         copies[3 + i].wait()
         for l in range(lo, hi):
             cf[l * pitch : l * pitch + cols, :] = c_v[l].astype(F32)
-        pack_chunk(parity, lo, levels, send_s, weights, tbl_o, rows_of, (0, 1), (s0, s1))
+        pack_chunk(parity, lo, levels, send_s, weights, tbl_o, rows_of, (0, 1, 2), (s0, s1, s2))
     if levels % 16 == 0:
-        pack_chunk(parity, levels, levels, send_s, weights, tbl_o, rows_of, (0, 1), (s0, s1))
+        pack_chunk(parity, levels, levels, send_s, weights, tbl_o, rows_of, (0, 1, 2), (s0, s1, s2))
     for copy in copies[3 + len(bounds) :]:
         copy.wait()
 
@@ -194,22 +194,13 @@
 
 
 def operator_kernel(
-    blk, c_ref, nbr_ref, nw_ref, sw_ref, wet_ref, cf, wts_ref, tbl_ref, send_h, v_h,
-    a_ref, state_ref, vt_ref, s2, exs, merged, vf, vts, v_ref, send_s, sems,
+    c_ref, nbr_ref, nw_ref, sw_ref, wet_ref, v_h, a_ref, state_ref, vt_ref, exs, merged, vf, vts, v_ref, sem
 ):
     levels, cols, width = c_ref.shape
     rows = padded(levels)
-    load = pltpu.make_async_copy(v_h, v_ref, sems.at[0])
+    load = pltpu.make_async_copy(v_h, v_ref, sem)
     load.start()
-    copy = pltpu.make_async_copy(send_h, send_s, sems.at[1])
-    copy.start()
     column_operator(nbr_ref, nw_ref, sw_ref, a_ref, merged)
-    copy.wait()
-    parity = lax.bitwise_and(lax.axis_index(blk), jnp.int32(1))
-    pitch = cols + 8
-    rows_of = lambda s, lo, n: cf[pl.ds(lo * pitch + s, n, stride=pitch), :]
-    for lo in range(0, levels + 1, 16):
-        pack_chunk(parity, lo, levels, send_s, wts_ref, tbl_ref, rows_of, (2,), (s2,))
     level_products(a_ref, lambda l: c_ref[l], exs, rows)
     level = lax.broadcasted_iota(jnp.int32, (levels, cols), 0)
     wet = wet_ref[...]
@@ -255,10 +246,9 @@
     levels, cols, width = out_h.shape
     rows = vt_ref.shape[1]
     add_edges((r0, r1, r2), levels, nedge, vt_ref, total, tbl_v, tbl_s, sems.at[0])
-    count = 5
-    edges = [levels * i // count for i in range(count + 1)]
+    bounds = [0, *range(4, levels, 8), levels]
     copies = []
-    for i, (lo, hi) in enumerate(zip(edges, edges[1:])):
+    for i, (lo, hi) in enumerate(zip(bounds, bounds[1:])):
         for l in range(lo, hi):
             out_v[l] = total[pl.ds(l, cols, stride=rows), :].astype(BF16)
         copies.append(pltpu.make_async_copy(out_v.at[pl.ds(lo, hi - lo)], out_h.at[pl.ds(lo, hi - lo)], sems.at[1 + i]))
@@ -286,13 +276,12 @@
     )(*ins)
 
 
-def odd_or_even(value, first, blk, basin):
-    n, b = lax.axis_size(blk), lax.axis_size(basin)
-    partner = {i: i + 1 for i in range(first, n - 1, 2)}
+def odd_or_even(value, first, blk):
+    n = lax.axis_size(blk)
+    order = [(i + first) % n for i in range(n)]
+    partner = {order[i]: order[i + 1] for i in range(0, n - 1, 2)}
     partner |= {j: i for i, j in partner.items()}
-    across = lambda g: g ^ 1 if g ^ 1 < b else g
-    route = [(g * n + i, g * n + partner[i] if i in partner else across(g) * n + i) for g in range(b) for i in range(n)]
-    return lax.ppermute(value, (basin, blk), route)
+    return lax.ppermute(value, blk, [(i, partner.get(i, i)) for i in range(n)])
 
 
 def along_basin(value, basin):
@@ -322,16 +311,16 @@
         functools.partial(gather_kernel, "blk"),
         (in_hbm(by_level), send_h, *map(in_hbm, (recv_cols, edge_by_entry, *loads[1:]))),
         [HB] * 8,
-        [message] * 2 + [same(x) for x in loads]
-        + [shape((128, 128), F32), shape((8, 128), F32), shape((rows * (cols + 8), width), F32)],
+        [message] * 3 + [same(x) for x in loads] + [shape((128, 128), F32), shape((8, 128), F32)],
         [VM] * 10,
         [
+            pltpu.VMEM((rows * (cols + 8), width), F32),
             pltpu.VMEM((128, 128), F32), pltpu.VMEM(recv_cols.shape, jnp.int32), pltpu.VMEM(edge_by_entry.shape, F32),
             send_table, DMA((7 + -(-levels // 16),)),
         ],
         16,
     )
-    (to_next, to_odd), (state, nbr, nbr_w, self_w, wet), (wts, tbl, by_row) = first[:2], first[2:7], first[7:]
+    (to_next, to_odd, to_even), loads, (wts, tbl) = first[:3], first[3:8], first[8:]
     operator_flops = 2 * levels * cols * cols * width
     vertical_flops = 2 * cols * rows * rows * width
 
@@ -339,16 +328,15 @@
     tables = [pltpu.VMEM((3, 8, 128), jnp.int32), pltpu.SMEM((3, 8, 128), jnp.int32)]
 
     along = along_basin(to_next, "basin")
-    odd = odd_or_even(to_odd, 1, "blk", "basin")
-    operator, partial, vt, to_even = call(
-        functools.partial(operator_kernel, "blk"),
-        (state, nbr, nbr_w, self_w, wet, by_row, wts, tbl, send_h, in_hbm(vert_inv)), [VM] * 8 + [HB] * 2,
-        [shape((levels // 2, cols, 2 * cols), BF16), columns, shape((cols, rows, 128), BF16), message], [VM] * 4,
+    odd = odd_or_even(to_odd, 1, "blk")
+    even = odd_or_even(to_even, 0, "blk")
+    operator, partial, vt = call(
+        operator_kernel, (*loads, in_hbm(vert_inv)), [VM] * 5 + [HB],
+        [shape((levels // 2, cols, 2 * cols), BF16), columns, shape((cols, rows, 128), BF16)], [VM] * 3,
         [flat, pltpu.VMEM((levels, 8, cols), F32), pltpu.VMEM((rows * rows, cols), F32), pltpu.VMEM((cols * rows, 128), F32),
-         pltpu.VMEM(vert_inv.shape, BF16), send_table, DMA((2,))],
+         pltpu.VMEM(vert_inv.shape, BF16), DMA],
         32, flops=operator_flops + vertical_flops,
     )
-    even = odd_or_even(to_even, 0, "blk", "basin")
     state, to_next, to_odd = call(
         functools.partial(send_kernel, "blk", levels),
         (along, odd, even, partial, vt, wts, tbl, send_h), [VM] * 7 + [HB],
@@ -356,16 +344,16 @@
         tables + [send_table, DMA((2,))], 16, flops=edge_flops, aliases={3: 0},
     )
     along = along_basin(to_next, "basin")
-    odd = odd_or_even(to_odd, 1, "blk", "basin")
+    odd = odd_or_even(to_odd, 1, "blk")
     partial, to_even = call(
         functools.partial(middle_kernel, "blk", levels), (state, operator, vt, wts, tbl, send_h), [VM] * 5 + [HB],
         [columns, message], [VM] * 2, [flat, send_table, DMA], 32, flops=operator_flops + vertical_flops,
     )
-    even = odd_or_even(to_even, 0, "blk", "basin")
+    even = odd_or_even(to_even, 0, "blk")
     out, _ = call(
         functools.partial(last_kernel, nedge), (along, odd, even, partial, vt), [VM] * 5,
         [shape((levels, cols, width), BF16), columns], [HB, VM],
-        [pltpu.VMEM((levels, cols, width), BF16)] + tables + [DMA((6,))], 16, flops=edge_flops, aliases={3: 1},
+        [pltpu.VMEM((levels, cols, width), BF16)] + tables + [DMA((2 + -(-levels // 8),))], 16, flops=edge_flops, aliases={3: 1},
     )
     return jnp.transpose(out, (1, 0, 2))
 

time: 26.4 us -> 26.4 us (level)
  waiting for transfers between devices: 4.94 us -> 1.45 us
  starting transfers between devices: 7.04 us -> 10.4 us
    ppermute x4, starting transfers between devices: 2.34 us -> 6.78 us  [odd_or_even(): return lax.ppermute(value, blk, [(i, partner.get(i, i)) for i in range(n)])]
    ppermute x4, waiting for transfers between devices: 3.32 us -> 1.03 us  [odd_or_even(): return lax.ppermute(value, blk, [(i, partner.get(i, i)) for i in range(n)])]
    ppermute x2, waiting for transfers between devices: 1.62 us -> 0.43 us  [along_basin(): return lax.ppermute(value, basin, [(i, (i + 1) % b) for i in range(b)])]
    ppermute x2, starting transfers between devices: 4.69 us -> 3.6 us  [along_basin(): return lax.ppermute(value, basin, [(i, (i + 1) % b) for i in range(b)])]
  transfers between devices with their start and end apart: 6 -> 6, of which waited for: 4 -> 3; matrix products, arithmetic and copies ran while one was open for 0% -> 0% of each run, Pallas kernels for 32% -> 31%
where the time goes in v11:
time: 26.4 us; the launch traced here: 26.2 us
  Pallas kernels  14.3 us (54%)
  starting transfers between devices  10.4 us (39%)
  waiting for transfers between devices  1.45 us (5%)
    pallas_call x5, Pallas kernels, call(): pl.pallas_call(kernel, out_shape=outs, in_specs=specs, out_specs=out_spec...  14.3 us
    ppermute x4, starting transfers between devices, odd_or_even(): return lax.ppermute(value, blk, [(i, partner.get(i, i)) for i in range(n)])  6.78 us
    ppermute x2, starting transfers between devices, along_basin(): return lax.ppermute(value, basin, [(i, (i + 1) % b) for i in range(b)])  3.6 us
    ppermute x4, waiting for transfers between devices, odd_or_even(): return lax.ppermute(value, blk, [(i, partner.get(i, i)) for i in range(n)])  1.03 us
  transfers between devices with their start and end apart: 6, of which 3 were waited for; matrix products, arithmetic and copies ran while one was open for 0% of the time, Pallas kernels for 31%

profile of v11, /device:TPU:0, one launch (start us, length us, event | category | flops | bytes accessed | tf_op | source)
XLA Modules:
  0.0 26.2 jit_solution(7569074830643080757)
XLA Ops:
  0.0 2.0 %shard_map.91 = (bf16[816,128]{1,0:T(8,128)(2,1)S(1)}, bf16[816,128]{1,0:T(8,128)(2,1)S(1)}, bf16[816,128]{1,0:T(8,128)(2,1)S(1)}, bf16[50,128,128]{2,1,0:T(8,12...) custom-call(bf16[50,128,128]{2,1,0:T(8,128)(2,1)} %bitcast.5, ...), custom_call_target="tpu_custom_call" | custom-call | bytes 4244224 | tf_op jit(solution)/shard_map/pallas_call | solution.py:267
  2.1 3.0 %collective-permute-start = (bf16[816,128]{1,0:T(8,128)(2,1)S(1)}, bf16[816,128]{1,0:T(8,128)(2,1)S(1)}, u32[]{:S(2)}, u32[]{:S(2)}) collective-permute-start(bf16[816,128]{1,0:T(8,128)(2,1)S(1)} %get-tuple-element.24), channel_id=1, source_target_pairs={{0,16},{16,0},{1,17},{17,1},{2,18},{18,2},{3,19},{19,3},{4,20},{20... | collective-permute-start | bytes 626696 | tf_op jit(solution)/shard_map/ppermute | solution.py:289
  5.1 3.7 %collective-permute-start.1 = (bf16[816,128]{1,0:T(8,128)(2,1)S(1)}, bf16[816,128]{1,0:T(8,128)(2,1)S(1)}, u32[]{:S(2)}, u32[]{:S(2)}) collective-permute-start(bf16[816,128]{1,0:T(8,128)(2,1)S(1)} %get-tuple-element.25), channel_id=1, source_target_pairs={{0,15},{1,2},{2,1},{3,4},{4,3},{5,6},{6,5},{7,8},{8,7},{9,10},{10,... | collective-permute-start | bytes 626696 | tf_op jit(solution)/shard_map/ppermute | solution.py:284
  8.8 0.0 collective-permute-start.2
  8.8 4.6 %shard_map.92 = (bf16[25,128,256]{2,1,0:T(8,128)(2,1)S(1)}, f32[7168,128]{1,0:T(8,128)S(1)}, bf16[128,56,128]{2,1,0:T(8,128)(2,1)S(1)}) custom-call(bf16[50,128,128]{2,1,0:T(8,128)(2,1)S(1)} %get-tuple-element.27.c_ref, s32[4,128]{1,0:T(4,128)S(1)} %get-tuple-element.28.nbr_ref, f32[50,4,128]{2,1,0:T(4,128)S(1)} %get-tuple-element.29.nw_ref, ...), custom_call_target="tpu_custom_call" | custom-call | flops 312475648 | bytes 9552384 | tf_op jit(solution)/shard_map/pallas_call | solution.py:267
  13.4 0.0 collective-permute-done.r0
  13.4 0.0 collective-permute-done.1.r1
  13.4 0.0 collective-permute-done.2.r2
  13.4 1.7 %shard_map.93 = (f32[7168,128]{1,0:T(8,128)S(1)}, bf16[816,128]{1,0:T(8,128)(2,1)S(1)}, bf16[816,128]{1,0:T(8,128)(2,1)S(1)}) custom-call(bf16[816,128]{1,0:T(8,128)(2,1)S(1)} %collective-permute-done.r0, bf16[816,128]{1,0:T(8,128)(2,1)S(1)} %collective-permute-done.1.r1, ...), custom_call_target="tpu_custom_call", output_to_operand_aliasing={{0}: (3, {})} | custom-call | flops 38535168 | bytes 10289344 | tf_op jit(solution)/shard_map/pallas_call | solution.py:267
  15.1 0.6 %collective-permute-start.3 = (bf16[816,128]{1,0:T(8,128)(2,1)S(1)}, bf16[816,128]{1,0:T(8,128)(2,1)S(1)}, u32[]{:S(2)}, u32[]{:S(2)}) collective-permute-start(bf16[816,128]{1,0:T(8,128)(2,1)S(1)} %get-tuple-element.36), channel_id=1, source_target_pairs={{0,16},{16,0},{1,17},{17,1},{2,18},{18,2},{3,19},{19,3},{4,20},{20... | collective-permute-start | bytes 626696 | tf_op jit(solution)/shard_map/ppermute | solution.py:289
  15.7 3.0 %collective-permute-start.4 = (bf16[816,128]{1,0:T(8,128)(2,1)S(1)}, bf16[816,128]{1,0:T(8,128)(2,1)S(1)}, u32[]{:S(2)}, u32[]{:S(2)}) collective-permute-start(bf16[816,128]{1,0:T(8,128)(2,1)S(1)} %get-tuple-element.37), channel_id=1, source_target_pairs={{0,15},{1,2},{2,1},{3,4},{4,3},{5,6},{6,5},{7,8},{8,7},{9,10},{10,... | collective-permute-start | bytes 626696 | tf_op jit(solution)/shard_map/ppermute | solution.py:284
  18.7 3.5 %shard_map.94 = (f32[7168,128]{1,0:T(8,128)S(1)}, bf16[816,128]{1,0:T(8,128)(2,1)S(1)}) custom-call(f32[7168,128]{1,0:T(8,128)S(1)} %get-tuple-element.38.cs, bf16[25,128,256]{2,1,0:T(8,128)(2,1)S(1)} %get-tuple-element.39.a_ref, bf16[128,56,128]{2,1,0:T(8,128)(2,1)S(1)} %get-tuple-element.33.vt_ref, f32[128,128]{1,0:T(8,128)S(1)} %get-tuple-element.34.wts_ref, ...), custom_call_target="tpu_custom_call" | custom-call | flops 312475648 | bytes 11092160 | tf_op jit(solution)/shard_map/pallas_call | solution.py:267
  22.2 0.1 collective-permute-start.5
  22.3 0.4 %collective-permute-done.3.r0 = bf16[816,128]{1,0:T(8,128)(2,1)S(1)} collective-permute-done((bf16[816,128]{1,0:T(8,128)(2,1)S(1)}, bf16[816,128]{1,0:T(8,128)(2,1)S(1)}, u32[]{:S(2)}, u32[]{:S(2)}) %collective-permute-start.3) | collective-permute-done | bytes 208928 | tf_op jit(solution)/shard_map/ppermute | solution.py:289
  22.7 0.9 %collective-permute-done.4.r1 = bf16[816,128]{1,0:T(8,128)(2,1)S(1)} collective-permute-done((bf16[816,128]{1,0:T(8,128)(2,1)S(1)}, bf16[816,128]{1,0:T(8,128)(2,1)S(1)}, u32[]{:S(2)}, u32[]{:S(2)}) %collective-permute-start.4) | collective-permute-done | bytes 208928 | tf_op jit(solution)/shard_map/ppermute | solution.py:284
  23.6 0.1 collective-permute-done.5.r2
  23.8 2.5 %shard_map.95 = (bf16[50,128,128]{2,1,0:T(8,128)(2,1)}, f32[7168,128]{1,0:T(8,128)S(1)}) custom-call(bf16[816,128]{1,0:T(8,128)(2,1)S(1)} %collective-permute-done.3.r0, bf16[816,128]{1,0:T(8,128)(2,1)S(1)} %collective-permute-done.4.r1, bf16[816,128]{1,0:T(8,128)(2,1)S(1)} %collective-permute-done.5.r2, ...), custom_call_target="tpu_custom_call", output_to_operand_aliasing={{1}: (3, {})} | custom-call | flops 38535168 | bytes 11440128 | tf_op jit(solution)/shard_map/pallas_call | solution.py:267
Async XLA Ops:
  2.1 11.3 %collective-permute-start = (bf16[816,128]{1,0:T(8,128)(2,1)S(1)}, bf16[816,128]{1,0:T(8,128)(2,1)S(1)}, u32[]{:S(2)}, u32[]{:S(2)}) collective-permute-start(bf16[816,128]{1,0:T(8,128)(2,1)S(1)} %get-tuple-element.24), channel_id=1, source_target_pairs={{0,16},{16,0},{1,17},{17,1},{2,18},{18,2},{3,19},{19,3},{4,20},{20... | collective-permute-start | bytes 626696 | tf_op jit(solution)/shard_map/ppermute | solution.py:289
  5.1 8.4 %collective-permute-start.1 = (bf16[816,128]{1,0:T(8,128)(2,1)S(1)}, bf16[816,128]{1,0:T(8,128)(2,1)S(1)}, u32[]{:S(2)}, u32[]{:S(2)}) collective-permute-start(bf16[816,128]{1,0:T(8,128)(2,1)S(1)} %get-tuple-element.25), channel_id=1, source_target_pairs={{0,15},{1,2},{2,1},{3,4},{4,3},{5,6},{6,5},{7,8},{8,7},{9,10},{10,... | collective-permute-start | bytes 626696 | tf_op jit(solution)/shard_map/ppermute | solution.py:284
  8.8 4.6 %collective-permute-start.2 = (bf16[816,128]{1,0:T(8,128)(2,1)S(1)}, bf16[816,128]{1,0:T(8,128)(2,1)S(1)}, u32[]{:S(2)}, u32[]{:S(2)}) collective-permute-start(bf16[816,128]{1,0:T(8,128)(2,1)S(1)} %get-tuple-element.26), channel_id=1, source_target_pairs={{0,1},{1,0},{2,3},{3,2},{4,5},{5,4},{6,7},{7,6},{8,9},{9,8},{10,11... | collective-permute-start | bytes 626696 | tf_op jit(solution)/shard_map/ppermute | solution.py:284
  15.1 7.6 %collective-permute-start.3 = (bf16[816,128]{1,0:T(8,128)(2,1)S(1)}, bf16[816,128]{1,0:T(8,128)(2,1)S(1)}, u32[]{:S(2)}, u32[]{:S(2)}) collective-permute-start(bf16[816,128]{1,0:T(8,128)(2,1)S(1)} %get-tuple-element.36), channel_id=1, source_target_pairs={{0,16},{16,0},{1,17},{17,1},{2,18},{18,2},{3,19},{19,3},{4,20},{20... | collective-permute-start | bytes 626696 | tf_op jit(solution)/shard_map/ppermute | solution.py:289
  15.7 7.9 %collective-permute-start.4 = (bf16[816,128]{1,0:T(8,128)(2,1)S(1)}, bf16[816,128]{1,0:T(8,128)(2,1)S(1)}, u32[]{:S(2)}, u32[]{:S(2)}) collective-permute-start(bf16[816,128]{1,0:T(8,128)(2,1)S(1)} %get-tuple-element.37), channel_id=1, source_target_pairs={{0,15},{1,2},{2,1},{3,4},{4,3},{5,6},{6,5},{7,8},{8,7},{9,10},{10,... | collective-permute-start | bytes 626696 | tf_op jit(solution)/shard_map/ppermute | solution.py:284
  22.2 1.5 %collective-permute-start.5 = (bf16[816,128]{1,0:T(8,128)(2,1)S(1)}, bf16[816,128]{1,0:T(8,128)(2,1)S(1)}, u32[]{:S(2)}, u32[]{:S(2)}) collective-permute-start(bf16[816,128]{1,0:T(8,128)(2,1)S(1)} %get-tuple-element.40), channel_id=1, source_target_pairs={{0,1},{1,0},{2,3},{3,2},{4,5},{5,4},{6,7},{7,6},{8,9},{9,8},{10,11... | collective-permute-start | bytes 626696 | tf_op jit(solution)/shard_map/ppermute | solution.py:284

commit v12 on v11

--- a/solution.py
+++ b/solution.py
@@ -33,7 +33,7 @@
     return jnp.where(first, at + 1 < count, at > 0)
 
 
-def pack_chunk(parity, lo, levels, send, weights, tbl, rows_of, slots, outs):
+def pack_chunk(parity, lo, levels, send, weights, rows_of, slots, outs):
     whole = whole_rows(levels)
     nedge = send.shape[1]
     rest = levels - whole
@@ -58,7 +58,7 @@
                 part = value if part is None else jnp.where(sub >= q * rest, value, part)
             if share:
                 parts.append(part)
-        table = jnp.broadcast_to(tbl[slot : slot + 1, :], (16, out.shape[1]))
+        table = jnp.broadcast_to(weights[0:16, 3 * nedge + slot : 3 * nedge + slot + 1], (16, out.shape[1]))
         out[nedge * whole :, :] = jnp.concatenate(parts + [table], axis=0).astype(BF16)
 
 
@@ -75,22 +75,18 @@
     lax.fori_loop(0, cols, column, 0, unroll=16)
 
 
-def add_edges(edges, levels, nedge, vt_ref, total, tbl_v, tbl_s, sem):
+def add_edges(edges, levels, nedge, vt_ref, total):
     whole = whole_rows(levels)
     rest = levels - whole
     share = 8 // rest if rest else 0
     rows = vt_ref.shape[1]
-    for i, ref in enumerate(edges):
-        tbl_v[i] = ref[levels * nedge :, :].astype(F32)[0:8].astype(jnp.int32)
-    copy = pltpu.make_async_copy(tbl_v, tbl_s, sem)
-    copy.start()
-    copy.wait()
     group = max(share, 4)
     pad = jnp.zeros((8, total.shape[1]), F32)
-    for i, ref in enumerate(edges):
+    for ref in edges:
+        table = ref[levels * nedge :, :].astype(F32).astype(jnp.int32)
         tails = ref[whole * nedge : levels * nedge, :].astype(F32) if rest else None
         for first in range(0, nedge, group):
-            targets = [tbl_s[i, 0, e] for e in range(first, first + group)]
+            targets = [table[e, 0] for e in range(first, first + group)]
             products = []
             for e, j in zip(range(first, first + group), targets):
                 x = ref[e * whole : (e + 1) * whole, :]
@@ -107,7 +103,7 @@
 
 def gather_kernel(
     blk, c_h, send_h, recv_h, edge_h, nbr_h, nw_h, sw_h, wet_h,
-    s0, s1, s2, c_v, nbr_v, nw_v, sw_v, wet_v, wts_o, tbl_o,
+    s0, s1, s2, c_v, nbr_v, nw_v, sw_v, wet_v, wts_o,
     cf, wts, recv_v, edge_v, send_s, sems,
 ):
     levels, cols, width = c_h.shape
@@ -122,7 +118,6 @@
         copy.start()
     parity = lax.bitwise_and(lax.axis_index(blk), jnp.int32(1))
     wts[...] = jnp.zeros_like(wts)
-    tbl_o[...] = jnp.zeros_like(tbl_o)
     for copy in copies[:3]:
         copy.wait()
     for slot in range(3):
@@ -131,7 +126,7 @@
         if slot:
             weight = jnp.where(has_partner(slot, lax.axis_index(blk), lax.axis_size(blk)), weight, 0.0)
         wts[slot * nedge : (slot + 1) * nedge, 0:levels] = weight
-        tbl_o[slot : slot + 1, 0:nedge] = recv_v[pl.ds(d, 1), :].astype(F32)
+        wts[3 * nedge + slot : 3 * nedge + slot + 1, 0:nedge] = recv_v[pl.ds(d, 1), :].astype(F32)
     weights = wts[...].T
     wts_o[...] = weights
     rows_of = lambda s, lo, n: cf[pl.ds(lo * pitch + s, n, stride=pitch), :]
@@ -139,9 +134,9 @@
         copies[3 + i].wait()
         for l in range(lo, hi):
             cf[l * pitch : l * pitch + cols, :] = c_v[l].astype(F32)
-        pack_chunk(parity, lo, levels, send_s, weights, tbl_o, rows_of, (0, 1, 2), (s0, s1, s2))
+        pack_chunk(parity, lo, levels, send_s, weights, rows_of, (0, 1, 2), (s0, s1, s2))
     if levels % 16 == 0:
-        pack_chunk(parity, levels, levels, send_s, weights, tbl_o, rows_of, (0, 1, 2), (s0, s1, s2))
+        pack_chunk(parity, levels, levels, send_s, weights, rows_of, (0, 1, 2), (s0, s1, s2))
     for copy in copies[3 + len(bounds) :]:
         copy.wait()
 
@@ -217,41 +212,41 @@
     vertical(vt_ref, exs, state_ref)
 
 
-def send_kernel(blk, levels, r0, r1, r2, local_ref, vt_ref, wts_ref, tbl_ref, send_h, state, s0, s1, tbl_v, tbl_s, send_s, sems):
-    copy = pltpu.make_async_copy(send_h, send_s, sems.at[1])
+def send_kernel(blk, levels, r0, r1, r2, local_ref, vt_ref, wts_ref, send_h, state, s0, s1, send_s, sem):
+    copy = pltpu.make_async_copy(send_h, send_s, sem)
     copy.start()
-    add_edges((r0, r1, r2), levels, send_h.shape[1], vt_ref, state, tbl_v, tbl_s, sems.at[0])
+    add_edges((r0, r1, r2), levels, send_h.shape[1], vt_ref, state)
     copy.wait()
-    pack_state(blk, levels, send_s, wts_ref, tbl_ref, state, vt_ref.shape[1], (0, 1), (s0, s1))
-
-
-def pack_state(blk, levels, send, weights, tbl, state, rows, slots, outs):
+    pack_state(blk, levels, send_s, wts_ref, state, vt_ref.shape[1], (0, 1), (s0, s1))
+
+
+def pack_state(blk, levels, send, weights, state, rows, slots, outs):
     parity = lax.bitwise_and(lax.axis_index(blk), jnp.int32(1))
     rows_of = lambda s, lo, n: state[pl.ds(pl.multiple_of(s * rows + lo, 8), n), :]
     for lo in range(0, levels + 1, 16):
-        pack_chunk(parity, lo, levels, send, weights, tbl, rows_of, slots, outs)
-
-
-def middle_kernel(blk, levels, cs, a_ref, vt_ref, wts_ref, tbl_ref, send_h, out_ref, s2, exs, send_s, sem):
+        pack_chunk(parity, lo, levels, send, weights, rows_of, slots, outs)
+
+
+def middle_kernel(blk, levels, cs, a_ref, vt_ref, wts_ref, send_h, out_ref, s2, exs, send_s, sem):
     copy = pltpu.make_async_copy(send_h, send_s, sem)
     copy.start()
     cols, rows, _ = vt_ref.shape
     level_products(a_ref, lambda l: cs[pl.ds(l, cols, stride=rows), :].astype(BF16), exs, rows)
     copy.wait()
-    pack_state(blk, levels, send_s, wts_ref, tbl_ref, cs, rows, (2,), (s2,))
+    pack_state(blk, levels, send_s, wts_ref, cs, rows, (2,), (s2,))
     vertical(vt_ref, exs, out_ref)
 
 
-def last_kernel(nedge, r0, r1, r2, local_ref, vt_ref, out_h, total, out_v, tbl_v, tbl_s, sems):
+def last_kernel(nedge, r0, r1, r2, local_ref, vt_ref, out_h, total, out_v, sems):
     levels, cols, width = out_h.shape
     rows = vt_ref.shape[1]
-    add_edges((r0, r1, r2), levels, nedge, vt_ref, total, tbl_v, tbl_s, sems.at[0])
+    add_edges((r0, r1, r2), levels, nedge, vt_ref, total)
     bounds = [0, *range(4, levels, 8), levels]
     copies = []
     for i, (lo, hi) in enumerate(zip(bounds, bounds[1:])):
         for l in range(lo, hi):
             out_v[l] = total[pl.ds(l, cols, stride=rows), :].astype(BF16)
-        copies.append(pltpu.make_async_copy(out_v.at[pl.ds(lo, hi - lo)], out_h.at[pl.ds(lo, hi - lo)], sems.at[1 + i]))
+        copies.append(pltpu.make_async_copy(out_v.at[pl.ds(lo, hi - lo)], out_h.at[pl.ds(lo, hi - lo)], sems.at[i]))
         copies[-1].start()
     for copy in copies:
         copy.wait()
@@ -276,12 +271,13 @@
     )(*ins)
 
 
-def odd_or_even(value, first, blk):
-    n = lax.axis_size(blk)
-    order = [(i + first) % n for i in range(n)]
-    partner = {order[i]: order[i + 1] for i in range(0, n - 1, 2)}
+def odd_or_even(value, first, blk, basin):
+    n, b = lax.axis_size(blk), lax.axis_size(basin)
+    partner = {i: i + 1 for i in range(first, n - 1, 2)}
     partner |= {j: i for i, j in partner.items()}
-    return lax.ppermute(value, blk, [(i, partner.get(i, i)) for i in range(n)])
+    across = lambda g: g ^ 1 if g ^ 1 < b else g
+    route = [(g * n + i, g * n + partner[i] if i in partner else across(g) * n + i) for g in range(b) for i in range(n)]
+    return lax.ppermute(value, (basin, blk), route)
 
 
 def along_basin(value, basin):
@@ -311,8 +307,8 @@
         functools.partial(gather_kernel, "blk"),
         (in_hbm(by_level), send_h, *map(in_hbm, (recv_cols, edge_by_entry, *loads[1:]))),
         [HB] * 8,
-        [message] * 3 + [same(x) for x in loads] + [shape((128, 128), F32), shape((8, 128), F32)],
-        [VM] * 10,
+        [message] * 3 + [same(x) for x in loads] + [shape((128, 128), F32)],
+        [VM] * 9,
         [
             pltpu.VMEM((rows * (cols + 8), width), F32),
             pltpu.VMEM((128, 128), F32), pltpu.VMEM(recv_cols.shape, jnp.int32), pltpu.VMEM(edge_by_entry.shape, F32),
@@ -320,16 +316,14 @@
         ],
         16,
     )
-    (to_next, to_odd, to_even), loads, (wts, tbl) = first[:3], first[3:8], first[8:]
+    (to_next, to_odd, to_even), loads, wts = first[:3], first[3:8], first[8]
     operator_flops = 2 * levels * cols * cols * width
     vertical_flops = 2 * cols * rows * rows * width
 
     edge_flops = 3 * nedge * 2 * rows * rows * width
-    tables = [pltpu.VMEM((3, 8, 128), jnp.int32), pltpu.SMEM((3, 8, 128), jnp.int32)]
-
     along = along_basin(to_next, "basin")
-    odd = odd_or_even(to_odd, 1, "blk")
-    even = odd_or_even(to_even, 0, "blk")
+    odd = odd_or_even(to_odd, 1, "blk", "basin")
+    even = odd_or_even(to_even, 0, "blk", "basin")
     operator, partial, vt = call(
         operator_kernel, (*loads, in_hbm(vert_inv)), [VM] * 5 + [HB],
         [shape((levels // 2, cols, 2 * cols), BF16), columns, shape((cols, rows, 128), BF16)], [VM] * 3,
@@ -339,21 +333,21 @@
     )
     state, to_next, to_odd = call(
         functools.partial(send_kernel, "blk", levels),
-        (along, odd, even, partial, vt, wts, tbl, send_h), [VM] * 7 + [HB],
+        (along, odd, even, partial, vt, wts, send_h), [VM] * 6 + [HB],
         [columns] + [message] * 2, [VM] * 3,
-        tables + [send_table, DMA((2,))], 16, flops=edge_flops, aliases={3: 0},
+        [send_table, DMA], 16, flops=edge_flops, aliases={3: 0},
     )
     along = along_basin(to_next, "basin")
-    odd = odd_or_even(to_odd, 1, "blk")
+    odd = odd_or_even(to_odd, 1, "blk", "basin")
     partial, to_even = call(
-        functools.partial(middle_kernel, "blk", levels), (state, operator, vt, wts, tbl, send_h), [VM] * 5 + [HB],
+        functools.partial(middle_kernel, "blk", levels), (state, operator, vt, wts, send_h), [VM] * 4 + [HB],
         [columns, message], [VM] * 2, [flat, send_table, DMA], 32, flops=operator_flops + vertical_flops,
     )
-    even = odd_or_even(to_even, 0, "blk")
+    even = odd_or_even(to_even, 0, "blk", "basin")
     out, _ = call(
         functools.partial(last_kernel, nedge), (along, odd, even, partial, vt), [VM] * 5,
         [shape((levels, cols, width), BF16), columns], [HB, VM],
-        [pltpu.VMEM((levels, cols, width), BF16)] + tables + [DMA((2 + -(-levels // 8),))], 16, flops=edge_flops, aliases={3: 1},
+        [pltpu.VMEM((levels, cols, width), BF16), DMA((1 + -(-levels // 8),))], 16, flops=edge_flops, aliases={3: 1},
     )
     return jnp.transpose(out, (1, 0, 2))
 

time: 26.4 us -> 24.5 us (0.928)
  starting transfers between devices: 10.4 us -> 7 us
  waiting for transfers between devices: 1.45 us -> 3.82 us
  Pallas kernels: 14.3 us -> 13.5 us
    ppermute x4, starting transfers between devices: 6.78 us -> 2.2 us  [odd_or_even(): return lax.ppermute(value, (basin, blk), route)]
    ppermute x4, waiting for transfers between devices: 1.03 us -> 3.39 us  [odd_or_even(): return lax.ppermute(value, (basin, blk), route)]
    ppermute x2, starting transfers between devices: 3.6 us -> 4.8 us  [along_basin(): return lax.ppermute(value, basin, [(i, (i + 1) % b) for i in range(b)])]
    pallas_call x5, Pallas kernels: 14.3 us -> 13.5 us  [call(): pl.pallas_call(kernel, out_shape=outs, in_specs=specs, out_specs=out_spec...]
  transfers between devices with their start and end apart: 6 -> 6, of which waited for: 3 -> 3; matrix products, arithmetic and copies ran while one was open for 0% -> 0% of each run, Pallas kernels for 31% -> 34%
where the time goes in v12:
time: 24.5 us; the launch traced here: 24.3 us
  Pallas kernels  13.5 us (55%)
  starting transfers between devices  7 us (29%)
  waiting for transfers between devices  3.82 us (16%)
    pallas_call x5, Pallas kernels, call(): pl.pallas_call(kernel, out_shape=outs, in_specs=specs, out_specs=out_spec...  13.5 us
    ppermute x2, starting transfers between devices, along_basin(): return lax.ppermute(value, basin, [(i, (i + 1) % b) for i in range(b)])  4.8 us
    ppermute x4, waiting for transfers between devices, odd_or_even(): return lax.ppermute(value, (basin, blk), route)  3.39 us
    ppermute x4, starting transfers between devices, odd_or_even(): return lax.ppermute(value, (basin, blk), route)  2.2 us
  transfers between devices with their start and end apart: 6, of which 3 were waited for; matrix products, arithmetic and copies ran while one was open for 0% of the time, Pallas kernels for 34%

profile of v12, /device:TPU:0, one launch (start us, length us, event | category | flops | bytes accessed | tf_op | source)
XLA Modules:
  0.0 24.3 jit_solution(3195094742048737765)
XLA Ops:
  0.0 2.0 %shard_map.91 = (bf16[816,128]{1,0:T(8,128)(2,1)S(1)}, bf16[816,128]{1,0:T(8,128)(2,1)S(1)}, bf16[816,128]{1,0:T(8,128)(2,1)S(1)}, bf16[50,128,128]{2,1,0:T(8,12...) custom-call(bf16[50,128,128]{2,1,0:T(8,128)(2,1)} %bitcast.5, ...), custom_call_target="tpu_custom_call" | custom-call | bytes 4240128 | tf_op jit(solution)/shard_map/pallas_call | solution.py:262
  2.1 3.0 %collective-permute-start = (bf16[816,128]{1,0:T(8,128)(2,1)S(1)}, bf16[816,128]{1,0:T(8,128)(2,1)S(1)}, u32[]{:S(2)}, u32[]{:S(2)}) collective-permute-start(bf16[816,128]{1,0:T(8,128)(2,1)S(1)} %get-tuple-element.23), channel_id=1, source_target_pairs={{0,16},{16,0},{1,17},{17,1},{2,18},{18,2},{3,19},{19,3},{4,20},{20... | collective-permute-start | bytes 626696 | tf_op jit(solution)/shard_map/ppermute | solution.py:285
  5.1 0.1 collective-permute-start.1
  5.1 1.6 %collective-permute-start.2 = (bf16[816,128]{1,0:T(8,128)(2,1)S(1)}, bf16[816,128]{1,0:T(8,128)(2,1)S(1)}, u32[]{:S(2)}, u32[]{:S(2)}) collective-permute-start(bf16[816,128]{1,0:T(8,128)(2,1)S(1)} %get-tuple-element.25), channel_id=1, source_target_pairs={{0,1},{1,0},{2,3},{3,2},{4,5},{5,4},{6,7},{7,6},{8,9},{9,8},{10,11... | collective-permute-start | bytes 626696 | tf_op jit(solution)/shard_map/ppermute | solution.py:280
  6.7 4.6 %shard_map.92 = (bf16[25,128,256]{2,1,0:T(8,128)(2,1)S(1)}, f32[7168,128]{1,0:T(8,128)S(1)}, bf16[128,56,128]{2,1,0:T(8,128)(2,1)S(1)}) custom-call(bf16[50,128,128]{2,1,0:T(8,128)(2,1)S(1)} %get-tuple-element.26.c_ref, s32[4,128]{1,0:T(4,128)S(1)} %get-tuple-element.27.nbr_ref, f32[50,4,128]{2,1,0:T(4,128)S(1)} %get-tuple-element.28.nw_ref, ...), custom_call_target="tpu_custom_call" | custom-call | flops 312475648 | bytes 9552384 | tf_op jit(solution)/shard_map/pallas_call | solution.py:262
  11.3 0.0 collective-permute-done.r0
  11.3 1.1 %collective-permute-done.1.r1 = bf16[816,128]{1,0:T(8,128)(2,1)S(1)} collective-permute-done((bf16[816,128]{1,0:T(8,128)(2,1)S(1)}, bf16[816,128]{1,0:T(8,128)(2,1)S(1)}, u32[]{:S(2)}, u32[]{:S(2)}) %collective-permute-start.1) | collective-permute-done | bytes 208928 | tf_op jit(solution)/shard_map/ppermute | solution.py:280
  12.5 0.0 collective-permute-done.2.r2
  12.5 1.5 %shard_map.93 = (f32[7168,128]{1,0:T(8,128)S(1)}, bf16[816,128]{1,0:T(8,128)(2,1)S(1)}, bf16[816,128]{1,0:T(8,128)(2,1)S(1)}) custom-call(bf16[816,128]{1,0:T(8,128)(2,1)S(1)} %collective-permute-done.r0, bf16[816,128]{1,0:T(8,128)(2,1)S(1)} %collective-permute-done.1.r1, ...), custom_call_target="tpu_custom_call", output_to_operand_aliasing={{0}: (3, {})} | custom-call | flops 38535168 | bytes 10285248 | tf_op jit(solution)/shard_map/pallas_call | solution.py:262
  14.0 1.8 %collective-permute-start.3 = (bf16[816,128]{1,0:T(8,128)(2,1)S(1)}, bf16[816,128]{1,0:T(8,128)(2,1)S(1)}, u32[]{:S(2)}, u32[]{:S(2)}) collective-permute-start(bf16[816,128]{1,0:T(8,128)(2,1)S(1)} %get-tuple-element.34), channel_id=1, source_target_pairs={{0,16},{16,0},{1,17},{17,1},{2,18},{18,2},{3,19},{19,3},{4,20},{20... | collective-permute-start | bytes 626696 | tf_op jit(solution)/shard_map/ppermute | solution.py:285
  15.8 0.3 %collective-permute-start.4 = (bf16[816,128]{1,0:T(8,128)(2,1)S(1)}, bf16[816,128]{1,0:T(8,128)(2,1)S(1)}, u32[]{:S(2)}, u32[]{:S(2)}) collective-permute-start(bf16[816,128]{1,0:T(8,128)(2,1)S(1)} %get-tuple-element.35), channel_id=1, source_target_pairs={{0,16},{1,2},{2,1},{3,4},{4,3},{5,6},{6,5},{7,8},{8,7},{9,10},{10,... | collective-permute-start | bytes 626696 | tf_op jit(solution)/shard_map/ppermute | solution.py:280
  16.1 3.5 %shard_map.94 = (f32[7168,128]{1,0:T(8,128)S(1)}, bf16[816,128]{1,0:T(8,128)(2,1)S(1)}) custom-call(f32[7168,128]{1,0:T(8,128)S(1)} %get-tuple-element.36.cs, bf16[25,128,256]{2,1,0:T(8,128)(2,1)S(1)} %get-tuple-element.37.a_ref, bf16[128,56,128]{2,1,0:T(8,128)(2,1)S(1)} %get-tuple-element.32.vt_ref, f32[128,128]{1,0:T(8,128)S(1)} %get-tuple-element.33.wts_ref, ...), custom_call_target="tpu_custom_call" | custom-call | flops 312475648 | bytes 11088064 | tf_op jit(solution)/shard_map/pallas_call | solution.py:262
  19.6 0.3 %collective-permute-start.5 = (bf16[816,128]{1,0:T(8,128)(2,1)S(1)}, bf16[816,128]{1,0:T(8,128)(2,1)S(1)}, u32[]{:S(2)}, u32[]{:S(2)}) collective-permute-start(bf16[816,128]{1,0:T(8,128)(2,1)S(1)} %get-tuple-element.38), channel_id=1, source_target_pairs={{0,1},{1,0},{2,3},{3,2},{4,5},{5,4},{6,7},{7,6},{8,9},{9,8},{10,11... | collective-permute-start | bytes 626696 | tf_op jit(solution)/shard_map/ppermute | solution.py:280
  19.9 0.4 %collective-permute-done.3.r0 = bf16[816,128]{1,0:T(8,128)(2,1)S(1)} collective-permute-done((bf16[816,128]{1,0:T(8,128)(2,1)S(1)}, bf16[816,128]{1,0:T(8,128)(2,1)S(1)}, u32[]{:S(2)}, u32[]{:S(2)}) %collective-permute-start.3) | collective-permute-done | bytes 208928 | tf_op jit(solution)/shard_map/ppermute | solution.py:285
  20.3 2.2 %collective-permute-done.4.r1 = bf16[816,128]{1,0:T(8,128)(2,1)S(1)} collective-permute-done((bf16[816,128]{1,0:T(8,128)(2,1)S(1)}, bf16[816,128]{1,0:T(8,128)(2,1)S(1)}, u32[]{:S(2)}, u32[]{:S(2)}) %collective-permute-start.4) | collective-permute-done | bytes 208928 | tf_op jit(solution)/shard_map/ppermute | solution.py:280
  22.6 0.0 collective-permute-done.5.r2
  22.6 1.8 %shard_map.95 = (bf16[50,128,128]{2,1,0:T(8,128)(2,1)}, f32[7168,128]{1,0:T(8,128)S(1)}) custom-call(bf16[816,128]{1,0:T(8,128)(2,1)S(1)} %collective-permute-done.3.r0, bf16[816,128]{1,0:T(8,128)(2,1)S(1)} %collective-permute-done.4.r1, bf16[816,128]{1,0:T(8,128)(2,1)S(1)} %collective-permute-done.5.r2, ...), custom_call_target="tpu_custom_call", output_to_operand_aliasing={{1}: (3, {})} | custom-call | flops 38535168 | bytes 11440128 | tf_op jit(solution)/shard_map/pallas_call | solution.py:262
Async XLA Ops:
  2.1 9.3 %collective-permute-start = (bf16[816,128]{1,0:T(8,128)(2,1)S(1)}, bf16[816,128]{1,0:T(8,128)(2,1)S(1)}, u32[]{:S(2)}, u32[]{:S(2)}) collective-permute-start(bf16[816,128]{1,0:T(8,128)(2,1)S(1)} %get-tuple-element.23), channel_id=1, source_target_pairs={{0,16},{16,0},{1,17},{17,1},{2,18},{18,2},{3,19},{19,3},{4,20},{20... | collective-permute-start | bytes 626696 | tf_op jit(solution)/shard_map/ppermute | solution.py:285
  5.1 7.4 %collective-permute-start.1 = (bf16[816,128]{1,0:T(8,128)(2,1)S(1)}, bf16[816,128]{1,0:T(8,128)(2,1)S(1)}, u32[]{:S(2)}, u32[]{:S(2)}) collective-permute-start(bf16[816,128]{1,0:T(8,128)(2,1)S(1)} %get-tuple-element.24), channel_id=1, source_target_pairs={{0,16},{1,2},{2,1},{3,4},{4,3},{5,6},{6,5},{7,8},{8,7},{9,10},{10,... | collective-permute-start | bytes 626696 | tf_op jit(solution)/shard_map/ppermute | solution.py:280
  5.1 7.3 %collective-permute-start.2 = (bf16[816,128]{1,0:T(8,128)(2,1)S(1)}, bf16[816,128]{1,0:T(8,128)(2,1)S(1)}, u32[]{:S(2)}, u32[]{:S(2)}) collective-permute-start(bf16[816,128]{1,0:T(8,128)(2,1)S(1)} %get-tuple-element.25), channel_id=1, source_target_pairs={{0,1},{1,0},{2,3},{3,2},{4,5},{5,4},{6,7},{7,6},{8,9},{9,8},{10,11... | collective-permute-start | bytes 626696 | tf_op jit(solution)/shard_map/ppermute | solution.py:280
  14.0 6.3 %collective-permute-start.3 = (bf16[816,128]{1,0:T(8,128)(2,1)S(1)}, bf16[816,128]{1,0:T(8,128)(2,1)S(1)}, u32[]{:S(2)}, u32[]{:S(2)}) collective-permute-start(bf16[816,128]{1,0:T(8,128)(2,1)S(1)} %get-tuple-element.34), channel_id=1, source_target_pairs={{0,16},{16,0},{1,17},{17,1},{2,18},{18,2},{3,19},{19,3},{4,20},{20... | collective-permute-start | bytes 626696 | tf_op jit(solution)/shard_map/ppermute | solution.py:285
  15.8 6.8 %collective-permute-start.4 = (bf16[816,128]{1,0:T(8,128)(2,1)S(1)}, bf16[816,128]{1,0:T(8,128)(2,1)S(1)}, u32[]{:S(2)}, u32[]{:S(2)}) collective-permute-start(bf16[816,128]{1,0:T(8,128)(2,1)S(1)} %get-tuple-element.35), channel_id=1, source_target_pairs={{0,16},{1,2},{2,1},{3,4},{4,3},{5,6},{6,5},{7,8},{8,7},{9,10},{10,... | collective-permute-start | bytes 626696 | tf_op jit(solution)/shard_map/ppermute | solution.py:280
  19.6 2.9 %collective-permute-start.5 = (bf16[816,128]{1,0:T(8,128)(2,1)S(1)}, bf16[816,128]{1,0:T(8,128)(2,1)S(1)}, u32[]{:S(2)}, u32[]{:S(2)}) collective-permute-start(bf16[816,128]{1,0:T(8,128)(2,1)S(1)} %get-tuple-element.38), channel_id=1, source_target_pairs={{0,1},{1,0},{2,3},{3,2},{4,5},{5,4},{6,7},{7,6},{8,9},{9,8},{10,11... | collective-permute-start | bytes 626696 | tf_op jit(solution)/shard_map/ppermute | solution.py:280

commit v13 on v12

--- a/solution.py
+++ b/solution.py
@@ -33,17 +33,15 @@
     return jnp.where(first, at + 1 < count, at > 0)
 
 
-def pack_chunk(parity, lo, levels, send, weights, rows_of, slots, outs):
+def pack_chunk(lo, levels, nedge, weights, rows_of, slots, outs):
     whole = whole_rows(levels)
-    nedge = send.shape[1]
     rest = levels - whole
     share = 8 // rest if rest else 0
     for slot, out in zip(slots, outs):
-        d = direction(slot, parity)
         if lo < whole:
             for e in range(nedge):
                 k = slot * nedge + e
-                value = rows_of(send[d, e], lo, 16) * weights[lo : lo + 16, k : k + 1]
+                value = rows_of(slot, e, lo, 16) * weights[lo : lo + 16, k : k + 1]
                 out[e * whole + lo : e * whole + lo + 16, :] = value.astype(BF16)
             continue
         sub = lax.broadcasted_iota(jnp.int32, (8, out.shape[1]), 0)
@@ -52,7 +50,7 @@
             part = None
             for q in range(share):
                 k = slot * nedge + first + q
-                value = rows_of(send[d, first + q], lo, 8) * weights[lo : lo + 8, k : k + 1]
+                value = rows_of(slot, first + q, lo, 8) * weights[lo : lo + 8, k : k + 1]
                 if q:
                     value = pltpu.roll(value, q * rest, 0)
                 part = value if part is None else jnp.where(sub >= q * rest, value, part)
@@ -104,13 +102,13 @@
 def gather_kernel(
     blk, c_h, send_h, recv_h, edge_h, nbr_h, nw_h, sw_h, wet_h,
     s0, s1, s2, c_v, nbr_v, nw_v, sw_v, wet_v, wts_o,
-    cf, wts, recv_v, edge_v, send_s, sems,
+    picked, wts, send_v, recv_v, edge_v, sems,
 ):
     levels, cols, width = c_h.shape
     nedge = edge_h.shape[1]
-    pitch = cols + 8
+    rows = padded(levels)
     bounds = [(lo, min(lo + 16, levels)) for lo in range(0, levels, 16)]
-    pairs = [(send_h, send_s), (recv_h, recv_v), (edge_h, edge_v)]
+    pairs = [(send_h, send_v), (recv_h, recv_v), (edge_h, edge_v)]
     pairs += [(c_h.at[pl.ds(lo, hi - lo)], c_v.at[pl.ds(lo, hi - lo)]) for lo, hi in bounds]
     pairs += [(nbr_h, nbr_v), (nw_h, nw_v), (sw_h, sw_v), (wet_h, wet_v)]
     copies = [pltpu.make_async_copy(a, b, sems.at[i]) for i, (a, b) in enumerate(pairs)]
@@ -127,16 +125,20 @@
             weight = jnp.where(has_partner(slot, lax.axis_index(blk), lax.axis_size(blk)), weight, 0.0)
         wts[slot * nedge : (slot + 1) * nedge, 0:levels] = weight
         wts[3 * nedge + slot : 3 * nedge + slot + 1, 0:nedge] = recv_v[pl.ds(d, 1), :].astype(F32)
+        wts[3 * nedge + 3 + slot : 3 * nedge + 4 + slot, 0:nedge] = send_v[pl.ds(d, 1), :].astype(F32)
     weights = wts[...].T
     wts_o[...] = weights
-    rows_of = lambda s, lo, n: cf[pl.ds(lo * pitch + s, n, stride=pitch), :]
+    lane = lax.broadcasted_iota(jnp.int32, (nedge, cols), 1).astype(F32)
+    pick = [lane == weights[0:nedge, 3 * nedge + 3 + slot : 3 * nedge + 4 + slot] for slot in range(3)]
+    pick = jnp.concatenate([p.astype(F32) for p in pick], axis=0).astype(BF16)
+    rows_of = lambda slot, e, lo, n: picked[(slot * nedge + e) * rows + lo : (slot * nedge + e) * rows + lo + n, :]
     for i, (lo, hi) in enumerate(bounds):
         copies[3 + i].wait()
         for l in range(lo, hi):
-            cf[l * pitch : l * pitch + cols, :] = c_v[l].astype(F32)
-        pack_chunk(parity, lo, levels, send_s, weights, rows_of, (0, 1, 2), (s0, s1, s2))
+            picked[pl.ds(l, 3 * nedge, stride=rows), :] = jnp.dot(pick, c_v[l], preferred_element_type=F32)
+        pack_chunk(lo, levels, nedge, weights, rows_of, (0, 1, 2), (s0, s1, s2))
     if levels % 16 == 0:
-        pack_chunk(parity, levels, levels, send_s, weights, rows_of, (0, 1, 2), (s0, s1, s2))
+        pack_chunk(levels, levels, nedge, weights, rows_of, (0, 1, 2), (s0, s1, s2))
     for copy in copies[3 + len(bounds) :]:
         copy.wait()
 
@@ -222,9 +224,12 @@
 
 def pack_state(blk, levels, send, weights, state, rows, slots, outs):
     parity = lax.bitwise_and(lax.axis_index(blk), jnp.int32(1))
-    rows_of = lambda s, lo, n: state[pl.ds(pl.multiple_of(s * rows + lo, 8), n), :]
+
+    def rows_of(slot, e, lo, n):
+        return state[pl.ds(pl.multiple_of(send[direction(slot, parity), e] * rows + lo, 8), n), :]
+
     for lo in range(0, levels + 1, 16):
-        pack_chunk(parity, lo, levels, send, weights, rows_of, slots, outs)
+        pack_chunk(lo, levels, send.shape[1], weights, rows_of, slots, outs)
 
 
 def middle_kernel(blk, levels, cs, a_ref, vt_ref, wts_ref, send_h, out_ref, s2, exs, send_s, sem):
@@ -310,9 +315,8 @@
         [message] * 3 + [same(x) for x in loads] + [shape((128, 128), F32)],
         [VM] * 9,
         [
-            pltpu.VMEM((rows * (cols + 8), width), F32),
-            pltpu.VMEM((128, 128), F32), pltpu.VMEM(recv_cols.shape, jnp.int32), pltpu.VMEM(edge_by_entry.shape, F32),
-            send_table, DMA((7 + -(-levels // 16),)),
+            pltpu.VMEM((3 * nedge * rows, width), F32), pltpu.VMEM((128, 128), F32), pltpu.VMEM(send_cols.shape, jnp.int32),
+            pltpu.VMEM(recv_cols.shape, jnp.int32), pltpu.VMEM(edge_by_entry.shape, F32), DMA((7 + -(-levels // 16),)),
         ],
         16,
     )

time: 24.5 us -> 24.8 us (1.012)
    pallas_call x5, Pallas kernels: 13.5 us -> 13.7 us  [call(): pl.pallas_call(kernel, out_shape=outs, in_specs=specs, out_specs=out_spec...]
  transfers between devices with their start and end apart: 6 -> 6, of which waited for: 3 -> 3; matrix products, arithmetic and copies ran while one was open for 0% -> 0% of each run, Pallas kernels for 34% -> 33%
where the time goes in v13:
time: 24.8 us; the launch traced here: 24.6 us
  Pallas kernels  13.7 us (55%)
  starting transfers between devices  7 us (28%)
  waiting for transfers between devices  3.81 us (15%)
    pallas_call x5, Pallas kernels, call(): pl.pallas_call(kernel, out_shape=outs, in_specs=specs, out_specs=out_spec...  13.7 us
    ppermute x2, starting transfers between devices, along_basin(): return lax.ppermute(value, basin, [(i, (i + 1) % b) for i in range(b)])  4.81 us
    ppermute x4, waiting for transfers between devices, odd_or_even(): return lax.ppermute(value, (basin, blk), route)  3.39 us
    ppermute x4, starting transfers between devices, odd_or_even(): return lax.ppermute(value, (basin, blk), route)  2.2 us
  transfers between devices with their start and end apart: 6, of which 3 were waited for; matrix products, arithmetic and copies ran while one was open for 0% of the time, Pallas kernels for 33%

profile of v13, /device:TPU:0, one launch (start us, length us, event | category | flops | bytes accessed | tf_op | source)
XLA Modules:
  0.0 24.6 jit_solution(15286762549401962836)
XLA Ops:
  0.0 2.3 %shard_map.91 = (bf16[816,128]{1,0:T(8,128)(2,1)S(1)}, bf16[816,128]{1,0:T(8,128)(2,1)S(1)}, bf16[816,128]{1,0:T(8,128)(2,1)S(1)}, bf16[50,128,128]{2,1,0:T(8,12...) custom-call(bf16[50,128,128]{2,1,0:T(8,128)(2,1)} %bitcast.5, ...), custom_call_target="tpu_custom_call" | custom-call | bytes 4240128 | tf_op jit(solution)/shard_map/pallas_call | solution.py:267
  2.3 3.0 %collective-permute-start = (bf16[816,128]{1,0:T(8,128)(2,1)S(1)}, bf16[816,128]{1,0:T(8,128)(2,1)S(1)}, u32[]{:S(2)}, u32[]{:S(2)}) collective-permute-start(bf16[816,128]{1,0:T(8,128)(2,1)S(1)} %get-tuple-element.23), channel_id=1, source_target_pairs={{0,16},{16,0},{1,17},{17,1},{2,18},{18,2},{3,19},{19,3},{4,20},{20... | collective-permute-start | bytes 626696 | tf_op jit(solution)/shard_map/ppermute | solution.py:290
  5.3 0.1 collective-permute-start.1
  5.4 1.6 %collective-permute-start.2 = (bf16[816,128]{1,0:T(8,128)(2,1)S(1)}, bf16[816,128]{1,0:T(8,128)(2,1)S(1)}, u32[]{:S(2)}, u32[]{:S(2)}) collective-permute-start(bf16[816,128]{1,0:T(8,128)(2,1)S(1)} %get-tuple-element.25), channel_id=1, source_target_pairs={{0,1},{1,0},{2,3},{3,2},{4,5},{5,4},{6,7},{7,6},{8,9},{9,8},{10,11... | collective-permute-start | bytes 626696 | tf_op jit(solution)/shard_map/ppermute | solution.py:285
  7.0 4.6 %shard_map.92 = (bf16[25,128,256]{2,1,0:T(8,128)(2,1)S(1)}, f32[7168,128]{1,0:T(8,128)S(1)}, bf16[128,56,128]{2,1,0:T(8,128)(2,1)S(1)}) custom-call(bf16[50,128,128]{2,1,0:T(8,128)(2,1)S(1)} %get-tuple-element.26.c_ref, s32[4,128]{1,0:T(4,128)S(1)} %get-tuple-element.27.nbr_ref, f32[50,4,128]{2,1,0:T(4,128)S(1)} %get-tuple-element.28.nw_ref, ...), custom_call_target="tpu_custom_call" | custom-call | flops 312475648 | bytes 9552384 | tf_op jit(solution)/shard_map/pallas_call | solution.py:267
  11.6 0.0 collective-permute-done.r0
  11.6 1.1 %collective-permute-done.1.r1 = bf16[816,128]{1,0:T(8,128)(2,1)S(1)} collective-permute-done((bf16[816,128]{1,0:T(8,128)(2,1)S(1)}, bf16[816,128]{1,0:T(8,128)(2,1)S(1)}, u32[]{:S(2)}, u32[]{:S(2)}) %collective-permute-start.1) | collective-permute-done | bytes 208928 | tf_op jit(solution)/shard_map/ppermute | solution.py:285
  12.7 0.0 collective-permute-done.2.r2
  12.7 1.5 %shard_map.93 = (f32[7168,128]{1,0:T(8,128)S(1)}, bf16[816,128]{1,0:T(8,128)(2,1)S(1)}, bf16[816,128]{1,0:T(8,128)(2,1)S(1)}) custom-call(bf16[816,128]{1,0:T(8,128)(2,1)S(1)} %collective-permute-done.r0, bf16[816,128]{1,0:T(8,128)(2,1)S(1)} %collective-permute-done.1.r1, ...), custom_call_target="tpu_custom_call", output_to_operand_aliasing={{0}: (3, {})} | custom-call | flops 38535168 | bytes 10285248 | tf_op jit(solution)/shard_map/pallas_call | solution.py:267
  14.2 1.8 %collective-permute-start.3 = (bf16[816,128]{1,0:T(8,128)(2,1)S(1)}, bf16[816,128]{1,0:T(8,128)(2,1)S(1)}, u32[]{:S(2)}, u32[]{:S(2)}) collective-permute-start(bf16[816,128]{1,0:T(8,128)(2,1)S(1)} %get-tuple-element.34), channel_id=1, source_target_pairs={{0,16},{16,0},{1,17},{17,1},{2,18},{18,2},{3,19},{19,3},{4,20},{20... | collective-permute-start | bytes 626696 | tf_op jit(solution)/shard_map/ppermute | solution.py:290
  16.0 0.3 %collective-permute-start.4 = (bf16[816,128]{1,0:T(8,128)(2,1)S(1)}, bf16[816,128]{1,0:T(8,128)(2,1)S(1)}, u32[]{:S(2)}, u32[]{:S(2)}) collective-permute-start(bf16[816,128]{1,0:T(8,128)(2,1)S(1)} %get-tuple-element.35), channel_id=1, source_target_pairs={{0,16},{1,2},{2,1},{3,4},{4,3},{5,6},{6,5},{7,8},{8,7},{9,10},{10,... | collective-permute-start | bytes 626696 | tf_op jit(solution)/shard_map/ppermute | solution.py:285
  16.3 3.6 %shard_map.94 = (f32[7168,128]{1,0:T(8,128)S(1)}, bf16[816,128]{1,0:T(8,128)(2,1)S(1)}) custom-call(f32[7168,128]{1,0:T(8,128)S(1)} %get-tuple-element.36.cs, bf16[25,128,256]{2,1,0:T(8,128)(2,1)S(1)} %get-tuple-element.37.a_ref, bf16[128,56,128]{2,1,0:T(8,128)(2,1)S(1)} %get-tuple-element.32.vt_ref, f32[128,128]{1,0:T(8,128)S(1)} %get-tuple-element.33.wts_ref, ...), custom_call_target="tpu_custom_call" | custom-call | flops 312475648 | bytes 11088064 | tf_op jit(solution)/shard_map/pallas_call | solution.py:267
  19.9 0.3 %collective-permute-start.5 = (bf16[816,128]{1,0:T(8,128)(2,1)S(1)}, bf16[816,128]{1,0:T(8,128)(2,1)S(1)}, u32[]{:S(2)}, u32[]{:S(2)}) collective-permute-start(bf16[816,128]{1,0:T(8,128)(2,1)S(1)} %get-tuple-element.38), channel_id=1, source_target_pairs={{0,1},{1,0},{2,3},{3,2},{4,5},{5,4},{6,7},{7,6},{8,9},{9,8},{10,11... | collective-permute-start | bytes 626696 | tf_op jit(solution)/shard_map/ppermute | solution.py:285
  20.2 0.4 %collective-permute-done.3.r0 = bf16[816,128]{1,0:T(8,128)(2,1)S(1)} collective-permute-done((bf16[816,128]{1,0:T(8,128)(2,1)S(1)}, bf16[816,128]{1,0:T(8,128)(2,1)S(1)}, u32[]{:S(2)}, u32[]{:S(2)}) %collective-permute-start.3) | collective-permute-done | bytes 208928 | tf_op jit(solution)/shard_map/ppermute | solution.py:290
  20.6 2.2 %collective-permute-done.4.r1 = bf16[816,128]{1,0:T(8,128)(2,1)S(1)} collective-permute-done((bf16[816,128]{1,0:T(8,128)(2,1)S(1)}, bf16[816,128]{1,0:T(8,128)(2,1)S(1)}, u32[]{:S(2)}, u32[]{:S(2)}) %collective-permute-start.4) | collective-permute-done | bytes 208928 | tf_op jit(solution)/shard_map/ppermute | solution.py:285
  22.8 0.0 collective-permute-done.5.r2
  22.8 1.8 %shard_map.95 = (bf16[50,128,128]{2,1,0:T(8,128)(2,1)}, f32[7168,128]{1,0:T(8,128)S(1)}) custom-call(bf16[816,128]{1,0:T(8,128)(2,1)S(1)} %collective-permute-done.3.r0, bf16[816,128]{1,0:T(8,128)(2,1)S(1)} %collective-permute-done.4.r1, bf16[816,128]{1,0:T(8,128)(2,1)S(1)} %collective-permute-done.5.r2, ...), custom_call_target="tpu_custom_call", output_to_operand_aliasing={{1}: (3, {})} | custom-call | flops 38535168 | bytes 11440128 | tf_op jit(solution)/shard_map/pallas_call | solution.py:267
Async XLA Ops:
  2.3 9.3 %collective-permute-start = (bf16[816,128]{1,0:T(8,128)(2,1)S(1)}, bf16[816,128]{1,0:T(8,128)(2,1)S(1)}, u32[]{:S(2)}, u32[]{:S(2)}) collective-permute-start(bf16[816,128]{1,0:T(8,128)(2,1)S(1)} %get-tuple-element.23), channel_id=1, source_target_pairs={{0,16},{16,0},{1,17},{17,1},{2,18},{18,2},{3,19},{19,3},{4,20},{20... | collective-permute-start | bytes 626696 | tf_op jit(solution)/shard_map/ppermute | solution.py:290
  5.3 7.4 %collective-permute-start.1 = (bf16[816,128]{1,0:T(8,128)(2,1)S(1)}, bf16[816,128]{1,0:T(8,128)(2,1)S(1)}, u32[]{:S(2)}, u32[]{:S(2)}) collective-permute-start(bf16[816,128]{1,0:T(8,128)(2,1)S(1)} %get-tuple-element.24), channel_id=1, source_target_pairs={{0,16},{1,2},{2,1},{3,4},{4,3},{5,6},{6,5},{7,8},{8,7},{9,10},{10,... | collective-permute-start | bytes 626696 | tf_op jit(solution)/shard_map/ppermute | solution.py:285
  5.4 7.3 %collective-permute-start.2 = (bf16[816,128]{1,0:T(8,128)(2,1)S(1)}, bf16[816,128]{1,0:T(8,128)(2,1)S(1)}, u32[]{:S(2)}, u32[]{:S(2)}) collective-permute-start(bf16[816,128]{1,0:T(8,128)(2,1)S(1)} %get-tuple-element.25), channel_id=1, source_target_pairs={{0,1},{1,0},{2,3},{3,2},{4,5},{5,4},{6,7},{7,6},{8,9},{9,8},{10,11... | collective-permute-start | bytes 626696 | tf_op jit(solution)/shard_map/ppermute | solution.py:285
  14.2 6.3 %collective-permute-start.3 = (bf16[816,128]{1,0:T(8,128)(2,1)S(1)}, bf16[816,128]{1,0:T(8,128)(2,1)S(1)}, u32[]{:S(2)}, u32[]{:S(2)}) collective-permute-start(bf16[816,128]{1,0:T(8,128)(2,1)S(1)} %get-tuple-element.34), channel_id=1, source_target_pairs={{0,16},{16,0},{1,17},{17,1},{2,18},{18,2},{3,19},{19,3},{4,20},{20... | collective-permute-start | bytes 626696 | tf_op jit(solution)/shard_map/ppermute | solution.py:290
  16.0 6.8 %collective-permute-start.4 = (bf16[816,128]{1,0:T(8,128)(2,1)S(1)}, bf16[816,128]{1,0:T(8,128)(2,1)S(1)}, u32[]{:S(2)}, u32[]{:S(2)}) collective-permute-start(bf16[816,128]{1,0:T(8,128)(2,1)S(1)} %get-tuple-element.35), channel_id=1, source_target_pairs={{0,16},{1,2},{2,1},{3,4},{4,3},{5,6},{6,5},{7,8},{8,7},{9,10},{10,... | collective-permute-start | bytes 626696 | tf_op jit(solution)/shard_map/ppermute | solution.py:285
  19.9 2.9 %collective-permute-start.5 = (bf16[816,128]{1,0:T(8,128)(2,1)S(1)}, bf16[816,128]{1,0:T(8,128)(2,1)S(1)}, u32[]{:S(2)}, u32[]{:S(2)}) collective-permute-start(bf16[816,128]{1,0:T(8,128)(2,1)S(1)} %get-tuple-element.38), channel_id=1, source_target_pairs={{0,1},{1,0},{2,3},{3,2},{4,5},{5,4},{6,7},{7,6},{8,9},{9,8},{10,11... | collective-permute-start | bytes 626696 | tf_op jit(solution)/shard_map/ppermute | solution.py:285

commit v14 on v12

--- a/solution.py
+++ b/solution.py
@@ -212,12 +212,16 @@
     vertical(vt_ref, exs, state_ref)
 
 
-def send_kernel(blk, levels, r0, r1, r2, local_ref, vt_ref, wts_ref, send_h, state, s0, s1, send_s, sem):
+def arrived_kernel(levels, nedge, r0, r2, local_ref, vt_ref, total):
+    add_edges((r0, r2), levels, nedge, vt_ref, total)
+
+
+def send_kernel(blk, levels, r1, local_ref, vt_ref, wts_ref, send_h, state, s0, s1, s2, send_s, sem):
     copy = pltpu.make_async_copy(send_h, send_s, sem)
     copy.start()
-    add_edges((r0, r1, r2), levels, send_h.shape[1], vt_ref, state)
+    add_edges((r1,), levels, send_h.shape[1], vt_ref, state)
     copy.wait()
-    pack_state(blk, levels, send_s, wts_ref, state, vt_ref.shape[1], (0, 1), (s0, s1))
+    pack_state(blk, levels, send_s, wts_ref, state, vt_ref.shape[1], (0, 1, 2), (s0, s1, s2))
 
 
 def pack_state(blk, levels, send, weights, state, rows, slots, outs):
@@ -227,20 +231,16 @@
         pack_chunk(parity, lo, levels, send, weights, rows_of, slots, outs)
 
 
-def middle_kernel(blk, levels, cs, a_ref, vt_ref, wts_ref, send_h, out_ref, s2, exs, send_s, sem):
-    copy = pltpu.make_async_copy(send_h, send_s, sem)
-    copy.start()
+def middle_kernel(cs, a_ref, vt_ref, out_ref, exs):
     cols, rows, _ = vt_ref.shape
     level_products(a_ref, lambda l: cs[pl.ds(l, cols, stride=rows), :].astype(BF16), exs, rows)
-    copy.wait()
-    pack_state(blk, levels, send_s, wts_ref, cs, rows, (2,), (s2,))
     vertical(vt_ref, exs, out_ref)
 
 
-def last_kernel(nedge, r0, r1, r2, local_ref, vt_ref, out_h, total, out_v, sems):
+def last_kernel(nedge, r1, local_ref, vt_ref, out_h, total, out_v, sems):
     levels, cols, width = out_h.shape
     rows = vt_ref.shape[1]
-    add_edges((r0, r1, r2), levels, nedge, vt_ref, total)
+    add_edges((r1,), levels, nedge, vt_ref, total)
     bounds = [0, *range(4, levels, 8), levels]
     copies = []
     for i, (lo, hi) in enumerate(zip(bounds, bounds[1:])):
@@ -320,7 +320,14 @@
     operator_flops = 2 * levels * cols * cols * width
     vertical_flops = 2 * cols * rows * rows * width
 
-    edge_flops = 3 * nedge * 2 * rows * rows * width
+    edge_flops = nedge * 2 * rows * rows * width
+
+    def arrived(along, even, partial):
+        return call(
+            functools.partial(arrived_kernel, levels, nedge), (along, even, partial, vt), [VM] * 4, [columns], [VM], [], 16,
+            flops=2 * edge_flops, aliases={2: 0},
+        )[0]
+
     along = along_basin(to_next, "basin")
     odd = odd_or_even(to_odd, 1, "blk", "basin")
     even = odd_or_even(to_even, 0, "blk", "basin")
@@ -331,23 +338,21 @@
          pltpu.VMEM(vert_inv.shape, BF16), DMA],
         32, flops=operator_flops + vertical_flops,
     )
-    state, to_next, to_odd = call(
+    state, to_next, to_odd, to_even = call(
         functools.partial(send_kernel, "blk", levels),
-        (along, odd, even, partial, vt, wts, send_h), [VM] * 6 + [HB],
-        [columns] + [message] * 2, [VM] * 3,
-        [send_table, DMA], 16, flops=edge_flops, aliases={3: 0},
+        (odd, arrived(along, even, partial), vt, wts, send_h), [VM] * 4 + [HB],
+        [columns] + [message] * 3, [VM] * 4, [send_table, DMA], 16, flops=edge_flops, aliases={1: 0},
     )
     along = along_basin(to_next, "basin")
     odd = odd_or_even(to_odd, 1, "blk", "basin")
-    partial, to_even = call(
-        functools.partial(middle_kernel, "blk", levels), (state, operator, vt, wts, send_h), [VM] * 4 + [HB],
-        [columns, message], [VM] * 2, [flat, send_table, DMA], 32, flops=operator_flops + vertical_flops,
-    )
     even = odd_or_even(to_even, 0, "blk", "basin")
+    (partial,) = call(
+        middle_kernel, (state, operator, vt), [VM] * 3, [columns], [VM], [flat], 32, flops=operator_flops + vertical_flops,
+    )
     out, _ = call(
-        functools.partial(last_kernel, nedge), (along, odd, even, partial, vt), [VM] * 5,
+        functools.partial(last_kernel, nedge), (odd, arrived(along, even, partial), vt), [VM] * 3,
         [shape((levels, cols, width), BF16), columns], [HB, VM],
-        [pltpu.VMEM((levels, cols, width), BF16), DMA((1 + -(-levels // 8),))], 16, flops=edge_flops, aliases={3: 1},
+        [pltpu.VMEM((levels, cols, width), BF16), DMA((1 + -(-levels // 8),))], 16, flops=edge_flops, aliases={1: 1},
     )
     return jnp.transpose(out, (1, 0, 2))
 

time: 24.5 us -> 24.2 us (0.988)
  waiting for transfers between devices: 3.82 us -> 5.57 us
  starting transfers between devices: 7 us -> 5.26 us
  Pallas kernels: 13.5 us -> 13.2 us
    ppermute x4, starting transfers between devices: 2.2 us -> 0.45 us  [odd_or_even(): return lax.ppermute(value, (basin, blk), route)]
    ppermute x2, waiting for transfers between devices: 0.43 us -> 1.83 us  [along_basin(): return lax.ppermute(value, basin, [(i, (i + 1) % b) for i in range(b)])]
    ppermute x4, waiting for transfers between devices: 3.39 us -> 3.74 us  [odd_or_even(): return lax.ppermute(value, (basin, blk), route)]
    pallas_call x5 -> x7, Pallas kernels: 13.5 us -> 13.2 us  [call(): pl.pallas_call(kernel, out_shape=outs, in_specs=specs, out_specs=out_spec...]
  transfers between devices with their start and end apart: 6 -> 6, of which waited for: 3 -> 4; matrix products, arithmetic and copies ran while one was open for 0% -> 0% of each run, Pallas kernels for 34% -> 34%
where the time goes in v14:
time: 24.2 us; the launch traced here: 24.1 us
  Pallas kernels  13.2 us (55%)
  waiting for transfers between devices  5.57 us (23%)
  starting transfers between devices  5.26 us (22%)
    pallas_call x7, Pallas kernels, call(): pl.pallas_call(kernel, out_shape=outs, in_specs=specs, out_specs=out_spec...  13.2 us
    ppermute x2, starting transfers between devices, along_basin(): return lax.ppermute(value, basin, [(i, (i + 1) % b) for i in range(b)])  4.81 us
    ppermute x4, waiting for transfers between devices, odd_or_even(): return lax.ppermute(value, (basin, blk), route)  3.74 us
    ppermute x2, waiting for transfers between devices, along_basin(): return lax.ppermute(value, basin, [(i, (i + 1) % b) for i in range(b)])  1.83 us
  transfers between devices with their start and end apart: 6, of which 4 were waited for; matrix products, arithmetic and copies ran while one was open for 0% of the time, Pallas kernels for 34%

profile of v14, /device:TPU:0, one launch (start us, length us, event | category | flops | bytes accessed | tf_op | source)
XLA Modules:
  0.0 24.1 jit_solution(15126229271973408108)
XLA Ops:
  0.0 2.0 %shard_map.91 = (bf16[816,128]{1,0:T(8,128)(2,1)S(1)}, bf16[816,128]{1,0:T(8,128)(2,1)S(1)}, bf16[816,128]{1,0:T(8,128)(2,1)S(1)}, bf16[50,128,128]{2,1,0:T(8,12...) custom-call(bf16[50,128,128]{2,1,0:T(8,128)(2,1)} %bitcast.5, ...), custom_call_target="tpu_custom_call" | custom-call | bytes 4240128 | tf_op jit(solution)/shard_map/pallas_call | solution.py:262
  2.1 3.0 %collective-permute-start.1 = (bf16[816,128]{1,0:T(8,128)(2,1)S(1)}, bf16[816,128]{1,0:T(8,128)(2,1)S(1)}, u32[]{:S(2)}, u32[]{:S(2)}) collective-permute-start(bf16[816,128]{1,0:T(8,128)(2,1)S(1)} %get-tuple-element.23), channel_id=1, source_target_pairs={{0,16},{16,0},{1,17},{17,1},{2,18},{18,2},{3,19},{19,3},{4,20},{20... | collective-permute-start | bytes 626696 | tf_op jit(solution)/shard_map/ppermute | solution.py:285
  5.1 0.0 collective-permute-start.2
  5.1 0.2 collective-permute-start
  5.2 4.6 %shard_map.92 = (bf16[25,128,256]{2,1,0:T(8,128)(2,1)S(1)}, f32[7168,128]{1,0:T(8,128)S(1)}, bf16[128,56,128]{2,1,0:T(8,128)(2,1)S(1)}) custom-call(bf16[50,128,128]{2,1,0:T(8,128)(2,1)S(1)} %get-tuple-element.25.c_ref, s32[4,128]{1,0:T(4,128)S(1)} %get-tuple-element.26.nbr_ref, f32[50,4,128]{2,1,0:T(4,128)S(1)} %get-tuple-element.27.nw_ref, ...), custom_call_target="tpu_custom_call" | custom-call | flops 312475648 | bytes 9552384 | tf_op jit(solution)/shard_map/pallas_call | solution.py:262
  9.8 0.4 %collective-permute-done.1.r0 = bf16[816,128]{1,0:T(8,128)(2,1)S(1)} collective-permute-done((bf16[816,128]{1,0:T(8,128)(2,1)S(1)}, bf16[816,128]{1,0:T(8,128)(2,1)S(1)}, u32[]{:S(2)}, u32[]{:S(2)}) %collective-permute-start.1) | collective-permute-done | bytes 208928 | tf_op jit(solution)/shard_map/ppermute | solution.py:285
  10.2 0.0 collective-permute-done.2.r2
  10.2 0.4 %shard_map.93.local_ref = f32[7168,128]{1,0:T(8,128)S(1)} custom-call(bf16[816,128]{1,0:T(8,128)(2,1)S(1)} %collective-permute-done.1.r0, bf16[816,128]{1,0:T(8,128)(2,1)S(1)} %collective-permute-done.2.r2, f32[7168,128]{1,0:T(8,128)S(1)} %get-tuple-element.30.local_ref, ...), custom_call_target="tpu_custom_call", output_to_operand_aliasing={{}: (2, {})} | custom-call | flops 25690112 | bytes 9592832 | tf_op jit(solution)/shard_map/pallas_call | solution.py:262
  10.6 1.9 %collective-permute-done.r1 = bf16[816,128]{1,0:T(8,128)(2,1)S(1)} collective-permute-done((bf16[816,128]{1,0:T(8,128)(2,1)S(1)}, bf16[816,128]{1,0:T(8,128)(2,1)S(1)}, u32[]{:S(2)}, u32[]{:S(2)}) %collective-permute-start) | collective-permute-done | bytes 208928 | tf_op jit(solution)/shard_map/ppermute | solution.py:280
  12.5 1.4 %shard_map.94 = (f32[7168,128]{1,0:T(8,128)S(1)}, bf16[816,128]{1,0:T(8,128)(2,1)S(1)}, bf16[816,128]{1,0:T(8,128)(2,1)S(1)}, bf16[816,128]{1,0:T(8,128)(2,1)S(1)}) custom-call(bf16[816,128]{1,0:T(8,128)(2,1)S(1)} %collective-permute-done.r1, f32[7168,128]{1,0:T(8,128)S(1)} %shard_map.93.local_ref, ...), custom_call_target="tpu_custom_call", output_to_operand_aliasing={{0}: (1, {})} | custom-call | flops 12845056 | bytes 10076352 | tf_op jit(solution)/shard_map/pallas_call | solution.py:262
  13.9 1.8 %collective-permute-start.4 = (bf16[816,128]{1,0:T(8,128)(2,1)S(1)}, bf16[816,128]{1,0:T(8,128)(2,1)S(1)}, u32[]{:S(2)}, u32[]{:S(2)}) collective-permute-start(bf16[816,128]{1,0:T(8,128)(2,1)S(1)} %get-tuple-element.34), channel_id=1, source_target_pairs={{0,16},{16,0},{1,17},{17,1},{2,18},{18,2},{3,19},{19,3},{4,20},{20... | collective-permute-start | bytes 626696 | tf_op jit(solution)/shard_map/ppermute | solution.py:285
  15.7 0.0 collective-permute-start.5
  15.7 0.3 %collective-permute-start.3 = (bf16[816,128]{1,0:T(8,128)(2,1)S(1)}, bf16[816,128]{1,0:T(8,128)(2,1)S(1)}, u32[]{:S(2)}, u32[]{:S(2)}) collective-permute-start(bf16[816,128]{1,0:T(8,128)(2,1)S(1)} %get-tuple-element.33), channel_id=1, source_target_pairs={{0,16},{1,2},{2,1},{3,4},{4,3},{5,6},{6,5},{7,8},{8,7},{9,10},{10,... | collective-permute-start | bytes 626696 | tf_op jit(solution)/shard_map/ppermute | solution.py:280
  16.0 2.8 %shard_map.95.local_ref = f32[7168,128]{1,0:T(8,128)S(1)} custom-call(f32[7168,128]{1,0:T(8,128)S(1)} %get-tuple-element.36.cs, bf16[25,128,256]{2,1,0:T(8,128)(2,1)S(1)} %get-tuple-element.37.a_ref, bf16[128,56,128]{2,1,0:T(8,128)(2,1)S(1)} %get-tuple-element.31.vt_ref), custom_call_target="tpu_custom_call" | custom-call | flops 312475648 | bytes 10813440 | tf_op jit(solution)/shard_map/pallas_call | solution.py:262
  18.8 1.4 %collective-permute-done.4.r0 = bf16[816,128]{1,0:T(8,128)(2,1)S(1)} collective-permute-done((bf16[816,128]{1,0:T(8,128)(2,1)S(1)}, bf16[816,128]{1,0:T(8,128)(2,1)S(1)}, u32[]{:S(2)}, u32[]{:S(2)}) %collective-permute-start.4) | collective-permute-done | bytes 208928 | tf_op jit(solution)/shard_map/ppermute | solution.py:285
  20.3 0.0 collective-permute-done.5.r2
  20.3 0.4 %shard_map.96.local_ref = f32[7168,128]{1,0:T(8,128)S(1)} custom-call(bf16[816,128]{1,0:T(8,128)(2,1)S(1)} %collective-permute-done.4.r0, bf16[816,128]{1,0:T(8,128)(2,1)S(1)} %collective-permute-done.5.r2, f32[7168,128]{1,0:T(8,128)S(1)} %shard_map.95.local_ref, bf16[128,56,128]{2,1,0:T(8,128)(2,1)S(1)} %get-tuple-element.31.vt_ref), custom_call_target="tpu_custom_call", output_to_operand_aliasing={{}: (2, {})} | custom-call | flops 25690112 | bytes 9592832 | tf_op jit(solution)/shard_map/pallas_call | solution.py:262
  20.6 1.9 %collective-permute-done.3.r1 = bf16[816,128]{1,0:T(8,128)(2,1)S(1)} collective-permute-done((bf16[816,128]{1,0:T(8,128)(2,1)S(1)}, bf16[816,128]{1,0:T(8,128)(2,1)S(1)}, u32[]{:S(2)}, u32[]{:S(2)}) %collective-permute-start.3) | collective-permute-done | bytes 208928 | tf_op jit(solution)/shard_map/ppermute | solution.py:280
  22.5 1.6 %shard_map.97 = (bf16[50,128,128]{2,1,0:T(8,128)(2,1)}, f32[7168,128]{1,0:T(8,128)S(1)}) custom-call(bf16[816,128]{1,0:T(8,128)(2,1)S(1)} %collective-permute-done.3.r1, f32[7168,128]{1,0:T(8,128)S(1)} %shard_map.96.local_ref, bf16[128,56,128]{2,1,0:T(8,128)(2,1)S(1)} %get-tuple-element.31.vt_ref), custom_call_target="tpu_custom_call", output_to_operand_aliasing={{1}: (1, {})} | custom-call | flops 12845056 | bytes 11022336 | tf_op jit(solution)/shard_map/pallas_call | solution.py:262
Async XLA Ops:
  2.1 8.2 %collective-permute-start.1 = (bf16[816,128]{1,0:T(8,128)(2,1)S(1)}, bf16[816,128]{1,0:T(8,128)(2,1)S(1)}, u32[]{:S(2)}, u32[]{:S(2)}) collective-permute-start(bf16[816,128]{1,0:T(8,128)(2,1)S(1)} %get-tuple-element.23), channel_id=1, source_target_pairs={{0,16},{16,0},{1,17},{17,1},{2,18},{18,2},{3,19},{19,3},{4,20},{20... | collective-permute-start | bytes 626696 | tf_op jit(solution)/shard_map/ppermute | solution.py:285
  5.1 5.2 %collective-permute-start.2 = (bf16[816,128]{1,0:T(8,128)(2,1)S(1)}, bf16[816,128]{1,0:T(8,128)(2,1)S(1)}, u32[]{:S(2)}, u32[]{:S(2)}) collective-permute-start(bf16[816,128]{1,0:T(8,128)(2,1)S(1)} %get-tuple-element.24), channel_id=1, source_target_pairs={{0,1},{1,0},{2,3},{3,2},{4,5},{5,4},{6,7},{7,6},{8,9},{9,8},{10,11... | collective-permute-start | bytes 626696 | tf_op jit(solution)/shard_map/ppermute | solution.py:280
  5.1 7.4 %collective-permute-start = (bf16[816,128]{1,0:T(8,128)(2,1)S(1)}, bf16[816,128]{1,0:T(8,128)(2,1)S(1)}, u32[]{:S(2)}, u32[]{:S(2)}) collective-permute-start(bf16[816,128]{1,0:T(8,128)(2,1)S(1)} %get-tuple-element.22), channel_id=1, source_target_pairs={{0,16},{1,2},{2,1},{3,4},{4,3},{5,6},{6,5},{7,8},{8,7},{9,10},{10,... | collective-permute-start | bytes 626696 | tf_op jit(solution)/shard_map/ppermute | solution.py:280
  13.9 6.4 %collective-permute-start.4 = (bf16[816,128]{1,0:T(8,128)(2,1)S(1)}, bf16[816,128]{1,0:T(8,128)(2,1)S(1)}, u32[]{:S(2)}, u32[]{:S(2)}) collective-permute-start(bf16[816,128]{1,0:T(8,128)(2,1)S(1)} %get-tuple-element.34), channel_id=1, source_target_pairs={{0,16},{16,0},{1,17},{17,1},{2,18},{18,2},{3,19},{19,3},{4,20},{20... | collective-permute-start | bytes 626696 | tf_op jit(solution)/shard_map/ppermute | solution.py:285
  15.7 4.6 %collective-permute-start.5 = (bf16[816,128]{1,0:T(8,128)(2,1)S(1)}, bf16[816,128]{1,0:T(8,128)(2,1)S(1)}, u32[]{:S(2)}, u32[]{:S(2)}) collective-permute-start(bf16[816,128]{1,0:T(8,128)(2,1)S(1)} %get-tuple-element.35), channel_id=1, source_target_pairs={{0,1},{1,0},{2,3},{3,2},{4,5},{5,4},{6,7},{7,6},{8,9},{9,8},{10,11... | collective-permute-start | bytes 626696 | tf_op jit(solution)/shard_map/ppermute | solution.py:280
  15.7 6.8 %collective-permute-start.3 = (bf16[816,128]{1,0:T(8,128)(2,1)S(1)}, bf16[816,128]{1,0:T(8,128)(2,1)S(1)}, u32[]{:S(2)}, u32[]{:S(2)}) collective-permute-start(bf16[816,128]{1,0:T(8,128)(2,1)S(1)} %get-tuple-element.33), channel_id=1, source_target_pairs={{0,16},{1,2},{2,1},{3,4},{4,3},{5,6},{6,5},{7,8},{8,7},{9,10},{10,... | collective-permute-start | bytes 626696 | tf_op jit(solution)/shard_map/ppermute | solution.py:280

commit v15 on v14

--- a/solution.py
+++ b/solution.py
@@ -33,17 +33,15 @@
     return jnp.where(first, at + 1 < count, at > 0)
 
 
-def pack_chunk(parity, lo, levels, send, weights, rows_of, slots, outs):
+def pack_chunk(lo, levels, nedge, source, weights, rows_of, slots, outs):
     whole = whole_rows(levels)
-    nedge = send.shape[1]
     rest = levels - whole
     share = 8 // rest if rest else 0
     for slot, out in zip(slots, outs):
-        d = direction(slot, parity)
         if lo < whole:
             for e in range(nedge):
                 k = slot * nedge + e
-                value = rows_of(send[d, e], lo, 16) * weights[lo : lo + 16, k : k + 1]
+                value = rows_of(source(slot, e), lo, 16) * weights[lo : lo + 16, k : k + 1]
                 out[e * whole + lo : e * whole + lo + 16, :] = value.astype(BF16)
             continue
         sub = lax.broadcasted_iota(jnp.int32, (8, out.shape[1]), 0)
@@ -52,14 +50,16 @@
             part = None
             for q in range(share):
                 k = slot * nedge + first + q
-                value = rows_of(send[d, first + q], lo, 8) * weights[lo : lo + 8, k : k + 1]
+                value = rows_of(source(slot, first + q), lo, 8) * weights[lo : lo + 8, k : k + 1]
                 if q:
                     value = pltpu.roll(value, q * rest, 0)
                 part = value if part is None else jnp.where(sub >= q * rest, value, part)
             if share:
                 parts.append(part)
-        table = jnp.broadcast_to(weights[0:16, 3 * nedge + slot : 3 * nedge + slot + 1], (16, out.shape[1]))
-        out[nedge * whole :, :] = jnp.concatenate(parts + [table], axis=0).astype(BF16)
+        if out.shape[0] > levels * nedge:
+            parts.append(jnp.broadcast_to(weights[0:16, 3 * nedge + slot : 3 * nedge + slot + 1], (16, out.shape[1])))
+        if parts:
+            out[nedge * whole :, :] = jnp.concatenate(parts, axis=0).astype(BF16)
 
 
 def vertical(vt_ref, exs, out):
@@ -82,8 +82,8 @@
     rows = vt_ref.shape[1]
     group = max(share, 4)
     pad = jnp.zeros((8, total.shape[1]), F32)
-    for ref in edges:
-        table = ref[levels * nedge :, :].astype(F32).astype(jnp.int32)
+    for ref, first_ref in edges:
+        table = first_ref[levels * nedge :, :].astype(F32).astype(jnp.int32)
         tails = ref[whole * nedge : levels * nedge, :].astype(F32) if rest else None
         for first in range(0, nedge, group):
             targets = [table[e, 0] for e in range(first, first + group)]
@@ -104,13 +104,13 @@
 def gather_kernel(
     blk, c_h, send_h, recv_h, edge_h, nbr_h, nw_h, sw_h, wet_h,
     s0, s1, s2, c_v, nbr_v, nw_v, sw_v, wet_v, wts_o,
-    cf, wts, recv_v, edge_v, send_s, sems,
+    cf, wts, recv_v, edge_v, send_v, send_s, sems,
 ):
     levels, cols, width = c_h.shape
     nedge = edge_h.shape[1]
     pitch = cols + 8
     bounds = [(lo, min(lo + 16, levels)) for lo in range(0, levels, 16)]
-    pairs = [(send_h, send_s), (recv_h, recv_v), (edge_h, edge_v)]
+    pairs = [(send_h, send_s), (send_h, send_v), (recv_h, recv_v), (edge_h, edge_v)]
     pairs += [(c_h.at[pl.ds(lo, hi - lo)], c_v.at[pl.ds(lo, hi - lo)]) for lo, hi in bounds]
     pairs += [(nbr_h, nbr_v), (nw_h, nw_v), (sw_h, sw_v), (wet_h, wet_v)]
     copies = [pltpu.make_async_copy(a, b, sems.at[i]) for i, (a, b) in enumerate(pairs)]
@@ -118,7 +118,7 @@
         copy.start()
     parity = lax.bitwise_and(lax.axis_index(blk), jnp.int32(1))
     wts[...] = jnp.zeros_like(wts)
-    for copy in copies[:3]:
+    for copy in copies[:4]:
         copy.wait()
     for slot in range(3):
         d = direction(slot, parity)
@@ -127,17 +127,19 @@
             weight = jnp.where(has_partner(slot, lax.axis_index(blk), lax.axis_size(blk)), weight, 0.0)
         wts[slot * nedge : (slot + 1) * nedge, 0:levels] = weight
         wts[3 * nedge + slot : 3 * nedge + slot + 1, 0:nedge] = recv_v[pl.ds(d, 1), :].astype(F32)
+        wts[3 * nedge + 3 + slot : 3 * nedge + 4 + slot, 0:nedge] = send_v[pl.ds(d, 1), :].astype(F32)
     weights = wts[...].T
     wts_o[...] = weights
+    source = lambda slot, e: send_s[direction(slot, parity), e]
     rows_of = lambda s, lo, n: cf[pl.ds(lo * pitch + s, n, stride=pitch), :]
     for i, (lo, hi) in enumerate(bounds):
-        copies[3 + i].wait()
+        copies[4 + i].wait()
         for l in range(lo, hi):
             cf[l * pitch : l * pitch + cols, :] = c_v[l].astype(F32)
-        pack_chunk(parity, lo, levels, send_s, weights, rows_of, (0, 1, 2), (s0, s1, s2))
+        pack_chunk(lo, levels, nedge, source, weights, rows_of, (0, 1, 2), (s0, s1, s2))
     if levels % 16 == 0:
-        pack_chunk(parity, levels, levels, send_s, weights, rows_of, (0, 1, 2), (s0, s1, s2))
-    for copy in copies[3 + len(bounds) :]:
+        pack_chunk(levels, levels, nedge, source, weights, rows_of, (0, 1, 2), (s0, s1, s2))
+    for copy in copies[4 + len(bounds) :]:
         copy.wait()
 
 
@@ -212,23 +214,18 @@
     vertical(vt_ref, exs, state_ref)
 
 
-def arrived_kernel(levels, nedge, r0, r2, local_ref, vt_ref, total):
-    add_edges((r0, r2), levels, nedge, vt_ref, total)
-
-
-def send_kernel(blk, levels, r1, local_ref, vt_ref, wts_ref, send_h, state, s0, s1, s2, send_s, sem):
-    copy = pltpu.make_async_copy(send_h, send_s, sem)
-    copy.start()
-    add_edges((r1,), levels, send_h.shape[1], vt_ref, state)
-    copy.wait()
-    pack_state(blk, levels, send_s, wts_ref, state, vt_ref.shape[1], (0, 1, 2), (s0, s1, s2))
-
-
-def pack_state(blk, levels, send, weights, state, rows, slots, outs):
-    parity = lax.bitwise_and(lax.axis_index(blk), jnp.int32(1))
+def arrived_kernel(levels, nedge, r0, r2, t0, t2, local_ref, vt_ref, total):
+    add_edges(((r0, t0), (r2, t2)), levels, nedge, vt_ref, total)
+
+
+def send_kernel(levels, nedge, r1, local_ref, vt_ref, wts_ref, state, s0, s1, s2):
+    rows = vt_ref.shape[1]
+    add_edges(((r1, r1),), levels, nedge, vt_ref, state)
+    tables = [wts_ref[0:nedge, 3 * nedge + 3 + slot : 3 * nedge + 4 + slot].astype(jnp.int32) for slot in range(3)]
+    source = lambda slot, e: tables[slot][e, 0]
     rows_of = lambda s, lo, n: state[pl.ds(pl.multiple_of(s * rows + lo, 8), n), :]
     for lo in range(0, levels + 1, 16):
-        pack_chunk(parity, lo, levels, send, weights, rows_of, slots, outs)
+        pack_chunk(lo, levels, nedge, source, wts_ref, rows_of, (0, 1, 2), (s0, s1, s2))
 
 
 def middle_kernel(cs, a_ref, vt_ref, out_ref, exs):
@@ -237,10 +234,10 @@
     vertical(vt_ref, exs, out_ref)
 
 
-def last_kernel(nedge, r1, local_ref, vt_ref, out_h, total, out_v, sems):
+def last_kernel(nedge, r1, t1, local_ref, vt_ref, out_h, total, out_v, sems):
     levels, cols, width = out_h.shape
     rows = vt_ref.shape[1]
-    add_edges((r1,), levels, nedge, vt_ref, total)
+    add_edges(((r1, t1),), levels, nedge, vt_ref, total)
     bounds = [0, *range(4, levels, 8), levels]
     copies = []
     for i, (lo, hi) in enumerate(zip(bounds, bounds[1:])):
@@ -301,7 +298,6 @@
     message = shape((message_rows(levels, nedge), width), BF16)
     columns = shape((cols * rows, width), F32)
     flat = pltpu.VMEM(columns.shape, F32)
-    send_table = pltpu.SMEM(send_cols.shape, jnp.int32)
 
     first = call(
         functools.partial(gather_kernel, "blk"),
@@ -312,7 +308,7 @@
         [
             pltpu.VMEM((rows * (cols + 8), width), F32),
             pltpu.VMEM((128, 128), F32), pltpu.VMEM(recv_cols.shape, jnp.int32), pltpu.VMEM(edge_by_entry.shape, F32),
-            send_table, DMA((7 + -(-levels // 16),)),
+            pltpu.VMEM(send_cols.shape, jnp.int32), pltpu.SMEM(send_cols.shape, jnp.int32), DMA((8 + -(-levels // 16),)),
         ],
         16,
     )
@@ -322,10 +318,10 @@
 
     edge_flops = nedge * 2 * rows * rows * width
 
-    def arrived(along, even, partial):
+    def arrived(along, even, along_table, even_table, partial):
         return call(
-            functools.partial(arrived_kernel, levels, nedge), (along, even, partial, vt), [VM] * 4, [columns], [VM], [], 16,
-            flops=2 * edge_flops, aliases={2: 0},
+            functools.partial(arrived_kernel, levels, nedge), (along, even, along_table, even_table, partial, vt), [VM] * 6,
+            [columns], [VM], [], 16, flops=2 * edge_flops, aliases={4: 0},
         )[0]
 
     along = along_basin(to_next, "basin")
@@ -339,10 +335,11 @@
         32, flops=operator_flops + vertical_flops,
     )
     state, to_next, to_odd, to_even = call(
-        functools.partial(send_kernel, "blk", levels),
-        (odd, arrived(along, even, partial), vt, wts, send_h), [VM] * 4 + [HB],
-        [columns] + [message] * 3, [VM] * 4, [send_table, DMA], 16, flops=edge_flops, aliases={1: 0},
-    )
+        functools.partial(send_kernel, levels, nedge),
+        (odd, arrived(along, even, along, even, partial), vt, wts), [VM] * 4,
+        [columns] + [shape((levels * nedge, width), BF16)] * 3, [VM] * 4, [], 16, flops=edge_flops, aliases={1: 0},
+    )
+    tables = (along, odd, even)
     along = along_basin(to_next, "basin")
     odd = odd_or_even(to_odd, 1, "blk", "basin")
     even = odd_or_even(to_even, 0, "blk", "basin")
@@ -350,9 +347,9 @@
         middle_kernel, (state, operator, vt), [VM] * 3, [columns], [VM], [flat], 32, flops=operator_flops + vertical_flops,
     )
     out, _ = call(
-        functools.partial(last_kernel, nedge), (odd, arrived(along, even, partial), vt), [VM] * 3,
+        functools.partial(last_kernel, nedge), (odd, tables[1], arrived(along, even, tables[0], tables[2], partial), vt), [VM] * 4,
         [shape((levels, cols, width), BF16), columns], [HB, VM],
-        [pltpu.VMEM((levels, cols, width), BF16), DMA((1 + -(-levels // 8),))], 16, flops=edge_flops, aliases={1: 1},
+        [pltpu.VMEM((levels, cols, width), BF16), DMA((1 + -(-levels // 8),))], 16, flops=edge_flops, aliases={2: 1},
     )
     return jnp.transpose(out, (1, 0, 2))
 

time: 24.2 us -> 23.5 us (0.971)
  Pallas kernels: 13.2 us -> 12.6 us
    pallas_call x7, Pallas kernels: 13.2 us -> 12.6 us  [call(): pl.pallas_call(kernel, out_shape=outs, in_specs=specs, out_specs=out_spec...]
  transfers between devices with their start and end apart: 6 -> 6, of which waited for: 4 -> 4; matrix products, arithmetic and copies ran while one was open for 0% -> 0% of each run, Pallas kernels for 34% -> 35%
where the time goes in v15:
time: 23.5 us; the launch traced here: 23.3 us
  Pallas kernels  12.6 us (54%)
  waiting for transfers between devices  5.42 us (23%)
  starting transfers between devices  5.25 us (22%)
    pallas_call x7, Pallas kernels, call(): pl.pallas_call(kernel, out_shape=outs, in_specs=specs, out_specs=out_spec...  12.6 us
    ppermute x2, starting transfers between devices, along_basin(): return lax.ppermute(value, basin, [(i, (i + 1) % b) for i in range(b)])  4.81 us
    ppermute x4, waiting for transfers between devices, odd_or_even(): return lax.ppermute(value, (basin, blk), route)  3.68 us
    ppermute x2, waiting for transfers between devices, along_basin(): return lax.ppermute(value, basin, [(i, (i + 1) % b) for i in range(b)])  1.74 us
  transfers between devices with their start and end apart: 6, of which 4 were waited for; matrix products, arithmetic and copies ran while one was open for 0% of the time, Pallas kernels for 35%

profile of v15, /device:TPU:0, one launch (start us, length us, event | category | flops | bytes accessed | tf_op | source)
XLA Modules:
  0.0 23.3 jit_solution(11335215464536096199)
XLA Ops:
  0.0 2.1 %shard_map.91 = (bf16[816,128]{1,0:T(8,128)(2,1)S(1)}, bf16[816,128]{1,0:T(8,128)(2,1)S(1)}, bf16[816,128]{1,0:T(8,128)(2,1)S(1)}, bf16[50,128,128]{2,1,0:T(8,12...) custom-call(bf16[50,128,128]{2,1,0:T(8,128)(2,1)} %bitcast.5, ...), custom_call_target="tpu_custom_call" | custom-call | bytes 4240128 | tf_op jit(solution)/shard_map/pallas_call | solution.py:259
  2.1 3.0 %collective-permute-start.1 = (bf16[816,128]{1,0:T(8,128)(2,1)S(1)}, bf16[816,128]{1,0:T(8,128)(2,1)S(1)}, u32[]{:S(2)}, u32[]{:S(2)}) collective-permute-start(bf16[816,128]{1,0:T(8,128)(2,1)S(1)} %get-tuple-element.23), channel_id=1, source_target_pairs={{0,16},{16,0},{1,17},{17,1},{2,18},{18,2},{3,19},{19,3},{4,20},{20... | collective-permute-start | bytes 626696 | tf_op jit(solution)/shard_map/ppermute | solution.py:282
  5.1 0.0 collective-permute-start.2
  5.1 0.2 collective-permute-start
  5.2 4.6 %shard_map.92 = (bf16[25,128,256]{2,1,0:T(8,128)(2,1)S(1)}, f32[7168,128]{1,0:T(8,128)S(1)}, bf16[128,56,128]{2,1,0:T(8,128)(2,1)S(1)}) custom-call(bf16[50,128,128]{2,1,0:T(8,128)(2,1)S(1)} %get-tuple-element.25.c_ref, s32[4,128]{1,0:T(4,128)S(1)} %get-tuple-element.26.nbr_ref, f32[50,4,128]{2,1,0:T(4,128)S(1)} %get-tuple-element.27.nw_ref, ...), custom_call_target="tpu_custom_call" | custom-call | flops 312475648 | bytes 9552384 | tf_op jit(solution)/shard_map/pallas_call | solution.py:259
  9.9 0.4 %collective-permute-done.1.r0.t0 = bf16[816,128]{1,0:T(8,128)(2,1)S(1)} collective-permute-done((bf16[816,128]{1,0:T(8,128)(2,1)S(1)}, bf16[816,128]{1,0:T(8,128)(2,1)S(1)}, u32[]{:S(2)}, u32[]{:S(2)}) %collective-permute-start.1) | collective-permute-done | bytes 208928 | tf_op jit(solution)/shard_map/ppermute | solution.py:282
  10.2 0.0 collective-permute-done.2.r2.t2
  10.3 0.4 %shard_map.93.local_ref = f32[7168,128]{1,0:T(8,128)S(1)} custom-call(bf16[816,128]{1,0:T(8,128)(2,1)S(1)} %collective-permute-done.1.r0.t0, bf16[816,128]{1,0:T(8,128)(2,1)S(1)} %collective-permute-done.2.r2.t2, bf16[816,128]{1,0:T(8,128)(2,1)S(1)} %collective-permute-done.1.r0.t0, ...), custom_call_target="tpu_custom_call", output_to_operand_aliasing={{}: (4, {})} | custom-call | flops 25690112 | bytes 10010624 | tf_op jit(solution)/shard_map/pallas_call | solution.py:259
  10.6 1.9 %collective-permute-done.r1.t1 = bf16[816,128]{1,0:T(8,128)(2,1)S(1)} collective-permute-done((bf16[816,128]{1,0:T(8,128)(2,1)S(1)}, bf16[816,128]{1,0:T(8,128)(2,1)S(1)}, u32[]{:S(2)}, u32[]{:S(2)}) %collective-permute-start) | collective-permute-done | bytes 208928 | tf_op jit(solution)/shard_map/ppermute | solution.py:277
  12.5 0.7 %shard_map.94 = (f32[7168,128]{1,0:T(8,128)S(1)}, bf16[800,128]{1,0:T(8,128)(2,1)S(1)}, bf16[800,128]{1,0:T(8,128)(2,1)S(1)}, bf16[800,128]{1,0:T(8,128)(2,1)S(1)}) custom-call(bf16[816,128]{1,0:T(8,128)(2,1)S(1)} %collective-permute-done.r1.t1, f32[7168,128]{1,0:T(8,128)S(1)} %shard_map.93.local_ref, ...), custom_call_target="tpu_custom_call", output_to_operand_aliasing={{0}: (1, {})} | custom-call | flops 12845056 | bytes 10063872 | tf_op jit(solution)/shard_map/pallas_call | solution.py:259
  13.2 1.8 %collective-permute-start.4 = (bf16[800,128]{1,0:T(8,128)(2,1)S(1)}, bf16[800,128]{1,0:T(8,128)(2,1)S(1)}, u32[]{:S(2)}, u32[]{:S(2)}) collective-permute-start(bf16[800,128]{1,0:T(8,128)(2,1)S(1)} %get-tuple-element.34), channel_id=1, source_target_pairs={{0,16},{16,0},{1,17},{17,1},{2,18},{18,2},{3,19},{19,3},{4,20},{20... | collective-permute-start | bytes 614408 | tf_op jit(solution)/shard_map/ppermute | solution.py:282
  15.0 0.0 collective-permute-start.5
  15.0 0.3 %collective-permute-start.3 = (bf16[800,128]{1,0:T(8,128)(2,1)S(1)}, bf16[800,128]{1,0:T(8,128)(2,1)S(1)}, u32[]{:S(2)}, u32[]{:S(2)}) collective-permute-start(bf16[800,128]{1,0:T(8,128)(2,1)S(1)} %get-tuple-element.33), channel_id=1, source_target_pairs={{0,16},{1,2},{2,1},{3,4},{4,3},{5,6},{6,5},{7,8},{8,7},{9,10},{10,... | collective-permute-start | bytes 614408 | tf_op jit(solution)/shard_map/ppermute | solution.py:277
  15.3 2.8 %shard_map.95.local_ref = f32[7168,128]{1,0:T(8,128)S(1)} custom-call(f32[7168,128]{1,0:T(8,128)S(1)} %get-tuple-element.36.cs, bf16[25,128,256]{2,1,0:T(8,128)(2,1)S(1)} %get-tuple-element.37.a_ref, bf16[128,56,128]{2,1,0:T(8,128)(2,1)S(1)} %get-tuple-element.31.vt_ref), custom_call_target="tpu_custom_call" | custom-call | flops 312475648 | bytes 10813440 | tf_op jit(solution)/shard_map/pallas_call | solution.py:259
  18.1 1.4 %collective-permute-done.4.r0 = bf16[800,128]{1,0:T(8,128)(2,1)S(1)} collective-permute-done((bf16[800,128]{1,0:T(8,128)(2,1)S(1)}, bf16[800,128]{1,0:T(8,128)(2,1)S(1)}, u32[]{:S(2)}, u32[]{:S(2)}) %collective-permute-start.4) | collective-permute-done | bytes 204832 | tf_op jit(solution)/shard_map/ppermute | solution.py:282
  19.5 0.0 collective-permute-done.5.r2
  19.5 0.4 %shard_map.96.local_ref = f32[7168,128]{1,0:T(8,128)S(1)} custom-call(bf16[800,128]{1,0:T(8,128)(2,1)S(1)} %collective-permute-done.4.r0, bf16[800,128]{1,0:T(8,128)(2,1)S(1)} %collective-permute-done.5.r2, bf16[816,128]{1,0:T(8,128)(2,1)S(1)} %collective-permute-done.1.r0.t0, ...), custom_call_target="tpu_custom_call", output_to_operand_aliasing={{}: (4, {})} | custom-call | flops 25690112 | bytes 10002432 | tf_op jit(solution)/shard_map/pallas_call | solution.py:259
  19.9 1.8 %collective-permute-done.3.r1 = bf16[800,128]{1,0:T(8,128)(2,1)S(1)} collective-permute-done((bf16[800,128]{1,0:T(8,128)(2,1)S(1)}, bf16[800,128]{1,0:T(8,128)(2,1)S(1)}, u32[]{:S(2)}, u32[]{:S(2)}) %collective-permute-start.3) | collective-permute-done | bytes 204832 | tf_op jit(solution)/shard_map/ppermute | solution.py:277
  21.7 1.6 %shard_map.97 = (bf16[50,128,128]{2,1,0:T(8,128)(2,1)}, f32[7168,128]{1,0:T(8,128)S(1)}) custom-call(bf16[800,128]{1,0:T(8,128)(2,1)S(1)} %collective-permute-done.3.r1, bf16[816,128]{1,0:T(8,128)(2,1)S(1)} %collective-permute-done.r1.t1, f32[7168,128]{1,0:T(8,128)S(1)} %shard_map.96.local_ref, ...), custom_call_target="tpu_custom_call", output_to_operand_aliasing={{1}: (2, {})} | custom-call | flops 12845056 | bytes 11227136 | tf_op jit(solution)/shard_map/pallas_call | solution.py:259
Async XLA Ops:
  2.1 8.2 %collective-permute-start.1 = (bf16[816,128]{1,0:T(8,128)(2,1)S(1)}, bf16[816,128]{1,0:T(8,128)(2,1)S(1)}, u32[]{:S(2)}, u32[]{:S(2)}) collective-permute-start(bf16[816,128]{1,0:T(8,128)(2,1)S(1)} %get-tuple-element.23), channel_id=1, source_target_pairs={{0,16},{16,0},{1,17},{17,1},{2,18},{18,2},{3,19},{19,3},{4,20},{20... | collective-permute-start | bytes 626696 | tf_op jit(solution)/shard_map/ppermute | solution.py:282
  5.1 5.2 %collective-permute-start.2 = (bf16[816,128]{1,0:T(8,128)(2,1)S(1)}, bf16[816,128]{1,0:T(8,128)(2,1)S(1)}, u32[]{:S(2)}, u32[]{:S(2)}) collective-permute-start(bf16[816,128]{1,0:T(8,128)(2,1)S(1)} %get-tuple-element.24), channel_id=1, source_target_pairs={{0,1},{1,0},{2,3},{3,2},{4,5},{5,4},{6,7},{7,6},{8,9},{9,8},{10,11... | collective-permute-start | bytes 626696 | tf_op jit(solution)/shard_map/ppermute | solution.py:277
  5.1 7.4 %collective-permute-start = (bf16[816,128]{1,0:T(8,128)(2,1)S(1)}, bf16[816,128]{1,0:T(8,128)(2,1)S(1)}, u32[]{:S(2)}, u32[]{:S(2)}) collective-permute-start(bf16[816,128]{1,0:T(8,128)(2,1)S(1)} %get-tuple-element.22), channel_id=1, source_target_pairs={{0,16},{1,2},{2,1},{3,4},{4,3},{5,6},{6,5},{7,8},{8,7},{9,10},{10,... | collective-permute-start | bytes 626696 | tf_op jit(solution)/shard_map/ppermute | solution.py:277
  13.2 6.3 %collective-permute-start.4 = (bf16[800,128]{1,0:T(8,128)(2,1)S(1)}, bf16[800,128]{1,0:T(8,128)(2,1)S(1)}, u32[]{:S(2)}, u32[]{:S(2)}) collective-permute-start(bf16[800,128]{1,0:T(8,128)(2,1)S(1)} %get-tuple-element.34), channel_id=1, source_target_pairs={{0,16},{16,0},{1,17},{17,1},{2,18},{18,2},{3,19},{19,3},{4,20},{20... | collective-permute-start | bytes 614408 | tf_op jit(solution)/shard_map/ppermute | solution.py:282
  15.0 4.5 %collective-permute-start.5 = (bf16[800,128]{1,0:T(8,128)(2,1)S(1)}, bf16[800,128]{1,0:T(8,128)(2,1)S(1)}, u32[]{:S(2)}, u32[]{:S(2)}) collective-permute-start(bf16[800,128]{1,0:T(8,128)(2,1)S(1)} %get-tuple-element.35), channel_id=1, source_target_pairs={{0,1},{1,0},{2,3},{3,2},{4,5},{5,4},{6,7},{7,6},{8,9},{9,8},{10,11... | collective-permute-start | bytes 614408 | tf_op jit(solution)/shard_map/ppermute | solution.py:277
  15.0 6.7 %collective-permute-start.3 = (bf16[800,128]{1,0:T(8,128)(2,1)S(1)}, bf16[800,128]{1,0:T(8,128)(2,1)S(1)}, u32[]{:S(2)}, u32[]{:S(2)}) collective-permute-start(bf16[800,128]{1,0:T(8,128)(2,1)S(1)} %get-tuple-element.33), channel_id=1, source_target_pairs={{0,16},{1,2},{2,1},{3,4},{4,3},{5,6},{6,5},{7,8},{8,7},{9,10},{10,... | collective-permute-start | bytes 614408 | tf_op jit(solution)/shard_map/ppermute | solution.py:277

commit v16 on v15

--- a/solution.py
+++ b/solution.py
@@ -31,6 +31,12 @@
 def has_partner(slot, at, count):
     first = lax.bitwise_and(at + slot // 2, jnp.int32(1)) == 1
     return jnp.where(first, at + 1 < count, at > 0)
+
+
+def source_columns(weights, nedge):
+    tables = [weights[0:nedge, 3 * nedge + 3 + slot : 3 * nedge + 4 + slot].astype(jnp.int32) for slot in range(3)]
+    columns = [[table[e, 0] for e in range(nedge)] for table in tables]
+    return lambda slot, e: columns[slot][e]
 
 
 def pack_chunk(lo, levels, nedge, source, weights, rows_of, slots, outs):
@@ -104,13 +110,13 @@
 def gather_kernel(
     blk, c_h, send_h, recv_h, edge_h, nbr_h, nw_h, sw_h, wet_h,
     s0, s1, s2, c_v, nbr_v, nw_v, sw_v, wet_v, wts_o,
-    cf, wts, recv_v, edge_v, send_v, send_s, sems,
+    cf, wts, recv_v, edge_v, send_v, sems,
 ):
     levels, cols, width = c_h.shape
     nedge = edge_h.shape[1]
     pitch = cols + 8
     bounds = [(lo, min(lo + 16, levels)) for lo in range(0, levels, 16)]
-    pairs = [(send_h, send_s), (send_h, send_v), (recv_h, recv_v), (edge_h, edge_v)]
+    pairs = [(send_h, send_v), (recv_h, recv_v), (edge_h, edge_v)]
     pairs += [(c_h.at[pl.ds(lo, hi - lo)], c_v.at[pl.ds(lo, hi - lo)]) for lo, hi in bounds]
     pairs += [(nbr_h, nbr_v), (nw_h, nw_v), (sw_h, sw_v), (wet_h, wet_v)]
     copies = [pltpu.make_async_copy(a, b, sems.at[i]) for i, (a, b) in enumerate(pairs)]
@@ -118,7 +124,7 @@
         copy.start()
     parity = lax.bitwise_and(lax.axis_index(blk), jnp.int32(1))
     wts[...] = jnp.zeros_like(wts)
-    for copy in copies[:4]:
+    for copy in copies[:3]:
         copy.wait()
     for slot in range(3):
         d = direction(slot, parity)
@@ -130,16 +136,16 @@
         wts[3 * nedge + 3 + slot : 3 * nedge + 4 + slot, 0:nedge] = send_v[pl.ds(d, 1), :].astype(F32)
     weights = wts[...].T
     wts_o[...] = weights
-    source = lambda slot, e: send_s[direction(slot, parity), e]
+    source = source_columns(weights, nedge)
     rows_of = lambda s, lo, n: cf[pl.ds(lo * pitch + s, n, stride=pitch), :]
     for i, (lo, hi) in enumerate(bounds):
-        copies[4 + i].wait()
+        copies[3 + i].wait()
         for l in range(lo, hi):
             cf[l * pitch : l * pitch + cols, :] = c_v[l].astype(F32)
         pack_chunk(lo, levels, nedge, source, weights, rows_of, (0, 1, 2), (s0, s1, s2))
     if levels % 16 == 0:
         pack_chunk(levels, levels, nedge, source, weights, rows_of, (0, 1, 2), (s0, s1, s2))
-    for copy in copies[4 + len(bounds) :]:
+    for copy in copies[3 + len(bounds) :]:
         copy.wait()
 
 
@@ -221,8 +227,7 @@
 def send_kernel(levels, nedge, r1, local_ref, vt_ref, wts_ref, state, s0, s1, s2):
     rows = vt_ref.shape[1]
     add_edges(((r1, r1),), levels, nedge, vt_ref, state)
-    tables = [wts_ref[0:nedge, 3 * nedge + 3 + slot : 3 * nedge + 4 + slot].astype(jnp.int32) for slot in range(3)]
-    source = lambda slot, e: tables[slot][e, 0]
+    source = source_columns(wts_ref, nedge)
     rows_of = lambda s, lo, n: state[pl.ds(pl.multiple_of(s * rows + lo, 8), n), :]
     for lo in range(0, levels + 1, 16):
         pack_chunk(lo, levels, nedge, source, wts_ref, rows_of, (0, 1, 2), (s0, s1, s2))
@@ -308,7 +313,7 @@
         [
             pltpu.VMEM((rows * (cols + 8), width), F32),
             pltpu.VMEM((128, 128), F32), pltpu.VMEM(recv_cols.shape, jnp.int32), pltpu.VMEM(edge_by_entry.shape, F32),
-            pltpu.VMEM(send_cols.shape, jnp.int32), pltpu.SMEM(send_cols.shape, jnp.int32), DMA((8 + -(-levels // 16),)),
+            pltpu.VMEM(send_cols.shape, jnp.int32), DMA((7 + -(-levels // 16),)),
         ],
         16,
     )

time: 23.5 us -> 23.5 us (level)
  no operation moved by 1% of the time
where the time goes in v16:
time: 23.5 us; the launch traced here: 23.3 us
  Pallas kernels  12.5 us (53%)
  waiting for transfers between devices  5.46 us (23%)
  starting transfers between devices  5.26 us (22%)
    pallas_call x7, Pallas kernels, call(): pl.pallas_call(kernel, out_shape=outs, in_specs=specs, out_specs=out_spec...  12.5 us
    ppermute x2, starting transfers between devices, along_basin(): return lax.ppermute(value, basin, [(i, (i + 1) % b) for i in range(b)])  4.81 us
    ppermute x4, waiting for transfers between devices, odd_or_even(): return lax.ppermute(value, (basin, blk), route)  3.7 us
    ppermute x2, waiting for transfers between devices, along_basin(): return lax.ppermute(value, basin, [(i, (i + 1) % b) for i in range(b)])  1.76 us
  transfers between devices with their start and end apart: 6, of which 4 were waited for; matrix products, arithmetic and copies ran while one was open for 0% of the time, Pallas kernels for 35%

profile of v16, /device:TPU:0, one launch (start us, length us, event | category | flops | bytes accessed | tf_op | source)
XLA Modules:
  0.0 23.3 jit_solution(12326448142750851329)
XLA Ops:
  0.0 2.1 %shard_map.91 = (bf16[816,128]{1,0:T(8,128)(2,1)S(1)}, bf16[816,128]{1,0:T(8,128)(2,1)S(1)}, bf16[816,128]{1,0:T(8,128)(2,1)S(1)}, bf16[50,128,128]{2,1,0:T(8,12...) custom-call(bf16[50,128,128]{2,1,0:T(8,128)(2,1)} %bitcast.5, ...), custom_call_target="tpu_custom_call" | custom-call | bytes 4240128 | tf_op jit(solution)/shard_map/pallas_call | solution.py:264
  2.1 3.0 %collective-permute-start.1 = (bf16[816,128]{1,0:T(8,128)(2,1)S(1)}, bf16[816,128]{1,0:T(8,128)(2,1)S(1)}, u32[]{:S(2)}, u32[]{:S(2)}) collective-permute-start(bf16[816,128]{1,0:T(8,128)(2,1)S(1)} %get-tuple-element.23), channel_id=1, source_target_pairs={{0,16},{16,0},{1,17},{17,1},{2,18},{18,2},{3,19},{19,3},{4,20},{20... | collective-permute-start | bytes 626696 | tf_op jit(solution)/shard_map/ppermute | solution.py:287
  5.1 0.0 collective-permute-start.2
  5.1 0.2 collective-permute-start
  5.2 4.6 %shard_map.92 = (bf16[25,128,256]{2,1,0:T(8,128)(2,1)S(1)}, f32[7168,128]{1,0:T(8,128)S(1)}, bf16[128,56,128]{2,1,0:T(8,128)(2,1)S(1)}) custom-call(bf16[50,128,128]{2,1,0:T(8,128)(2,1)S(1)} %get-tuple-element.25.c_ref, s32[4,128]{1,0:T(4,128)S(1)} %get-tuple-element.26.nbr_ref, f32[50,4,128]{2,1,0:T(4,128)S(1)} %get-tuple-element.27.nw_ref, ...), custom_call_target="tpu_custom_call" | custom-call | flops 312475648 | bytes 9552384 | tf_op jit(solution)/shard_map/pallas_call | solution.py:264
  9.9 0.4 %collective-permute-done.1.r0.t0 = bf16[816,128]{1,0:T(8,128)(2,1)S(1)} collective-permute-done((bf16[816,128]{1,0:T(8,128)(2,1)S(1)}, bf16[816,128]{1,0:T(8,128)(2,1)S(1)}, u32[]{:S(2)}, u32[]{:S(2)}) %collective-permute-start.1) | collective-permute-done | bytes 208928 | tf_op jit(solution)/shard_map/ppermute | solution.py:287
  10.2 0.0 collective-permute-done.2.r2.t2
  10.2 0.4 %shard_map.93.local_ref = f32[7168,128]{1,0:T(8,128)S(1)} custom-call(bf16[816,128]{1,0:T(8,128)(2,1)S(1)} %collective-permute-done.1.r0.t0, bf16[816,128]{1,0:T(8,128)(2,1)S(1)} %collective-permute-done.2.r2.t2, bf16[816,128]{1,0:T(8,128)(2,1)S(1)} %collective-permute-done.1.r0.t0, ...), custom_call_target="tpu_custom_call", output_to_operand_aliasing={{}: (4, {})} | custom-call | flops 25690112 | bytes 10010624 | tf_op jit(solution)/shard_map/pallas_call | solution.py:264
  10.6 1.9 %collective-permute-done.r1.t1 = bf16[816,128]{1,0:T(8,128)(2,1)S(1)} collective-permute-done((bf16[816,128]{1,0:T(8,128)(2,1)S(1)}, bf16[816,128]{1,0:T(8,128)(2,1)S(1)}, u32[]{:S(2)}, u32[]{:S(2)}) %collective-permute-start) | collective-permute-done | bytes 208928 | tf_op jit(solution)/shard_map/ppermute | solution.py:282
  12.5 0.7 %shard_map.94 = (f32[7168,128]{1,0:T(8,128)S(1)}, bf16[800,128]{1,0:T(8,128)(2,1)S(1)}, bf16[800,128]{1,0:T(8,128)(2,1)S(1)}, bf16[800,128]{1,0:T(8,128)(2,1)S(1)}) custom-call(bf16[816,128]{1,0:T(8,128)(2,1)S(1)} %collective-permute-done.r1.t1, f32[7168,128]{1,0:T(8,128)S(1)} %shard_map.93.local_ref, ...), custom_call_target="tpu_custom_call", output_to_operand_aliasing={{0}: (1, {})} | custom-call | flops 12845056 | bytes 10063872 | tf_op jit(solution)/shard_map/pallas_call | solution.py:264
  13.2 1.8 %collective-permute-start.4 = (bf16[800,128]{1,0:T(8,128)(2,1)S(1)}, bf16[800,128]{1,0:T(8,128)(2,1)S(1)}, u32[]{:S(2)}, u32[]{:S(2)}) collective-permute-start(bf16[800,128]{1,0:T(8,128)(2,1)S(1)} %get-tuple-element.34), channel_id=1, source_target_pairs={{0,16},{16,0},{1,17},{17,1},{2,18},{18,2},{3,19},{19,3},{4,20},{20... | collective-permute-start | bytes 614408 | tf_op jit(solution)/shard_map/ppermute | solution.py:287
  15.0 0.0 collective-permute-start.5
  15.0 0.3 %collective-permute-start.3 = (bf16[800,128]{1,0:T(8,128)(2,1)S(1)}, bf16[800,128]{1,0:T(8,128)(2,1)S(1)}, u32[]{:S(2)}, u32[]{:S(2)}) collective-permute-start(bf16[800,128]{1,0:T(8,128)(2,1)S(1)} %get-tuple-element.33), channel_id=1, source_target_pairs={{0,16},{1,2},{2,1},{3,4},{4,3},{5,6},{6,5},{7,8},{8,7},{9,10},{10,... | collective-permute-start | bytes 614408 | tf_op jit(solution)/shard_map/ppermute | solution.py:282
  15.3 2.8 %shard_map.95.local_ref = f32[7168,128]{1,0:T(8,128)S(1)} custom-call(f32[7168,128]{1,0:T(8,128)S(1)} %get-tuple-element.36.cs, bf16[25,128,256]{2,1,0:T(8,128)(2,1)S(1)} %get-tuple-element.37.a_ref, bf16[128,56,128]{2,1,0:T(8,128)(2,1)S(1)} %get-tuple-element.31.vt_ref), custom_call_target="tpu_custom_call" | custom-call | flops 312475648 | bytes 10813440 | tf_op jit(solution)/shard_map/pallas_call | solution.py:264
  18.1 1.4 %collective-permute-done.4.r0 = bf16[800,128]{1,0:T(8,128)(2,1)S(1)} collective-permute-done((bf16[800,128]{1,0:T(8,128)(2,1)S(1)}, bf16[800,128]{1,0:T(8,128)(2,1)S(1)}, u32[]{:S(2)}, u32[]{:S(2)}) %collective-permute-start.4) | collective-permute-done | bytes 204832 | tf_op jit(solution)/shard_map/ppermute | solution.py:287
  19.5 0.0 collective-permute-done.5.r2
  19.5 0.4 %shard_map.96.local_ref = f32[7168,128]{1,0:T(8,128)S(1)} custom-call(bf16[800,128]{1,0:T(8,128)(2,1)S(1)} %collective-permute-done.4.r0, bf16[800,128]{1,0:T(8,128)(2,1)S(1)} %collective-permute-done.5.r2, bf16[816,128]{1,0:T(8,128)(2,1)S(1)} %collective-permute-done.1.r0.t0, ...), custom_call_target="tpu_custom_call", output_to_operand_aliasing={{}: (4, {})} | custom-call | flops 25690112 | bytes 10002432 | tf_op jit(solution)/shard_map/pallas_call | solution.py:264
  19.9 1.8 %collective-permute-done.3.r1 = bf16[800,128]{1,0:T(8,128)(2,1)S(1)} collective-permute-done((bf16[800,128]{1,0:T(8,128)(2,1)S(1)}, bf16[800,128]{1,0:T(8,128)(2,1)S(1)}, u32[]{:S(2)}, u32[]{:S(2)}) %collective-permute-start.3) | collective-permute-done | bytes 204832 | tf_op jit(solution)/shard_map/ppermute | solution.py:282
  21.7 1.6 %shard_map.97 = (bf16[50,128,128]{2,1,0:T(8,128)(2,1)}, f32[7168,128]{1,0:T(8,128)S(1)}) custom-call(bf16[800,128]{1,0:T(8,128)(2,1)S(1)} %collective-permute-done.3.r1, bf16[816,128]{1,0:T(8,128)(2,1)S(1)} %collective-permute-done.r1.t1, f32[7168,128]{1,0:T(8,128)S(1)} %shard_map.96.local_ref, ...), custom_call_target="tpu_custom_call", output_to_operand_aliasing={{1}: (2, {})} | custom-call | flops 12845056 | bytes 11227136 | tf_op jit(solution)/shard_map/pallas_call | solution.py:264
Async XLA Ops:
  2.1 8.2 %collective-permute-start.1 = (bf16[816,128]{1,0:T(8,128)(2,1)S(1)}, bf16[816,128]{1,0:T(8,128)(2,1)S(1)}, u32[]{:S(2)}, u32[]{:S(2)}) collective-permute-start(bf16[816,128]{1,0:T(8,128)(2,1)S(1)} %get-tuple-element.23), channel_id=1, source_target_pairs={{0,16},{16,0},{1,17},{17,1},{2,18},{18,2},{3,19},{19,3},{4,20},{20... | collective-permute-start | bytes 626696 | tf_op jit(solution)/shard_map/ppermute | solution.py:287
  5.1 5.2 %collective-permute-start.2 = (bf16[816,128]{1,0:T(8,128)(2,1)S(1)}, bf16[816,128]{1,0:T(8,128)(2,1)S(1)}, u32[]{:S(2)}, u32[]{:S(2)}) collective-permute-start(bf16[816,128]{1,0:T(8,128)(2,1)S(1)} %get-tuple-element.24), channel_id=1, source_target_pairs={{0,1},{1,0},{2,3},{3,2},{4,5},{5,4},{6,7},{7,6},{8,9},{9,8},{10,11... | collective-permute-start | bytes 626696 | tf_op jit(solution)/shard_map/ppermute | solution.py:282
  5.1 7.4 %collective-permute-start = (bf16[816,128]{1,0:T(8,128)(2,1)S(1)}, bf16[816,128]{1,0:T(8,128)(2,1)S(1)}, u32[]{:S(2)}, u32[]{:S(2)}) collective-permute-start(bf16[816,128]{1,0:T(8,128)(2,1)S(1)} %get-tuple-element.22), channel_id=1, source_target_pairs={{0,16},{1,2},{2,1},{3,4},{4,3},{5,6},{6,5},{7,8},{8,7},{9,10},{10,... | collective-permute-start | bytes 626696 | tf_op jit(solution)/shard_map/ppermute | solution.py:282
  13.2 6.3 %collective-permute-start.4 = (bf16[800,128]{1,0:T(8,128)(2,1)S(1)}, bf16[800,128]{1,0:T(8,128)(2,1)S(1)}, u32[]{:S(2)}, u32[]{:S(2)}) collective-permute-start(bf16[800,128]{1,0:T(8,128)(2,1)S(1)} %get-tuple-element.34), channel_id=1, source_target_pairs={{0,16},{16,0},{1,17},{17,1},{2,18},{18,2},{3,19},{19,3},{4,20},{20... | collective-permute-start | bytes 614408 | tf_op jit(solution)/shard_map/ppermute | solution.py:287
  15.0 4.5 %collective-permute-start.5 = (bf16[800,128]{1,0:T(8,128)(2,1)S(1)}, bf16[800,128]{1,0:T(8,128)(2,1)S(1)}, u32[]{:S(2)}, u32[]{:S(2)}) collective-permute-start(bf16[800,128]{1,0:T(8,128)(2,1)S(1)} %get-tuple-element.35), channel_id=1, source_target_pairs={{0,1},{1,0},{2,3},{3,2},{4,5},{5,4},{6,7},{7,6},{8,9},{9,8},{10,11... | collective-permute-start | bytes 614408 | tf_op jit(solution)/shard_map/ppermute | solution.py:282
  15.0 6.7 %collective-permute-start.3 = (bf16[800,128]{1,0:T(8,128)(2,1)S(1)}, bf16[800,128]{1,0:T(8,128)(2,1)S(1)}, u32[]{:S(2)}, u32[]{:S(2)}) collective-permute-start(bf16[800,128]{1,0:T(8,128)(2,1)S(1)} %get-tuple-element.33), channel_id=1, source_target_pairs={{0,16},{1,2},{2,1},{3,4},{4,3},{5,6},{6,5},{7,8},{8,7},{9,10},{10,... | collective-permute-start | bytes 614408 | tf_op jit(solution)/shard_map/ppermute | solution.py:282

commit v17 on v16

--- a/solution.py
+++ b/solution.py
@@ -81,7 +81,7 @@
     lax.fori_loop(0, cols, column, 0, unroll=16)
 
 
-def add_edges(edges, levels, nedge, vt_ref, total):
+def add_edges(edges, levels, nedge, vt_ref, total, place=None):
     whole = whole_rows(levels)
     rest = levels - whole
     share = 8 // rest if rest else 0
@@ -103,7 +103,7 @@
                     x = jnp.concatenate([x, jnp.concatenate([tail, pad], axis=0).astype(BF16)], axis=0)
                 products.append(jnp.dot(vt_ref[j][:, 0 : x.shape[0]], x, preferred_element_type=F32))
             for j, part in zip(targets, products):
-                at = pl.ds(pl.multiple_of(j * rows, 8), rows)
+                at = place(j) if place else pl.ds(pl.multiple_of(j * rows, 8), rows)
                 total[at, :] = total[at, :] + part
 
 
@@ -117,7 +117,8 @@
     pitch = cols + 8
     bounds = [(lo, min(lo + 16, levels)) for lo in range(0, levels, 16)]
     pairs = [(send_h, send_v), (recv_h, recv_v), (edge_h, edge_v)]
-    pairs += [(c_h.at[pl.ds(lo, hi - lo)], c_v.at[pl.ds(lo, hi - lo)]) for lo, hi in bounds]
+    pieces = [(lo, min(lo + 4, levels)) for lo in range(0, levels, 4)]
+    pairs += [(c_h.at[pl.ds(lo, hi - lo)], c_v.at[pl.ds(lo, hi - lo)]) for lo, hi in pieces]
     pairs += [(nbr_h, nbr_v), (nw_h, nw_v), (sw_h, sw_v), (wet_h, wet_v)]
     copies = [pltpu.make_async_copy(a, b, sems.at[i]) for i, (a, b) in enumerate(pairs)]
     for copy in copies:
@@ -138,14 +139,16 @@
     wts_o[...] = weights
     source = source_columns(weights, nedge)
     rows_of = lambda s, lo, n: cf[pl.ds(lo * pitch + s, n, stride=pitch), :]
-    for i, (lo, hi) in enumerate(bounds):
-        copies[3 + i].wait()
-        for l in range(lo, hi):
-            cf[l * pitch : l * pitch + cols, :] = c_v[l].astype(F32)
+    for lo, hi in bounds:
+        for i, (first, last) in enumerate(pieces):
+            if lo <= first < hi:
+                copies[3 + i].wait()
+                for l in range(first, last):
+                    cf[l * pitch : l * pitch + cols, :] = c_v[l].astype(F32)
         pack_chunk(lo, levels, nedge, source, weights, rows_of, (0, 1, 2), (s0, s1, s2))
     if levels % 16 == 0:
         pack_chunk(levels, levels, nedge, source, weights, rows_of, (0, 1, 2), (s0, s1, s2))
-    for copy in copies[3 + len(bounds) :]:
+    for copy in copies[3 + len(pieces) :]:
         copy.wait()
 
 
@@ -224,6 +227,14 @@
     add_edges(((r0, t0), (r2, t2)), levels, nedge, vt_ref, total)
 
 
+def turned_kernel(levels, nedge, r0, r2, t0, t2, local_ref, vt_ref, total, by_level):
+    cols, rows, _ = vt_ref.shape
+    pitch = cols + 8
+    add_edges(((r0, t0), (r2, t2)), levels, nedge, vt_ref, total)
+    for l in range(rows):
+        by_level[l * pitch : l * pitch + cols, :] = total[pl.ds(l, cols, stride=rows), :]
+
+
 def send_kernel(levels, nedge, r1, local_ref, vt_ref, wts_ref, state, s0, s1, s2):
     rows = vt_ref.shape[1]
     add_edges(((r1, r1),), levels, nedge, vt_ref, state)
@@ -239,15 +250,16 @@
     vertical(vt_ref, exs, out_ref)
 
 
-def last_kernel(nedge, r1, t1, local_ref, vt_ref, out_h, total, out_v, sems):
+def last_kernel(nedge, r1, t1, local_ref, vt_ref, out_h, by_level, out_v, sems):
     levels, cols, width = out_h.shape
     rows = vt_ref.shape[1]
-    add_edges(((r1, t1),), levels, nedge, vt_ref, total)
+    pitch = cols + 8
+    add_edges(((r1, t1),), levels, nedge, vt_ref, by_level, lambda j: pl.ds(j, rows, stride=pitch))
     bounds = [0, *range(4, levels, 8), levels]
     copies = []
     for i, (lo, hi) in enumerate(zip(bounds, bounds[1:])):
         for l in range(lo, hi):
-            out_v[l] = total[pl.ds(l, cols, stride=rows), :].astype(BF16)
+            out_v[l] = by_level[l * pitch : l * pitch + cols, :].astype(BF16)
         copies.append(pltpu.make_async_copy(out_v.at[pl.ds(lo, hi - lo)], out_h.at[pl.ds(lo, hi - lo)], sems.at[i]))
         copies[-1].start()
     for copy in copies:
@@ -313,7 +325,7 @@
         [
             pltpu.VMEM((rows * (cols + 8), width), F32),
             pltpu.VMEM((128, 128), F32), pltpu.VMEM(recv_cols.shape, jnp.int32), pltpu.VMEM(edge_by_entry.shape, F32),
-            pltpu.VMEM(send_cols.shape, jnp.int32), DMA((7 + -(-levels // 16),)),
+            pltpu.VMEM(send_cols.shape, jnp.int32), DMA((7 + -(-levels // 4),)),
         ],
         16,
     )
@@ -322,12 +334,6 @@
     vertical_flops = 2 * cols * rows * rows * width
 
     edge_flops = nedge * 2 * rows * rows * width
-
-    def arrived(along, even, along_table, even_table, partial):
-        return call(
-            functools.partial(arrived_kernel, levels, nedge), (along, even, along_table, even_table, partial, vt), [VM] * 6,
-            [columns], [VM], [], 16, flops=2 * edge_flops, aliases={4: 0},
-        )[0]
 
     along = along_basin(to_next, "basin")
     odd = odd_or_even(to_odd, 1, "blk", "basin")
@@ -339,9 +345,13 @@
          pltpu.VMEM(vert_inv.shape, BF16), DMA],
         32, flops=operator_flops + vertical_flops,
     )
+    (partial,) = call(
+        functools.partial(arrived_kernel, levels, nedge), (along, even, along, even, partial, vt), [VM] * 6,
+        [columns], [VM], [], 16, flops=2 * edge_flops, aliases={4: 0},
+    )
     state, to_next, to_odd, to_even = call(
         functools.partial(send_kernel, levels, nedge),
-        (odd, arrived(along, even, along, even, partial), vt, wts), [VM] * 4,
+        (odd, partial, vt, wts), [VM] * 4,
         [columns] + [shape((levels * nedge, width), BF16)] * 3, [VM] * 4, [], 16, flops=edge_flops, aliases={1: 0},
     )
     tables = (along, odd, even)
@@ -351,9 +361,14 @@
     (partial,) = call(
         middle_kernel, (state, operator, vt), [VM] * 3, [columns], [VM], [flat], 32, flops=operator_flops + vertical_flops,
     )
+    turned = shape((rows * (cols + 8), width), F32)
+    _, by_level = call(
+        functools.partial(turned_kernel, levels, nedge), (along, even, tables[0], tables[2], partial, vt), [VM] * 6,
+        [columns, turned], [VM] * 2, [], 16, flops=2 * edge_flops, aliases={4: 0},
+    )
     out, _ = call(
-        functools.partial(last_kernel, nedge), (odd, tables[1], arrived(along, even, tables[0], tables[2], partial), vt), [VM] * 4,
-        [shape((levels, cols, width), BF16), columns], [HB, VM],
+        functools.partial(last_kernel, nedge), (odd, tables[1], by_level, vt), [VM] * 4,
+        [shape((levels, cols, width), BF16), turned], [HB, VM],
         [pltpu.VMEM((levels, cols, width), BF16), DMA((1 + -(-levels // 8),))], 16, flops=edge_flops, aliases={2: 1},
     )
     return jnp.transpose(out, (1, 0, 2))

time: 23.5 us -> 23.6 us (level)
  Pallas kernels: 12.5 us -> 13.4 us
  waiting for transfers between devices: 5.46 us -> 4.82 us
    pallas_call x7, Pallas kernels: 12.5 us -> 13.4 us  [call(): pl.pallas_call(kernel, out_shape=outs, in_specs=specs, out_specs=out_spec...]
    ppermute x4, waiting for transfers between devices: 3.7 us -> 3.06 us  [odd_or_even(): return lax.ppermute(value, (basin, blk), route)]
  transfers between devices with their start and end apart: 6 -> 6, of which waited for: 4 -> 4; matrix products, arithmetic and copies ran while one was open for 0% -> 0% of each run, Pallas kernels for 35% -> 37%
where the time goes in v17:
time: 23.6 us; the launch traced here: 23.5 us
  Pallas kernels  13.4 us (57%)
  starting transfers between devices  5.25 us (22%)
  waiting for transfers between devices  4.82 us (20%)
    pallas_call x7, Pallas kernels, call(): pl.pallas_call(kernel, out_shape=outs, in_specs=specs, out_specs=out_spec...  13.4 us
    ppermute x2, starting transfers between devices, along_basin(): return lax.ppermute(value, basin, [(i, (i + 1) % b) for i in range(b)])  4.82 us
    ppermute x4, waiting for transfers between devices, odd_or_even(): return lax.ppermute(value, (basin, blk), route)  3.06 us
    ppermute x2, waiting for transfers between devices, along_basin(): return lax.ppermute(value, basin, [(i, (i + 1) % b) for i in range(b)])  1.76 us
  transfers between devices with their start and end apart: 6, of which 4 were waited for; matrix products, arithmetic and copies ran while one was open for 0% of the time, Pallas kernels for 37%

profile of v17, /device:TPU:0, one launch (start us, length us, event | category | flops | bytes accessed | tf_op | source)
XLA Modules:
  0.0 23.5 jit_solution(3846685238254235008)
XLA Ops:
  0.0 2.3 %shard_map.91 = (bf16[816,128]{1,0:T(8,128)(2,1)S(1)}, bf16[816,128]{1,0:T(8,128)(2,1)S(1)}, bf16[816,128]{1,0:T(8,128)(2,1)S(1)}, bf16[50,128,128]{2,1,0:T(8,12...) custom-call(bf16[50,128,128]{2,1,0:T(8,128)(2,1)} %bitcast.5, ...), custom_call_target="tpu_custom_call" | custom-call | bytes 4240128 | tf_op jit(solution)/shard_map/pallas_call | solution.py:276
  2.3 3.0 %collective-permute-start.1 = (bf16[816,128]{1,0:T(8,128)(2,1)S(1)}, bf16[816,128]{1,0:T(8,128)(2,1)S(1)}, u32[]{:S(2)}, u32[]{:S(2)}) collective-permute-start(bf16[816,128]{1,0:T(8,128)(2,1)S(1)} %get-tuple-element.24), channel_id=1, source_target_pairs={{0,16},{16,0},{1,17},{17,1},{2,18},{18,2},{3,19},{19,3},{4,20},{20... | collective-permute-start | bytes 626696 | tf_op jit(solution)/shard_map/ppermute | solution.py:299
  5.3 0.0 collective-permute-start.2
  5.3 0.2 collective-permute-start
  5.4 4.6 %shard_map.92 = (bf16[25,128,256]{2,1,0:T(8,128)(2,1)S(1)}, f32[7168,128]{1,0:T(8,128)S(1)}, bf16[128,56,128]{2,1,0:T(8,128)(2,1)S(1)}) custom-call(bf16[50,128,128]{2,1,0:T(8,128)(2,1)S(1)} %get-tuple-element.26.c_ref, s32[4,128]{1,0:T(4,128)S(1)} %get-tuple-element.27.nbr_ref, f32[50,4,128]{2,1,0:T(4,128)S(1)} %get-tuple-element.28.nw_ref, ...), custom_call_target="tpu_custom_call" | custom-call | flops 312475648 | bytes 9552384 | tf_op jit(solution)/shard_map/pallas_call | solution.py:276
  10.1 0.4 %collective-permute-done.1.r0.t0 = bf16[816,128]{1,0:T(8,128)(2,1)S(1)} collective-permute-done((bf16[816,128]{1,0:T(8,128)(2,1)S(1)}, bf16[816,128]{1,0:T(8,128)(2,1)S(1)}, u32[]{:S(2)}, u32[]{:S(2)}) %collective-permute-start.1) | collective-permute-done | bytes 208928 | tf_op jit(solution)/shard_map/ppermute | solution.py:299
  10.5 0.0 collective-permute-done.2.r2.t2
  10.5 0.4 %shard_map.93.local_ref = f32[7168,128]{1,0:T(8,128)S(1)} custom-call(bf16[816,128]{1,0:T(8,128)(2,1)S(1)} %collective-permute-done.1.r0.t0, bf16[816,128]{1,0:T(8,128)(2,1)S(1)} %collective-permute-done.2.r2.t2, bf16[816,128]{1,0:T(8,128)(2,1)S(1)} %collective-permute-done.1.r0.t0, ...), custom_call_target="tpu_custom_call", output_to_operand_aliasing={{}: (4, {})} | custom-call | flops 25690112 | bytes 10010624 | tf_op jit(solution)/shard_map/pallas_call | solution.py:276
  10.8 1.9 %collective-permute-done.r1.t1 = bf16[816,128]{1,0:T(8,128)(2,1)S(1)} collective-permute-done((bf16[816,128]{1,0:T(8,128)(2,1)S(1)}, bf16[816,128]{1,0:T(8,128)(2,1)S(1)}, u32[]{:S(2)}, u32[]{:S(2)}) %collective-permute-start) | collective-permute-done | bytes 208928 | tf_op jit(solution)/shard_map/ppermute | solution.py:294
  12.7 0.7 %shard_map.94 = (f32[7168,128]{1,0:T(8,128)S(1)}, bf16[800,128]{1,0:T(8,128)(2,1)S(1)}, bf16[800,128]{1,0:T(8,128)(2,1)S(1)}, bf16[800,128]{1,0:T(8,128)(2,1)S(1)}) custom-call(bf16[816,128]{1,0:T(8,128)(2,1)S(1)} %collective-permute-done.r1.t1, f32[7168,128]{1,0:T(8,128)S(1)} %shard_map.93.local_ref, ...), custom_call_target="tpu_custom_call", output_to_operand_aliasing={{0}: (1, {})} | custom-call | flops 12845056 | bytes 10063872 | tf_op jit(solution)/shard_map/pallas_call | solution.py:276
  13.4 1.8 %collective-permute-start.4 = (bf16[800,128]{1,0:T(8,128)(2,1)S(1)}, bf16[800,128]{1,0:T(8,128)(2,1)S(1)}, u32[]{:S(2)}, u32[]{:S(2)}) collective-permute-start(bf16[800,128]{1,0:T(8,128)(2,1)S(1)} %get-tuple-element.35), channel_id=1, source_target_pairs={{0,16},{16,0},{1,17},{17,1},{2,18},{18,2},{3,19},{19,3},{4,20},{20... | collective-permute-start | bytes 614408 | tf_op jit(solution)/shard_map/ppermute | solution.py:299
  15.2 0.0 collective-permute-start.5
  15.2 0.3 %collective-permute-start.3 = (bf16[800,128]{1,0:T(8,128)(2,1)S(1)}, bf16[800,128]{1,0:T(8,128)(2,1)S(1)}, u32[]{:S(2)}, u32[]{:S(2)}) collective-permute-start(bf16[800,128]{1,0:T(8,128)(2,1)S(1)} %get-tuple-element.34), channel_id=1, source_target_pairs={{0,16},{1,2},{2,1},{3,4},{4,3},{5,6},{6,5},{7,8},{8,7},{9,10},{10,... | collective-permute-start | bytes 614408 | tf_op jit(solution)/shard_map/ppermute | solution.py:294
  15.5 2.8 %shard_map.95.local_ref = f32[7168,128]{1,0:T(8,128)S(1)} custom-call(f32[7168,128]{1,0:T(8,128)S(1)} %get-tuple-element.37.cs, bf16[25,128,256]{2,1,0:T(8,128)(2,1)S(1)} %get-tuple-element.38.a_ref, bf16[128,56,128]{2,1,0:T(8,128)(2,1)S(1)} %get-tuple-element.32.vt_ref), custom_call_target="tpu_custom_call" | custom-call | flops 312475648 | bytes 10813440 | tf_op jit(solution)/shard_map/pallas_call | solution.py:276
  18.3 1.4 %collective-permute-done.4.r0 = bf16[800,128]{1,0:T(8,128)(2,1)S(1)} collective-permute-done((bf16[800,128]{1,0:T(8,128)(2,1)S(1)}, bf16[800,128]{1,0:T(8,128)(2,1)S(1)}, u32[]{:S(2)}, u32[]{:S(2)}) %collective-permute-start.4) | collective-permute-done | bytes 204832 | tf_op jit(solution)/shard_map/ppermute | solution.py:299
  19.7 0.0 collective-permute-done.5.r2
  19.7 1.0 %shard_map.96 = (f32[7168,128]{1,0:T(8,128)S(1)}, f32[7616,128]{1,0:T(8,128)S(1)}) custom-call(bf16[800,128]{1,0:T(8,128)(2,1)S(1)} %collective-permute-done.4.r0, bf16[800,128]{1,0:T(8,128)(2,1)S(1)} %collective-permute-done.5.r2, bf16[816,128]{1,0:T(8,128)(2,1)S(1)} %collective-permute-done.1.r0.t0, ...), custom_call_target="tpu_custom_call", output_to_operand_aliasing={{0}: (4, {})} | custom-call | flops 25690112 | bytes 13901824 | tf_op jit(solution)/shard_map/pallas_call | solution.py:276
  20.7 1.2 %collective-permute-done.3.r1 = bf16[800,128]{1,0:T(8,128)(2,1)S(1)} collective-permute-done((bf16[800,128]{1,0:T(8,128)(2,1)S(1)}, bf16[800,128]{1,0:T(8,128)(2,1)S(1)}, u32[]{:S(2)}, u32[]{:S(2)}) %collective-permute-start.3) | collective-permute-done | bytes 204832 | tf_op jit(solution)/shard_map/ppermute | solution.py:294
  21.9 1.6 %shard_map.97 = (bf16[50,128,128]{2,1,0:T(8,128)(2,1)}, f32[7616,128]{1,0:T(8,128)S(1)}) custom-call(bf16[800,128]{1,0:T(8,128)(2,1)S(1)} %collective-permute-done.3.r1, bf16[816,128]{1,0:T(8,128)(2,1)S(1)} %collective-permute-done.r1.t1, f32[7616,128]{1,0:T(8,128)S(1)} %get-tuple-element.39.local_ref, ...), custom_call_target="tpu_custom_call", output_to_operand_aliasing={{1}: (2, {})} | custom-call | flops 12845056 | bytes 11685888 | tf_op jit(solution)/shard_map/pallas_call | solution.py:276
Async XLA Ops:
  2.3 8.2 %collective-permute-start.1 = (bf16[816,128]{1,0:T(8,128)(2,1)S(1)}, bf16[816,128]{1,0:T(8,128)(2,1)S(1)}, u32[]{:S(2)}, u32[]{:S(2)}) collective-permute-start(bf16[816,128]{1,0:T(8,128)(2,1)S(1)} %get-tuple-element.24), channel_id=1, source_target_pairs={{0,16},{16,0},{1,17},{17,1},{2,18},{18,2},{3,19},{19,3},{4,20},{20... | collective-permute-start | bytes 626696 | tf_op jit(solution)/shard_map/ppermute | solution.py:299
  5.3 5.2 %collective-permute-start.2 = (bf16[816,128]{1,0:T(8,128)(2,1)S(1)}, bf16[816,128]{1,0:T(8,128)(2,1)S(1)}, u32[]{:S(2)}, u32[]{:S(2)}) collective-permute-start(bf16[816,128]{1,0:T(8,128)(2,1)S(1)} %get-tuple-element.25), channel_id=1, source_target_pairs={{0,1},{1,0},{2,3},{3,2},{4,5},{5,4},{6,7},{7,6},{8,9},{9,8},{10,11... | collective-permute-start | bytes 626696 | tf_op jit(solution)/shard_map/ppermute | solution.py:294
  5.3 7.4 %collective-permute-start = (bf16[816,128]{1,0:T(8,128)(2,1)S(1)}, bf16[816,128]{1,0:T(8,128)(2,1)S(1)}, u32[]{:S(2)}, u32[]{:S(2)}) collective-permute-start(bf16[816,128]{1,0:T(8,128)(2,1)S(1)} %get-tuple-element.23), channel_id=1, source_target_pairs={{0,16},{1,2},{2,1},{3,4},{4,3},{5,6},{6,5},{7,8},{8,7},{9,10},{10,... | collective-permute-start | bytes 626696 | tf_op jit(solution)/shard_map/ppermute | solution.py:294
  13.4 6.3 %collective-permute-start.4 = (bf16[800,128]{1,0:T(8,128)(2,1)S(1)}, bf16[800,128]{1,0:T(8,128)(2,1)S(1)}, u32[]{:S(2)}, u32[]{:S(2)}) collective-permute-start(bf16[800,128]{1,0:T(8,128)(2,1)S(1)} %get-tuple-element.35), channel_id=1, source_target_pairs={{0,16},{16,0},{1,17},{17,1},{2,18},{18,2},{3,19},{19,3},{4,20},{20... | collective-permute-start | bytes 614408 | tf_op jit(solution)/shard_map/ppermute | solution.py:299
  15.2 4.5 %collective-permute-start.5 = (bf16[800,128]{1,0:T(8,128)(2,1)S(1)}, bf16[800,128]{1,0:T(8,128)(2,1)S(1)}, u32[]{:S(2)}, u32[]{:S(2)}) collective-permute-start(bf16[800,128]{1,0:T(8,128)(2,1)S(1)} %get-tuple-element.36), channel_id=1, source_target_pairs={{0,1},{1,0},{2,3},{3,2},{4,5},{5,4},{6,7},{7,6},{8,9},{9,8},{10,11... | collective-permute-start | bytes 614408 | tf_op jit(solution)/shard_map/ppermute | solution.py:294
  15.2 6.7 %collective-permute-start.3 = (bf16[800,128]{1,0:T(8,128)(2,1)S(1)}, bf16[800,128]{1,0:T(8,128)(2,1)S(1)}, u32[]{:S(2)}, u32[]{:S(2)}) collective-permute-start(bf16[800,128]{1,0:T(8,128)(2,1)S(1)} %get-tuple-element.34), channel_id=1, source_target_pairs={{0,16},{1,2},{2,1},{3,4},{4,3},{5,6},{6,5},{7,8},{8,7},{9,10},{10,... | collective-permute-start | bytes 614408 | tf_op jit(solution)/shard_map/ppermute | solution.py:294

commit v18 on v16

--- a/solution.py
+++ b/solution.py
@@ -115,16 +115,18 @@
     levels, cols, width = c_h.shape
     nedge = edge_h.shape[1]
     pitch = cols + 8
-    bounds = [(lo, min(lo + 16, levels)) for lo in range(0, levels, 16)]
-    pairs = [(send_h, send_v), (recv_h, recv_v), (edge_h, edge_v)]
-    pairs += [(c_h.at[pl.ds(lo, hi - lo)], c_v.at[pl.ds(lo, hi - lo)]) for lo, hi in bounds]
+    whole = whole_rows(levels)
+    bounds = [(lo, lo + 16 if lo + 16 < whole else levels) for lo in range(0, whole, 16)]
+    pairs = [(c_h.at[pl.ds(lo, hi - lo)], c_v.at[pl.ds(lo, hi - lo)]) for lo, hi in bounds]
+    tracer_copies = len(pairs)
+    pairs += [(send_h, send_v), (recv_h, recv_v), (edge_h, edge_v)]
     pairs += [(nbr_h, nbr_v), (nw_h, nw_v), (sw_h, sw_v), (wet_h, wet_v)]
     copies = [pltpu.make_async_copy(a, b, sems.at[i]) for i, (a, b) in enumerate(pairs)]
     for copy in copies:
         copy.start()
     parity = lax.bitwise_and(lax.axis_index(blk), jnp.int32(1))
     wts[...] = jnp.zeros_like(wts)
-    for copy in copies[:3]:
+    for copy in copies[tracer_copies : tracer_copies + 3]:
         copy.wait()
     for slot in range(3):
         d = direction(slot, parity)
@@ -139,13 +141,12 @@
     source = source_columns(weights, nedge)
     rows_of = lambda s, lo, n: cf[pl.ds(lo * pitch + s, n, stride=pitch), :]
     for i, (lo, hi) in enumerate(bounds):
-        copies[3 + i].wait()
+        copies[i].wait()
         for l in range(lo, hi):
             cf[l * pitch : l * pitch + cols, :] = c_v[l].astype(F32)
         pack_chunk(lo, levels, nedge, source, weights, rows_of, (0, 1, 2), (s0, s1, s2))
-    if levels % 16 == 0:
-        pack_chunk(levels, levels, nedge, source, weights, rows_of, (0, 1, 2), (s0, s1, s2))
-    for copy in copies[3 + len(bounds) :]:
+    pack_chunk(whole, levels, nedge, source, weights, rows_of, (0, 1, 2), (s0, s1, s2))
+    for copy in copies[tracer_copies + 3 :]:
         copy.wait()
 
 

time: 23.5 us -> 23.8 us (1.013)
  Pallas kernels: 12.5 us -> 12.9 us
    pallas_call x7, Pallas kernels: 12.5 us -> 12.9 us  [call(): pl.pallas_call(kernel, out_shape=outs, in_specs=specs, out_specs=out_spec...]
where the time goes in v18:
time: 23.8 us; the launch traced here: 23.7 us
  Pallas kernels  12.9 us (54%)
  waiting for transfers between devices  5.46 us (23%)
  starting transfers between devices  5.25 us (22%)
    pallas_call x7, Pallas kernels, call(): pl.pallas_call(kernel, out_shape=outs, in_specs=specs, out_specs=out_spec...  12.9 us
    ppermute x2, starting transfers between devices, along_basin(): return lax.ppermute(value, basin, [(i, (i + 1) % b) for i in range(b)])  4.81 us
    ppermute x4, waiting for transfers between devices, odd_or_even(): return lax.ppermute(value, (basin, blk), route)  3.7 us
    ppermute x2, waiting for transfers between devices, along_basin(): return lax.ppermute(value, basin, [(i, (i + 1) % b) for i in range(b)])  1.76 us
  transfers between devices with their start and end apart: 6, of which 4 were waited for; matrix products, arithmetic and copies ran while one was open for 0% of the time, Pallas kernels for 35%

profile of v18, /device:TPU:0, one launch (start us, length us, event | category | flops | bytes accessed | tf_op | source)
XLA Modules:
  0.0 23.7 jit_solution(10980076473344912387)
XLA Ops:
  0.0 2.5 %shard_map.91 = (bf16[816,128]{1,0:T(8,128)(2,1)S(1)}, bf16[816,128]{1,0:T(8,128)(2,1)S(1)}, bf16[816,128]{1,0:T(8,128)(2,1)S(1)}, bf16[50,128,128]{2,1,0:T(8,12...) custom-call(bf16[50,128,128]{2,1,0:T(8,128)(2,1)} %bitcast.5, ...), custom_call_target="tpu_custom_call" | custom-call | bytes 4240128 | tf_op jit(solution)/shard_map/pallas_call | solution.py:265
  2.5 3.0 %collective-permute-start.1 = (bf16[816,128]{1,0:T(8,128)(2,1)S(1)}, bf16[816,128]{1,0:T(8,128)(2,1)S(1)}, u32[]{:S(2)}, u32[]{:S(2)}) collective-permute-start(bf16[816,128]{1,0:T(8,128)(2,1)S(1)} %get-tuple-element.23), channel_id=1, source_target_pairs={{0,16},{16,0},{1,17},{17,1},{2,18},{18,2},{3,19},{19,3},{4,20},{20... | collective-permute-start | bytes 626696 | tf_op jit(solution)/shard_map/ppermute | solution.py:288
  5.5 0.0 collective-permute-start.2
  5.5 0.2 collective-permute-start
  5.6 4.6 %shard_map.92 = (bf16[25,128,256]{2,1,0:T(8,128)(2,1)S(1)}, f32[7168,128]{1,0:T(8,128)S(1)}, bf16[128,56,128]{2,1,0:T(8,128)(2,1)S(1)}) custom-call(bf16[50,128,128]{2,1,0:T(8,128)(2,1)S(1)} %get-tuple-element.25.c_ref, s32[4,128]{1,0:T(4,128)S(1)} %get-tuple-element.26.nbr_ref, f32[50,4,128]{2,1,0:T(4,128)S(1)} %get-tuple-element.27.nw_ref, ...), custom_call_target="tpu_custom_call" | custom-call | flops 312475648 | bytes 9552384 | tf_op jit(solution)/shard_map/pallas_call | solution.py:265
  10.3 0.4 %collective-permute-done.1.r0.t0 = bf16[816,128]{1,0:T(8,128)(2,1)S(1)} collective-permute-done((bf16[816,128]{1,0:T(8,128)(2,1)S(1)}, bf16[816,128]{1,0:T(8,128)(2,1)S(1)}, u32[]{:S(2)}, u32[]{:S(2)}) %collective-permute-start.1) | collective-permute-done | bytes 208928 | tf_op jit(solution)/shard_map/ppermute | solution.py:288
  10.6 0.0 collective-permute-done.2.r2.t2
  10.6 0.4 %shard_map.93.local_ref = f32[7168,128]{1,0:T(8,128)S(1)} custom-call(bf16[816,128]{1,0:T(8,128)(2,1)S(1)} %collective-permute-done.1.r0.t0, bf16[816,128]{1,0:T(8,128)(2,1)S(1)} %collective-permute-done.2.r2.t2, bf16[816,128]{1,0:T(8,128)(2,1)S(1)} %collective-permute-done.1.r0.t0, ...), custom_call_target="tpu_custom_call", output_to_operand_aliasing={{}: (4, {})} | custom-call | flops 25690112 | bytes 10010624 | tf_op jit(solution)/shard_map/pallas_call | solution.py:265
  11.0 1.9 %collective-permute-done.r1.t1 = bf16[816,128]{1,0:T(8,128)(2,1)S(1)} collective-permute-done((bf16[816,128]{1,0:T(8,128)(2,1)S(1)}, bf16[816,128]{1,0:T(8,128)(2,1)S(1)}, u32[]{:S(2)}, u32[]{:S(2)}) %collective-permute-start) | collective-permute-done | bytes 208928 | tf_op jit(solution)/shard_map/ppermute | solution.py:283
  12.9 0.7 %shard_map.94 = (f32[7168,128]{1,0:T(8,128)S(1)}, bf16[800,128]{1,0:T(8,128)(2,1)S(1)}, bf16[800,128]{1,0:T(8,128)(2,1)S(1)}, bf16[800,128]{1,0:T(8,128)(2,1)S(1)}) custom-call(bf16[816,128]{1,0:T(8,128)(2,1)S(1)} %collective-permute-done.r1.t1, f32[7168,128]{1,0:T(8,128)S(1)} %shard_map.93.local_ref, ...), custom_call_target="tpu_custom_call", output_to_operand_aliasing={{0}: (1, {})} | custom-call | flops 12845056 | bytes 10063872 | tf_op jit(solution)/shard_map/pallas_call | solution.py:265
  13.6 1.8 %collective-permute-start.4 = (bf16[800,128]{1,0:T(8,128)(2,1)S(1)}, bf16[800,128]{1,0:T(8,128)(2,1)S(1)}, u32[]{:S(2)}, u32[]{:S(2)}) collective-permute-start(bf16[800,128]{1,0:T(8,128)(2,1)S(1)} %get-tuple-element.34), channel_id=1, source_target_pairs={{0,16},{16,0},{1,17},{17,1},{2,18},{18,2},{3,19},{19,3},{4,20},{20... | collective-permute-start | bytes 614408 | tf_op jit(solution)/shard_map/ppermute | solution.py:288
  15.4 0.0 collective-permute-start.5
  15.4 0.3 %collective-permute-start.3 = (bf16[800,128]{1,0:T(8,128)(2,1)S(1)}, bf16[800,128]{1,0:T(8,128)(2,1)S(1)}, u32[]{:S(2)}, u32[]{:S(2)}) collective-permute-start(bf16[800,128]{1,0:T(8,128)(2,1)S(1)} %get-tuple-element.33), channel_id=1, source_target_pairs={{0,16},{1,2},{2,1},{3,4},{4,3},{5,6},{6,5},{7,8},{8,7},{9,10},{10,... | collective-permute-start | bytes 614408 | tf_op jit(solution)/shard_map/ppermute | solution.py:283
  15.7 2.8 %shard_map.95.local_ref = f32[7168,128]{1,0:T(8,128)S(1)} custom-call(f32[7168,128]{1,0:T(8,128)S(1)} %get-tuple-element.36.cs, bf16[25,128,256]{2,1,0:T(8,128)(2,1)S(1)} %get-tuple-element.37.a_ref, bf16[128,56,128]{2,1,0:T(8,128)(2,1)S(1)} %get-tuple-element.31.vt_ref), custom_call_target="tpu_custom_call" | custom-call | flops 312475648 | bytes 10813440 | tf_op jit(solution)/shard_map/pallas_call | solution.py:265
  18.5 1.4 %collective-permute-done.4.r0 = bf16[800,128]{1,0:T(8,128)(2,1)S(1)} collective-permute-done((bf16[800,128]{1,0:T(8,128)(2,1)S(1)}, bf16[800,128]{1,0:T(8,128)(2,1)S(1)}, u32[]{:S(2)}, u32[]{:S(2)}) %collective-permute-start.4) | collective-permute-done | bytes 204832 | tf_op jit(solution)/shard_map/ppermute | solution.py:288
  19.9 0.0 collective-permute-done.5.r2
  19.9 0.4 %shard_map.96.local_ref = f32[7168,128]{1,0:T(8,128)S(1)} custom-call(bf16[800,128]{1,0:T(8,128)(2,1)S(1)} %collective-permute-done.4.r0, bf16[800,128]{1,0:T(8,128)(2,1)S(1)} %collective-permute-done.5.r2, bf16[816,128]{1,0:T(8,128)(2,1)S(1)} %collective-permute-done.1.r0.t0, ...), custom_call_target="tpu_custom_call", output_to_operand_aliasing={{}: (4, {})} | custom-call | flops 25690112 | bytes 10002432 | tf_op jit(solution)/shard_map/pallas_call | solution.py:265
  20.3 1.8 %collective-permute-done.3.r1 = bf16[800,128]{1,0:T(8,128)(2,1)S(1)} collective-permute-done((bf16[800,128]{1,0:T(8,128)(2,1)S(1)}, bf16[800,128]{1,0:T(8,128)(2,1)S(1)}, u32[]{:S(2)}, u32[]{:S(2)}) %collective-permute-start.3) | collective-permute-done | bytes 204832 | tf_op jit(solution)/shard_map/ppermute | solution.py:283
  22.1 1.6 %shard_map.97 = (bf16[50,128,128]{2,1,0:T(8,128)(2,1)}, f32[7168,128]{1,0:T(8,128)S(1)}) custom-call(bf16[800,128]{1,0:T(8,128)(2,1)S(1)} %collective-permute-done.3.r1, bf16[816,128]{1,0:T(8,128)(2,1)S(1)} %collective-permute-done.r1.t1, f32[7168,128]{1,0:T(8,128)S(1)} %shard_map.96.local_ref, ...), custom_call_target="tpu_custom_call", output_to_operand_aliasing={{1}: (2, {})} | custom-call | flops 12845056 | bytes 11227136 | tf_op jit(solution)/shard_map/pallas_call | solution.py:265
Async XLA Ops:
  2.5 8.2 %collective-permute-start.1 = (bf16[816,128]{1,0:T(8,128)(2,1)S(1)}, bf16[816,128]{1,0:T(8,128)(2,1)S(1)}, u32[]{:S(2)}, u32[]{:S(2)}) collective-permute-start(bf16[816,128]{1,0:T(8,128)(2,1)S(1)} %get-tuple-element.23), channel_id=1, source_target_pairs={{0,16},{16,0},{1,17},{17,1},{2,18},{18,2},{3,19},{19,3},{4,20},{20... | collective-permute-start | bytes 626696 | tf_op jit(solution)/shard_map/ppermute | solution.py:288
  5.5 5.2 %collective-permute-start.2 = (bf16[816,128]{1,0:T(8,128)(2,1)S(1)}, bf16[816,128]{1,0:T(8,128)(2,1)S(1)}, u32[]{:S(2)}, u32[]{:S(2)}) collective-permute-start(bf16[816,128]{1,0:T(8,128)(2,1)S(1)} %get-tuple-element.24), channel_id=1, source_target_pairs={{0,1},{1,0},{2,3},{3,2},{4,5},{5,4},{6,7},{7,6},{8,9},{9,8},{10,11... | collective-permute-start | bytes 626696 | tf_op jit(solution)/shard_map/ppermute | solution.py:283
  5.5 7.4 %collective-permute-start = (bf16[816,128]{1,0:T(8,128)(2,1)S(1)}, bf16[816,128]{1,0:T(8,128)(2,1)S(1)}, u32[]{:S(2)}, u32[]{:S(2)}) collective-permute-start(bf16[816,128]{1,0:T(8,128)(2,1)S(1)} %get-tuple-element.22), channel_id=1, source_target_pairs={{0,16},{1,2},{2,1},{3,4},{4,3},{5,6},{6,5},{7,8},{8,7},{9,10},{10,... | collective-permute-start | bytes 626696 | tf_op jit(solution)/shard_map/ppermute | solution.py:283
  13.6 6.4 %collective-permute-start.4 = (bf16[800,128]{1,0:T(8,128)(2,1)S(1)}, bf16[800,128]{1,0:T(8,128)(2,1)S(1)}, u32[]{:S(2)}, u32[]{:S(2)}) collective-permute-start(bf16[800,128]{1,0:T(8,128)(2,1)S(1)} %get-tuple-element.34), channel_id=1, source_target_pairs={{0,16},{16,0},{1,17},{17,1},{2,18},{18,2},{3,19},{19,3},{4,20},{20... | collective-permute-start | bytes 614408 | tf_op jit(solution)/shard_map/ppermute | solution.py:288
  15.4 4.5 %collective-permute-start.5 = (bf16[800,128]{1,0:T(8,128)(2,1)S(1)}, bf16[800,128]{1,0:T(8,128)(2,1)S(1)}, u32[]{:S(2)}, u32[]{:S(2)}) collective-permute-start(bf16[800,128]{1,0:T(8,128)(2,1)S(1)} %get-tuple-element.35), channel_id=1, source_target_pairs={{0,1},{1,0},{2,3},{3,2},{4,5},{5,4},{6,7},{7,6},{8,9},{9,8},{10,11... | collective-permute-start | bytes 614408 | tf_op jit(solution)/shard_map/ppermute | solution.py:283
  15.4 6.7 %collective-permute-start.3 = (bf16[800,128]{1,0:T(8,128)(2,1)S(1)}, bf16[800,128]{1,0:T(8,128)(2,1)S(1)}, u32[]{:S(2)}, u32[]{:S(2)}) collective-permute-start(bf16[800,128]{1,0:T(8,128)(2,1)S(1)} %get-tuple-element.33), channel_id=1, source_target_pairs={{0,16},{1,2},{2,1},{3,4},{4,3},{5,6},{6,5},{7,8},{8,7},{9,10},{10,... | collective-permute-start | bytes 614408 | tf_op jit(solution)/shard_map/ppermute | solution.py:283

commit v19 on v16

--- a/solution.py
+++ b/solution.py
@@ -108,8 +108,7 @@
 
 
 def gather_kernel(
-    blk, c_h, send_h, recv_h, edge_h, nbr_h, nw_h, sw_h, wet_h,
-    s0, s1, s2, c_v, nbr_v, nw_v, sw_v, wet_v, wts_o,
+    blk, c_h, send_h, recv_h, edge_h, s0, s1, s2, c_v, wts_o,
     cf, wts, recv_v, edge_v, send_v, sems,
 ):
     levels, cols, width = c_h.shape
@@ -118,7 +117,6 @@
     bounds = [(lo, min(lo + 16, levels)) for lo in range(0, levels, 16)]
     pairs = [(send_h, send_v), (recv_h, recv_v), (edge_h, edge_v)]
     pairs += [(c_h.at[pl.ds(lo, hi - lo)], c_v.at[pl.ds(lo, hi - lo)]) for lo, hi in bounds]
-    pairs += [(nbr_h, nbr_v), (nw_h, nw_v), (sw_h, sw_v), (wet_h, wet_v)]
     copies = [pltpu.make_async_copy(a, b, sems.at[i]) for i, (a, b) in enumerate(pairs)]
     for copy in copies:
         copy.start()
@@ -145,8 +143,6 @@
         pack_chunk(lo, levels, nedge, source, weights, rows_of, (0, 1, 2), (s0, s1, s2))
     if levels % 16 == 0:
         pack_chunk(levels, levels, nedge, source, weights, rows_of, (0, 1, 2), (s0, s1, s2))
-    for copy in copies[3 + len(bounds) :]:
-        copy.wait()
 
 
 def column_operator(nbr_ref, nw_ref, sw_ref, a_ref, merged):
@@ -197,17 +193,22 @@
 
 
 def operator_kernel(
-    c_ref, nbr_ref, nw_ref, sw_ref, wet_ref, v_h, a_ref, state_ref, vt_ref, exs, merged, vf, vts, v_ref, sem
+    c_ref, nbr_h, nw_h, sw_h, wet_h, v_h, a_ref, state_ref, vt_ref,
+    exs, merged, vf, vts, nbr_ref, nw_ref, sw_ref, wet_ref, v_ref, sems
 ):
     levels, cols, width = c_ref.shape
     rows = padded(levels)
-    load = pltpu.make_async_copy(v_h, v_ref, sem)
-    load.start()
+    pairs = [(nbr_h, nbr_ref), (nw_h, nw_ref), (sw_h, sw_ref), (wet_h, wet_ref), (v_h, v_ref)]
+    copies = [pltpu.make_async_copy(a, b, sems.at[i]) for i, (a, b) in enumerate(pairs)]
+    for copy in copies:
+        copy.start()
+    for copy in copies[:4]:
+        copy.wait()
     column_operator(nbr_ref, nw_ref, sw_ref, a_ref, merged)
     level_products(a_ref, lambda l: c_ref[l], exs, rows)
     level = lax.broadcasted_iota(jnp.int32, (levels, cols), 0)
     wet = wet_ref[...]
-    load.wait()
+    copies[4].wait()
     vf[...] = jnp.zeros_like(vf)
     for m in range(levels):
         keep = jnp.maximum(level, m) < wet
@@ -298,7 +299,7 @@
     wet = wet_levels.reshape(1, cols)
     in_hbm = lambda x: pltpu.with_memory_space_constraint(x, pltpu.HBM)
     send_h = in_hbm(send_cols)
-    loads = [by_level, nbr_cols, nbr_by_level, self_wts, wet]
+    loads = [nbr_cols, nbr_by_level, self_wts, wet]
     same = lambda x: shape(x.shape, x.dtype)
     message = shape((message_rows(levels, nedge), width), BF16)
     columns = shape((cols * rows, width), F32)
@@ -306,18 +307,19 @@
 
     first = call(
         functools.partial(gather_kernel, "blk"),
-        (in_hbm(by_level), send_h, *map(in_hbm, (recv_cols, edge_by_entry, *loads[1:]))),
-        [HB] * 8,
-        [message] * 3 + [same(x) for x in loads] + [shape((128, 128), F32)],
-        [VM] * 9,
+        (in_hbm(by_level), send_h, *map(in_hbm, (recv_cols, edge_by_entry))),
+        [HB] * 4,
+        [message] * 3 + [same(by_level), shape((128, 128), F32)],
+        [VM] * 5,
         [
             pltpu.VMEM((rows * (cols + 8), width), F32),
             pltpu.VMEM((128, 128), F32), pltpu.VMEM(recv_cols.shape, jnp.int32), pltpu.VMEM(edge_by_entry.shape, F32),
-            pltpu.VMEM(send_cols.shape, jnp.int32), DMA((7 + -(-levels // 16),)),
+            pltpu.VMEM(send_cols.shape, jnp.int32), DMA((3 + -(-levels // 16),)),
         ],
         16,
     )
-    (to_next, to_odd, to_even), loads, wts = first[:3], first[3:8], first[8]
+    *messages, state, wts = first
+    to_next, to_odd, to_even = messages
     operator_flops = 2 * levels * cols * cols * width
     vertical_flops = 2 * cols * rows * rows * width
 
@@ -333,10 +335,10 @@
     odd = odd_or_even(to_odd, 1, "blk", "basin")
     even = odd_or_even(to_even, 0, "blk", "basin")
     operator, partial, vt = call(
-        operator_kernel, (*loads, in_hbm(vert_inv)), [VM] * 5 + [HB],
+        operator_kernel, (state, *map(in_hbm, (*loads, vert_inv))), [VM] + [HB] * 5,
         [shape((levels // 2, cols, 2 * cols), BF16), columns, shape((cols, rows, 128), BF16)], [VM] * 3,
         [flat, pltpu.VMEM((levels, 8, cols), F32), pltpu.VMEM((rows * rows, cols), F32), pltpu.VMEM((cols * rows, 128), F32),
-         pltpu.VMEM(vert_inv.shape, BF16), DMA],
+         *[pltpu.VMEM(x.shape, x.dtype) for x in (*loads, vert_inv)], DMA((5,))],
         32, flops=operator_flops + vertical_flops,
     )
     state, to_next, to_odd, to_even = call(

time: 23.5 us -> 24.3 us (1.034)
  Pallas kernels: 12.5 us -> 13.4 us
    pallas_call x7, Pallas kernels: 12.5 us -> 13.4 us  [call(): pl.pallas_call(kernel, out_shape=outs, in_specs=specs, out_specs=out_spec...]
    ppermute x4, waiting for transfers between devices: 3.7 us -> 3.13 us  [odd_or_even(): return lax.ppermute(value, (basin, blk), route)]
    ppermute x2, waiting for transfers between devices: 1.76 us -> 2.29 us  [along_basin(): return lax.ppermute(value, basin, [(i, (i + 1) % b) for i in range(b)])]
  transfers between devices with their start and end apart: 6 -> 6, of which waited for: 4 -> 3; matrix products, arithmetic and copies ran while one was open for 0% -> 0% of each run, Pallas kernels for 35% -> 38%
where the time goes in v19:
time: 24.3 us; the launch traced here: 24.1 us
  Pallas kernels  13.4 us (55%)
  waiting for transfers between devices  5.42 us (22%)
  starting transfers between devices  5.25 us (22%)
    pallas_call x7, Pallas kernels, call(): pl.pallas_call(kernel, out_shape=outs, in_specs=specs, out_specs=out_spec...  13.4 us
    ppermute x2, starting transfers between devices, along_basin(): return lax.ppermute(value, basin, [(i, (i + 1) % b) for i in range(b)])  4.8 us
    ppermute x4, waiting for transfers between devices, odd_or_even(): return lax.ppermute(value, (basin, blk), route)  3.13 us
    ppermute x2, waiting for transfers between devices, along_basin(): return lax.ppermute(value, basin, [(i, (i + 1) % b) for i in range(b)])  2.29 us
  transfers between devices with their start and end apart: 6, of which 3 were waited for; matrix products, arithmetic and copies ran while one was open for 0% of the time, Pallas kernels for 38%

profile of v19, /device:TPU:0, one launch (start us, length us, event | category | flops | bytes accessed | tf_op | source)
XLA Modules:
  0.0 24.1 jit_solution(8339448915465455858)
XLA Ops:
  0.0 2.0 %shard_map.91 = (bf16[816,128]{1,0:T(8,128)(2,1)S(1)}, bf16[816,128]{1,0:T(8,128)(2,1)S(1)}, bf16[816,128]{1,0:T(8,128)(2,1)S(1)}, bf16[50,128,128]{2,1,0:T(8,128)(2,1)S(1)}, f32[128,128]{1,0:T(8,128)S(1)}) custom-call(bf16[50,128,128]{2,1,0:T(8,128)(2,1)} %bitcast.5, s32[3,16]{1,0:T(4,128)} %send_h.1, s32[3,16]{1,0:T(4,128)} %recv_h.1, f32[3,16,50]{2,1,0:T(8,128)} %bitcast.7), custom_call_target="tpu_custom_call" | custom-call | bytes 3979008 | tf_op jit(solution)/shard_map/pallas_call | solution.py:265
  2.0 3.0 %collective-permute-start.1 = (bf16[816,128]{1,0:T(8,128)(2,1)S(1)}, bf16[816,128]{1,0:T(8,128)(2,1)S(1)}, u32[]{:S(2)}, u32[]{:S(2)}) collective-permute-start(bf16[816,128]{1,0:T(8,128)(2,1)S(1)} %get-tuple-element.19), channel_id=1, source_target_pairs={{0,16},{16,0},{1,17},{17,1},{2,18},{18,2},{3,19},{19,3},{4,20},{20... | collective-permute-start | bytes 626696 | tf_op jit(solution)/shard_map/ppermute | solution.py:288
  5.0 0.0 collective-permute-start.2
  5.0 0.2 collective-permute-start
  5.2 5.5 %shard_map.92 = (bf16[25,128,256]{2,1,0:T(8,128)(2,1)S(1)}, f32[7168,128]{1,0:T(8,128)S(1)}, bf16[128,56,128]{2,1,0:T(8,128)(2,1)S(1)}) custom-call(bf16[50,128,128]{2,1,0:T(8,128)(2,1)S(1)} %get-tuple-element.21.c_ref, s32[4,128]{1,0:T(4,128)} %nbr_h.1, f32[50,4,128]{2,1,0:T(4,128)} %bitcast.6, f32[50,128]{1,0:T(8,128)} %sw_h.1, s32[1,128]{1,0:T(1,128)} %bitcast.8, ...), custom_call_target="tpu_custom_call" | custom-call | flops 312475648 | bytes 9552384 | tf_op jit(solution)/shard_map/pallas_call | solution.py:265
  10.7 0.0 collective-permute-done.1.r0.t0
  10.8 0.0 collective-permute-done.2.r2.t2
  10.8 0.4 %shard_map.93.local_ref = f32[7168,128]{1,0:T(8,128)S(1)} custom-call(bf16[816,128]{1,0:T(8,128)(2,1)S(1)} %collective-permute-done.1.r0.t0, bf16[816,128]{1,0:T(8,128)(2,1)S(1)} %collective-permute-done.2.r2.t2, bf16[816,128]{1,0:T(8,128)(2,1)S(1)} %collective-permute-done.1.r0.t0, ...), custom_call_target="tpu_custom_call", output_to_operand_aliasing={{}: (4, {})} | custom-call | flops 25690112 | bytes 10010624 | tf_op jit(solution)/shard_map/pallas_call | solution.py:265
  11.1 1.3 %collective-permute-done.r1.t1 = bf16[816,128]{1,0:T(8,128)(2,1)S(1)} collective-permute-done((bf16[816,128]{1,0:T(8,128)(2,1)S(1)}, bf16[816,128]{1,0:T(8,128)(2,1)S(1)}, u32[]{:S(2)}, u32[]{:S(2)}) %collective-permute-start) | collective-permute-done | bytes 208928 | tf_op jit(solution)/shard_map/ppermute | solution.py:283
  12.4 0.7 %shard_map.94 = (f32[7168,128]{1,0:T(8,128)S(1)}, bf16[800,128]{1,0:T(8,128)(2,1)S(1)}, bf16[800,128]{1,0:T(8,128)(2,1)S(1)}, bf16[800,128]{1,0:T(8,128)(2,1)S(1)}) custom-call(bf16[816,128]{1,0:T(8,128)(2,1)S(1)} %collective-permute-done.r1.t1, f32[7168,128]{1,0:T(8,128)S(1)} %shard_map.93.local_ref, ...), custom_call_target="tpu_custom_call", output_to_operand_aliasing={{0}: (1, {})} | custom-call | flops 12845056 | bytes 10063872 | tf_op jit(solution)/shard_map/pallas_call | solution.py:265
  13.2 1.8 %collective-permute-start.4 = (bf16[800,128]{1,0:T(8,128)(2,1)S(1)}, bf16[800,128]{1,0:T(8,128)(2,1)S(1)}, u32[]{:S(2)}, u32[]{:S(2)}) collective-permute-start(bf16[800,128]{1,0:T(8,128)(2,1)S(1)} %get-tuple-element.26), channel_id=1, source_target_pairs={{0,16},{16,0},{1,17},{17,1},{2,18},{18,2},{3,19},{19,3},{4,20},{20... | collective-permute-start | bytes 614408 | tf_op jit(solution)/shard_map/ppermute | solution.py:288
  15.0 0.0 collective-permute-start.5
  15.0 0.3 %collective-permute-start.3 = (bf16[800,128]{1,0:T(8,128)(2,1)S(1)}, bf16[800,128]{1,0:T(8,128)(2,1)S(1)}, u32[]{:S(2)}, u32[]{:S(2)}) collective-permute-start(bf16[800,128]{1,0:T(8,128)(2,1)S(1)} %get-tuple-element.25), channel_id=1, source_target_pairs={{0,16},{1,2},{2,1},{3,4},{4,3},{5,6},{6,5},{7,8},{8,7},{9,10},{10,... | collective-permute-start | bytes 614408 | tf_op jit(solution)/shard_map/ppermute | solution.py:283
  15.3 2.8 %shard_map.95.local_ref = f32[7168,128]{1,0:T(8,128)S(1)} custom-call(f32[7168,128]{1,0:T(8,128)S(1)} %get-tuple-element.28.cs, bf16[25,128,256]{2,1,0:T(8,128)(2,1)S(1)} %get-tuple-element.29.a_ref, bf16[128,56,128]{2,1,0:T(8,128)(2,1)S(1)} %get-tuple-element.23.vt_ref), custom_call_target="tpu_custom_call" | custom-call | flops 312475648 | bytes 10813440 | tf_op jit(solution)/shard_map/pallas_call | solution.py:265
  18.1 2.3 %collective-permute-done.4.r0 = bf16[800,128]{1,0:T(8,128)(2,1)S(1)} collective-permute-done((bf16[800,128]{1,0:T(8,128)(2,1)S(1)}, bf16[800,128]{1,0:T(8,128)(2,1)S(1)}, u32[]{:S(2)}, u32[]{:S(2)}) %collective-permute-start.4) | collective-permute-done | bytes 204832 | tf_op jit(solution)/shard_map/ppermute | solution.py:288
  20.4 0.0 collective-permute-done.5.r2
  20.4 0.4 %shard_map.96.local_ref = f32[7168,128]{1,0:T(8,128)S(1)} custom-call(bf16[800,128]{1,0:T(8,128)(2,1)S(1)} %collective-permute-done.4.r0, bf16[800,128]{1,0:T(8,128)(2,1)S(1)} %collective-permute-done.5.r2, bf16[816,128]{1,0:T(8,128)(2,1)S(1)} %collective-permute-done.1.r0.t0, ...), custom_call_target="tpu_custom_call", output_to_operand_aliasing={{}: (4, {})} | custom-call | flops 25690112 | bytes 10002432 | tf_op jit(solution)/shard_map/pallas_call | solution.py:265
  20.8 1.8 %collective-permute-done.3.r1 = bf16[800,128]{1,0:T(8,128)(2,1)S(1)} collective-permute-done((bf16[800,128]{1,0:T(8,128)(2,1)S(1)}, bf16[800,128]{1,0:T(8,128)(2,1)S(1)}, u32[]{:S(2)}, u32[]{:S(2)}) %collective-permute-start.3) | collective-permute-done | bytes 204832 | tf_op jit(solution)/shard_map/ppermute | solution.py:283
  22.6 1.6 %shard_map.97 = (bf16[50,128,128]{2,1,0:T(8,128)(2,1)}, f32[7168,128]{1,0:T(8,128)S(1)}) custom-call(bf16[800,128]{1,0:T(8,128)(2,1)S(1)} %collective-permute-done.3.r1, bf16[816,128]{1,0:T(8,128)(2,1)S(1)} %collective-permute-done.r1.t1, f32[7168,128]{1,0:T(8,128)S(1)} %shard_map.96.local_ref, ...), custom_call_target="tpu_custom_call", output_to_operand_aliasing={{1}: (2, {})} | custom-call | flops 12845056 | bytes 11227136 | tf_op jit(solution)/shard_map/pallas_call | solution.py:265
Async XLA Ops:
  2.0 8.7 %collective-permute-start.1 = (bf16[816,128]{1,0:T(8,128)(2,1)S(1)}, bf16[816,128]{1,0:T(8,128)(2,1)S(1)}, u32[]{:S(2)}, u32[]{:S(2)}) collective-permute-start(bf16[816,128]{1,0:T(8,128)(2,1)S(1)} %get-tuple-element.19), channel_id=1, source_target_pairs={{0,16},{16,0},{1,17},{17,1},{2,18},{18,2},{3,19},{19,3},{4,20},{20... | collective-permute-start | bytes 626696 | tf_op jit(solution)/shard_map/ppermute | solution.py:288
  5.0 5.7 %collective-permute-start.2 = (bf16[816,128]{1,0:T(8,128)(2,1)S(1)}, bf16[816,128]{1,0:T(8,128)(2,1)S(1)}, u32[]{:S(2)}, u32[]{:S(2)}) collective-permute-start(bf16[816,128]{1,0:T(8,128)(2,1)S(1)} %get-tuple-element.20), channel_id=1, source_target_pairs={{0,1},{1,0},{2,3},{3,2},{4,5},{5,4},{6,7},{7,6},{8,9},{9,8},{10,11... | collective-permute-start | bytes 626696 | tf_op jit(solution)/shard_map/ppermute | solution.py:283
  5.0 7.4 %collective-permute-start = (bf16[816,128]{1,0:T(8,128)(2,1)S(1)}, bf16[816,128]{1,0:T(8,128)(2,1)S(1)}, u32[]{:S(2)}, u32[]{:S(2)}) collective-permute-start(bf16[816,128]{1,0:T(8,128)(2,1)S(1)} %get-tuple-element.18), channel_id=1, source_target_pairs={{0,16},{1,2},{2,1},{3,4},{4,3},{5,6},{6,5},{7,8},{8,7},{9,10},{10,... | collective-permute-start | bytes 626696 | tf_op jit(solution)/shard_map/ppermute | solution.py:283
  13.2 7.2 %collective-permute-start.4 = (bf16[800,128]{1,0:T(8,128)(2,1)S(1)}, bf16[800,128]{1,0:T(8,128)(2,1)S(1)}, u32[]{:S(2)}, u32[]{:S(2)}) collective-permute-start(bf16[800,128]{1,0:T(8,128)(2,1)S(1)} %get-tuple-element.26), channel_id=1, source_target_pairs={{0,16},{16,0},{1,17},{17,1},{2,18},{18,2},{3,19},{19,3},{4,20},{20... | collective-permute-start | bytes 614408 | tf_op jit(solution)/shard_map/ppermute | solution.py:288
  15.0 5.4 %collective-permute-start.5 = (bf16[800,128]{1,0:T(8,128)(2,1)S(1)}, bf16[800,128]{1,0:T(8,128)(2,1)S(1)}, u32[]{:S(2)}, u32[]{:S(2)}) collective-permute-start(bf16[800,128]{1,0:T(8,128)(2,1)S(1)} %get-tuple-element.27), channel_id=1, source_target_pairs={{0,1},{1,0},{2,3},{3,2},{4,5},{5,4},{6,7},{7,6},{8,9},{9,8},{10,11... | collective-permute-start | bytes 614408 | tf_op jit(solution)/shard_map/ppermute | solution.py:283
  15.0 7.6 %collective-permute-start.3 = (bf16[800,128]{1,0:T(8,128)(2,1)S(1)}, bf16[800,128]{1,0:T(8,128)(2,1)S(1)}, u32[]{:S(2)}, u32[]{:S(2)}) collective-permute-start(bf16[800,128]{1,0:T(8,128)(2,1)S(1)} %get-tuple-element.25), channel_id=1, source_target_pairs={{0,16},{1,2},{2,1},{3,4},{4,3},{5,6},{6,5},{7,8},{8,7},{9,10},{10,... | collective-permute-start | bytes 614408 | tf_op jit(solution)/shard_map/ppermute | solution.py:283

commit v20 on v16

--- a/solution.py
+++ b/solution.py
@@ -115,7 +115,8 @@
     levels, cols, width = c_h.shape
     nedge = edge_h.shape[1]
     pitch = cols + 8
-    bounds = [(lo, min(lo + 16, levels)) for lo in range(0, levels, 16)]
+    whole = whole_rows(levels)
+    bounds = [(lo, lo + 16 if lo + 16 < whole else levels) for lo in range(0, whole, 16)]
     pairs = [(send_h, send_v), (recv_h, recv_v), (edge_h, edge_v)]
     pairs += [(c_h.at[pl.ds(lo, hi - lo)], c_v.at[pl.ds(lo, hi - lo)]) for lo, hi in bounds]
     pairs += [(nbr_h, nbr_v), (nw_h, nw_v), (sw_h, sw_v), (wet_h, wet_v)]
@@ -143,8 +144,7 @@
         for l in range(lo, hi):
             cf[l * pitch : l * pitch + cols, :] = c_v[l].astype(F32)
         pack_chunk(lo, levels, nedge, source, weights, rows_of, (0, 1, 2), (s0, s1, s2))
-    if levels % 16 == 0:
-        pack_chunk(levels, levels, nedge, source, weights, rows_of, (0, 1, 2), (s0, s1, s2))
+    pack_chunk(whole, levels, nedge, source, weights, rows_of, (0, 1, 2), (s0, s1, s2))
     for copy in copies[3 + len(bounds) :]:
         copy.wait()
 
@@ -243,7 +243,7 @@
     levels, cols, width = out_h.shape
     rows = vt_ref.shape[1]
     add_edges(((r1, t1),), levels, nedge, vt_ref, total)
-    bounds = [0, *range(4, levels, 8), levels]
+    bounds = [0, *range(8, levels - 8, 14), levels]
     copies = []
     for i, (lo, hi) in enumerate(zip(bounds, bounds[1:])):
         for l in range(lo, hi):

time: 23.5 us -> 23.5 us (level)
  no operation moved by 1% of the time
where the time goes in v20:
time: 23.5 us; the launch traced here: 23.3 us
  Pallas kernels  12.6 us (54%)
  waiting for transfers between devices  5.44 us (23%)
  starting transfers between devices  5.25 us (22%)
    pallas_call x7, Pallas kernels, call(): pl.pallas_call(kernel, out_shape=outs, in_specs=specs, out_specs=out_spec...  12.6 us
    ppermute x2, starting transfers between devices, along_basin(): return lax.ppermute(value, basin, [(i, (i + 1) % b) for i in range(b)])  4.81 us
    ppermute x4, waiting for transfers between devices, odd_or_even(): return lax.ppermute(value, (basin, blk), route)  3.69 us
    ppermute x2, waiting for transfers between devices, along_basin(): return lax.ppermute(value, basin, [(i, (i + 1) % b) for i in range(b)])  1.74 us
  transfers between devices with their start and end apart: 6, of which 4 were waited for; matrix products, arithmetic and copies ran while one was open for 0% of the time, Pallas kernels for 35%

profile of v20, /device:TPU:0, one launch (start us, length us, event | category | flops | bytes accessed | tf_op | source)
XLA Modules:
  0.0 23.3 jit_solution(8090042660773802750)
XLA Ops:
  0.0 2.0 %shard_map.91 = (bf16[816,128]{1,0:T(8,128)(2,1)S(1)}, bf16[816,128]{1,0:T(8,128)(2,1)S(1)}, bf16[816,128]{1,0:T(8,128)(2,1)S(1)}, bf16[50,128,128]{2,1,0:T(8,12...) custom-call(bf16[50,128,128]{2,1,0:T(8,128)(2,1)} %bitcast.5, ...), custom_call_target="tpu_custom_call" | custom-call | bytes 4240128 | tf_op jit(solution)/shard_map/pallas_call | solution.py:264
  2.0 3.0 %collective-permute-start.1 = (bf16[816,128]{1,0:T(8,128)(2,1)S(1)}, bf16[816,128]{1,0:T(8,128)(2,1)S(1)}, u32[]{:S(2)}, u32[]{:S(2)}) collective-permute-start(bf16[816,128]{1,0:T(8,128)(2,1)S(1)} %get-tuple-element.23), channel_id=1, source_target_pairs={{0,16},{16,0},{1,17},{17,1},{2,18},{18,2},{3,19},{19,3},{4,20},{20... | collective-permute-start | bytes 626696 | tf_op jit(solution)/shard_map/ppermute | solution.py:287
  5.0 0.0 collective-permute-start.2
  5.0 0.2 collective-permute-start
  5.2 4.6 %shard_map.92 = (bf16[25,128,256]{2,1,0:T(8,128)(2,1)S(1)}, f32[7168,128]{1,0:T(8,128)S(1)}, bf16[128,56,128]{2,1,0:T(8,128)(2,1)S(1)}) custom-call(bf16[50,128,128]{2,1,0:T(8,128)(2,1)S(1)} %get-tuple-element.25.c_ref, s32[4,128]{1,0:T(4,128)S(1)} %get-tuple-element.26.nbr_ref, f32[50,4,128]{2,1,0:T(4,128)S(1)} %get-tuple-element.27.nw_ref, ...), custom_call_target="tpu_custom_call" | custom-call | flops 312475648 | bytes 9552384 | tf_op jit(solution)/shard_map/pallas_call | solution.py:264
  9.8 0.4 %collective-permute-done.1.r0.t0 = bf16[816,128]{1,0:T(8,128)(2,1)S(1)} collective-permute-done((bf16[816,128]{1,0:T(8,128)(2,1)S(1)}, bf16[816,128]{1,0:T(8,128)(2,1)S(1)}, u32[]{:S(2)}, u32[]{:S(2)}) %collective-permute-start.1) | collective-permute-done | bytes 208928 | tf_op jit(solution)/shard_map/ppermute | solution.py:287
  10.2 0.0 collective-permute-done.2.r2.t2
  10.2 0.4 %shard_map.93.local_ref = f32[7168,128]{1,0:T(8,128)S(1)} custom-call(bf16[816,128]{1,0:T(8,128)(2,1)S(1)} %collective-permute-done.1.r0.t0, bf16[816,128]{1,0:T(8,128)(2,1)S(1)} %collective-permute-done.2.r2.t2, bf16[816,128]{1,0:T(8,128)(2,1)S(1)} %collective-permute-done.1.r0.t0, ...), custom_call_target="tpu_custom_call", output_to_operand_aliasing={{}: (4, {})} | custom-call | flops 25690112 | bytes 10010624 | tf_op jit(solution)/shard_map/pallas_call | solution.py:264
  10.6 1.9 %collective-permute-done.r1.t1 = bf16[816,128]{1,0:T(8,128)(2,1)S(1)} collective-permute-done((bf16[816,128]{1,0:T(8,128)(2,1)S(1)}, bf16[816,128]{1,0:T(8,128)(2,1)S(1)}, u32[]{:S(2)}, u32[]{:S(2)}) %collective-permute-start) | collective-permute-done | bytes 208928 | tf_op jit(solution)/shard_map/ppermute | solution.py:282
  12.4 0.7 %shard_map.94 = (f32[7168,128]{1,0:T(8,128)S(1)}, bf16[800,128]{1,0:T(8,128)(2,1)S(1)}, bf16[800,128]{1,0:T(8,128)(2,1)S(1)}, bf16[800,128]{1,0:T(8,128)(2,1)S(1)}) custom-call(bf16[816,128]{1,0:T(8,128)(2,1)S(1)} %collective-permute-done.r1.t1, f32[7168,128]{1,0:T(8,128)S(1)} %shard_map.93.local_ref, ...), custom_call_target="tpu_custom_call", output_to_operand_aliasing={{0}: (1, {})} | custom-call | flops 12845056 | bytes 10063872 | tf_op jit(solution)/shard_map/pallas_call | solution.py:264
  13.1 1.8 %collective-permute-start.4 = (bf16[800,128]{1,0:T(8,128)(2,1)S(1)}, bf16[800,128]{1,0:T(8,128)(2,1)S(1)}, u32[]{:S(2)}, u32[]{:S(2)}) collective-permute-start(bf16[800,128]{1,0:T(8,128)(2,1)S(1)} %get-tuple-element.34), channel_id=1, source_target_pairs={{0,16},{16,0},{1,17},{17,1},{2,18},{18,2},{3,19},{19,3},{4,20},{20... | collective-permute-start | bytes 614408 | tf_op jit(solution)/shard_map/ppermute | solution.py:287
  14.9 0.0 collective-permute-start.5
  15.0 0.3 %collective-permute-start.3 = (bf16[800,128]{1,0:T(8,128)(2,1)S(1)}, bf16[800,128]{1,0:T(8,128)(2,1)S(1)}, u32[]{:S(2)}, u32[]{:S(2)}) collective-permute-start(bf16[800,128]{1,0:T(8,128)(2,1)S(1)} %get-tuple-element.33), channel_id=1, source_target_pairs={{0,16},{1,2},{2,1},{3,4},{4,3},{5,6},{6,5},{7,8},{8,7},{9,10},{10,... | collective-permute-start | bytes 614408 | tf_op jit(solution)/shard_map/ppermute | solution.py:282
  15.2 2.8 %shard_map.95.local_ref = f32[7168,128]{1,0:T(8,128)S(1)} custom-call(f32[7168,128]{1,0:T(8,128)S(1)} %get-tuple-element.36.cs, bf16[25,128,256]{2,1,0:T(8,128)(2,1)S(1)} %get-tuple-element.37.a_ref, bf16[128,56,128]{2,1,0:T(8,128)(2,1)S(1)} %get-tuple-element.31.vt_ref), custom_call_target="tpu_custom_call" | custom-call | flops 312475648 | bytes 10813440 | tf_op jit(solution)/shard_map/pallas_call | solution.py:264
  18.1 1.4 %collective-permute-done.4.r0 = bf16[800,128]{1,0:T(8,128)(2,1)S(1)} collective-permute-done((bf16[800,128]{1,0:T(8,128)(2,1)S(1)}, bf16[800,128]{1,0:T(8,128)(2,1)S(1)}, u32[]{:S(2)}, u32[]{:S(2)}) %collective-permute-start.4) | collective-permute-done | bytes 204832 | tf_op jit(solution)/shard_map/ppermute | solution.py:287
  19.5 0.0 collective-permute-done.5.r2
  19.5 0.4 %shard_map.96.local_ref = f32[7168,128]{1,0:T(8,128)S(1)} custom-call(bf16[800,128]{1,0:T(8,128)(2,1)S(1)} %collective-permute-done.4.r0, bf16[800,128]{1,0:T(8,128)(2,1)S(1)} %collective-permute-done.5.r2, bf16[816,128]{1,0:T(8,128)(2,1)S(1)} %collective-permute-done.1.r0.t0, ...), custom_call_target="tpu_custom_call", output_to_operand_aliasing={{}: (4, {})} | custom-call | flops 25690112 | bytes 10002432 | tf_op jit(solution)/shard_map/pallas_call | solution.py:264
  19.8 1.8 %collective-permute-done.3.r1 = bf16[800,128]{1,0:T(8,128)(2,1)S(1)} collective-permute-done((bf16[800,128]{1,0:T(8,128)(2,1)S(1)}, bf16[800,128]{1,0:T(8,128)(2,1)S(1)}, u32[]{:S(2)}, u32[]{:S(2)}) %collective-permute-start.3) | collective-permute-done | bytes 204832 | tf_op jit(solution)/shard_map/ppermute | solution.py:282
  21.7 1.6 %shard_map.97 = (bf16[50,128,128]{2,1,0:T(8,128)(2,1)}, f32[7168,128]{1,0:T(8,128)S(1)}) custom-call(bf16[800,128]{1,0:T(8,128)(2,1)S(1)} %collective-permute-done.3.r1, bf16[816,128]{1,0:T(8,128)(2,1)S(1)} %collective-permute-done.r1.t1, f32[7168,128]{1,0:T(8,128)S(1)} %shard_map.96.local_ref, ...), custom_call_target="tpu_custom_call", output_to_operand_aliasing={{1}: (2, {})} | custom-call | flops 12845056 | bytes 11227136 | tf_op jit(solution)/shard_map/pallas_call | solution.py:264
Async XLA Ops:
  2.0 8.2 %collective-permute-start.1 = (bf16[816,128]{1,0:T(8,128)(2,1)S(1)}, bf16[816,128]{1,0:T(8,128)(2,1)S(1)}, u32[]{:S(2)}, u32[]{:S(2)}) collective-permute-start(bf16[816,128]{1,0:T(8,128)(2,1)S(1)} %get-tuple-element.23), channel_id=1, source_target_pairs={{0,16},{16,0},{1,17},{17,1},{2,18},{18,2},{3,19},{19,3},{4,20},{20... | collective-permute-start | bytes 626696 | tf_op jit(solution)/shard_map/ppermute | solution.py:287
  5.0 5.2 %collective-permute-start.2 = (bf16[816,128]{1,0:T(8,128)(2,1)S(1)}, bf16[816,128]{1,0:T(8,128)(2,1)S(1)}, u32[]{:S(2)}, u32[]{:S(2)}) collective-permute-start(bf16[816,128]{1,0:T(8,128)(2,1)S(1)} %get-tuple-element.24), channel_id=1, source_target_pairs={{0,1},{1,0},{2,3},{3,2},{4,5},{5,4},{6,7},{7,6},{8,9},{9,8},{10,11... | collective-permute-start | bytes 626696 | tf_op jit(solution)/shard_map/ppermute | solution.py:282
  5.0 7.4 %collective-permute-start = (bf16[816,128]{1,0:T(8,128)(2,1)S(1)}, bf16[816,128]{1,0:T(8,128)(2,1)S(1)}, u32[]{:S(2)}, u32[]{:S(2)}) collective-permute-start(bf16[816,128]{1,0:T(8,128)(2,1)S(1)} %get-tuple-element.22), channel_id=1, source_target_pairs={{0,16},{1,2},{2,1},{3,4},{4,3},{5,6},{6,5},{7,8},{8,7},{9,10},{10,... | collective-permute-start | bytes 626696 | tf_op jit(solution)/shard_map/ppermute | solution.py:282
  13.1 6.3 %collective-permute-start.4 = (bf16[800,128]{1,0:T(8,128)(2,1)S(1)}, bf16[800,128]{1,0:T(8,128)(2,1)S(1)}, u32[]{:S(2)}, u32[]{:S(2)}) collective-permute-start(bf16[800,128]{1,0:T(8,128)(2,1)S(1)} %get-tuple-element.34), channel_id=1, source_target_pairs={{0,16},{16,0},{1,17},{17,1},{2,18},{18,2},{3,19},{19,3},{4,20},{20... | collective-permute-start | bytes 614408 | tf_op jit(solution)/shard_map/ppermute | solution.py:287
  14.9 4.5 %collective-permute-start.5 = (bf16[800,128]{1,0:T(8,128)(2,1)S(1)}, bf16[800,128]{1,0:T(8,128)(2,1)S(1)}, u32[]{:S(2)}, u32[]{:S(2)}) collective-permute-start(bf16[800,128]{1,0:T(8,128)(2,1)S(1)} %get-tuple-element.35), channel_id=1, source_target_pairs={{0,1},{1,0},{2,3},{3,2},{4,5},{5,4},{6,7},{7,6},{8,9},{9,8},{10,11... | collective-permute-start | bytes 614408 | tf_op jit(solution)/shard_map/ppermute | solution.py:282
  15.0 6.7 %collective-permute-start.3 = (bf16[800,128]{1,0:T(8,128)(2,1)S(1)}, bf16[800,128]{1,0:T(8,128)(2,1)S(1)}, u32[]{:S(2)}, u32[]{:S(2)}) collective-permute-start(bf16[800,128]{1,0:T(8,128)(2,1)S(1)} %get-tuple-element.33), channel_id=1, source_target_pairs={{0,16},{1,2},{2,1},{3,4},{4,3},{5,6},{6,5},{7,8},{8,7},{9,10},{10,... | collective-permute-start | bytes 614408 | tf_op jit(solution)/shard_map/ppermute | solution.py:282

commit v21 on v20

--- a/solution.py
+++ b/solution.py
@@ -243,7 +243,7 @@
     levels, cols, width = out_h.shape
     rows = vt_ref.shape[1]
     add_edges(((r1, t1),), levels, nedge, vt_ref, total)
-    bounds = [0, *range(8, levels - 8, 14), levels]
+    bounds = [0, *range(4, levels, 8), levels]
     copies = []
     for i, (lo, hi) in enumerate(zip(bounds, bounds[1:])):
         for l in range(lo, hi):

time: 23.5 us -> 23.4 us (level)
  no operation moved by 1% of the time
where the time goes in v21:
time: 23.4 us; the launch traced here: 23.3 us
  Pallas kernels  12.5 us (53%)
  waiting for transfers between devices  5.46 us (23%)
  starting transfers between devices  5.25 us (22%)
    pallas_call x7, Pallas kernels, call(): pl.pallas_call(kernel, out_shape=outs, in_specs=specs, out_specs=out_spec...  12.5 us
    ppermute x2, starting transfers between devices, along_basin(): return lax.ppermute(value, basin, [(i, (i + 1) % b) for i in range(b)])  4.81 us
    ppermute x4, waiting for transfers between devices, odd_or_even(): return lax.ppermute(value, (basin, blk), route)  3.7 us
    ppermute x2, waiting for transfers between devices, along_basin(): return lax.ppermute(value, basin, [(i, (i + 1) % b) for i in range(b)])  1.76 us
  transfers between devices with their start and end apart: 6, of which 4 were waited for; matrix products, arithmetic and copies ran while one was open for 0% of the time, Pallas kernels for 35%

profile of v21, /device:TPU:0, one launch (start us, length us, event | category | flops | bytes accessed | tf_op | source)
XLA Modules:
  0.0 23.3 jit_solution(348041214358198747)
XLA Ops:
  0.0 2.0 %shard_map.91 = (bf16[816,128]{1,0:T(8,128)(2,1)S(1)}, bf16[816,128]{1,0:T(8,128)(2,1)S(1)}, bf16[816,128]{1,0:T(8,128)(2,1)S(1)}, bf16[50,128,128]{2,1,0:T(8,12...) custom-call(bf16[50,128,128]{2,1,0:T(8,128)(2,1)} %bitcast.5, ...), custom_call_target="tpu_custom_call" | custom-call | bytes 4240128 | tf_op jit(solution)/shard_map/pallas_call | solution.py:264
  2.0 3.0 %collective-permute-start.1 = (bf16[816,128]{1,0:T(8,128)(2,1)S(1)}, bf16[816,128]{1,0:T(8,128)(2,1)S(1)}, u32[]{:S(2)}, u32[]{:S(2)}) collective-permute-start(bf16[816,128]{1,0:T(8,128)(2,1)S(1)} %get-tuple-element.23), channel_id=1, source_target_pairs={{0,16},{16,0},{1,17},{17,1},{2,18},{18,2},{3,19},{19,3},{4,20},{20... | collective-permute-start | bytes 626696 | tf_op jit(solution)/shard_map/ppermute | solution.py:287
  5.0 0.0 collective-permute-start.2
  5.0 0.2 collective-permute-start
  5.2 4.6 %shard_map.92 = (bf16[25,128,256]{2,1,0:T(8,128)(2,1)S(1)}, f32[7168,128]{1,0:T(8,128)S(1)}, bf16[128,56,128]{2,1,0:T(8,128)(2,1)S(1)}) custom-call(bf16[50,128,128]{2,1,0:T(8,128)(2,1)S(1)} %get-tuple-element.25.c_ref, s32[4,128]{1,0:T(4,128)S(1)} %get-tuple-element.26.nbr_ref, f32[50,4,128]{2,1,0:T(4,128)S(1)} %get-tuple-element.27.nw_ref, ...), custom_call_target="tpu_custom_call" | custom-call | flops 312475648 | bytes 9552384 | tf_op jit(solution)/shard_map/pallas_call | solution.py:264
  9.8 0.4 %collective-permute-done.1.r0.t0 = bf16[816,128]{1,0:T(8,128)(2,1)S(1)} collective-permute-done((bf16[816,128]{1,0:T(8,128)(2,1)S(1)}, bf16[816,128]{1,0:T(8,128)(2,1)S(1)}, u32[]{:S(2)}, u32[]{:S(2)}) %collective-permute-start.1) | collective-permute-done | bytes 208928 | tf_op jit(solution)/shard_map/ppermute | solution.py:287
  10.2 0.0 collective-permute-done.2.r2.t2
  10.2 0.4 %shard_map.93.local_ref = f32[7168,128]{1,0:T(8,128)S(1)} custom-call(bf16[816,128]{1,0:T(8,128)(2,1)S(1)} %collective-permute-done.1.r0.t0, bf16[816,128]{1,0:T(8,128)(2,1)S(1)} %collective-permute-done.2.r2.t2, bf16[816,128]{1,0:T(8,128)(2,1)S(1)} %collective-permute-done.1.r0.t0, ...), custom_call_target="tpu_custom_call", output_to_operand_aliasing={{}: (4, {})} | custom-call | flops 25690112 | bytes 10010624 | tf_op jit(solution)/shard_map/pallas_call | solution.py:264
  10.6 1.9 %collective-permute-done.r1.t1 = bf16[816,128]{1,0:T(8,128)(2,1)S(1)} collective-permute-done((bf16[816,128]{1,0:T(8,128)(2,1)S(1)}, bf16[816,128]{1,0:T(8,128)(2,1)S(1)}, u32[]{:S(2)}, u32[]{:S(2)}) %collective-permute-start) | collective-permute-done | bytes 208928 | tf_op jit(solution)/shard_map/ppermute | solution.py:282
  12.4 0.7 %shard_map.94 = (f32[7168,128]{1,0:T(8,128)S(1)}, bf16[800,128]{1,0:T(8,128)(2,1)S(1)}, bf16[800,128]{1,0:T(8,128)(2,1)S(1)}, bf16[800,128]{1,0:T(8,128)(2,1)S(1)}) custom-call(bf16[816,128]{1,0:T(8,128)(2,1)S(1)} %collective-permute-done.r1.t1, f32[7168,128]{1,0:T(8,128)S(1)} %shard_map.93.local_ref, ...), custom_call_target="tpu_custom_call", output_to_operand_aliasing={{0}: (1, {})} | custom-call | flops 12845056 | bytes 10063872 | tf_op jit(solution)/shard_map/pallas_call | solution.py:264
  13.1 1.8 %collective-permute-start.4 = (bf16[800,128]{1,0:T(8,128)(2,1)S(1)}, bf16[800,128]{1,0:T(8,128)(2,1)S(1)}, u32[]{:S(2)}, u32[]{:S(2)}) collective-permute-start(bf16[800,128]{1,0:T(8,128)(2,1)S(1)} %get-tuple-element.34), channel_id=1, source_target_pairs={{0,16},{16,0},{1,17},{17,1},{2,18},{18,2},{3,19},{19,3},{4,20},{20... | collective-permute-start | bytes 614408 | tf_op jit(solution)/shard_map/ppermute | solution.py:287
  14.9 0.0 collective-permute-start.5
  14.9 0.3 %collective-permute-start.3 = (bf16[800,128]{1,0:T(8,128)(2,1)S(1)}, bf16[800,128]{1,0:T(8,128)(2,1)S(1)}, u32[]{:S(2)}, u32[]{:S(2)}) collective-permute-start(bf16[800,128]{1,0:T(8,128)(2,1)S(1)} %get-tuple-element.33), channel_id=1, source_target_pairs={{0,16},{1,2},{2,1},{3,4},{4,3},{5,6},{6,5},{7,8},{8,7},{9,10},{10,... | collective-permute-start | bytes 614408 | tf_op jit(solution)/shard_map/ppermute | solution.py:282
  15.2 2.8 %shard_map.95.local_ref = f32[7168,128]{1,0:T(8,128)S(1)} custom-call(f32[7168,128]{1,0:T(8,128)S(1)} %get-tuple-element.36.cs, bf16[25,128,256]{2,1,0:T(8,128)(2,1)S(1)} %get-tuple-element.37.a_ref, bf16[128,56,128]{2,1,0:T(8,128)(2,1)S(1)} %get-tuple-element.31.vt_ref), custom_call_target="tpu_custom_call" | custom-call | flops 312475648 | bytes 10813440 | tf_op jit(solution)/shard_map/pallas_call | solution.py:264
  18.1 1.4 %collective-permute-done.4.r0 = bf16[800,128]{1,0:T(8,128)(2,1)S(1)} collective-permute-done((bf16[800,128]{1,0:T(8,128)(2,1)S(1)}, bf16[800,128]{1,0:T(8,128)(2,1)S(1)}, u32[]{:S(2)}, u32[]{:S(2)}) %collective-permute-start.4) | collective-permute-done | bytes 204832 | tf_op jit(solution)/shard_map/ppermute | solution.py:287
  19.5 0.0 collective-permute-done.5.r2
  19.5 0.4 %shard_map.96.local_ref = f32[7168,128]{1,0:T(8,128)S(1)} custom-call(bf16[800,128]{1,0:T(8,128)(2,1)S(1)} %collective-permute-done.4.r0, bf16[800,128]{1,0:T(8,128)(2,1)S(1)} %collective-permute-done.5.r2, bf16[816,128]{1,0:T(8,128)(2,1)S(1)} %collective-permute-done.1.r0.t0, ...), custom_call_target="tpu_custom_call", output_to_operand_aliasing={{}: (4, {})} | custom-call | flops 25690112 | bytes 10002432 | tf_op jit(solution)/shard_map/pallas_call | solution.py:264
  19.9 1.8 %collective-permute-done.3.r1 = bf16[800,128]{1,0:T(8,128)(2,1)S(1)} collective-permute-done((bf16[800,128]{1,0:T(8,128)(2,1)S(1)}, bf16[800,128]{1,0:T(8,128)(2,1)S(1)}, u32[]{:S(2)}, u32[]{:S(2)}) %collective-permute-start.3) | collective-permute-done | bytes 204832 | tf_op jit(solution)/shard_map/ppermute | solution.py:282
  21.7 1.6 %shard_map.97 = (bf16[50,128,128]{2,1,0:T(8,128)(2,1)}, f32[7168,128]{1,0:T(8,128)S(1)}) custom-call(bf16[800,128]{1,0:T(8,128)(2,1)S(1)} %collective-permute-done.3.r1, bf16[816,128]{1,0:T(8,128)(2,1)S(1)} %collective-permute-done.r1.t1, f32[7168,128]{1,0:T(8,128)S(1)} %shard_map.96.local_ref, ...), custom_call_target="tpu_custom_call", output_to_operand_aliasing={{1}: (2, {})} | custom-call | flops 12845056 | bytes 11227136 | tf_op jit(solution)/shard_map/pallas_call | solution.py:264
Async XLA Ops:
  2.0 8.2 %collective-permute-start.1 = (bf16[816,128]{1,0:T(8,128)(2,1)S(1)}, bf16[816,128]{1,0:T(8,128)(2,1)S(1)}, u32[]{:S(2)}, u32[]{:S(2)}) collective-permute-start(bf16[816,128]{1,0:T(8,128)(2,1)S(1)} %get-tuple-element.23), channel_id=1, source_target_pairs={{0,16},{16,0},{1,17},{17,1},{2,18},{18,2},{3,19},{19,3},{4,20},{20... | collective-permute-start | bytes 626696 | tf_op jit(solution)/shard_map/ppermute | solution.py:287
  5.0 5.2 %collective-permute-start.2 = (bf16[816,128]{1,0:T(8,128)(2,1)S(1)}, bf16[816,128]{1,0:T(8,128)(2,1)S(1)}, u32[]{:S(2)}, u32[]{:S(2)}) collective-permute-start(bf16[816,128]{1,0:T(8,128)(2,1)S(1)} %get-tuple-element.24), channel_id=1, source_target_pairs={{0,1},{1,0},{2,3},{3,2},{4,5},{5,4},{6,7},{7,6},{8,9},{9,8},{10,11... | collective-permute-start | bytes 626696 | tf_op jit(solution)/shard_map/ppermute | solution.py:282
  5.0 7.4 %collective-permute-start = (bf16[816,128]{1,0:T(8,128)(2,1)S(1)}, bf16[816,128]{1,0:T(8,128)(2,1)S(1)}, u32[]{:S(2)}, u32[]{:S(2)}) collective-permute-start(bf16[816,128]{1,0:T(8,128)(2,1)S(1)} %get-tuple-element.22), channel_id=1, source_target_pairs={{0,16},{1,2},{2,1},{3,4},{4,3},{5,6},{6,5},{7,8},{8,7},{9,10},{10,... | collective-permute-start | bytes 626696 | tf_op jit(solution)/shard_map/ppermute | solution.py:282
  13.1 6.3 %collective-permute-start.4 = (bf16[800,128]{1,0:T(8,128)(2,1)S(1)}, bf16[800,128]{1,0:T(8,128)(2,1)S(1)}, u32[]{:S(2)}, u32[]{:S(2)}) collective-permute-start(bf16[800,128]{1,0:T(8,128)(2,1)S(1)} %get-tuple-element.34), channel_id=1, source_target_pairs={{0,16},{16,0},{1,17},{17,1},{2,18},{18,2},{3,19},{19,3},{4,20},{20... | collective-permute-start | bytes 614408 | tf_op jit(solution)/shard_map/ppermute | solution.py:287
  14.9 4.5 %collective-permute-start.5 = (bf16[800,128]{1,0:T(8,128)(2,1)S(1)}, bf16[800,128]{1,0:T(8,128)(2,1)S(1)}, u32[]{:S(2)}, u32[]{:S(2)}) collective-permute-start(bf16[800,128]{1,0:T(8,128)(2,1)S(1)} %get-tuple-element.35), channel_id=1, source_target_pairs={{0,1},{1,0},{2,3},{3,2},{4,5},{5,4},{6,7},{7,6},{8,9},{9,8},{10,11... | collective-permute-start | bytes 614408 | tf_op jit(solution)/shard_map/ppermute | solution.py:282
  14.9 6.7 %collective-permute-start.3 = (bf16[800,128]{1,0:T(8,128)(2,1)S(1)}, bf16[800,128]{1,0:T(8,128)(2,1)S(1)}, u32[]{:S(2)}, u32[]{:S(2)}) collective-permute-start(bf16[800,128]{1,0:T(8,128)(2,1)S(1)} %get-tuple-element.33), channel_id=1, source_target_pairs={{0,16},{1,2},{2,1},{3,4},{4,3},{5,6},{6,5},{7,8},{8,7},{9,10},{10,... | collective-permute-start | bytes 614408 | tf_op jit(solution)/shard_map/ppermute | solution.py:282
